TPU v7x, 32 devices: a whole 2x2x4 slice. The times are simulated.
32 devices in a mesh: group: 2 (over x), batch: 8 (over z, y), mp: 2 (over core).
Axes of the slice: x: 2, y: 2, z: 4, core: 2. Of those that a mesh axis runs over, the one named last changes fastest.
Arguments:
- tokens: bfloat16 [256, 6144], P(('group', 'batch'), 'mp'), parts along dimension 0, may hold values from -6 to 6
- expert_ids: int32 [256, 2], P(('group', 'batch')), parts along dimension 0, may hold values from 0 to 3, all different within a row; in each aligned block of 128 rows (0 to 127, 128 to 255, ...) at most 96 rows name the same one
- router: bfloat16 [6144, 4], P('mp'), may hold values from -0.15625 to 0.15625
- w_gate: bfloat16 [4, 8192, 6144], P(None, 'batch', 'mp'), may hold values from -0.078125 to 0.078125
- w_up: bfloat16 [4, 8192, 6144], P(None, 'batch', 'mp'), may hold values from -0.078125 to 0.078125
- w_down: bfloat16 [4, 8192, 6144], P(None, 'batch', 'mp'), may hold values from -0.0625 to 0.0625
Outputs:
- expert_output: bfloat16 [256, 6144], P(('group', 'batch'), 'mp'), parts along dimension 0
There are 2 independent parts, one for each index of `group`. A program takes and returns all parts, laid end to end along the dimension named above; an argument that names none is the same for every part. Nothing has to cross between parts.
Inputs may be any that keep to these rules, and one draw needn't show every extreme that they name: `expert_ids`: each token names two different experts; no expert is named by more than 96 tokens of a replica, a bound that some block reaches.
All inputs are finite; a program needn't handle non-finite values.
Results may differ from a plain program's by a relative error of at most 0.0051.
Values may be sent and summed in bfloat16 or wider, within the bound.
No kernel may reach another device: no remote copies, remote signals or barrier semaphores. Data moves between devices by JAX's collectives and lax.ppermute only.
A program may use at most 192 MiB of HBM per device.

v0:
```python
import jax
import jax.numpy as jnp
from jax import lax
from jax.sharding import PartitionSpec as P


def per_device(tokens, expert_ids, router, w_gate, w_up, w_down):
    gathered, all_ids = (
        lax.all_gather(tokens, "batch", axis=0, tiled=True),
        lax.all_gather(expert_ids, "batch", axis=0, tiled=True),
    )
    token_count = gathered.shape[0]
    half_width = gathered.shape[1]
    experts = w_gate.shape[0]
    capacity = 3 * token_count // 4
    pair_expert = all_ids.reshape(-1)
    onehot = (pair_expert[:, None] == jnp.arange(experts, dtype=jnp.int32)[None, :]).astype(
        jnp.int32
    )
    position = jnp.sum((jnp.cumsum(onehot, axis=0) - 1) * onehot, axis=1)
    pair_token = jnp.arange(2 * token_count, dtype=jnp.int32) // 2
    slot_token = (
        jnp.full((experts, capacity), token_count, jnp.int32)
        .at[pair_expert, position]
        .set(pair_token)
    )
    slot_rows = jnp.take(gathered, jnp.minimum(slot_token, token_count - 1), axis=0)
    logit_part = jnp.dot(gathered, router, preferred_element_type=jnp.float32)
    gate_part = jnp.einsum("ecd,efd->ecf", slot_rows, w_gate, preferred_element_type=jnp.float32)
    up_part = jnp.einsum("ecd,efd->ecf", slot_rows, w_up, preferred_element_type=jnp.float32)
    logits, gate_sum, up_sum = lax.psum((logit_part, gate_part, up_part), "mp")
    chosen = jnp.take_along_axis(logits, all_ids, axis=1)
    weights = 1.0 / (1.0 + jnp.exp(chosen[:, ::-1] - chosen))
    slot_weight = (
        jnp.zeros((experts, capacity), jnp.float32)
        .at[pair_expert, position]
        .set(weights.reshape(-1))
    )
    hidden = (jax.nn.silu(gate_sum) * up_sum).astype(jnp.bfloat16)
    slot_out = (
        jnp.einsum("ecf,efd->ecd", hidden, w_down, preferred_element_type=jnp.float32)
        * slot_weight[:, :, None]
    )
    partial_value = (
        jnp.zeros((token_count, half_width), jnp.float32)
        .at[slot_token.reshape(-1)]
        .add(slot_out.reshape(-1, half_width), mode="drop")
    )
    mine = lax.psum_scatter(partial_value, "batch", scatter_dimension=0, tiled=True)
    return mine.astype(jnp.bfloat16)


def solution(mesh):
    in_specs = (
        P(("group", "batch"), "mp"),
        P(("group", "batch"), None),
        P("mp", None),
        P(None, "batch", "mp"),
        P(None, "batch", "mp"),
        P(None, "batch", "mp"),
    )
    out_specs = P(("group", "batch"), "mp")
    return jax.shard_map(
        per_device, mesh=mesh, in_specs=in_specs, out_specs=out_specs, check_vma=False
    )
```

profile of v0, /device:TPU:0, one launch (start us, length us, event | category | flops | bytes accessed | tf_op | source)
XLA Modules:
  0.0 226.0 jit_solution(3821804650792053160)
XLA Ops:
  6.5 0.0 copy-start
  6.5 0.0 copy-start.2
  6.5 0.0 all-reduce.3.cloned.1.call-start
  6.5 22.6 %all-gather = s32[8,16,2]{1,2,0:T(2,128)S(1)} all-gather(s32[1,16,2]{1,2,0:T(2,128)} %bitcast.40), channel_id=1, replica_groups=mesh['group'=2,'batch'=8,'mp'=2] {'batch'}, dimensions={0}, use_global_device_ids=true | all-gather | bytes 1152 | tf_op jit(solution)/shard_map/all_gather | solution.py:10
  29.2 0.1 copy.18
  29.3 0.1 eq.29
  29.5 0.1 eq.25
  29.6 0.1 reshape.115
  29.8 1.2 reduce-window.6
  31.0 0.1 slice.16
  31.1 0.1 copy.21
  31.2 0.1 copy.22
  31.3 0.1 add_bitcast_fusion
  31.4 11.4 %scatter_fusion = s32[4,96]{1,0:T(4,128)S(1)} fusion(s32[4,96]{1,0:T(4,128)S(1)} %broadcast_in_dim.33, s32[256]{0:T(256)S(1)} %bitcast.33, s32[256]{0:T(256)S(1)} %and_select_fusion.1), kind=kCustom, calls=%fused_computation.2 | custom fusion | bytes 5120 | tf_op jit(solution)/shard_map/scatter | solution.py:25
  42.9 0.1 reshape.123
  43.0 0.0 copy-done.2
  43.0 32.3 %all_gather.7 = bf16[128,3072]{1,0:T(8,128)(2,1)S(1)} all-gather(bf16[16,3072]{1,0:T(8,128)(2,1)S(1)} %copy-done.2), channel_id=1, replica_groups=mesh['group'=2,'batch'=8,'mp'=2] {'batch'}, dimensions={0}, use_global_device_ids=true | all-gather | bytes 884736 | tf_op jit(solution)/shard_map/all_gather | solution.py:9
  75.3 2.9 %gather_fusion = bf16[384,3072]{1,0:T(8,128)(2,1)S(1)} fusion(bf16[128,3072]{1,0:T(8,128)(2,1)S(1)} %all_gather.7, s32[1024]{0:T(1024)S(1)} %pad_clamp_fusion), kind=kCustom, calls=%fused_computation | custom fusion | bytes 4720128 | tf_op jit(solution)/shard_map/jit(_take)/gather | solution.py:27
  78.2 13.7 %fusion = f32[4,96,1024]{2,1,0:T(8,128)} fusion(bf16[4,1024,3072]{2,1,0:T(8,128)(2,1)} %param.10, bf16[4,96,3072]{2,1,0:T(8,128)(2,1)S(1)} %bitcast.35, pred[4,96]{1,0:T(4,128)(4,1)S(1)} %compare_and_fusion), kind=kOutput, calls=%fused_computation.7 | convolution fusion | flops 2417098752 | bytes 29098368 | tf_op jit(solution)/shard_map/ecd,efd->ecf/dot_general | solution.py:30
  91.9 13.7 %fusion.1 = f32[4,96,1024]{2,1,0:T(8,128)} fusion(bf16[4,1024,3072]{2,1,0:T(8,128)(2,1)} %param.9, bf16[4,96,3072]{2,1,0:T(8,128)(2,1)S(1)} %bitcast.36, pred[4,96]{1,0:T(4,128)(4,1)S(1)} %compare_and_fusion), kind=kOutput, calls=%fused_computation.8 | convolution fusion | flops 2417098752 | bytes 29098368 | tf_op jit(solution)/shard_map/ecd,efd->ecf/dot_general | solution.py:29
  105.5 0.0 all-reduce.3.cloned.1.call-update
  105.5 0.0 reduce-scatter.2.cloned.1.call-start
  105.6 0.1 reshape.117
  105.7 0.1 reshape.163
  105.8 0.1 copy.24
  105.9 0.1 reshape.129
  106.0 0.0 copy-done
  106.0 0.3 fusion.14
  106.3 2.6 %psum.23 = f32[128,4]{0,1:T(4,128)S(1)} all-reduce(f32[128,4]{0,1:T(4,128)S(1)} %fusion.14), channel_id=1, replica_groups=mesh['group'=2,'batch'=8,'mp'=2] {'mp'}, use_global_device_ids=true, to_apply=%region_6.7 | all-reduce | flops 512 | bytes 4096 | tf_op jit(solution)/shard_map/psum | solution.py:31
  109.0 2.4 %gather_fusion.1 = f32[256]{0:T(256)S(1)} fusion(f32[128,4]{0,1:T(4,128)S(1)} %psum.23, s32[256]{0:T(256)S(1)} %reshape.129), kind=kCustom, calls=%fused_computation.1 | custom fusion | bytes 4096 | tf_op jit(solution)/shard_map/jit(take_along_axis)/gather | solution.py:32
  111.4 0.1 reshape.132
  111.5 0.1 copy.25
  111.6 0.1 copy.26
  111.8 0.1 reshape.143
  111.9 11.4 %scatter_fusion.1 = f32[4,96]{1,0:T(4,128)S(1)} fusion(f32[4,96]{1,0:T(4,128)S(1)} %broadcast_in_dim.37, s32[256]{0:T(256)S(1)} %bitcast.34, f32[256]{0:T(256)S(1)} %reshape.143), kind=kCustom, calls=%fused_computation.3 | custom fusion | bytes 5120 | tf_op jit(solution)/shard_map/scatter | solution.py:37
  123.4 2.8 %all-reduce.3.cloned.1.call-done = (f32[4,96,1024]{2,1,0:T(8,128)}, f32[4,96,1024]{2,1,0:T(8,128)}) async-done(((f32[4,96,1024]{2,1,0:T(8,128)}, f32[4,96,1024]{2,1,0:T(8,128)}), (f32[4,96,1024]{2,1,0:T(8,128)}, f32[4,96,1024]{2,1,0:T(8,128)})) %all-reduce.3.cloned.1.call-update) | async-done | bytes 3145744 | tf_op jit(solution)/shard_map/psum | solution.py:31
  126.2 0.0 copy-start.1
  126.2 15.4 %convolution_multiply_fusion = f32[4,96,3072]{2,1,0:T(8,128)} fusion(bf16[4,1024,3072]{2,1,0:T(8,128)(2,1)} %param.11, f32[4,96]{1,0:T(4,128)S(1)} %scatter_fusion.1, f32[4,96,1024]{2,1,0:T(8,128)} %get-tuple-element.5, f32[4,96,1024]{2,1,0:T(8,128)} %get-tuple-element.6), kind=kOutput, calls=%fused_computation.5 | convolution fusion | flops 2419458048 | bytes 33031680 | tf_op jit(solution)/shard_map/ecf,efd->ecd/dot_general | solution.py:41
  141.7 9.7 %scatter_custom_fusion.2 = f32[128,3072]{1,0:T(8,128)} fusion(s32[384]{0:T(512)S(1)} %fusion.9, f32[384,3072]{1,0:T(8,128)} %bitcast.37, f32[]{:T(128)} %constant.36.clone.1), kind=kCustom, calls=%fused_computation.13 | custom fusion | flops 1179648 | bytes 1573376 | tf_op jit(solution)/shard_map/scatter-add | solution.py:47
  151.3 0.0 reduce-scatter.2.cloned.1.call-update
  151.4 66.3 %reduce-scatter.2.cloned.1.call-done = f32[16,3072]{1,0:T(8,128)} async-done(((f32[128,3072]{1,0:T(8,128)}), f32[16,3072]{1,0:T(8,128)}) %reduce-scatter.2.cloned.1.call-update) | async-done | bytes 196624 | tf_op jit(solution)/shard_map/reduce_scatter | solution.py:49
  217.6 1.6 convert_element_type.13
  219.2 0.0 copy-done.1
  (17 shorter events, 0.2 us)
Async XLA Ops:
  6.5 99.5 %copy-start = (bf16[3072,4]{0,1:T(4,128)(2,1)S(1)}, bf16[3072,4]{0,1:T(4,128)(2,1)}, u32[]{:S(2)}) copy-start(bf16[3072,4]{0,1:T(4,128)(2,1)} %param.8) | copy-start | bytes 73732
  6.5 36.5 %copy-start.2 = (bf16[16,3072]{1,0:T(8,128)(2,1)S(1)}, bf16[16,3072]{1,0:T(8,128)(2,1)}, u32[]{:S(2)}) copy-start(bf16[16,3072]{1,0:T(8,128)(2,1)} %param.6) | copy-start | bytes 294916
  6.5 119.7 %all-reduce.3.cloned.1.call-start = ((), (), s32[]{:S(2)}) async-start(), calls=%async_computation.2 | async-start | bytes 6291456 | tf_op jit(solution)/shard_map/psum | solution.py:31
  105.5 112.1 %reduce-scatter.2.cloned.1.call-start = ((), (), s32[]{:S(2)}) async-start(), calls=%async_computation.1 | async-start | bytes 1769472 | tf_op jit(solution)/shard_map/reduce_scatter | solution.py:49
  126.2 93.0 %copy-start.1 = (bf16[3072,4]{0,1:T(4,128)(2,1)S(1)}, bf16[3072,4]{0,1:T(4,128)(2,1)}, u32[]{:S(2)}) copy-start(bf16[3072,4]{0,1:T(4,128)(2,1)} %param.8) | copy-start | bytes 73732
Sparse Core Ops, SparseCore 0:
  105.7 20.5 all-reduce.2
  151.5 66.0 reduce-scatter.1
where the time goes:
time: 226 us
  waiting for transfers between devices  69.1 us (31%)
  blocking collectives  57.6 us (25%)
  matrix products  43 us (19%)
  local copies, waits for them, and re-layouts  30 us (13%)
  between operations  13.5 us (6%)
  other arithmetic  12.7 us (6%)
    reduce_scatter x1, waiting for transfers between devices, per_device(): lax.psum_scatter(partial_value, 'batch', scatter_dimension=0, tiled=True)  66.3 us
    all_gather x1, blocking collectives, per_device(): lax.all_gather(tokens, 'batch', axis=0, tiled=True)  32.3 us
    all_gather x1, blocking collectives, per_device(): lax.all_gather(expert_ids, 'batch', axis=0, tiled=True)  22.6 us
    dot_general x1, matrix products, per_device(): jnp.einsum('ecf,efd->ecd', hidden, w_down, preferred_element_type=jnp.flo...  15.4 us
    dot_general x1, matrix products, per_device(): jnp.einsum('ecd,efd->ecf', slot_rows, w_up, preferred_element_type=jnp.fl...  13.7 us
    dot_general x1, matrix products, per_device(): jnp.einsum('ecd,efd->ecf', slot_rows, w_gate, preferred_element_type=jnp....  13.7 us
    scatter x1, local copies, waits for them, and re-layouts, per_device(): slot_token = jnp.full((experts, capacity), token_count, jnp.int32).at[pai...  11.4 us
    scatter x1, local copies, waits for them, and re-layouts, per_device(): slot_weight = jnp.zeros((experts, capacity), jnp.float32).at[pair_expert,...  11.4 us
  transfers between devices with their start and end apart: 2, of which 2 were waited for; matrix products, arithmetic and copies ran while one was open for 7% of the time, Pallas kernels for 0%

commit v1 on v0

v1 whole, which is shorter than its diff:
```python
import functools
import jax
import jax.numpy as jnp
from jax import lax
from jax.experimental import pallas as pl
from jax.experimental.pallas import tpu as pltpu
from jax.sharding import PartitionSpec as P

F32, BF16 = jnp.float32, jnp.bfloat16
IDS = 128
SWAP = [(0, 1), (1, 0)]
HBM_BLOCK = pl.BlockSpec(memory_space=pltpu.HBM)
VMEM_BLOCK = pl.BlockSpec(memory_space=pltpu.VMEM)


def xor_send(block, mask):
    return lax.ppermute(block, "batch", [(i, i ^ mask) for i in range(8)])


def in_vmem(array):
    return pltpu.with_memory_space_constraint(array, pltpu.VMEM)


def call(kernel, outs, args, flops, size, vmem, scratch=(), hbm=()):
    specs = [HBM_BLOCK if i in hbm else VMEM_BLOCK for i in range(len(args))]
    return pl.pallas_call(
        kernel,
        out_shape=outs,
        in_specs=specs,
        out_specs=[VMEM_BLOCK] * len(outs),
        scratch_shapes=list(scratch),
        compiler_params=pltpu.CompilerParams(vmem_limit_bytes=int(vmem * 2**20)),
        cost_estimate=pl.CostEstimate(flops=flops, bytes_accessed=size, transcendentals=0),
    )(*args)


def pack_kernel(tokens_ref, ids_ref, out_ref):
    rows, width = tokens_ref.shape
    out_ref[:, :width] = tokens_ref[...]
    ids = ids_ref[...].astype(F32)
    lane = lax.broadcasted_iota(jnp.int32, (rows, IDS), 1)
    out_ref[:, width:] = jnp.where(lane == 0, ids[:, 0:1], ids[:, 1:2]).astype(BF16)


def stream(w_ref, held_ref, sems, experts, part_ref, load):
    hidden, width = w_ref.shape[1:]
    slots, tile = held_ref.shape[:2]
    steps = [(e, f) for e in experts for f in range(0, hidden, tile)]

    def copy(step):
        e, f = steps[step]
        slot = step % slots
        return pltpu.make_async_copy(
            w_ref.at[e, pl.ds(f, tile)], held_ref.at[slot], sems.at[slot]
        )

    for step in range(min(slots, len(steps))):
        copy(step).start()
    x = load()
    for step in range(len(steps)):
        copy(step).wait()
        part_ref[step * tile : (step + 1) * tile] = jnp.dot(
            held_ref[step % slots], x, preferred_element_type=F32
        )
        if step + slots < len(steps):
            copy(step + slots).start()


def gate_kernel(*refs):
    blocks, (router_ref, w_ref, turned_ref, part_ref) = refs[:8], refs[8:12]
    rows_ref, held_ref, sems = refs[12:]
    experts, hidden, width = w_ref.shape

    def load():
        rows = blocks[0].shape[0]
        for j, block in enumerate(blocks):
            rows_ref[j * rows : (j + 1) * rows] = block[...].astype(F32)
        turned_ref[...] = rows_ref[...].T.astype(BF16)
        x = turned_ref[:width]
        part_ref[experts * hidden :] = jnp.dot(
            router_ref[...], x, preferred_element_type=F32
        )
        return x

    stream(w_ref, held_ref, sems, range(experts), part_ref, load)


def up_kernel(experts, turned_ref, w_ref, part_ref, held_ref, sems):
    width = w_ref.shape[2]
    stream(w_ref, held_ref, sems, experts, part_ref, lambda: turned_ref[:width])


def factors(turned_ref, gate_a, gate_b, width, base, experts):
    ids = turned_ref[width : width + 16].astype(F32)
    a, b = ids[0:1], ids[1:2]
    logits = gate_a[base : base + 16] + gate_b[base : base + 16]
    row = lax.broadcasted_iota(jnp.int32, logits.shape, 0).astype(F32)
    is_a, is_b = row == a, row == b
    la = jnp.sum(jnp.where(is_a, logits, 0.0), axis=0, keepdims=True)
    lb = jnp.sum(jnp.where(is_b, logits, 0.0), axis=0, keepdims=True)
    wa = 1.0 / (1.0 + jnp.exp(lb - la))
    wb = 1.0 / (1.0 + jnp.exp(la - lb))
    return (jnp.where(is_a, wa, 0.0) + jnp.where(is_b, wb, 0.0)).T


def down_terms(first, count, turned_ref, gate_a, gate_b, up_a, up_b, w_ref):
    experts, hidden, width = w_ref.shape
    factor = factors(turned_ref, gate_a, gate_b, width, experts * hidden, experts)
    total = None
    for i in range(count):
        e = first + i
        own = slice(e * hidden, (e + 1) * hidden)
        mine = slice(i * hidden, (i + 1) * hidden)
        gate = gate_a[own] + gate_b[own]
        up = up_a[mine] + up_b[mine]
        h = (gate / (1.0 + jnp.exp(-gate)) * up).T.astype(BF16)
        term = factor[:, e : e + 1] * jnp.dot(h, w_ref[e], preferred_element_type=F32)
        total = term if total is None else total + term
    return total


def down_first(count, turned_ref, gate_a, gate_b, up_a, up_b, w_ref, out_ref):
    out_ref[...] = down_terms(0, count, turned_ref, gate_a, gate_b, up_a, up_b, w_ref)


def down_last(first, count, turned_ref, gate_a, gate_b, up_a, up_b, w_ref, sum_ref, *outs):
    total = sum_ref[...] + down_terms(
        first, count, turned_ref, gate_a, gate_b, up_a, up_b, w_ref
    )
    rows = outs[0].shape[0]
    for j, out in enumerate(outs):
        out[...] = total[j * rows : (j + 1) * rows].astype(out.dtype)


def fast(tokens, expert_ids, router, w_gate, w_up, w_down):
    rows, width = tokens.shape
    experts, hidden, _ = w_gate.shape
    count = 8 * rows
    shape = lambda *s, dtype=F32: jax.ShapeDtypeStruct(s, dtype)
    (own,) = call(
        pack_kernel, [shape(rows, width + IDS, dtype=BF16)], [tokens, expert_ids], 0, 4 * rows * width, 1
    )
    far = xor_send(own, 4)
    near = [xor_send(own, k) for k in (1, 2, 3)]
    forwarded = [xor_send(far, k) for k in (1, 2, 3)]
    blocks = [own, *near, far, *forwarded]

    w_gate = pltpu.with_memory_space_constraint(w_gate, pltpu.HBM)
    w_up = pltpu.with_memory_space_constraint(w_up, pltpu.HBM)
    w_down = in_vmem(w_down)
    flops = 2 * count * hidden * width
    size = 2 * hidden * width
    slots, tile = 4, min(hidden, 256)
    held = [pltpu.VMEM((slots, tile, width), BF16), pltpu.SemaphoreType.DMA((slots,))]
    turned, gate = call(
        gate_kernel,
        [shape(width + IDS, count, dtype=BF16), shape(experts * hidden + 16, count)],
        [*blocks, jnp.pad(router.T, ((0, 16 - experts), (0, 0))), w_gate],
        experts * flops,
        experts * size,
        10,
        [pltpu.VMEM((count, width + IDS), F32), *held],
        hbm=(9,),
    )
    gate_other = lax.ppermute(gate, "mp", SWAP)
    half = experts // 2
    ups = []
    for first in (0, half):
        (up,) = call(
            functools.partial(up_kernel, range(first, first + half)),
            [shape(half * hidden, count)],
            [turned, w_up],
            half * flops,
            half * size,
            10,
            held,
            hbm=(1,),
        )
        ups.append((up, lax.ppermute(up, "mp", SWAP)))
    (partial_sum,) = call(
        functools.partial(down_first, half),
        [shape(count, width)],
        [turned, gate, gate_other, *ups[0], w_down],
        half * flops,
        half * size,
        8,
    )
    parts = call(
        functools.partial(down_last, half, half),
        [shape(rows, width)] + [shape(rows, width, dtype=BF16)] * 7,
        [turned, gate, gate_other, *ups[1], w_down, partial_sum],
        half * flops,
        half * size,
        8,
    )
    far_sums = [xor_send(parts[4 ^ k], k) for k in (1, 2, 3)]
    near_sums = [xor_send(parts[k], k) for k in (1, 2, 3)]
    add = lambda arrays: sum(a.astype(F32) for a in arrays)
    crossing = xor_send(add([parts[4], *far_sums]).astype(BF16), 4)
    return add([parts[0], *near_sums, crossing]).astype(BF16)


def general(tokens, expert_ids, router, w_gate, w_up, w_down):
    gathered, all_ids = (
        lax.all_gather(tokens, "batch", axis=0, tiled=True),
        lax.all_gather(expert_ids, "batch", axis=0, tiled=True),
    )
    token_count = gathered.shape[0]
    half_width = gathered.shape[1]
    experts = w_gate.shape[0]
    capacity = 3 * token_count // 4
    pair_expert = all_ids.reshape(-1)
    onehot = (pair_expert[:, None] == jnp.arange(experts, dtype=jnp.int32)[None, :]).astype(
        jnp.int32
    )
    position = jnp.sum((jnp.cumsum(onehot, axis=0) - 1) * onehot, axis=1)
    pair_token = jnp.arange(2 * token_count, dtype=jnp.int32) // 2
    slot_token = (
        jnp.full((experts, capacity), token_count, jnp.int32)
        .at[pair_expert, position]
        .set(pair_token)
    )
    slot_rows = jnp.take(gathered, jnp.minimum(slot_token, token_count - 1), axis=0)
    logit_part = jnp.dot(gathered, router, preferred_element_type=F32)
    gate_part = jnp.einsum("ecd,efd->ecf", slot_rows, w_gate, preferred_element_type=F32)
    up_part = jnp.einsum("ecd,efd->ecf", slot_rows, w_up, preferred_element_type=F32)
    logits, gate_sum, up_sum = lax.psum((logit_part, gate_part, up_part), "mp")
    chosen = jnp.take_along_axis(logits, all_ids, axis=1)
    weights = 1.0 / (1.0 + jnp.exp(chosen[:, ::-1] - chosen))
    slot_weight = (
        jnp.zeros((experts, capacity), F32)
        .at[pair_expert, position]
        .set(weights.reshape(-1))
    )
    hidden = (jax.nn.silu(gate_sum) * up_sum).astype(BF16)
    slot_out = (
        jnp.einsum("ecf,efd->ecd", hidden, w_down, preferred_element_type=F32)
        * slot_weight[:, :, None]
    )
    partial_value = (
        jnp.zeros((token_count, half_width), F32)
        .at[slot_token.reshape(-1)]
        .add(slot_out.reshape(-1, half_width), mode="drop")
    )
    mine = lax.psum_scatter(partial_value, "batch", scatter_dimension=0, tiled=True)
    return mine.astype(BF16)


def solution(mesh):
    def per_device(*args):
        rows, (experts, hidden, _) = args[0].shape[0], args[3].shape
        fits = mesh.shape["batch"] == 8 and rows % 16 == 0 and 8 * rows <= 128
        if fits and experts == 4 and hidden <= 1024:
            return fast(*args)
        return general(*args)

    in_specs = (
        P(("group", "batch"), "mp"),
        P(("group", "batch"), None),
        P("mp", None),
        P(None, "batch", "mp"),
        P(None, "batch", "mp"),
        P(None, "batch", "mp"),
    )
    out_specs = P(("group", "batch"), "mp")
    return jax.shard_map(
        per_device, mesh=mesh, in_specs=in_specs, out_specs=out_specs, check_vma=False
    )
```

time: 226 us -> 76.1 us (0.34)
  blocking collectives: 57.6 us -> 0 us
  waiting for transfers between devices: 69.1 us -> 12.7 us
  matrix products: 43 us -> 0 us
  Pallas kernels: 0 us -> 29 us
  starting transfers between devices: 0.04 us -> 21.8 us
  local copies, waits for them, and re-layouts: 30 us -> 11.5 us
  between operations: 13.5 us -> 0.18 us
  other arithmetic: 12.7 us -> 0.76 us
    reduce_scatter x1 -> x0, waiting for transfers between devices: 66.3 us -> none  [per_device(): lax.psum_scatter(partial_value, 'batch', scatter_dimension=0, tiled=True)]
    all_gather x2 -> x0, blocking collectives: 55 us -> none  [the longest x1 32.3 us: per_device(): lax.all_gather(tokens, 'batch', axis=0, tiled=True)]
    dot_general x4 -> x0, matrix products: 43 us -> none  [the longest x1 15.4 us: per_device(): jnp.einsum('ecf,efd->ecd', hidden, w_down, preferred_element_type=jnp.flo...]
    pallas_call x0 -> x6, Pallas kernels: none -> 29 us  [call(): pl.pallas_call(kernel, out_shape=outs, in_specs=specs, out_specs=[VMEM_BL...]
    scatter x2 -> x0, local copies, waits for them, and re-layouts: 22.9 us -> none  [the longest x1 11.4 us: per_device(): slot_token = jnp.full((experts, capacity), token_count, jnp.int32).at[pai...]
    ppermute x0 -> x17, starting transfers between devices: none -> 21.8 us  [the longest x14 20.9 us: xor_send(): return lax.ppermute(block, 'batch', [(i, i ^ mask) for i in range(8)])]
    ppermute x0 -> x17, waiting for transfers between devices: none -> 12.7 us  [the longest x14 12.7 us: xor_send(): return lax.ppermute(block, 'batch', [(i, i ^ mask) for i in range(8)])]
    unnamed x7 -> x17, local copies, waits for them, and re-layouts: 0.09 us -> 10.7 us
  transfers between devices with their start and end apart: 2 -> 17, of which waited for: 2 -> 8; matrix products, arithmetic and copies ran while one was open for 7% -> 1% of each run, Pallas kernels for 0% -> 21%
where the time goes in v1:
time: 76.1 us; the launch traced here: 75.9 us
  Pallas kernels  29 us (38%)
  starting transfers between devices  21.8 us (29%)
  waiting for transfers between devices  12.7 us (17%)
  local copies, waits for them, and re-layouts  11.5 us (15%)
    pallas_call x6, Pallas kernels, call(): pl.pallas_call(kernel, out_shape=outs, in_specs=specs, out_specs=[VMEM_BL...  29 us
    ppermute x14, starting transfers between devices, xor_send(): return lax.ppermute(block, 'batch', [(i, i ^ mask) for i in range(8)])  20.9 us
    ppermute x14, waiting for transfers between devices, xor_send(): return lax.ppermute(block, 'batch', [(i, i ^ mask) for i in range(8)])  12.7 us
    unnamed x17, local copies, waits for them, and re-layouts  10.7 us
  transfers between devices with their start and end apart: 17, of which 8 were waited for; matrix products, arithmetic and copies ran while one was open for 1% of the time, Pallas kernels for 21%

profile of v1, /device:TPU:0, one launch (start us, length us, event | category | flops | bytes accessed | tf_op | source)
XLA Modules:
  0.0 75.9 jit_solution(6368021090667631755)
XLA Ops:
  0.0 0.8 copy.7.ids_ref
  0.8 0.9 %copy-done.1 = bf16[16,3072]{1,0:T(8,128)(2,1)S(1)} copy-done((bf16[16,3072]{1,0:T(8,128)(2,1)S(1)}, bf16[16,3072]{1,0:T(8,128)(2,1)}, u32[]{:S(2)}) %copy-start.1) | copy-done | bytes 98328
  1.6 0.1 shard_map.64.refs_0_
  1.7 4.0 %collective-permute-start.3 = (bf16[16,3200]{1,0:T(8,128)(2,1)S(1)}, bf16[16,3200]{1,0:T(8,128)(2,1)S(1)}, u32[]{:S(2)}, u32[]{:S(2)}) collective-permute-start(bf16[16,3200]{1,0:T(8,128)(2,1)S(1)} %shard_map.64.refs_0_), channel_id=1, source_target_pairs={{0,8},{2,10},{4,12},{6,14},{8,0},{10,2},{12,4},{14,6},{1,9},{3,11}... | collective-permute-start | bytes 307208 | tf_op jit(solution)/shard_map/ppermute | solution.py:17
  5.8 1.5 %collective-permute-start = (bf16[16,3200]{1,0:T(8,128)(2,1)S(1)}, bf16[16,3200]{1,0:T(8,128)(2,1)S(1)}, u32[]{:S(2)}, u32[]{:S(2)}) collective-permute-start(bf16[16,3200]{1,0:T(8,128)(2,1)S(1)} %shard_map.64.refs_0_), channel_id=1, source_target_pairs={{0,2},{2,0},{4,6},{6,4},{8,10},{10,8},{12,14},{14,12},{1,3},{3,1},... | collective-permute-start | bytes 307208 | tf_op jit(solution)/shard_map/ppermute | solution.py:17
  7.3 1.6 %collective-permute-start.1 = (bf16[16,3200]{1,0:T(8,128)(2,1)S(1)}, bf16[16,3200]{1,0:T(8,128)(2,1)S(1)}, u32[]{:S(2)}, u32[]{:S(2)}) collective-permute-start(bf16[16,3200]{1,0:T(8,128)(2,1)S(1)} %shard_map.64.refs_0_), channel_id=1, source_target_pairs={{0,4},{2,6},{4,0},{6,2},{8,12},{10,14},{12,8},{14,10},{1,5},{3,7},... | collective-permute-start | bytes 307208 | tf_op jit(solution)/shard_map/ppermute | solution.py:17
  8.9 0.4 collective-permute-start.2
  9.3 1.7 %collective-permute-done.3.refs_4_ = bf16[16,3200]{1,0:T(8,128)(2,1)S(1)} collective-permute-done((bf16[16,3200]{1,0:T(8,128)(2,1)S(1)}, bf16[16,3200]{1,0:T(8,128)(2,1)S(1)}, u32[]{:S(2)}, u32[]{:S(2)}) %collective-permute-start.3) | collective-permute-done | bytes 102432 | tf_op jit(solution)/shard_map/ppermute | solution.py:17
  10.9 1.6 %collective-permute-start.4 = (bf16[16,3200]{1,0:T(8,128)(2,1)S(1)}, bf16[16,3200]{1,0:T(8,128)(2,1)S(1)}, u32[]{:S(2)}, u32[]{:S(2)}) collective-permute-start(bf16[16,3200]{1,0:T(8,128)(2,1)S(1)} %collective-permute-done.3.refs_4_), channel_id=1, source_target_pairs={{0,2},{2,0},{4,6},{6,4},{8,10},{10,8},{12,14},{14,12},{1,3},{3,1},... | collective-permute-start | bytes 307208 | tf_op jit(solution)/shard_map/ppermute | solution.py:17
  12.5 0.6 collective-permute-start.5
  13.1 1.4 %collective-permute-start.6 = (bf16[16,3200]{1,0:T(8,128)(2,1)S(1)}, bf16[16,3200]{1,0:T(8,128)(2,1)S(1)}, u32[]{:S(2)}, u32[]{:S(2)}) collective-permute-start(bf16[16,3200]{1,0:T(8,128)(2,1)S(1)} %collective-permute-done.3.refs_4_), channel_id=1, source_target_pairs={{0,6},{2,4},{4,2},{6,0},{8,14},{10,12},{12,10},{14,8},{1,7},{3,5},... | collective-permute-start | bytes 307208 | tf_op jit(solution)/shard_map/ppermute | solution.py:17
  14.4 0.8 pad.4.refs_8_
  15.2 0.0 collective-permute-done.1.refs_2_
  15.2 0.4 collective-permute-done.2.refs_3_
  15.6 0.9 %collective-permute-done.4.refs_5_ = bf16[16,3200]{1,0:T(8,128)(2,1)S(1)} collective-permute-done((bf16[16,3200]{1,0:T(8,128)(2,1)S(1)}, bf16[16,3200]{1,0:T(8,128)(2,1)S(1)}, u32[]{:S(2)}, u32[]{:S(2)}) %collective-permute-start.4) | collective-permute-done | bytes 102432 | tf_op jit(solution)/shard_map/ppermute | solution.py:17
  16.5 1.3 %collective-permute-done.5.refs_6_ = bf16[16,3200]{1,0:T(8,128)(2,1)S(1)} collective-permute-done((bf16[16,3200]{1,0:T(8,128)(2,1)S(1)}, bf16[16,3200]{1,0:T(8,128)(2,1)S(1)}, u32[]{:S(2)}, u32[]{:S(2)}) %collective-permute-start.5) | collective-permute-done | bytes 102432 | tf_op jit(solution)/shard_map/ppermute | solution.py:17
  17.8 1.4 %collective-permute-done.6.refs_7_ = bf16[16,3200]{1,0:T(8,128)(2,1)S(1)} collective-permute-done((bf16[16,3200]{1,0:T(8,128)(2,1)S(1)}, bf16[16,3200]{1,0:T(8,128)(2,1)S(1)}, u32[]{:S(2)}, u32[]{:S(2)}) %collective-permute-start.6) | collective-permute-done | bytes 102432 | tf_op jit(solution)/shard_map/ppermute | solution.py:17
  19.3 10.3 %shard_map.65 = (bf16[3200,128]{1,0:T(8,128)(2,1)S(1)}, f32[4112,128]{1,0:T(8,128)S(1)}) custom-call(bf16[16,3200]{1,0:T(8,128)(2,1)S(1)} %shard_map.64.refs_0_, bf16[16,3200]{1,0:T(8,128)(2,1)S(1)} %collective-permute-done.refs_1_, bf16[16,3200]{1,0:T(8,128)(2,1)S(1)} %collective-permute-done.1.refs_2_, ...), custom_call_target="tpu_custom_call" | custom-call | flops 3221225472 | bytes 25165824 | tf_op jit(solution)/shard_map/pallas_call | solution.py:26
  29.6 0.1 collective-permute-start.7
  29.7 0.0 slice-start
  29.7 0.0 slice-start.1
  29.7 0.0 slice-start.2
  29.7 0.0 slice-start.3
  29.7 6.7 %shard_map.67.up_a = f32[2048,128]{1,0:T(8,128)S(1)} custom-call(bf16[3200,128]{1,0:T(8,128)(2,1)S(1)} %get-tuple-element.15.turned_ref, bf16[4,1024,3072]{2,1,0:T(8,128)(2,1)} %w_ref.5), custom_call_target="tpu_custom_call" | custom-call | flops 1610612736 | bytes 12582912 | tf_op jit(solution)/shard_map/pallas_call | solution.py:26
  36.4 0.0 slice-start.4
  36.5 0.0 slice-start.5
  36.5 0.5 collective-permute-start.9
  37.0 7.4 %shard_map.66.up_a = f32[2048,128]{1,0:T(8,128)S(1)} custom-call(bf16[3200,128]{1,0:T(8,128)(2,1)S(1)} %get-tuple-element.15.turned_ref, bf16[4,1024,3072]{2,1,0:T(8,128)(2,1)} %w_ref.5), custom_call_target="tpu_custom_call" | custom-call | flops 1610612736 | bytes 12582912 | tf_op jit(solution)/shard_map/pallas_call | solution.py:26
  44.4 0.3 collective-permute-start.8
  44.7 0.0 collective-permute-done.9.up_b
  44.7 0.0 collective-permute-done.7.gate_b
  44.7 0.9 %slice-done.5 = s8[4194304]{0:T(1024)(128)(4,1)S(1)} async-done(((s8[25165824]{0:T(1024)(128)(4,1)}), s8[4194304]{0:T(1024)(128)(4,1)S(1)}, s32[]{:S(2)}) %slice-start.5) | async-done | bytes 4194328
  45.6 2.1 %shard_map.68.sum_ref = f32[128,3072]{1,0:T(8,128)S(1)} custom-call(bf16[3200,128]{1,0:T(8,128)(2,1)S(1)} %get-tuple-element.15.turned_ref, f32[4112,128]{1,0:T(8,128)S(1)} %get-tuple-element.16.gate_a, f32[4112,128]{1,0:T(8,128)S(1)} %collective-permute-done.7.gate_b, f32[2048,128]{1,0:T(8,128)S(1)} %shard_map.67.up_a, ...), custom_call_target="tpu_custom_call" | custom-call | flops 1610612736 | bytes 12582912 | tf_op jit(solution)/shard_map/pallas_call | solution.py:26
  47.8 0.0 copy-start
  47.8 8.1 %copy-done = bf16[4,1024,3072]{2,1,0:T(8,128)(2,1)S(1)} copy-done((bf16[4,1024,3072]{2,1,0:T(8,128)(2,1)S(1)}, bf16[4,1024,3072]{2,1,0:T(8,128)(2,1)}, u32[]{:S(2)}) %copy-start) | copy-done | bytes 25165848
  55.9 2.3 %shard_map.69 = (f32[16,3072]{1,0:T(8,128)S(1)}, bf16[16,3072]{1,0:T(8,128)(2,1)S(1)}, bf16[16,3072]{1,0:T(8,128)(2,1)S(1)}, bf16[16,3072]{1,0:T(8,128)(2,1)S(1)...) custom-call(bf16[3200,128]{1,0:T(8,128)(2,1)S(1)} %get-tuple-element, ...), custom_call_target="tpu_custom_call" | custom-call | flops 1610612736 | bytes 12582912 | tf_op jit(solution)/shard_map/pallas_call | solution.py:26
  58.2 1.2 %collective-permute-start.13 = (bf16[16,3072]{1,0:T(8,128)(2,1)S(1)}, bf16[16,3072]{1,0:T(8,128)(2,1)S(1)}, u32[]{:S(2)}, u32[]{:S(2)}) collective-permute-start(bf16[16,3072]{1,0:T(8,128)(2,1)S(1)} %get-tuple-element.22), channel_id=1, source_target_pairs={{0,2},{2,0},{4,6},{6,4},{8,10},{10,8},{12,14},{14,12},{1,3},{3,1},... | collective-permute-start | bytes 294920 | tf_op jit(solution)/shard_map/ppermute | solution.py:17
  59.4 0.9 %collective-permute-start.14 = (bf16[16,3072]{1,0:T(8,128)(2,1)S(1)}, bf16[16,3072]{1,0:T(8,128)(2,1)S(1)}, u32[]{:S(2)}, u32[]{:S(2)}) collective-permute-start(bf16[16,3072]{1,0:T(8,128)(2,1)S(1)} %get-tuple-element.23), channel_id=1, source_target_pairs={{0,4},{2,6},{4,0},{6,2},{8,12},{10,14},{12,8},{14,10},{1,5},{3,7},... | collective-permute-start | bytes 294920 | tf_op jit(solution)/shard_map/ppermute | solution.py:17
  60.3 1.5 %collective-permute-start.15 = (bf16[16,3072]{1,0:T(8,128)(2,1)S(1)}, bf16[16,3072]{1,0:T(8,128)(2,1)S(1)}, u32[]{:S(2)}, u32[]{:S(2)}) collective-permute-start(bf16[16,3072]{1,0:T(8,128)(2,1)S(1)} %get-tuple-element.24), channel_id=1, source_target_pairs={{0,6},{2,4},{4,2},{6,0},{8,14},{10,12},{12,10},{14,8},{1,7},{3,5},... | collective-permute-start | bytes 294920 | tf_op jit(solution)/shard_map/ppermute | solution.py:17
  61.8 1.1 %collective-permute-start.10 = (bf16[16,3072]{1,0:T(8,128)(2,1)S(1)}, bf16[16,3072]{1,0:T(8,128)(2,1)S(1)}, u32[]{:S(2)}, u32[]{:S(2)}) collective-permute-start(bf16[16,3072]{1,0:T(8,128)(2,1)S(1)} %get-tuple-element.18), channel_id=1, source_target_pairs={{0,2},{2,0},{4,6},{6,4},{8,10},{10,8},{12,14},{14,12},{1,3},{3,1},... | collective-permute-start | bytes 294920 | tf_op jit(solution)/shard_map/ppermute | solution.py:17
  62.9 0.9 %collective-permute-start.11 = (bf16[16,3072]{1,0:T(8,128)(2,1)S(1)}, bf16[16,3072]{1,0:T(8,128)(2,1)S(1)}, u32[]{:S(2)}, u32[]{:S(2)}) collective-permute-start(bf16[16,3072]{1,0:T(8,128)(2,1)S(1)} %get-tuple-element.19), channel_id=1, source_target_pairs={{0,4},{2,6},{4,0},{6,2},{8,12},{10,14},{12,8},{14,10},{1,5},{3,7},... | collective-permute-start | bytes 294920 | tf_op jit(solution)/shard_map/ppermute | solution.py:17
  63.8 1.5 %collective-permute-start.12 = (bf16[16,3072]{1,0:T(8,128)(2,1)S(1)}, bf16[16,3072]{1,0:T(8,128)(2,1)S(1)}, u32[]{:S(2)}, u32[]{:S(2)}) collective-permute-start(bf16[16,3072]{1,0:T(8,128)(2,1)S(1)} %get-tuple-element.20), channel_id=1, source_target_pairs={{0,6},{2,4},{4,2},{6,0},{8,14},{10,12},{12,10},{14,8},{1,7},{3,5},... | collective-permute-start | bytes 294920 | tf_op jit(solution)/shard_map/ppermute | solution.py:17
  65.3 2.2 %collective-permute-done.15 = bf16[16,3072]{1,0:T(8,128)(2,1)S(1)} collective-permute-done((bf16[16,3072]{1,0:T(8,128)(2,1)S(1)}, bf16[16,3072]{1,0:T(8,128)(2,1)S(1)}, u32[]{:S(2)}, u32[]{:S(2)}) %collective-permute-start.15) | collective-permute-done | bytes 98336 | tf_op jit(solution)/shard_map/ppermute | solution.py:17
  67.5 0.1 add_convert_fusion.1
  67.5 2.9 %collective-permute-start.16 = (bf16[16,3072]{1,0:T(8,128)(2,1)S(1)}, bf16[16,3072]{1,0:T(8,128)(2,1)S(1)}, u32[]{:S(2)}, u32[]{:S(2)}) collective-permute-start(bf16[16,3072]{1,0:T(8,128)(2,1)S(1)} %add_convert_fusion.1), channel_id=1, source_target_pairs={{0,8},{2,10},{4,12},{6,14},{8,0},{10,2},{12,4},{14,6},{1,9},{3,11}... | collective-permute-start | bytes 294920 | tf_op jit(solution)/shard_map/ppermute | solution.py:17
  70.4 1.6 %collective-permute-done.12 = bf16[16,3072]{1,0:T(8,128)(2,1)S(1)} collective-permute-done((bf16[16,3072]{1,0:T(8,128)(2,1)S(1)}, bf16[16,3072]{1,0:T(8,128)(2,1)S(1)}, u32[]{:S(2)}, u32[]{:S(2)}) %collective-permute-start.12) | collective-permute-done | bytes 98336 | tf_op jit(solution)/shard_map/ppermute | solution.py:17
  72.0 3.1 %collective-permute-done.16 = bf16[16,3072]{1,0:T(8,128)(2,1)S(1)} collective-permute-done((bf16[16,3072]{1,0:T(8,128)(2,1)S(1)}, bf16[16,3072]{1,0:T(8,128)(2,1)S(1)}, u32[]{:S(2)}, u32[]{:S(2)}) %collective-permute-start.16) | collective-permute-done | bytes 98336 | tf_op jit(solution)/shard_map/ppermute | solution.py:17
  75.1 0.7 add_convert_fusion
  (13 shorter events, 0.0 us)
Async XLA Ops:
  0.8 0.9 %copy-start.1 = (bf16[16,3072]{1,0:T(8,128)(2,1)S(1)}, bf16[16,3072]{1,0:T(8,128)(2,1)}, u32[]{:S(2)}) copy-start(bf16[16,3072]{1,0:T(8,128)(2,1)} %tokens_ref.1) | copy-start | bytes 294916
  1.7 9.2 %collective-permute-start.3 = (bf16[16,3200]{1,0:T(8,128)(2,1)S(1)}, bf16[16,3200]{1,0:T(8,128)(2,1)S(1)}, u32[]{:S(2)}, u32[]{:S(2)}) collective-permute-start(bf16[16,3200]{1,0:T(8,128)(2,1)S(1)} %shard_map.64.refs_0_), channel_id=1, source_target_pairs={{0,8},{2,10},{4,12},{6,14},{8,0},{10,2},{12,4},{14,6},{1,9},{3,11}... | collective-permute-start | bytes 307208 | tf_op jit(solution)/shard_map/ppermute | solution.py:17
  5.8 7.3 %collective-permute-start = (bf16[16,3200]{1,0:T(8,128)(2,1)S(1)}, bf16[16,3200]{1,0:T(8,128)(2,1)S(1)}, u32[]{:S(2)}, u32[]{:S(2)}) collective-permute-start(bf16[16,3200]{1,0:T(8,128)(2,1)S(1)} %shard_map.64.refs_0_), channel_id=1, source_target_pairs={{0,2},{2,0},{4,6},{6,4},{8,10},{10,8},{12,14},{14,12},{1,3},{3,1},... | collective-permute-start | bytes 307208 | tf_op jit(solution)/shard_map/ppermute | solution.py:17
  7.3 7.9 %collective-permute-start.1 = (bf16[16,3200]{1,0:T(8,128)(2,1)S(1)}, bf16[16,3200]{1,0:T(8,128)(2,1)S(1)}, u32[]{:S(2)}, u32[]{:S(2)}) collective-permute-start(bf16[16,3200]{1,0:T(8,128)(2,1)S(1)} %shard_map.64.refs_0_), channel_id=1, source_target_pairs={{0,4},{2,6},{4,0},{6,2},{8,12},{10,14},{12,8},{14,10},{1,5},{3,7},... | collective-permute-start | bytes 307208 | tf_op jit(solution)/shard_map/ppermute | solution.py:17
  8.9 6.7 %collective-permute-start.2 = (bf16[16,3200]{1,0:T(8,128)(2,1)S(1)}, bf16[16,3200]{1,0:T(8,128)(2,1)S(1)}, u32[]{:S(2)}, u32[]{:S(2)}) collective-permute-start(bf16[16,3200]{1,0:T(8,128)(2,1)S(1)} %shard_map.64.refs_0_), channel_id=1, source_target_pairs={{0,6},{2,4},{4,2},{6,0},{8,14},{10,12},{12,10},{14,8},{1,7},{3,5},... | collective-permute-start | bytes 307208 | tf_op jit(solution)/shard_map/ppermute | solution.py:17
  10.9 5.6 %collective-permute-start.4 = (bf16[16,3200]{1,0:T(8,128)(2,1)S(1)}, bf16[16,3200]{1,0:T(8,128)(2,1)S(1)}, u32[]{:S(2)}, u32[]{:S(2)}) collective-permute-start(bf16[16,3200]{1,0:T(8,128)(2,1)S(1)} %collective-permute-done.3.refs_4_), channel_id=1, source_target_pairs={{0,2},{2,0},{4,6},{6,4},{8,10},{10,8},{12,14},{14,12},{1,3},{3,1},... | collective-permute-start | bytes 307208 | tf_op jit(solution)/shard_map/ppermute | solution.py:17
  12.5 5.3 %collective-permute-start.5 = (bf16[16,3200]{1,0:T(8,128)(2,1)S(1)}, bf16[16,3200]{1,0:T(8,128)(2,1)S(1)}, u32[]{:S(2)}, u32[]{:S(2)}) collective-permute-start(bf16[16,3200]{1,0:T(8,128)(2,1)S(1)} %collective-permute-done.3.refs_4_), channel_id=1, source_target_pairs={{0,4},{2,6},{4,0},{6,2},{8,12},{10,14},{12,8},{14,10},{1,5},{3,7},... | collective-permute-start | bytes 307208 | tf_op jit(solution)/shard_map/ppermute | solution.py:17
  13.1 6.2 %collective-permute-start.6 = (bf16[16,3200]{1,0:T(8,128)(2,1)S(1)}, bf16[16,3200]{1,0:T(8,128)(2,1)S(1)}, u32[]{:S(2)}, u32[]{:S(2)}) collective-permute-start(bf16[16,3200]{1,0:T(8,128)(2,1)S(1)} %collective-permute-done.3.refs_4_), channel_id=1, source_target_pairs={{0,6},{2,4},{4,2},{6,0},{8,14},{10,12},{12,10},{14,8},{1,7},{3,5},... | collective-permute-start | bytes 307208 | tf_op jit(solution)/shard_map/ppermute | solution.py:17
  29.6 15.1 %collective-permute-start.7 = (f32[4112,128]{1,0:T(8,128)S(1)}, f32[4112,128]{1,0:T(8,128)S(1)}, u32[]{:S(2)}, u32[]{:S(2)}) collective-permute-start(f32[4112,128]{1,0:T(8,128)S(1)} %get-tuple-element.16.gate_a), channel_id=1, source_target_pairs={{0,1},{1,0},{2,3},{3,2},{4,5},{5,4},{6,7},{7,6},{8,9},{9,8},{10,11... | collective-permute-start | bytes 6316040 | tf_op jit(solution)/shard_map/ppermute | solution.py:165
  29.7 15.0 %slice-start = ((s8[25165824]{0:T(1024)(128)(4,1)}), s8[4194304]{0:T(1024)(128)(4,1)S(1)}, s32[]{:S(2)}) async-start(s8[25165824]{0:T(1024)(128)(4,1)} %bitcast.1), calls=%async_computation | async-start | bytes 8388608
  29.7 15.0 %slice-start.1 = ((s8[25165824]{0:T(1024)(128)(4,1)}), s8[4194304]{0:T(1024)(128)(4,1)S(1)}, s32[]{:S(2)}) async-start(s8[25165824]{0:T(1024)(128)(4,1)} %bitcast.1), calls=%async_computation.1 | async-start | bytes 8388608
  29.7 15.0 %slice-start.2 = ((s8[25165824]{0:T(1024)(128)(4,1)}), s8[4194304]{0:T(1024)(128)(4,1)S(1)}, s32[]{:S(2)}) async-start(s8[25165824]{0:T(1024)(128)(4,1)} %bitcast.1), calls=%async_computation.2 | async-start | bytes 8388608
  29.7 15.0 %slice-start.3 = ((s8[25165824]{0:T(1024)(128)(4,1)}), s8[4194304]{0:T(1024)(128)(4,1)S(1)}, s32[]{:S(2)}) async-start(s8[25165824]{0:T(1024)(128)(4,1)} %bitcast.1), calls=%async_computation.3 | async-start | bytes 8388608
  36.4 8.3 %slice-start.4 = ((s8[25165824]{0:T(1024)(128)(4,1)}), s8[4194304]{0:T(1024)(128)(4,1)S(1)}, s32[]{:S(2)}) async-start(s8[25165824]{0:T(1024)(128)(4,1)} %bitcast.1), calls=%async_computation.4 | async-start | bytes 8388608
  36.5 9.2 %slice-start.5 = ((s8[25165824]{0:T(1024)(128)(4,1)}), s8[4194304]{0:T(1024)(128)(4,1)S(1)}, s32[]{:S(2)}) async-start(s8[25165824]{0:T(1024)(128)(4,1)} %bitcast.1), calls=%async_computation.5 | async-start | bytes 8388608
  36.5 8.2 %collective-permute-start.9 = (f32[2048,128]{1,0:T(8,128)S(1)}, f32[2048,128]{1,0:T(8,128)S(1)}, u32[]{:S(2)}, u32[]{:S(2)}) collective-permute-start(f32[2048,128]{1,0:T(8,128)S(1)} %shard_map.67.up_a), channel_id=1, source_target_pairs={{0,1},{1,0},{2,3},{3,2},{4,5},{5,4},{6,7},{7,6},{8,9},{9,8},{10,11... | collective-permute-start | bytes 3145736 | tf_op jit(solution)/shard_map/ppermute | solution.py:179
  44.4 3.3 %collective-permute-start.8 = (f32[2048,128]{1,0:T(8,128)S(1)}, f32[2048,128]{1,0:T(8,128)S(1)}, u32[]{:S(2)}, u32[]{:S(2)}) collective-permute-start(f32[2048,128]{1,0:T(8,128)S(1)} %shard_map.66.up_a), channel_id=1, source_target_pairs={{0,1},{1,0},{2,3},{3,2},{4,5},{5,4},{6,7},{7,6},{8,9},{9,8},{10,11... | collective-permute-start | bytes 3145736 | tf_op jit(solution)/shard_map/ppermute | solution.py:179
  47.8 8.2 %copy-start = (bf16[4,1024,3072]{2,1,0:T(8,128)(2,1)S(1)}, bf16[4,1024,3072]{2,1,0:T(8,128)(2,1)}, u32[]{:S(2)}) copy-start(bf16[4,1024,3072]{2,1,0:T(8,128)(2,1)} %w_ref.7) | copy-start | bytes 75497472
  58.2 5.6 %collective-permute-start.13 = (bf16[16,3072]{1,0:T(8,128)(2,1)S(1)}, bf16[16,3072]{1,0:T(8,128)(2,1)S(1)}, u32[]{:S(2)}, u32[]{:S(2)}) collective-permute-start(bf16[16,3072]{1,0:T(8,128)(2,1)S(1)} %get-tuple-element.22), channel_id=1, source_target_pairs={{0,2},{2,0},{4,6},{6,4},{8,10},{10,8},{12,14},{14,12},{1,3},{3,1},... | collective-permute-start | bytes 294920 | tf_op jit(solution)/shard_map/ppermute | solution.py:17
  59.4 5.9 %collective-permute-start.14 = (bf16[16,3072]{1,0:T(8,128)(2,1)S(1)}, bf16[16,3072]{1,0:T(8,128)(2,1)S(1)}, u32[]{:S(2)}, u32[]{:S(2)}) collective-permute-start(bf16[16,3072]{1,0:T(8,128)(2,1)S(1)} %get-tuple-element.23), channel_id=1, source_target_pairs={{0,4},{2,6},{4,0},{6,2},{8,12},{10,14},{12,8},{14,10},{1,5},{3,7},... | collective-permute-start | bytes 294920 | tf_op jit(solution)/shard_map/ppermute | solution.py:17
  60.3 7.2 %collective-permute-start.15 = (bf16[16,3072]{1,0:T(8,128)(2,1)S(1)}, bf16[16,3072]{1,0:T(8,128)(2,1)S(1)}, u32[]{:S(2)}, u32[]{:S(2)}) collective-permute-start(bf16[16,3072]{1,0:T(8,128)(2,1)S(1)} %get-tuple-element.24), channel_id=1, source_target_pairs={{0,6},{2,4},{4,2},{6,0},{8,14},{10,12},{12,10},{14,8},{1,7},{3,5},... | collective-permute-start | bytes 294920 | tf_op jit(solution)/shard_map/ppermute | solution.py:17
  61.8 8.6 %collective-permute-start.10 = (bf16[16,3072]{1,0:T(8,128)(2,1)S(1)}, bf16[16,3072]{1,0:T(8,128)(2,1)S(1)}, u32[]{:S(2)}, u32[]{:S(2)}) collective-permute-start(bf16[16,3072]{1,0:T(8,128)(2,1)S(1)} %get-tuple-element.18), channel_id=1, source_target_pairs={{0,2},{2,0},{4,6},{6,4},{8,10},{10,8},{12,14},{14,12},{1,3},{3,1},... | collective-permute-start | bytes 294920 | tf_op jit(solution)/shard_map/ppermute | solution.py:17
  62.9 7.5 %collective-permute-start.11 = (bf16[16,3072]{1,0:T(8,128)(2,1)S(1)}, bf16[16,3072]{1,0:T(8,128)(2,1)S(1)}, u32[]{:S(2)}, u32[]{:S(2)}) collective-permute-start(bf16[16,3072]{1,0:T(8,128)(2,1)S(1)} %get-tuple-element.19), channel_id=1, source_target_pairs={{0,4},{2,6},{4,0},{6,2},{8,12},{10,14},{12,8},{14,10},{1,5},{3,7},... | collective-permute-start | bytes 294920 | tf_op jit(solution)/shard_map/ppermute | solution.py:17
  63.8 8.3 %collective-permute-start.12 = (bf16[16,3072]{1,0:T(8,128)(2,1)S(1)}, bf16[16,3072]{1,0:T(8,128)(2,1)S(1)}, u32[]{:S(2)}, u32[]{:S(2)}) collective-permute-start(bf16[16,3072]{1,0:T(8,128)(2,1)S(1)} %get-tuple-element.20), channel_id=1, source_target_pairs={{0,6},{2,4},{4,2},{6,0},{8,14},{10,12},{12,10},{14,8},{1,7},{3,5},... | collective-permute-start | bytes 294920 | tf_op jit(solution)/shard_map/ppermute | solution.py:17
  67.5 7.6 %collective-permute-start.16 = (bf16[16,3072]{1,0:T(8,128)(2,1)S(1)}, bf16[16,3072]{1,0:T(8,128)(2,1)S(1)}, u32[]{:S(2)}, u32[]{:S(2)}) collective-permute-start(bf16[16,3072]{1,0:T(8,128)(2,1)S(1)} %add_convert_fusion.1), channel_id=1, source_target_pairs={{0,8},{2,10},{4,12},{6,14},{8,0},{10,2},{12,4},{14,6},{1,9},{3,11}... | collective-permute-start | bytes 294920 | tf_op jit(solution)/shard_map/ppermute | solution.py:17

commit v2 on v1

--- a/solution.py
+++ b/solution.py
@@ -85,9 +85,10 @@
     stream(w_ref, held_ref, sems, range(experts), part_ref, load)
 
 
-def up_kernel(experts, turned_ref, w_ref, part_ref, held_ref, sems):
+def up_kernel(experts, turned_ref, w_ref, _, part_ref, sent_ref, held_ref, sems):
     width = w_ref.shape[2]
     stream(w_ref, held_ref, sems, experts, part_ref, lambda: turned_ref[:width])
+    sent_ref[...] = part_ref[...].astype(BF16)
 
 
 def factors(turned_ref, gate_a, gate_b, width, base, experts):
@@ -103,30 +104,31 @@
     return (jnp.where(is_a, wa, 0.0) + jnp.where(is_b, wb, 0.0)).T
 
 
-def down_terms(first, count, turned_ref, gate_a, gate_b, up_a, up_b, w_ref):
+def hidden_units(e, i, hidden, gate_a, gate_b, up_a, up_b):
+    own = slice(e * hidden, (e + 1) * hidden)
+    mine = slice(i * hidden, (i + 1) * hidden)
+    gate = gate_a[own] + gate_b[own]
+    up = up_a[mine] + up_b[mine].astype(F32)
+    return (gate / (1.0 + jnp.exp(-gate)) * up).T.astype(BF16)
+
+
+def hidden_kernel(experts, gate_a, gate_b, up_a, up_b, _, out_ref):
+    hidden = out_ref.shape[2]
+    for i, e in enumerate(experts):
+        out_ref[i] = hidden_units(e, i, hidden, gate_a, gate_b, up_a, up_b)
+
+
+def down_kernel(first, turned_ref, gate_a, gate_b, up_a, up_b, h_ref, w_ref, *outs):
     experts, hidden, width = w_ref.shape
     factor = factors(turned_ref, gate_a, gate_b, width, experts * hidden, experts)
     total = None
-    for i in range(count):
-        e = first + i
-        own = slice(e * hidden, (e + 1) * hidden)
-        mine = slice(i * hidden, (i + 1) * hidden)
-        gate = gate_a[own] + gate_b[own]
-        up = up_a[mine] + up_b[mine]
-        h = (gate / (1.0 + jnp.exp(-gate)) * up).T.astype(BF16)
+    for e in range(experts):
+        if e < first:
+            h = h_ref[e]
+        else:
+            h = hidden_units(e, e - first, hidden, gate_a, gate_b, up_a, up_b)
         term = factor[:, e : e + 1] * jnp.dot(h, w_ref[e], preferred_element_type=F32)
         total = term if total is None else total + term
-    return total
-
-
-def down_first(count, turned_ref, gate_a, gate_b, up_a, up_b, w_ref, out_ref):
-    out_ref[...] = down_terms(0, count, turned_ref, gate_a, gate_b, up_a, up_b, w_ref)
-
-
-def down_last(first, count, turned_ref, gate_a, gate_b, up_a, up_b, w_ref, sum_ref, *outs):
-    total = sum_ref[...] + down_terms(
-        first, count, turned_ref, gate_a, gate_b, up_a, up_b, w_ref
-    )
     rows = outs[0].shape[0]
     for j, out in enumerate(outs):
         out[...] = total[j * rows : (j + 1) * rows].astype(out.dtype)
@@ -150,7 +152,7 @@
     w_down = in_vmem(w_down)
     flops = 2 * count * hidden * width
     size = 2 * hidden * width
-    slots, tile = 4, min(hidden, 256)
+    slots, tile = 3, min(hidden, 256)
     held = [pltpu.VMEM((slots, tile, width), BF16), pltpu.SemaphoreType.DMA((slots,))]
     turned, gate = call(
         gate_kernel,
@@ -158,7 +160,7 @@
         [*blocks, jnp.pad(router.T, ((0, 16 - experts), (0, 0))), w_gate],
         experts * flops,
         experts * size,
-        10,
+        8,
         [pltpu.VMEM((count, width + IDS), F32), *held],
         hbm=(9,),
     )
@@ -166,32 +168,32 @@
     half = experts // 2
     ups = []
     for first in (0, half):
-        (up,) = call(
+        up, sent = call(
             functools.partial(up_kernel, range(first, first + half)),
-            [shape(half * hidden, count)],
-            [turned, w_up],
+            [shape(half * hidden, count), shape(half * hidden, count, dtype=BF16)],
+            [turned, w_up, w_down],
             half * flops,
             half * size,
-            10,
+            8,
             held,
             hbm=(1,),
         )
-        ups.append((up, lax.ppermute(up, "mp", SWAP)))
-    (partial_sum,) = call(
-        functools.partial(down_first, half),
-        [shape(count, width)],
-        [turned, gate, gate_other, *ups[0], w_down],
-        half * flops,
-        half * size,
-        8,
+        ups.append((up, lax.ppermute(sent, "mp", SWAP)))
+    (units,) = call(
+        functools.partial(hidden_kernel, range(half)),
+        [shape(half, count, hidden, dtype=BF16)],
+        [gate, gate_other, *ups[0], w_down],
+        0,
+        12 * half * hidden * count,
+        4,
     )
     parts = call(
-        functools.partial(down_last, half, half),
+        functools.partial(down_kernel, half),
         [shape(rows, width)] + [shape(rows, width, dtype=BF16)] * 7,
-        [turned, gate, gate_other, *ups[1], w_down, partial_sum],
-        half * flops,
-        half * size,
-        8,
+        [turned, gate, gate_other, *ups[1], units, w_down],
+        experts * flops,
+        experts * size,
+        5,
     )
     far_sums = [xor_send(parts[4 ^ k], k) for k in (1, 2, 3)]
     near_sums = [xor_send(parts[k], k) for k in (1, 2, 3)]

time: 76.1 us -> 68.7 us (0.903)
  local copies, waits for them, and re-layouts: 11.5 us -> 2.4 us
  waiting for transfers between devices: 12.7 us -> 13.9 us
    unnamed x17 -> x5, local copies, waits for them, and re-layouts: 10.7 us -> 1.65 us
    ppermute x2, waiting for transfers between devices: 0.01 us -> 1.39 us  [fast(): ups.append((up, lax.ppermute(sent, 'mp', SWAP)))]
  transfers between devices with their start and end apart: 17 -> 17, of which waited for: 8 -> 9; matrix products, arithmetic and copies ran while one was open for 1% -> 1% of each run, Pallas kernels for 21% -> 20%
where the time goes in v2:
time: 68.7 us; the launch traced here: 68.4 us
  Pallas kernels  29.4 us (43%)
  starting transfers between devices  21.8 us (32%)
  waiting for transfers between devices  13.9 us (20%)
  local copies, waits for them, and re-layouts  2.4 us (3%)
  other arithmetic  0.75 us (1%)
    pallas_call x6, Pallas kernels, call(): pl.pallas_call(kernel, out_shape=outs, in_specs=specs, out_specs=[VMEM_BL...  29.4 us
    ppermute x14, starting transfers between devices, xor_send(): return lax.ppermute(block, 'batch', [(i, i ^ mask) for i in range(8)])  20.9 us
    ppermute x14, waiting for transfers between devices, xor_send(): return lax.ppermute(block, 'batch', [(i, i ^ mask) for i in range(8)])  12.5 us
    unnamed x5, local copies, waits for them, and re-layouts  1.65 us
    ppermute x2, waiting for transfers between devices, fast(): ups.append((up, lax.ppermute(sent, 'mp', SWAP)))  1.39 us
  transfers between devices with their start and end apart: 17, of which 9 were waited for; matrix products, arithmetic and copies ran while one was open for 1% of the time, Pallas kernels for 20%

profile of v2, /device:TPU:0, one launch (start us, length us, event | category | flops | bytes accessed | tf_op | source)
XLA Modules:
  0.0 68.4 jit_solution(12745850441998079014)
XLA Ops:
  0.0 0.8 %copy.7.ids_ref = s32[16,2]{1,0:T(8,128)S(1)} copy(s32[16,2]{0,1:T(2,128)} %param.7) | data formatting | bytes 256 | tf_op args[1]
  0.8 0.0 copy-start.1
  0.8 0.9 %copy-done.1 = bf16[16,3072]{1,0:T(8,128)(2,1)S(1)} copy-done((bf16[16,3072]{1,0:T(8,128)(2,1)S(1)}, bf16[16,3072]{1,0:T(8,128)(2,1)}, u32[]{:S(2)}) %copy-start.1) | copy-done | bytes 98328
  1.6 0.0 copy-start
  1.7 0.1 shard_map.64.refs_0_
  1.7 4.0 %collective-permute-start.3 = (bf16[16,3200]{1,0:T(8,128)(2,1)S(1)}, bf16[16,3200]{1,0:T(8,128)(2,1)S(1)}, u32[]{:S(2)}, u32[]{:S(2)}) collective-permute-start(bf16[16,3200]{1,0:T(8,128)(2,1)S(1)} %shard_map.64.refs_0_), channel_id=1, source_target_pairs={{0,8},{2,10},{4,12},{6,14},{8,0},{10,2},{12,4},{14,6},{1,9},{3,11}... | collective-permute-start | bytes 307208 | tf_op jit(solution)/shard_map/ppermute | solution.py:17
  5.8 1.5 %collective-permute-start = (bf16[16,3200]{1,0:T(8,128)(2,1)S(1)}, bf16[16,3200]{1,0:T(8,128)(2,1)S(1)}, u32[]{:S(2)}, u32[]{:S(2)}) collective-permute-start(bf16[16,3200]{1,0:T(8,128)(2,1)S(1)} %shard_map.64.refs_0_), channel_id=1, source_target_pairs={{0,2},{2,0},{4,6},{6,4},{8,10},{10,8},{12,14},{14,12},{1,3},{3,1},... | collective-permute-start | bytes 307208 | tf_op jit(solution)/shard_map/ppermute | solution.py:17
  7.3 1.6 %collective-permute-start.1 = (bf16[16,3200]{1,0:T(8,128)(2,1)S(1)}, bf16[16,3200]{1,0:T(8,128)(2,1)S(1)}, u32[]{:S(2)}, u32[]{:S(2)}) collective-permute-start(bf16[16,3200]{1,0:T(8,128)(2,1)S(1)} %shard_map.64.refs_0_), channel_id=1, source_target_pairs={{0,4},{2,6},{4,0},{6,2},{8,12},{10,14},{12,8},{14,10},{1,5},{3,7},... | collective-permute-start | bytes 307208 | tf_op jit(solution)/shard_map/ppermute | solution.py:17
  8.9 0.4 collective-permute-start.2
  9.3 1.7 %collective-permute-done.3.refs_4_ = bf16[16,3200]{1,0:T(8,128)(2,1)S(1)} collective-permute-done((bf16[16,3200]{1,0:T(8,128)(2,1)S(1)}, bf16[16,3200]{1,0:T(8,128)(2,1)S(1)}, u32[]{:S(2)}, u32[]{:S(2)}) %collective-permute-start.3) | collective-permute-done | bytes 102432 | tf_op jit(solution)/shard_map/ppermute | solution.py:17
  11.0 1.6 %collective-permute-start.4 = (bf16[16,3200]{1,0:T(8,128)(2,1)S(1)}, bf16[16,3200]{1,0:T(8,128)(2,1)S(1)}, u32[]{:S(2)}, u32[]{:S(2)}) collective-permute-start(bf16[16,3200]{1,0:T(8,128)(2,1)S(1)} %collective-permute-done.3.refs_4_), channel_id=1, source_target_pairs={{0,2},{2,0},{4,6},{6,4},{8,10},{10,8},{12,14},{14,12},{1,3},{3,1},... | collective-permute-start | bytes 307208 | tf_op jit(solution)/shard_map/ppermute | solution.py:17
  12.5 0.6 collective-permute-start.5
  13.1 0.0 collective-permute-done.refs_1_
  13.1 1.4 %collective-permute-start.6 = (bf16[16,3200]{1,0:T(8,128)(2,1)S(1)}, bf16[16,3200]{1,0:T(8,128)(2,1)S(1)}, u32[]{:S(2)}, u32[]{:S(2)}) collective-permute-start(bf16[16,3200]{1,0:T(8,128)(2,1)S(1)} %collective-permute-done.3.refs_4_), channel_id=1, source_target_pairs={{0,6},{2,4},{4,2},{6,0},{8,14},{10,12},{12,10},{14,8},{1,7},{3,5},... | collective-permute-start | bytes 307208 | tf_op jit(solution)/shard_map/ppermute | solution.py:17
  14.4 0.8 %pad.4.refs_8_ = bf16[16,3072]{1,0:T(8,128)(2,1)S(1)} pad(bf16[4,3072]{1,0:T(4,128)(2,1)} %bitcast.1, bf16[]{:T(256)} %constant.2.clone.1), padding=0_12x0_0 | pad | bytes 122882 | tf_op jit(solution)/shard_map/jit(_pad)/pad | solution.py:160
  15.2 0.0 collective-permute-done.1.refs_2_
  15.2 0.4 collective-permute-done.2.refs_3_
  15.6 0.9 %collective-permute-done.4.refs_5_ = bf16[16,3200]{1,0:T(8,128)(2,1)S(1)} collective-permute-done((bf16[16,3200]{1,0:T(8,128)(2,1)S(1)}, bf16[16,3200]{1,0:T(8,128)(2,1)S(1)}, u32[]{:S(2)}, u32[]{:S(2)}) %collective-permute-start.4) | collective-permute-done | bytes 102432 | tf_op jit(solution)/shard_map/ppermute | solution.py:17
  16.5 1.3 %collective-permute-done.5.refs_6_ = bf16[16,3200]{1,0:T(8,128)(2,1)S(1)} collective-permute-done((bf16[16,3200]{1,0:T(8,128)(2,1)S(1)}, bf16[16,3200]{1,0:T(8,128)(2,1)S(1)}, u32[]{:S(2)}, u32[]{:S(2)}) %collective-permute-start.5) | collective-permute-done | bytes 102432 | tf_op jit(solution)/shard_map/ppermute | solution.py:17
  17.8 1.4 %collective-permute-done.6.refs_7_ = bf16[16,3200]{1,0:T(8,128)(2,1)S(1)} collective-permute-done((bf16[16,3200]{1,0:T(8,128)(2,1)S(1)}, bf16[16,3200]{1,0:T(8,128)(2,1)S(1)}, u32[]{:S(2)}, u32[]{:S(2)}) %collective-permute-start.6) | collective-permute-done | bytes 102432 | tf_op jit(solution)/shard_map/ppermute | solution.py:17
  19.3 11.9 %shard_map.65 = (bf16[3200,128]{1,0:T(8,128)(2,1)S(1)}, f32[4112,128]{1,0:T(8,128)S(1)}) custom-call(bf16[16,3200]{1,0:T(8,128)(2,1)S(1)} %shard_map.64.refs_0_, bf16[16,3200]{1,0:T(8,128)(2,1)S(1)} %collective-permute-done.refs_1_, bf16[16,3200]{1,0:T(8,128)(2,1)S(1)} %collective-permute-done.1.refs_2_, ...), custom_call_target="tpu_custom_call" | custom-call | flops 3221225472 | bytes 25165824 | tf_op jit(solution)/shard_map/pallas_call | solution.py:26
  31.2 0.1 collective-permute-start.7
  31.3 0.0 copy-done
  31.3 6.5 %shard_map.67 = (f32[2048,128]{1,0:T(8,128)S(1)}, bf16[2048,128]{1,0:T(8,128)(2,1)S(1)}) custom-call(bf16[3200,128]{1,0:T(8,128)(2,1)S(1)} %get-tuple-element.19.turned_ref, bf16[4,1024,3072]{2,1,0:T(8,128)(2,1)} %w_ref.4, bf16[4,1024,3072]{2,1,0:T(8,128)(2,1)S(1)} %copy-done), custom_call_target="tpu_custom_call" | custom-call | flops 1610612736 | bytes 12582912 | tf_op jit(solution)/shard_map/pallas_call | solution.py:26
  37.8 0.7 %collective-permute-start.9 = (bf16[2048,128]{1,0:T(8,128)(2,1)S(1)}, bf16[2048,128]{1,0:T(8,128)(2,1)S(1)}, u32[]{:S(2)}, u32[]{:S(2)}) collective-permute-start(bf16[2048,128]{1,0:T(8,128)(2,1)S(1)} %get-tuple-element.24), channel_id=1, source_target_pairs={{0,1},{1,0},{2,3},{3,2},{4,5},{5,4},{6,7},{7,6},{8,9},{9,8},{10,11... | collective-permute-start | bytes 1572872 | tf_op jit(solution)/shard_map/ppermute | solution.py:181
  38.6 6.5 %shard_map.66 = (f32[2048,128]{1,0:T(8,128)S(1)}, bf16[2048,128]{1,0:T(8,128)(2,1)S(1)}) custom-call(bf16[3200,128]{1,0:T(8,128)(2,1)S(1)} %get-tuple-element.19.turned_ref, bf16[4,1024,3072]{2,1,0:T(8,128)(2,1)} %w_ref.4, bf16[4,1024,3072]{2,1,0:T(8,128)(2,1)S(1)} %copy-done), custom_call_target="tpu_custom_call" | custom-call | flops 1610612736 | bytes 12582912 | tf_op jit(solution)/shard_map/pallas_call | solution.py:26
  45.1 0.1 collective-permute-start.8
  45.2 0.0 collective-permute-done.9.up_b
  45.2 0.0 collective-permute-done.7.gate_b
  45.2 0.5 shard_map.68.h_ref
  45.7 1.4 %collective-permute-done.8.up_b = bf16[2048,128]{1,0:T(8,128)(2,1)S(1)} collective-permute-done((bf16[2048,128]{1,0:T(8,128)(2,1)S(1)}, bf16[2048,128]{1,0:T(8,128)(2,1)S(1)}, u32[]{:S(2)}, u32[]{:S(2)}) %collective-permute-start.8) | collective-permute-done | bytes 524320 | tf_op jit(solution)/shard_map/ppermute | solution.py:181
  47.1 3.9 %shard_map.69 = (f32[16,3072]{1,0:T(8,128)S(1)}, bf16[16,3072]{1,0:T(8,128)(2,1)S(1)}, bf16[16,3072]{1,0:T(8,128)(2,1)S(1)}, bf16[16,3072]{1,0:T(8,128)(2,1)S(1)...) custom-call(bf16[3200,128]{1,0:T(8,128)(2,1)S(1)} %get-tuple-element, ...), custom_call_target="tpu_custom_call" | custom-call | flops 3221225472 | bytes 25165824 | tf_op jit(solution)/shard_map/pallas_call | solution.py:26
  51.0 1.2 %collective-permute-start.13 = (bf16[16,3072]{1,0:T(8,128)(2,1)S(1)}, bf16[16,3072]{1,0:T(8,128)(2,1)S(1)}, u32[]{:S(2)}, u32[]{:S(2)}) collective-permute-start(bf16[16,3072]{1,0:T(8,128)(2,1)S(1)} %get-tuple-element.30), channel_id=1, source_target_pairs={{0,2},{2,0},{4,6},{6,4},{8,10},{10,8},{12,14},{14,12},{1,3},{3,1},... | collective-permute-start | bytes 294920 | tf_op jit(solution)/shard_map/ppermute | solution.py:17
  52.1 0.9 %collective-permute-start.14 = (bf16[16,3072]{1,0:T(8,128)(2,1)S(1)}, bf16[16,3072]{1,0:T(8,128)(2,1)S(1)}, u32[]{:S(2)}, u32[]{:S(2)}) collective-permute-start(bf16[16,3072]{1,0:T(8,128)(2,1)S(1)} %get-tuple-element.31), channel_id=1, source_target_pairs={{0,4},{2,6},{4,0},{6,2},{8,12},{10,14},{12,8},{14,10},{1,5},{3,7},... | collective-permute-start | bytes 294920 | tf_op jit(solution)/shard_map/ppermute | solution.py:17
  53.0 1.5 %collective-permute-start.15 = (bf16[16,3072]{1,0:T(8,128)(2,1)S(1)}, bf16[16,3072]{1,0:T(8,128)(2,1)S(1)}, u32[]{:S(2)}, u32[]{:S(2)}) collective-permute-start(bf16[16,3072]{1,0:T(8,128)(2,1)S(1)} %get-tuple-element.32), channel_id=1, source_target_pairs={{0,6},{2,4},{4,2},{6,0},{8,14},{10,12},{12,10},{14,8},{1,7},{3,5},... | collective-permute-start | bytes 294920 | tf_op jit(solution)/shard_map/ppermute | solution.py:17
  54.5 1.1 %collective-permute-start.10 = (bf16[16,3072]{1,0:T(8,128)(2,1)S(1)}, bf16[16,3072]{1,0:T(8,128)(2,1)S(1)}, u32[]{:S(2)}, u32[]{:S(2)}) collective-permute-start(bf16[16,3072]{1,0:T(8,128)(2,1)S(1)} %get-tuple-element.26), channel_id=1, source_target_pairs={{0,2},{2,0},{4,6},{6,4},{8,10},{10,8},{12,14},{14,12},{1,3},{3,1},... | collective-permute-start | bytes 294920 | tf_op jit(solution)/shard_map/ppermute | solution.py:17
  55.6 0.9 %collective-permute-start.11 = (bf16[16,3072]{1,0:T(8,128)(2,1)S(1)}, bf16[16,3072]{1,0:T(8,128)(2,1)S(1)}, u32[]{:S(2)}, u32[]{:S(2)}) collective-permute-start(bf16[16,3072]{1,0:T(8,128)(2,1)S(1)} %get-tuple-element.27), channel_id=1, source_target_pairs={{0,4},{2,6},{4,0},{6,2},{8,12},{10,14},{12,8},{14,10},{1,5},{3,7},... | collective-permute-start | bytes 294920 | tf_op jit(solution)/shard_map/ppermute | solution.py:17
  56.5 0.0 collective-permute-done.13
  56.5 1.5 %collective-permute-start.12 = (bf16[16,3072]{1,0:T(8,128)(2,1)S(1)}, bf16[16,3072]{1,0:T(8,128)(2,1)S(1)}, u32[]{:S(2)}, u32[]{:S(2)}) collective-permute-start(bf16[16,3072]{1,0:T(8,128)(2,1)S(1)} %get-tuple-element.28), channel_id=1, source_target_pairs={{0,6},{2,4},{4,2},{6,0},{8,14},{10,12},{12,10},{14,8},{1,7},{3,5},... | collective-permute-start | bytes 294920 | tf_op jit(solution)/shard_map/ppermute | solution.py:17
  58.0 0.0 collective-permute-done.14
  58.0 2.2 %collective-permute-done.15 = bf16[16,3072]{1,0:T(8,128)(2,1)S(1)} collective-permute-done((bf16[16,3072]{1,0:T(8,128)(2,1)S(1)}, bf16[16,3072]{1,0:T(8,128)(2,1)S(1)}, u32[]{:S(2)}, u32[]{:S(2)}) %collective-permute-start.15) | collective-permute-done | bytes 98336 | tf_op jit(solution)/shard_map/ppermute | solution.py:17
  60.2 0.1 add_convert_fusion.1
  60.3 2.9 %collective-permute-start.16 = (bf16[16,3072]{1,0:T(8,128)(2,1)S(1)}, bf16[16,3072]{1,0:T(8,128)(2,1)S(1)}, u32[]{:S(2)}, u32[]{:S(2)}) collective-permute-start(bf16[16,3072]{1,0:T(8,128)(2,1)S(1)} %add_convert_fusion.1), channel_id=1, source_target_pairs={{0,8},{2,10},{4,12},{6,14},{8,0},{10,2},{12,4},{14,6},{1,9},{3,11}... | collective-permute-start | bytes 294920 | tf_op jit(solution)/shard_map/ppermute | solution.py:17
  63.2 0.0 collective-permute-done.10
  63.2 0.0 collective-permute-done.11
  63.2 1.3 %collective-permute-done.12 = bf16[16,3072]{1,0:T(8,128)(2,1)S(1)} collective-permute-done((bf16[16,3072]{1,0:T(8,128)(2,1)S(1)}, bf16[16,3072]{1,0:T(8,128)(2,1)S(1)}, u32[]{:S(2)}, u32[]{:S(2)}) %collective-permute-start.12) | collective-permute-done | bytes 98336 | tf_op jit(solution)/shard_map/ppermute | solution.py:17
  64.5 3.2 %collective-permute-done.16 = bf16[16,3072]{1,0:T(8,128)(2,1)S(1)} collective-permute-done((bf16[16,3072]{1,0:T(8,128)(2,1)S(1)}, bf16[16,3072]{1,0:T(8,128)(2,1)S(1)}, u32[]{:S(2)}, u32[]{:S(2)}) %collective-permute-start.16) | collective-permute-done | bytes 98336 | tf_op jit(solution)/shard_map/ppermute | solution.py:17
  67.7 0.7 %add_convert_fusion = bf16[16,3072]{1,0:T(8,128)(2,1)} fusion(bf16[16,3072]{1,0:T(8,128)(2,1)S(1)} %collective-permute-done.16, bf16[16,3072]{1,0:T(8,128)(2,1)S(1)} %collective-permute-done.12, bf16[16,3072]{1,0:T(8,128)(2,1)S(1)} %collective-permute-done.11, f32[16,3072]{1,0:T(8,128)S(1)} %get-tuple-element.25, bf16[16,3072]{1,0:T(8,128)(2,1)S(1)} %collective-permute-done.10), kind=kLoop, calls=%fused_computation | loop fusion | flops 442368 | bytes 688128 | tf_op jit(solution)/shard_map/convert_element_type | solution.py:202
Async XLA Ops:
  0.8 0.9 %copy-start.1 = (bf16[16,3072]{1,0:T(8,128)(2,1)S(1)}, bf16[16,3072]{1,0:T(8,128)(2,1)}, u32[]{:S(2)}) copy-start(bf16[16,3072]{1,0:T(8,128)(2,1)} %tokens_ref.1) | copy-start | bytes 294916
  1.6 29.6 %copy-start = (bf16[4,1024,3072]{2,1,0:T(8,128)(2,1)S(1)}, bf16[4,1024,3072]{2,1,0:T(8,128)(2,1)}, u32[]{:S(2)}) copy-start(bf16[4,1024,3072]{2,1,0:T(8,128)(2,1)} %w_ref.5) | copy-start | bytes 75497472
  1.7 9.2 %collective-permute-start.3 = (bf16[16,3200]{1,0:T(8,128)(2,1)S(1)}, bf16[16,3200]{1,0:T(8,128)(2,1)S(1)}, u32[]{:S(2)}, u32[]{:S(2)}) collective-permute-start(bf16[16,3200]{1,0:T(8,128)(2,1)S(1)} %shard_map.64.refs_0_), channel_id=1, source_target_pairs={{0,8},{2,10},{4,12},{6,14},{8,0},{10,2},{12,4},{14,6},{1,9},{3,11}... | collective-permute-start | bytes 307208 | tf_op jit(solution)/shard_map/ppermute | solution.py:17
  5.8 7.3 %collective-permute-start = (bf16[16,3200]{1,0:T(8,128)(2,1)S(1)}, bf16[16,3200]{1,0:T(8,128)(2,1)S(1)}, u32[]{:S(2)}, u32[]{:S(2)}) collective-permute-start(bf16[16,3200]{1,0:T(8,128)(2,1)S(1)} %shard_map.64.refs_0_), channel_id=1, source_target_pairs={{0,2},{2,0},{4,6},{6,4},{8,10},{10,8},{12,14},{14,12},{1,3},{3,1},... | collective-permute-start | bytes 307208 | tf_op jit(solution)/shard_map/ppermute | solution.py:17
  7.3 7.9 %collective-permute-start.1 = (bf16[16,3200]{1,0:T(8,128)(2,1)S(1)}, bf16[16,3200]{1,0:T(8,128)(2,1)S(1)}, u32[]{:S(2)}, u32[]{:S(2)}) collective-permute-start(bf16[16,3200]{1,0:T(8,128)(2,1)S(1)} %shard_map.64.refs_0_), channel_id=1, source_target_pairs={{0,4},{2,6},{4,0},{6,2},{8,12},{10,14},{12,8},{14,10},{1,5},{3,7},... | collective-permute-start | bytes 307208 | tf_op jit(solution)/shard_map/ppermute | solution.py:17
  8.9 6.7 %collective-permute-start.2 = (bf16[16,3200]{1,0:T(8,128)(2,1)S(1)}, bf16[16,3200]{1,0:T(8,128)(2,1)S(1)}, u32[]{:S(2)}, u32[]{:S(2)}) collective-permute-start(bf16[16,3200]{1,0:T(8,128)(2,1)S(1)} %shard_map.64.refs_0_), channel_id=1, source_target_pairs={{0,6},{2,4},{4,2},{6,0},{8,14},{10,12},{12,10},{14,8},{1,7},{3,5},... | collective-permute-start | bytes 307208 | tf_op jit(solution)/shard_map/ppermute | solution.py:17
  11.0 5.6 %collective-permute-start.4 = (bf16[16,3200]{1,0:T(8,128)(2,1)S(1)}, bf16[16,3200]{1,0:T(8,128)(2,1)S(1)}, u32[]{:S(2)}, u32[]{:S(2)}) collective-permute-start(bf16[16,3200]{1,0:T(8,128)(2,1)S(1)} %collective-permute-done.3.refs_4_), channel_id=1, source_target_pairs={{0,2},{2,0},{4,6},{6,4},{8,10},{10,8},{12,14},{14,12},{1,3},{3,1},... | collective-permute-start | bytes 307208 | tf_op jit(solution)/shard_map/ppermute | solution.py:17
  12.5 5.3 %collective-permute-start.5 = (bf16[16,3200]{1,0:T(8,128)(2,1)S(1)}, bf16[16,3200]{1,0:T(8,128)(2,1)S(1)}, u32[]{:S(2)}, u32[]{:S(2)}) collective-permute-start(bf16[16,3200]{1,0:T(8,128)(2,1)S(1)} %collective-permute-done.3.refs_4_), channel_id=1, source_target_pairs={{0,4},{2,6},{4,0},{6,2},{8,12},{10,14},{12,8},{14,10},{1,5},{3,7},... | collective-permute-start | bytes 307208 | tf_op jit(solution)/shard_map/ppermute | solution.py:17
  13.1 6.2 %collective-permute-start.6 = (bf16[16,3200]{1,0:T(8,128)(2,1)S(1)}, bf16[16,3200]{1,0:T(8,128)(2,1)S(1)}, u32[]{:S(2)}, u32[]{:S(2)}) collective-permute-start(bf16[16,3200]{1,0:T(8,128)(2,1)S(1)} %collective-permute-done.3.refs_4_), channel_id=1, source_target_pairs={{0,6},{2,4},{4,2},{6,0},{8,14},{10,12},{12,10},{14,8},{1,7},{3,5},... | collective-permute-start | bytes 307208 | tf_op jit(solution)/shard_map/ppermute | solution.py:17
  31.2 14.0 %collective-permute-start.7 = (f32[4112,128]{1,0:T(8,128)S(1)}, f32[4112,128]{1,0:T(8,128)S(1)}, u32[]{:S(2)}, u32[]{:S(2)}) collective-permute-start(f32[4112,128]{1,0:T(8,128)S(1)} %get-tuple-element.20.gate_a), channel_id=1, source_target_pairs={{0,1},{1,0},{2,3},{3,2},{4,5},{5,4},{6,7},{7,6},{8,9},{9,8},{10,11... | collective-permute-start | bytes 6316040 | tf_op jit(solution)/shard_map/ppermute | solution.py:167
  37.8 7.4 %collective-permute-start.9 = (bf16[2048,128]{1,0:T(8,128)(2,1)S(1)}, bf16[2048,128]{1,0:T(8,128)(2,1)S(1)}, u32[]{:S(2)}, u32[]{:S(2)}) collective-permute-start(bf16[2048,128]{1,0:T(8,128)(2,1)S(1)} %get-tuple-element.24), channel_id=1, source_target_pairs={{0,1},{1,0},{2,3},{3,2},{4,5},{5,4},{6,7},{7,6},{8,9},{9,8},{10,11... | collective-permute-start | bytes 1572872 | tf_op jit(solution)/shard_map/ppermute | solution.py:181
  45.1 2.0 %collective-permute-start.8 = (bf16[2048,128]{1,0:T(8,128)(2,1)S(1)}, bf16[2048,128]{1,0:T(8,128)(2,1)S(1)}, u32[]{:S(2)}, u32[]{:S(2)}) collective-permute-start(bf16[2048,128]{1,0:T(8,128)(2,1)S(1)} %get-tuple-element.22), channel_id=1, source_target_pairs={{0,1},{1,0},{2,3},{3,2},{4,5},{5,4},{6,7},{7,6},{8,9},{9,8},{10,11... | collective-permute-start | bytes 1572872 | tf_op jit(solution)/shard_map/ppermute | solution.py:181
  51.0 5.6 %collective-permute-start.13 = (bf16[16,3072]{1,0:T(8,128)(2,1)S(1)}, bf16[16,3072]{1,0:T(8,128)(2,1)S(1)}, u32[]{:S(2)}, u32[]{:S(2)}) collective-permute-start(bf16[16,3072]{1,0:T(8,128)(2,1)S(1)} %get-tuple-element.30), channel_id=1, source_target_pairs={{0,2},{2,0},{4,6},{6,4},{8,10},{10,8},{12,14},{14,12},{1,3},{3,1},... | collective-permute-start | bytes 294920 | tf_op jit(solution)/shard_map/ppermute | solution.py:17
  52.1 5.9 %collective-permute-start.14 = (bf16[16,3072]{1,0:T(8,128)(2,1)S(1)}, bf16[16,3072]{1,0:T(8,128)(2,1)S(1)}, u32[]{:S(2)}, u32[]{:S(2)}) collective-permute-start(bf16[16,3072]{1,0:T(8,128)(2,1)S(1)} %get-tuple-element.31), channel_id=1, source_target_pairs={{0,4},{2,6},{4,0},{6,2},{8,12},{10,14},{12,8},{14,10},{1,5},{3,7},... | collective-permute-start | bytes 294920 | tf_op jit(solution)/shard_map/ppermute | solution.py:17
  53.0 7.2 %collective-permute-start.15 = (bf16[16,3072]{1,0:T(8,128)(2,1)S(1)}, bf16[16,3072]{1,0:T(8,128)(2,1)S(1)}, u32[]{:S(2)}, u32[]{:S(2)}) collective-permute-start(bf16[16,3072]{1,0:T(8,128)(2,1)S(1)} %get-tuple-element.32), channel_id=1, source_target_pairs={{0,6},{2,4},{4,2},{6,0},{8,14},{10,12},{12,10},{14,8},{1,7},{3,5},... | collective-permute-start | bytes 294920 | tf_op jit(solution)/shard_map/ppermute | solution.py:17
  54.5 8.6 %collective-permute-start.10 = (bf16[16,3072]{1,0:T(8,128)(2,1)S(1)}, bf16[16,3072]{1,0:T(8,128)(2,1)S(1)}, u32[]{:S(2)}, u32[]{:S(2)}) collective-permute-start(bf16[16,3072]{1,0:T(8,128)(2,1)S(1)} %get-tuple-element.26), channel_id=1, source_target_pairs={{0,2},{2,0},{4,6},{6,4},{8,10},{10,8},{12,14},{14,12},{1,3},{3,1},... | collective-permute-start | bytes 294920 | tf_op jit(solution)/shard_map/ppermute | solution.py:17
  55.6 7.5 %collective-permute-start.11 = (bf16[16,3072]{1,0:T(8,128)(2,1)S(1)}, bf16[16,3072]{1,0:T(8,128)(2,1)S(1)}, u32[]{:S(2)}, u32[]{:S(2)}) collective-permute-start(bf16[16,3072]{1,0:T(8,128)(2,1)S(1)} %get-tuple-element.27), channel_id=1, source_target_pairs={{0,4},{2,6},{4,0},{6,2},{8,12},{10,14},{12,8},{14,10},{1,5},{3,7},... | collective-permute-start | bytes 294920 | tf_op jit(solution)/shard_map/ppermute | solution.py:17
  56.5 8.0 %collective-permute-start.12 = (bf16[16,3072]{1,0:T(8,128)(2,1)S(1)}, bf16[16,3072]{1,0:T(8,128)(2,1)S(1)}, u32[]{:S(2)}, u32[]{:S(2)}) collective-permute-start(bf16[16,3072]{1,0:T(8,128)(2,1)S(1)} %get-tuple-element.28), channel_id=1, source_target_pairs={{0,6},{2,4},{4,2},{6,0},{8,14},{10,12},{12,10},{14,8},{1,7},{3,5},... | collective-permute-start | bytes 294920 | tf_op jit(solution)/shard_map/ppermute | solution.py:17
  60.3 7.4 %collective-permute-start.16 = (bf16[16,3072]{1,0:T(8,128)(2,1)S(1)}, bf16[16,3072]{1,0:T(8,128)(2,1)S(1)}, u32[]{:S(2)}, u32[]{:S(2)}) collective-permute-start(bf16[16,3072]{1,0:T(8,128)(2,1)S(1)} %add_convert_fusion.1), channel_id=1, source_target_pairs={{0,8},{2,10},{4,12},{6,14},{8,0},{10,2},{12,4},{14,6},{1,9},{3,11}... | collective-permute-start | bytes 294920 | tf_op jit(solution)/shard_map/ppermute | solution.py:17

commit v3 on v2

--- a/solution.py
+++ b/solution.py
@@ -34,74 +34,126 @@
     )(*args)
 
 
+def column(row, rows):
+    diagonal = lax.broadcasted_iota(jnp.int32, (rows, rows), 0) == lax.broadcasted_iota(
+        jnp.int32, (rows, rows), 1
+    )
+    return jnp.sum(jnp.where(diagonal, row, 0.0), axis=1, keepdims=True)
+
+
 def pack_kernel(tokens_ref, ids_ref, out_ref):
     rows, width = tokens_ref.shape
     out_ref[:, :width] = tokens_ref[...]
     ids = ids_ref[...].astype(F32)
     lane = lax.broadcasted_iota(jnp.int32, (rows, IDS), 1)
-    out_ref[:, width:] = jnp.where(lane == 0, ids[:, 0:1], ids[:, 1:2]).astype(BF16)
-
-
-def stream(w_ref, held_ref, sems, experts, part_ref, load):
-    hidden, width = w_ref.shape[1:]
+    out_ref[:, width:] = jnp.where(
+        lane == 0, column(ids[0:1], rows), column(ids[1:2], rows)
+    ).astype(BF16)
+
+
+def over_width(a, b):
+    return lax.dot_general(a, b, (((1,), (1,)), ((), ())), preferred_element_type=F32)
+
+
+def fetch_kernel(_, source_ref, out_ref, sems):
+    copies = [
+        pltpu.make_async_copy(source_ref.at[i], out_ref.at[i], sems.at[i])
+        for i in range(out_ref.shape[0])
+    ]
+    for copy in copies:
+        copy.start()
+    for copy in copies:
+        copy.wait()
+
+
+def stream(steps, held_ref, sems, x, first):
     slots, tile = held_ref.shape[:2]
-    steps = [(e, f) for e in experts for f in range(0, hidden, tile)]
 
     def copy(step):
-        e, f = steps[step]
+        w_ref, e, f, _ = steps[step]
         slot = step % slots
         return pltpu.make_async_copy(
             w_ref.at[e, pl.ds(f, tile)], held_ref.at[slot], sems.at[slot]
         )
 
-    for step in range(min(slots, len(steps))):
+    for step in range(slots):
         copy(step).start()
-    x = load()
-    for step in range(len(steps)):
+    first()
+    for step, (*_, store) in enumerate(steps):
         copy(step).wait()
-        part_ref[step * tile : (step + 1) * tile] = jnp.dot(
-            held_ref[step % slots], x, preferred_element_type=F32
-        )
+        store(over_width(held_ref[step % slots], x))
         if step + slots < len(steps):
             copy(step + slots).start()
 
 
+def up_store(part_ref, sent_ref, at):
+    def store(part):
+        own = slice(at, at + part.shape[0])
+        part_ref[own] = part
+        sent_ref[own] = part.astype(BF16)
+
+    return store
+
+
+def gate_store(part_ref, at):
+    def store(part):
+        part_ref[at : at + part.shape[0]] = part
+
+    return store
+
+
 def gate_kernel(*refs):
-    blocks, (router_ref, w_ref, turned_ref, part_ref) = refs[:8], refs[8:12]
-    rows_ref, held_ref, sems = refs[12:]
-    experts, hidden, width = w_ref.shape
-
-    def load():
-        rows = blocks[0].shape[0]
-        for j, block in enumerate(blocks):
-            rows_ref[j * rows : (j + 1) * rows] = block[...].astype(F32)
-        turned_ref[...] = rows_ref[...].T.astype(BF16)
-        x = turned_ref[:width]
-        part_ref[experts * hidden :] = jnp.dot(
-            router_ref[...], x, preferred_element_type=F32
-        )
-        return x
-
-    stream(w_ref, held_ref, sems, range(experts), part_ref, load)
-
-
-def up_kernel(experts, turned_ref, w_ref, _, part_ref, sent_ref, held_ref, sems):
-    width = w_ref.shape[2]
-    stream(w_ref, held_ref, sems, experts, part_ref, lambda: turned_ref[:width])
-    sent_ref[...] = part_ref[...].astype(BF16)
-
-
-def factors(turned_ref, gate_a, gate_b, width, base, experts):
-    ids = turned_ref[width : width + 16].astype(F32)
-    a, b = ids[0:1], ids[1:2]
-    logits = gate_a[base : base + 16] + gate_b[base : base + 16]
-    row = lax.broadcasted_iota(jnp.int32, logits.shape, 0).astype(F32)
-    is_a, is_b = row == a, row == b
-    la = jnp.sum(jnp.where(is_a, logits, 0.0), axis=0, keepdims=True)
-    lb = jnp.sum(jnp.where(is_b, logits, 0.0), axis=0, keepdims=True)
+    blocks, refs = refs[:8], refs[8:]
+    router_ref, early_ref, gate_ref, up_ref, x_ref, part_ref, up_part, up_sent, *scratch = refs
+    held_ref, sems = scratch
+    experts, hidden, width = gate_ref.shape
+    tile = held_ref.shape[1]
+    early, half = early_ref.shape[0], experts // 2
+    rows = blocks[0].shape[0]
+    for j, block in enumerate(blocks):
+        x_ref[j * rows : (j + 1) * rows] = block[...]
+    x = x_ref[:, :width]
+
+    def first():
+        part_ref[experts * hidden :] = over_width(x, router_ref[...])
+        for e in range(early):
+            part_ref[e * hidden : (e + 1) * hidden] = over_width(early_ref[e], x)
+
+    steps = [
+        (gate_ref, e, f, gate_store(part_ref, e * hidden + f))
+        for e in range(early, experts)
+        for f in range(0, hidden, tile)
+    ] + [
+        (up_ref, e, f, up_store(up_part, up_sent, e * hidden + f))
+        for e in range(half)
+        for f in range(0, hidden, tile)
+    ]
+    stream(steps, held_ref, sems, x, first)
+
+
+def up_kernel(x_ref, up_ref, _, part_ref, sent_ref, held_ref, sems):
+    experts, hidden, width = up_ref.shape
+    tile, half = held_ref.shape[1], experts // 2
+    steps = [
+        (up_ref, half + i, f, up_store(part_ref, sent_ref, i * hidden + f))
+        for i in range(half)
+        for f in range(0, hidden, tile)
+    ]
+    stream(steps, held_ref, sems, x_ref[:, :width], lambda: None)
+
+
+def factors(x_ref, gate_a, gate_b, width, base):
+    count = x_ref.shape[0]
+    ids = x_ref[:, width:].astype(F32)
+    a, b = ids[:, 0:1], ids[:, 1:2]
+    logits = gate_a[base : base + count] + gate_b[base : base + count]
+    lane = lax.broadcasted_iota(jnp.int32, logits.shape, 1).astype(F32)
+    is_a, is_b = lane == a, lane == b
+    la = jnp.sum(jnp.where(is_a, logits, 0.0), axis=1, keepdims=True)
+    lb = jnp.sum(jnp.where(is_b, logits, 0.0), axis=1, keepdims=True)
     wa = 1.0 / (1.0 + jnp.exp(lb - la))
     wb = 1.0 / (1.0 + jnp.exp(la - lb))
-    return (jnp.where(is_a, wa, 0.0) + jnp.where(is_b, wb, 0.0)).T
+    return jnp.where(is_a, wa, 0.0) + jnp.where(is_b, wb, 0.0)
 
 
 def hidden_units(e, i, hidden, gate_a, gate_b, up_a, up_b):
@@ -118,15 +170,16 @@
         out_ref[i] = hidden_units(e, i, hidden, gate_a, gate_b, up_a, up_b)
 
 
-def down_kernel(first, turned_ref, gate_a, gate_b, up_a, up_b, h_ref, w_ref, *outs):
+def down_kernel(x_ref, gate_a, gate_b, up_a, up_b, h_ref, w_ref, *outs):
     experts, hidden, width = w_ref.shape
-    factor = factors(turned_ref, gate_a, gate_b, width, experts * hidden, experts)
+    half = h_ref.shape[0]
+    factor = factors(x_ref, gate_a, gate_b, width, experts * hidden)
     total = None
     for e in range(experts):
-        if e < first:
+        if e < half:
             h = h_ref[e]
         else:
-            h = hidden_units(e, e - first, hidden, gate_a, gate_b, up_a, up_b)
+            h = hidden_units(e, e - half, hidden, gate_a, gate_b, up_a, up_b)
         term = factor[:, e : e + 1] * jnp.dot(h, w_ref[e], preferred_element_type=F32)
         total = term if total is None else total + term
     rows = outs[0].shape[0]
@@ -137,69 +190,83 @@
 def fast(tokens, expert_ids, router, w_gate, w_up, w_down):
     rows, width = tokens.shape
     experts, hidden, _ = w_gate.shape
-    count = 8 * rows
+    count, half = 8 * rows, experts // 2
     shape = lambda *s, dtype=F32: jax.ShapeDtypeStruct(s, dtype)
     (own,) = call(
-        pack_kernel, [shape(rows, width + IDS, dtype=BF16)], [tokens, expert_ids], 0, 4 * rows * width, 1
+        pack_kernel,
+        [shape(rows, width + IDS, dtype=BF16)],
+        [tokens, expert_ids.T],
+        0,
+        4 * rows * width,
+        1,
     )
     far = xor_send(own, 4)
     near = [xor_send(own, k) for k in (1, 2, 3)]
     forwarded = [xor_send(far, k) for k in (1, 2, 3)]
     blocks = [own, *near, far, *forwarded]
 
-    w_gate = pltpu.with_memory_space_constraint(w_gate, pltpu.HBM)
-    w_up = pltpu.with_memory_space_constraint(w_up, pltpu.HBM)
-    w_down = in_vmem(w_down)
+    in_hbm = lambda array: pltpu.with_memory_space_constraint(array, pltpu.HBM)
+    w_gate, w_up, w_down = in_hbm(w_gate), in_hbm(w_up), in_vmem(w_down)
     flops = 2 * count * hidden * width
     size = 2 * hidden * width
-    slots, tile = 3, min(hidden, 256)
+    lines = jnp.pad(router.T, ((0, 128 - experts), (0, 0)))
+    slots, tile, early = 4, min(hidden, 256), 2
     held = [pltpu.VMEM((slots, tile, width), BF16), pltpu.SemaphoreType.DMA((slots,))]
-    turned, gate = call(
+    (w_early,) = call(
+        fetch_kernel,
+        [pltpu.VMEM((early, hidden, width), BF16)],
+        [far[:, :128], w_gate],
+        0,
+        0,
+        1,
+        [pltpu.SemaphoreType.DMA((early,))],
+        hbm=(1,),
+    )
+    up_shapes = [shape(half * hidden, count), shape(half * hidden, count, dtype=BF16)]
+    x, gate, up_a, sent_a = call(
         gate_kernel,
-        [shape(width + IDS, count, dtype=BF16), shape(experts * hidden + 16, count)],
-        [*blocks, jnp.pad(router.T, ((0, 16 - experts), (0, 0))), w_gate],
+        [
+            shape(count, width + IDS, dtype=BF16),
+            shape(experts * hidden + count, count),
+            *up_shapes,
+        ],
+        [*blocks, lines, w_early, w_gate, w_up],
         experts * flops,
         experts * size,
         8,
-        [pltpu.VMEM((count, width + IDS), F32), *held],
-        hbm=(9,),
+        held,
+        hbm=(10, 11),
     )
     gate_other = lax.ppermute(gate, "mp", SWAP)
-    half = experts // 2
-    ups = []
-    for first in (0, half):
-        up, sent = call(
-            functools.partial(up_kernel, range(first, first + half)),
-            [shape(half * hidden, count), shape(half * hidden, count, dtype=BF16)],
-            [turned, w_up, w_down],
-            half * flops,
-            half * size,
-            8,
-            held,
-            hbm=(1,),
-        )
-        ups.append((up, lax.ppermute(sent, "mp", SWAP)))
+    up_other_a = lax.ppermute(sent_a, "mp", SWAP)
+    up_b, sent_b = call(
+        up_kernel, up_shapes, [x, w_up, w_down], half * flops, half * size, 7, held, hbm=(1,)
+    )
+    up_other_b = lax.ppermute(sent_b, "mp", SWAP)
     (units,) = call(
         functools.partial(hidden_kernel, range(half)),
         [shape(half, count, hidden, dtype=BF16)],
-        [gate, gate_other, *ups[0], w_down],
+        [gate, gate_other, up_a, up_other_a, w_down],
         0,
         12 * half * hidden * count,
         4,
     )
     parts = call(
-        functools.partial(down_kernel, half),
+        down_kernel,
         [shape(rows, width)] + [shape(rows, width, dtype=BF16)] * 7,
-        [turned, gate, gate_other, *ups[1], units, w_down],
+        [x, gate, gate_other, up_b, up_other_b, units, w_down],
         experts * flops,
         experts * size,
         5,
     )
-    far_sums = [xor_send(parts[4 ^ k], k) for k in (1, 2, 3)]
-    near_sums = [xor_send(parts[k], k) for k in (1, 2, 3)]
     add = lambda arrays: sum(a.astype(F32) for a in arrays)
-    crossing = xor_send(add([parts[4], *far_sums]).astype(BF16), 4)
-    return add([parts[0], *near_sums, crossing]).astype(BF16)
+    far_sums = [xor_send(parts[4 ^ k], k) for k in (3, 2, 1)]
+    leaving, *kept = lax.optimization_barrier(
+        (add([parts[4], *far_sums]).astype(BF16), *parts[1:4])
+    )
+    near_sums = [xor_send(kept[k - 1], k) for k in (3, 2, 1)]
+    crossing = xor_send(leaving, 4)
+    return add([parts[0], crossing, *near_sums]).astype(BF16)
 
 
 def general(tokens, expert_ids, router, w_gate, w_up, w_down):

time: 68.7 us -> 74.2 us (1.080)
  Pallas kernels: 29.4 us -> 37.5 us
  waiting for transfers between devices: 13.9 us -> 12 us
    pallas_call x6, Pallas kernels: 29.4 us -> 37.5 us  [call(): pl.pallas_call(kernel, out_shape=outs, in_specs=specs, out_specs=[VMEM_BL...]
    ppermute x14, waiting for transfers between devices: 12.5 us -> 10.7 us  [xor_send(): return lax.ppermute(block, 'batch', [(i, i ^ mask) for i in range(8)])]
    unnamed x5 -> x16, local copies, waits for them, and re-layouts: 1.65 us -> 1.61 us
  transfers between devices with their start and end apart: 17 -> 17, of which waited for: 9 -> 7; matrix products, arithmetic and copies ran while one was open for 1% -> 1% of each run, Pallas kernels for 20% -> 20%
where the time goes in v3:
time: 74.2 us; the launch traced here: 74 us
  Pallas kernels  37.5 us (51%)
  starting transfers between devices  21.1 us (28%)
  waiting for transfers between devices  12 us (16%)
  local copies, waits for them, and re-layouts  2.41 us (3%)
  other arithmetic  0.76 us (1%)
    pallas_call x6, Pallas kernels, call(): pl.pallas_call(kernel, out_shape=outs, in_specs=specs, out_specs=[VMEM_BL...  37.5 us
    ppermute x14, starting transfers between devices, xor_send(): return lax.ppermute(block, 'batch', [(i, i ^ mask) for i in range(8)])  20.4 us
    ppermute x14, waiting for transfers between devices, xor_send(): return lax.ppermute(block, 'batch', [(i, i ^ mask) for i in range(8)])  10.7 us
    unnamed x16, local copies, waits for them, and re-layouts  1.61 us
  transfers between devices with their start and end apart: 17, of which 7 were waited for; matrix products, arithmetic and copies ran while one was open for 1% of the time, Pallas kernels for 20%

profile of v3, /device:TPU:0, one launch (start us, length us, event | category | flops | bytes accessed | tf_op | source)
XLA Modules:
  0.0 74.0 jit_solution(13294395269216947551)
XLA Ops:
  0.0 0.9 %copy-done = bf16[16,3072]{1,0:T(8,128)(2,1)S(1)} copy-done((bf16[16,3072]{1,0:T(8,128)(2,1)S(1)}, bf16[16,3072]{1,0:T(8,128)(2,1)}, u32[]{:S(2)}) %copy-start) | copy-done | bytes 98328
  0.9 0.7 copy-done.1
  1.6 0.1 shard_map.64.refs_0_
  1.7 4.0 %collective-permute-start.3 = (bf16[16,3200]{1,0:T(8,128)(2,1)S(1)}, bf16[16,3200]{1,0:T(8,128)(2,1)S(1)}, u32[]{:S(2)}, u32[]{:S(2)}) collective-permute-start(bf16[16,3200]{1,0:T(8,128)(2,1)S(1)} %shard_map.64.refs_0_), channel_id=1, source_target_pairs={{0,8},{2,10},{4,12},{6,14},{8,0},{10,2},{12,4},{14,6},{1,9},{3,11}... | collective-permute-start | bytes 307208 | tf_op jit(solution)/shard_map/ppermute | solution.py:17
  5.7 2.5 %collective-permute-start.2 = (bf16[16,3200]{1,0:T(8,128)(2,1)S(1)}, bf16[16,3200]{1,0:T(8,128)(2,1)S(1)}, u32[]{:S(2)}, u32[]{:S(2)}) collective-permute-start(bf16[16,3200]{1,0:T(8,128)(2,1)S(1)} %shard_map.64.refs_0_), channel_id=1, source_target_pairs={{0,6},{2,4},{4,2},{6,0},{8,14},{10,12},{12,10},{14,8},{1,7},{3,5},... | collective-permute-start | bytes 307208 | tf_op jit(solution)/shard_map/ppermute | solution.py:17
  8.2 0.4 collective-permute-start.1
  8.7 0.5 collective-permute-start
  9.2 1.6 %collective-permute-done.3.refs_4_ = bf16[16,3200]{1,0:T(8,128)(2,1)S(1)} collective-permute-done((bf16[16,3200]{1,0:T(8,128)(2,1)S(1)}, bf16[16,3200]{1,0:T(8,128)(2,1)S(1)}, u32[]{:S(2)}, u32[]{:S(2)}) %collective-permute-start.3) | collective-permute-done | bytes 102432 | tf_op jit(solution)/shard_map/ppermute | solution.py:17
  10.8 1.7 %collective-permute-start.6 = (bf16[16,3200]{1,0:T(8,128)(2,1)S(1)}, bf16[16,3200]{1,0:T(8,128)(2,1)S(1)}, u32[]{:S(2)}, u32[]{:S(2)}) collective-permute-start(bf16[16,3200]{1,0:T(8,128)(2,1)S(1)} %collective-permute-done.3.refs_4_), channel_id=1, source_target_pairs={{0,6},{2,4},{4,2},{6,0},{8,14},{10,12},{12,10},{14,8},{1,7},{3,5},... | collective-permute-start | bytes 307208 | tf_op jit(solution)/shard_map/ppermute | solution.py:17
  12.5 1.4 %collective-permute-start.5 = (bf16[16,3200]{1,0:T(8,128)(2,1)S(1)}, bf16[16,3200]{1,0:T(8,128)(2,1)S(1)}, u32[]{:S(2)}, u32[]{:S(2)}) collective-permute-start(bf16[16,3200]{1,0:T(8,128)(2,1)S(1)} %collective-permute-done.3.refs_4_), channel_id=1, source_target_pairs={{0,4},{2,6},{4,0},{6,2},{8,12},{10,14},{12,8},{14,10},{1,5},{3,7},... | collective-permute-start | bytes 307208 | tf_op jit(solution)/shard_map/ppermute | solution.py:17
  13.9 0.0 collective-permute-done.2.refs_3_
  13.9 0.3 collective-permute-start.4
  14.2 0.8 %pad.4.refs_8_ = bf16[128,3072]{1,0:T(8,128)(2,1)S(1)} pad(bf16[4,3072]{1,0:T(4,128)(2,1)} %bitcast.5, bf16[]{:T(256)} %constant.2.clone.1), padding=0_124x0_0 | pad | bytes 811010 | tf_op jit(solution)/shard_map/jit(_pad)/pad | solution.py:212
  15.1 0.0 slice-start
  15.1 0.0 slice-start.1
  15.1 0.0 slice-start.2
  15.1 4.8 %shard_map.65.refs_9_ = bf16[2,1024,3072]{2,1,0:T(8,128)(2,1)S(1)} custom-call(bf16[16,128]{1,0:T(8,128)(2,1)S(1)} %slice.4._, bf16[4,1024,3072]{2,1,0:T(8,128)(2,1)} %refs_10_.1), custom_call_target="tpu_custom_call" | custom-call | tf_op jit(solution)/shard_map/pallas_call | solution.py:26
  19.9 0.0 slice-start.3
  19.9 0.0 slice-start.4
  19.9 0.0 slice-start.5
  19.9 0.0 collective-permute-done.1.refs_2_
  19.9 0.0 collective-permute-done.refs_1_
  19.9 0.0 collective-permute-done.5.refs_6_
  20.0 0.0 collective-permute-done.4.refs_5_
  20.0 19.1 %shard_map.66 = (bf16[128,3200]{1,0:T(8,128)(2,1)S(1)}, f32[4224,128]{1,0:T(8,128)S(1)}, f32[2048,128]{1,0:T(8,128)S(1)}, bf16[2048,128]{1,0:T(8,128)(2,1)S(1)}) custom-call(bf16[16,3200]{1,0:T(8,128)(2,1)S(1)} %shard_map.64.refs_0_, bf16[16,3200]{1,0:T(8,128)(2,1)S(1)} %collective-permute-done.refs_1_, bf16[16,3200]{1,0:T(8,128)(2,1)S(1)} %collective-permute-done.1.refs_2_, ...), custom_call_target="tpu_custom_call" | custom-call | flops 3221225472 | bytes 25165824 | tf_op jit(solution)/shard_map/pallas_call | solution.py:26
  39.1 0.1 collective-permute-start.7
  39.2 0.5 collective-permute-start.9
  39.7 9.3 %shard_map.67 = (f32[2048,128]{1,0:T(8,128)S(1)}, bf16[2048,128]{1,0:T(8,128)(2,1)S(1)}) custom-call(bf16[128,3200]{1,0:T(8,128)(2,1)S(1)} %get-tuple-element.23.x_ref, bf16[4,1024,3072]{2,1,0:T(8,128)(2,1)} %up_ref.1, bf16[4,1024,3072]{2,1,0:T(8,128)(2,1)S(1)} %bitcast.3), custom_call_target="tpu_custom_call" | custom-call | flops 1610612736 | bytes 12582912 | tf_op jit(solution)/shard_map/pallas_call | solution.py:26
  49.0 0.1 collective-permute-start.8
  49.1 0.0 collective-permute-done.7.gate_b
  49.1 0.5 shard_map.68.h_ref
  49.6 1.3 %collective-permute-done.8.up_b = bf16[2048,128]{1,0:T(8,128)(2,1)S(1)} collective-permute-done((bf16[2048,128]{1,0:T(8,128)(2,1)S(1)}, bf16[2048,128]{1,0:T(8,128)(2,1)S(1)}, u32[]{:S(2)}, u32[]{:S(2)}) %collective-permute-start.8) | collective-permute-done | bytes 524320 | tf_op jit(solution)/shard_map/ppermute | solution.py:245
  50.9 3.8 %shard_map.69 = (f32[16,3072]{1,0:T(8,128)S(1)}, bf16[16,3072]{1,0:T(8,128)(2,1)S(1)}, bf16[16,3072]{1,0:T(8,128)(2,1)S(1)}, bf16[16,3072]{1,0:T(8,128)(2,1)S(1)...) custom-call(bf16[128,3200]{1,0:T(8,128)(2,1)S(1)} %get-tuple-element, ...), custom_call_target="tpu_custom_call" | custom-call | flops 3221225472 | bytes 25165824 | tf_op jit(solution)/shard_map/pallas_call | solution.py:26
  54.7 1.8 %collective-permute-start.10 = (bf16[16,3072]{1,0:T(8,128)(2,1)S(1)}, bf16[16,3072]{1,0:T(8,128)(2,1)S(1)}, u32[]{:S(2)}, u32[]{:S(2)}) collective-permute-start(bf16[16,3072]{1,0:T(8,128)(2,1)S(1)} %get-tuple-element.31), channel_id=1, source_target_pairs={{0,6},{2,4},{4,2},{6,0},{8,14},{10,12},{12,10},{14,8},{1,7},{3,5},... | collective-permute-start | bytes 294920 | tf_op jit(solution)/shard_map/ppermute | solution.py:17
  56.6 1.4 %collective-permute-start.11 = (bf16[16,3072]{1,0:T(8,128)(2,1)S(1)}, bf16[16,3072]{1,0:T(8,128)(2,1)S(1)}, u32[]{:S(2)}, u32[]{:S(2)}) collective-permute-start(bf16[16,3072]{1,0:T(8,128)(2,1)S(1)} %get-tuple-element.32), channel_id=1, source_target_pairs={{0,4},{2,6},{4,0},{6,2},{8,12},{10,14},{12,8},{14,10},{1,5},{3,7},... | collective-permute-start | bytes 294920 | tf_op jit(solution)/shard_map/ppermute | solution.py:17
  58.0 0.3 collective-permute-start.12
  58.3 3.1 %collective-permute-done.10 = bf16[16,3072]{1,0:T(8,128)(2,1)S(1)} collective-permute-done((bf16[16,3072]{1,0:T(8,128)(2,1)S(1)}, bf16[16,3072]{1,0:T(8,128)(2,1)S(1)}, u32[]{:S(2)}, u32[]{:S(2)}) %collective-permute-start.10) | collective-permute-done | bytes 98336 | tf_op jit(solution)/shard_map/ppermute | solution.py:17
  61.4 1.5 %collective-permute-done.11 = bf16[16,3072]{1,0:T(8,128)(2,1)S(1)} collective-permute-done((bf16[16,3072]{1,0:T(8,128)(2,1)S(1)}, bf16[16,3072]{1,0:T(8,128)(2,1)S(1)}, u32[]{:S(2)}, u32[]{:S(2)}) %collective-permute-start.11) | collective-permute-done | bytes 98336 | tf_op jit(solution)/shard_map/ppermute | solution.py:17
  62.9 0.1 add_convert_fusion.1
  62.9 2.4 %collective-permute-start.13 = (bf16[16,3072]{1,0:T(8,128)(2,1)S(1)}, bf16[16,3072]{1,0:T(8,128)(2,1)S(1)}, u32[]{:S(2)}, u32[]{:S(2)}) collective-permute-start(bf16[16,3072]{1,0:T(8,128)(2,1)S(1)} %add_convert_fusion.1), channel_id=1, source_target_pairs={{0,8},{2,10},{4,12},{6,14},{8,0},{10,2},{12,4},{14,6},{1,9},{3,11}... | collective-permute-start | bytes 294920 | tf_op jit(solution)/shard_map/ppermute | solution.py:17
  65.3 2.6 %collective-permute-start.14 = (bf16[16,3072]{1,0:T(8,128)(2,1)S(1)}, bf16[16,3072]{1,0:T(8,128)(2,1)S(1)}, u32[]{:S(2)}, u32[]{:S(2)}) collective-permute-start(bf16[16,3072]{1,0:T(8,128)(2,1)S(1)} %get-tuple-element.38), channel_id=1, source_target_pairs={{0,6},{2,4},{4,2},{6,0},{8,14},{10,12},{12,10},{14,8},{1,7},{3,5},... | collective-permute-start | bytes 294920 | tf_op jit(solution)/shard_map/ppermute | solution.py:17
  67.9 0.0 collective-permute-start.15
  68.0 0.8 %collective-permute-start.16 = (bf16[16,3072]{1,0:T(8,128)(2,1)S(1)}, bf16[16,3072]{1,0:T(8,128)(2,1)S(1)}, u32[]{:S(2)}, u32[]{:S(2)}) collective-permute-start(bf16[16,3072]{1,0:T(8,128)(2,1)S(1)} %get-tuple-element.40), channel_id=1, source_target_pairs={{0,2},{2,0},{4,6},{6,4},{8,10},{10,8},{12,14},{14,12},{1,3},{3,1},... | collective-permute-start | bytes 294920 | tf_op jit(solution)/shard_map/ppermute | solution.py:17
  68.8 1.2 %collective-permute-done.13 = bf16[16,3072]{1,0:T(8,128)(2,1)S(1)} collective-permute-done((bf16[16,3072]{1,0:T(8,128)(2,1)S(1)}, bf16[16,3072]{1,0:T(8,128)(2,1)S(1)}, u32[]{:S(2)}, u32[]{:S(2)}) %collective-permute-start.13) | collective-permute-done | bytes 98336 | tf_op jit(solution)/shard_map/ppermute | solution.py:17
  70.0 2.8 %collective-permute-done.14 = bf16[16,3072]{1,0:T(8,128)(2,1)S(1)} collective-permute-done((bf16[16,3072]{1,0:T(8,128)(2,1)S(1)}, bf16[16,3072]{1,0:T(8,128)(2,1)S(1)}, u32[]{:S(2)}, u32[]{:S(2)}) %collective-permute-start.14) | collective-permute-done | bytes 98336 | tf_op jit(solution)/shard_map/ppermute | solution.py:17
  72.9 0.4 collective-permute-done.15
  73.3 0.0 collective-permute-done.16
  73.3 0.7 add_convert_fusion
  (13 shorter events, 0.0 us)
Async XLA Ops:
  0.0 0.9 %copy-start = (bf16[16,3072]{1,0:T(8,128)(2,1)S(1)}, bf16[16,3072]{1,0:T(8,128)(2,1)}, u32[]{:S(2)}) copy-start(bf16[16,3072]{1,0:T(8,128)(2,1)} %tokens_ref.1) | copy-start | bytes 294916
  0.9 0.7 copy-start.1
  1.7 9.1 %collective-permute-start.3 = (bf16[16,3200]{1,0:T(8,128)(2,1)S(1)}, bf16[16,3200]{1,0:T(8,128)(2,1)S(1)}, u32[]{:S(2)}, u32[]{:S(2)}) collective-permute-start(bf16[16,3200]{1,0:T(8,128)(2,1)S(1)} %shard_map.64.refs_0_), channel_id=1, source_target_pairs={{0,8},{2,10},{4,12},{6,14},{8,0},{10,2},{12,4},{14,6},{1,9},{3,11}... | collective-permute-start | bytes 307208 | tf_op jit(solution)/shard_map/ppermute | solution.py:17
  5.7 8.2 %collective-permute-start.2 = (bf16[16,3200]{1,0:T(8,128)(2,1)S(1)}, bf16[16,3200]{1,0:T(8,128)(2,1)S(1)}, u32[]{:S(2)}, u32[]{:S(2)}) collective-permute-start(bf16[16,3200]{1,0:T(8,128)(2,1)S(1)} %shard_map.64.refs_0_), channel_id=1, source_target_pairs={{0,6},{2,4},{4,2},{6,0},{8,14},{10,12},{12,10},{14,8},{1,7},{3,5},... | collective-permute-start | bytes 307208 | tf_op jit(solution)/shard_map/ppermute | solution.py:17
  8.2 11.7 %collective-permute-start.1 = (bf16[16,3200]{1,0:T(8,128)(2,1)S(1)}, bf16[16,3200]{1,0:T(8,128)(2,1)S(1)}, u32[]{:S(2)}, u32[]{:S(2)}) collective-permute-start(bf16[16,3200]{1,0:T(8,128)(2,1)S(1)} %shard_map.64.refs_0_), channel_id=1, source_target_pairs={{0,4},{2,6},{4,0},{6,2},{8,12},{10,14},{12,8},{14,10},{1,5},{3,7},... | collective-permute-start | bytes 307208 | tf_op jit(solution)/shard_map/ppermute | solution.py:17
  8.7 11.3 %collective-permute-start = (bf16[16,3200]{1,0:T(8,128)(2,1)S(1)}, bf16[16,3200]{1,0:T(8,128)(2,1)S(1)}, u32[]{:S(2)}, u32[]{:S(2)}) collective-permute-start(bf16[16,3200]{1,0:T(8,128)(2,1)S(1)} %shard_map.64.refs_0_), channel_id=1, source_target_pairs={{0,2},{2,0},{4,6},{6,4},{8,10},{10,8},{12,14},{14,12},{1,3},{3,1},... | collective-permute-start | bytes 307208 | tf_op jit(solution)/shard_map/ppermute | solution.py:17
  10.8 9.2 %collective-permute-start.6 = (bf16[16,3200]{1,0:T(8,128)(2,1)S(1)}, bf16[16,3200]{1,0:T(8,128)(2,1)S(1)}, u32[]{:S(2)}, u32[]{:S(2)}) collective-permute-start(bf16[16,3200]{1,0:T(8,128)(2,1)S(1)} %collective-permute-done.3.refs_4_), channel_id=1, source_target_pairs={{0,6},{2,4},{4,2},{6,0},{8,14},{10,12},{12,10},{14,8},{1,7},{3,5},... | collective-permute-start | bytes 307208 | tf_op jit(solution)/shard_map/ppermute | solution.py:17
  12.5 7.5 %collective-permute-start.5 = (bf16[16,3200]{1,0:T(8,128)(2,1)S(1)}, bf16[16,3200]{1,0:T(8,128)(2,1)S(1)}, u32[]{:S(2)}, u32[]{:S(2)}) collective-permute-start(bf16[16,3200]{1,0:T(8,128)(2,1)S(1)} %collective-permute-done.3.refs_4_), channel_id=1, source_target_pairs={{0,4},{2,6},{4,0},{6,2},{8,12},{10,14},{12,8},{14,10},{1,5},{3,7},... | collective-permute-start | bytes 307208 | tf_op jit(solution)/shard_map/ppermute | solution.py:17
  13.9 6.1 %collective-permute-start.4 = (bf16[16,3200]{1,0:T(8,128)(2,1)S(1)}, bf16[16,3200]{1,0:T(8,128)(2,1)S(1)}, u32[]{:S(2)}, u32[]{:S(2)}) collective-permute-start(bf16[16,3200]{1,0:T(8,128)(2,1)S(1)} %collective-permute-done.3.refs_4_), channel_id=1, source_target_pairs={{0,2},{2,0},{4,6},{6,4},{8,10},{10,8},{12,14},{14,12},{1,3},{3,1},... | collective-permute-start | bytes 307208 | tf_op jit(solution)/shard_map/ppermute | solution.py:17
  15.1 24.6 %slice-start = ((s8[25165824]{0:T(1024)(128)(4,1)}), s8[4194304]{0:T(1024)(128)(4,1)S(1)}, s32[]{:S(2)}) async-start(s8[25165824]{0:T(1024)(128)(4,1)} %bitcast.2), calls=%async_computation | async-start | bytes 8388608
  15.1 24.6 %slice-start.1 = ((s8[25165824]{0:T(1024)(128)(4,1)}), s8[4194304]{0:T(1024)(128)(4,1)S(1)}, s32[]{:S(2)}) async-start(s8[25165824]{0:T(1024)(128)(4,1)} %bitcast.2), calls=%async_computation.1 | async-start | bytes 8388608
  15.1 24.6 %slice-start.2 = ((s8[25165824]{0:T(1024)(128)(4,1)}), s8[4194304]{0:T(1024)(128)(4,1)S(1)}, s32[]{:S(2)}) async-start(s8[25165824]{0:T(1024)(128)(4,1)} %bitcast.2), calls=%async_computation.2 | async-start | bytes 8388608
  19.9 19.8 %slice-start.3 = ((s8[25165824]{0:T(1024)(128)(4,1)}), s8[4194304]{0:T(1024)(128)(4,1)S(1)}, s32[]{:S(2)}) async-start(s8[25165824]{0:T(1024)(128)(4,1)} %bitcast.2), calls=%async_computation.3 | async-start | bytes 8388608
  19.9 19.8 %slice-start.4 = ((s8[25165824]{0:T(1024)(128)(4,1)}), s8[4194304]{0:T(1024)(128)(4,1)S(1)}, s32[]{:S(2)}) async-start(s8[25165824]{0:T(1024)(128)(4,1)} %bitcast.2), calls=%async_computation.4 | async-start | bytes 8388608
  19.9 19.8 %slice-start.5 = ((s8[25165824]{0:T(1024)(128)(4,1)}), s8[4194304]{0:T(1024)(128)(4,1)S(1)}, s32[]{:S(2)}) async-start(s8[25165824]{0:T(1024)(128)(4,1)} %bitcast.2), calls=%async_computation.5 | async-start | bytes 8388608
  39.1 10.0 %collective-permute-start.7 = (f32[4224,128]{1,0:T(8,128)S(1)}, f32[4224,128]{1,0:T(8,128)S(1)}, u32[]{:S(2)}, u32[]{:S(2)}) collective-permute-start(f32[4224,128]{1,0:T(8,128)S(1)} %get-tuple-element.24.gate_a), channel_id=1, source_target_pairs={{0,1},{1,0},{2,3},{3,2},{4,5},{5,4},{6,7},{7,6},{8,9},{9,8},{10,11... | collective-permute-start | bytes 6488072 | tf_op jit(solution)/shard_map/ppermute | solution.py:240
  39.2 9.9 %collective-permute-start.9 = (bf16[2048,128]{1,0:T(8,128)(2,1)S(1)}, bf16[2048,128]{1,0:T(8,128)(2,1)S(1)}, u32[]{:S(2)}, u32[]{:S(2)}) collective-permute-start(bf16[2048,128]{1,0:T(8,128)(2,1)S(1)} %get-tuple-element.28), channel_id=1, source_target_pairs={{0,1},{1,0},{2,3},{3,2},{4,5},{5,4},{6,7},{7,6},{8,9},{9,8},{10,11... | collective-permute-start | bytes 1572872 | tf_op jit(solution)/shard_map/ppermute | solution.py:241
  49.0 2.0 %collective-permute-start.8 = (bf16[2048,128]{1,0:T(8,128)(2,1)S(1)}, bf16[2048,128]{1,0:T(8,128)(2,1)S(1)}, u32[]{:S(2)}, u32[]{:S(2)}) collective-permute-start(bf16[2048,128]{1,0:T(8,128)(2,1)S(1)} %get-tuple-element.26), channel_id=1, source_target_pairs={{0,1},{1,0},{2,3},{3,2},{4,5},{5,4},{6,7},{7,6},{8,9},{9,8},{10,11... | collective-permute-start | bytes 1572872 | tf_op jit(solution)/shard_map/ppermute | solution.py:245
  54.7 6.6 %collective-permute-start.10 = (bf16[16,3072]{1,0:T(8,128)(2,1)S(1)}, bf16[16,3072]{1,0:T(8,128)(2,1)S(1)}, u32[]{:S(2)}, u32[]{:S(2)}) collective-permute-start(bf16[16,3072]{1,0:T(8,128)(2,1)S(1)} %get-tuple-element.31), channel_id=1, source_target_pairs={{0,6},{2,4},{4,2},{6,0},{8,14},{10,12},{12,10},{14,8},{1,7},{3,5},... | collective-permute-start | bytes 294920 | tf_op jit(solution)/shard_map/ppermute | solution.py:17
  56.6 6.3 %collective-permute-start.11 = (bf16[16,3072]{1,0:T(8,128)(2,1)S(1)}, bf16[16,3072]{1,0:T(8,128)(2,1)S(1)}, u32[]{:S(2)}, u32[]{:S(2)}) collective-permute-start(bf16[16,3072]{1,0:T(8,128)(2,1)S(1)} %get-tuple-element.32), channel_id=1, source_target_pairs={{0,4},{2,6},{4,0},{6,2},{8,12},{10,14},{12,8},{14,10},{1,5},{3,7},... | collective-permute-start | bytes 294920 | tf_op jit(solution)/shard_map/ppermute | solution.py:17
  58.0 4.9 %collective-permute-start.12 = (bf16[16,3072]{1,0:T(8,128)(2,1)S(1)}, bf16[16,3072]{1,0:T(8,128)(2,1)S(1)}, u32[]{:S(2)}, u32[]{:S(2)}) collective-permute-start(bf16[16,3072]{1,0:T(8,128)(2,1)S(1)} %get-tuple-element.33), channel_id=1, source_target_pairs={{0,2},{2,0},{4,6},{6,4},{8,10},{10,8},{12,14},{14,12},{1,3},{3,1},... | collective-permute-start | bytes 294920 | tf_op jit(solution)/shard_map/ppermute | solution.py:17
  62.9 7.1 %collective-permute-start.13 = (bf16[16,3072]{1,0:T(8,128)(2,1)S(1)}, bf16[16,3072]{1,0:T(8,128)(2,1)S(1)}, u32[]{:S(2)}, u32[]{:S(2)}) collective-permute-start(bf16[16,3072]{1,0:T(8,128)(2,1)S(1)} %add_convert_fusion.1), channel_id=1, source_target_pairs={{0,8},{2,10},{4,12},{6,14},{8,0},{10,2},{12,4},{14,6},{1,9},{3,11}... | collective-permute-start | bytes 294920 | tf_op jit(solution)/shard_map/ppermute | solution.py:17
  65.3 7.6 %collective-permute-start.14 = (bf16[16,3072]{1,0:T(8,128)(2,1)S(1)}, bf16[16,3072]{1,0:T(8,128)(2,1)S(1)}, u32[]{:S(2)}, u32[]{:S(2)}) collective-permute-start(bf16[16,3072]{1,0:T(8,128)(2,1)S(1)} %get-tuple-element.38), channel_id=1, source_target_pairs={{0,6},{2,4},{4,2},{6,0},{8,14},{10,12},{12,10},{14,8},{1,7},{3,5},... | collective-permute-start | bytes 294920 | tf_op jit(solution)/shard_map/ppermute | solution.py:17
  67.9 5.4 %collective-permute-start.15 = (bf16[16,3072]{1,0:T(8,128)(2,1)S(1)}, bf16[16,3072]{1,0:T(8,128)(2,1)S(1)}, u32[]{:S(2)}, u32[]{:S(2)}) collective-permute-start(bf16[16,3072]{1,0:T(8,128)(2,1)S(1)} %get-tuple-element.39), channel_id=1, source_target_pairs={{0,4},{2,6},{4,0},{6,2},{8,12},{10,14},{12,8},{14,10},{1,5},{3,7},... | collective-permute-start | bytes 294920 | tf_op jit(solution)/shard_map/ppermute | solution.py:17
  68.0 5.3 %collective-permute-start.16 = (bf16[16,3072]{1,0:T(8,128)(2,1)S(1)}, bf16[16,3072]{1,0:T(8,128)(2,1)S(1)}, u32[]{:S(2)}, u32[]{:S(2)}) collective-permute-start(bf16[16,3072]{1,0:T(8,128)(2,1)S(1)} %get-tuple-element.40), channel_id=1, source_target_pairs={{0,2},{2,0},{4,6},{6,4},{8,10},{10,8},{12,14},{14,12},{1,3},{3,1},... | collective-permute-start | bytes 294920 | tf_op jit(solution)/shard_map/ppermute | solution.py:17

commit v4 on v3

--- a/solution.py
+++ b/solution.py
@@ -55,91 +55,56 @@
     return lax.dot_general(a, b, (((1,), (1,)), ((), ())), preferred_element_type=F32)
 
 
-def fetch_kernel(_, source_ref, out_ref, sems):
-    copies = [
-        pltpu.make_async_copy(source_ref.at[i], out_ref.at[i], sems.at[i])
-        for i in range(out_ref.shape[0])
+def fetches(source_ref, experts, targets, sems, at=0):
+    return [
+        pltpu.make_async_copy(source_ref.at[e], target, sems.at[at + i])
+        for i, (e, target) in enumerate(zip(experts, targets))
     ]
+
+
+def fetch_kernel(fetched, _, source_ref, *refs):
+    *held, sems = refs
+    copies = fetches(source_ref, fetched, held, sems)
     for copy in copies:
         copy.start()
     for copy in copies:
         copy.wait()
 
 
-def stream(steps, held_ref, sems, x, first):
-    slots, tile = held_ref.shape[:2]
-
-    def copy(step):
-        w_ref, e, f, _ = steps[step]
-        slot = step % slots
-        return pltpu.make_async_copy(
-            w_ref.at[e, pl.ds(f, tile)], held_ref.at[slot], sems.at[slot]
-        )
-
-    for step in range(slots):
-        copy(step).start()
-    first()
-    for step, (*_, store) in enumerate(steps):
-        copy(step).wait()
-        store(over_width(held_ref[step % slots], x))
-        if step + slots < len(steps):
-            copy(step + slots).start()
-
-
-def up_store(part_ref, sent_ref, at):
-    def store(part):
-        own = slice(at, at + part.shape[0])
-        part_ref[own] = part
-        sent_ref[own] = part.astype(BF16)
-
-    return store
-
-
-def gate_store(part_ref, at):
-    def store(part):
-        part_ref[at : at + part.shape[0]] = part
-
-    return store
-
-
-def gate_kernel(*refs):
-    blocks, refs = refs[:8], refs[8:]
-    router_ref, early_ref, gate_ref, up_ref, x_ref, part_ref, up_part, up_sent, *scratch = refs
-    held_ref, sems = scratch
-    experts, hidden, width = gate_ref.shape
-    tile = held_ref.shape[1]
-    early, half = early_ref.shape[0], experts // 2
+def gate_kernel(fetched, *refs):
+    blocks, (router_ref, w_ref, up_ref, _, x_ref, part_ref, *held, sems) = refs[:8], refs[8:]
+    experts, hidden, width = w_ref.shape
+    copies = fetches(up_ref, fetched, held, sems)
+    for copy in copies:
+        copy.start()
     rows = blocks[0].shape[0]
     for j, block in enumerate(blocks):
         x_ref[j * rows : (j + 1) * rows] = block[...]
     x = x_ref[:, :width]
-
-    def first():
-        part_ref[experts * hidden :] = over_width(x, router_ref[...])
-        for e in range(early):
-            part_ref[e * hidden : (e + 1) * hidden] = over_width(early_ref[e], x)
-
-    steps = [
-        (gate_ref, e, f, gate_store(part_ref, e * hidden + f))
-        for e in range(early, experts)
-        for f in range(0, hidden, tile)
-    ] + [
-        (up_ref, e, f, up_store(up_part, up_sent, e * hidden + f))
-        for e in range(half)
-        for f in range(0, hidden, tile)
-    ]
-    stream(steps, held_ref, sems, x, first)
-
-
-def up_kernel(x_ref, up_ref, _, part_ref, sent_ref, held_ref, sems):
-    experts, hidden, width = up_ref.shape
-    tile, half = held_ref.shape[1], experts // 2
-    steps = [
-        (up_ref, half + i, f, up_store(part_ref, sent_ref, i * hidden + f))
-        for i in range(half)
-        for f in range(0, hidden, tile)
-    ]
-    stream(steps, held_ref, sems, x_ref[:, :width], lambda: None)
+    part_ref[experts * hidden :] = over_width(x, router_ref[...])
+    for e in range(experts):
+        part_ref[e * hidden : (e + 1) * hidden] = over_width(w_ref[e], x)
+    for copy in copies:
+        copy.wait()
+
+
+def up_kernel(up_fetched, down_fetched, x_ref, up_ref, down_ref, *refs):
+    weights, (part_ref, sent_ref, *held, sems) = refs[:2], refs[2:]
+    hidden, width = weights[0].shape
+    n = len(up_fetched)
+    copies = fetches(up_ref, up_fetched, held[:n], sems) + fetches(
+        down_ref, down_fetched, held[n:], sems, n
+    )
+    for copy in copies:
+        copy.start()
+    x = x_ref[:, :width]
+    for i, w_ref in enumerate(weights):
+        own = slice(i * hidden, (i + 1) * hidden)
+        part = over_width(w_ref[...], x)
+        part_ref[own] = part
+        sent_ref[own] = part.astype(BF16)
+    for copy in copies:
+        copy.wait()
 
 
 def factors(x_ref, gate_a, gate_b, width, base):
@@ -164,14 +129,25 @@
     return (gate / (1.0 + jnp.exp(-gate)) * up).T.astype(BF16)
 
 
-def hidden_kernel(experts, gate_a, gate_b, up_a, up_b, _, out_ref):
+def hidden_kernel(experts, fetched, gate_a, gate_b, up_a, up_b, down_ref, out_ref, *refs):
+    *held, sems = refs
+    copies = fetches(down_ref, fetched, held, sems)
+    for copy in copies:
+        copy.start()
     hidden = out_ref.shape[2]
     for i, e in enumerate(experts):
         out_ref[i] = hidden_units(e, i, hidden, gate_a, gate_b, up_a, up_b)
-
-
-def down_kernel(x_ref, gate_a, gate_b, up_a, up_b, h_ref, w_ref, *outs):
-    experts, hidden, width = w_ref.shape
+    for copy in copies:
+        copy.wait()
+
+
+def down_kernel(ready, x_ref, gate_a, gate_b, up_a, up_b, h_ref, down_ref, *refs):
+    weights, outs, (held_ref, sems) = refs[:ready], refs[ready : ready + 8], refs[ready + 8 :]
+    experts, hidden, width = down_ref.shape
+    late = [held_ref.at[i] for i in range(experts - ready)]
+    copies = fetches(down_ref, range(ready, experts), late, sems)
+    for copy in copies:
+        copy.start()
     half = h_ref.shape[0]
     factor = factors(x_ref, gate_a, gate_b, width, experts * hidden)
     total = None
@@ -180,7 +156,12 @@
             h = h_ref[e]
         else:
             h = hidden_units(e, e - half, hidden, gate_a, gate_b, up_a, up_b)
-        term = factor[:, e : e + 1] * jnp.dot(h, w_ref[e], preferred_element_type=F32)
+        if e < ready:
+            w = weights[e][...]
+        else:
+            copies[e - ready].wait()
+            w = late[e - ready][...]
+        term = factor[:, e : e + 1] * jnp.dot(h, w, preferred_element_type=F32)
         total = term if total is None else total + term
     rows = outs[0].shape[0]
     for j, out in enumerate(outs):
@@ -196,7 +177,7 @@
         pack_kernel,
         [shape(rows, width + IDS, dtype=BF16)],
         [tokens, expert_ids.T],
-        0,
+        30_000_000_000,
         4 * rows * width,
         1,
     )
@@ -206,67 +187,83 @@
     blocks = [own, *near, far, *forwarded]
 
     in_hbm = lambda array: pltpu.with_memory_space_constraint(array, pltpu.HBM)
-    w_gate, w_up, w_down = in_hbm(w_gate), in_hbm(w_up), in_vmem(w_down)
+    w_gate, w_up, w_down = in_vmem(w_gate), in_hbm(w_up), in_hbm(w_down)
     flops = 2 * count * hidden * width
     size = 2 * hidden * width
     lines = jnp.pad(router.T, ((0, 128 - experts), (0, 0)))
-    slots, tile, early = 4, min(hidden, 256), 2
-    held = [pltpu.VMEM((slots, tile, width), BF16), pltpu.SemaphoreType.DMA((slots,))]
-    (w_early,) = call(
-        fetch_kernel,
-        [pltpu.VMEM((early, hidden, width), BF16)],
-        [far[:, :128], w_gate],
-        0,
+    one = pltpu.VMEM((hidden, width), BF16)
+    sems = lambda n: [pltpu.SemaphoreType.DMA((n,))]
+    (up0,) = call(
+        functools.partial(fetch_kernel, (0,)),
+        [one],
+        [far[:, :128], w_up],
+        14_000_000_000,
         0,
         1,
-        [pltpu.SemaphoreType.DMA((early,))],
+        sems(1),
         hbm=(1,),
     )
-    up_shapes = [shape(half * hidden, count), shape(half * hidden, count, dtype=BF16)]
-    x, gate, up_a, sent_a = call(
-        gate_kernel,
+    x, gate, up1, up2 = call(
+        functools.partial(gate_kernel, (1, 2)),
         [
             shape(count, width + IDS, dtype=BF16),
             shape(experts * hidden + count, count),
-            *up_shapes,
+            *[one] * 2,
         ],
-        [*blocks, lines, w_early, w_gate, w_up],
+        [*blocks, lines, w_gate, w_up, up0],
         experts * flops,
         experts * size,
-        8,
-        held,
-        hbm=(10, 11),
+        3,
+        sems(2),
+        hbm=(10,),
     )
     gate_other = lax.ppermute(gate, "mp", SWAP)
-    up_other_a = lax.ppermute(sent_a, "mp", SWAP)
-    up_b, sent_b = call(
-        up_kernel, up_shapes, [x, w_up, w_down], half * flops, half * size, 7, held, hbm=(1,)
-    )
-    up_other_b = lax.ppermute(sent_b, "mp", SWAP)
-    (units,) = call(
-        functools.partial(hidden_kernel, range(half)),
-        [shape(half, count, hidden, dtype=BF16)],
-        [gate, gate_other, up_a, up_other_a, w_down],
+
+    def up_call(up_fetched, down_fetched, weights):
+        n = len(up_fetched) + len(down_fetched)
+        part, sent, *held = call(
+            functools.partial(up_kernel, up_fetched, down_fetched),
+            [
+                shape(half * hidden, count),
+                shape(half * hidden, count, dtype=BF16),
+                *[one] * n,
+            ],
+            [x, w_up, w_down, *weights],
+            half * flops,
+            half * size,
+            3,
+            sems(n),
+            hbm=(1, 2),
+        )
+        return (part, lax.ppermute(sent, "mp", SWAP)), held
+
+    first, (up3,) = up_call((3,), (), (up0, up1))
+    second, (down0, down1) = up_call((), (0, 1), (up2, up3))
+    units, down2 = call(
+        functools.partial(hidden_kernel, range(half), (2,)),
+        [shape(half, count, hidden, dtype=BF16), one],
+        [gate, gate_other, *first, w_down],
         0,
         12 * half * hidden * count,
         4,
+        sems(1),
+        hbm=(4,),
     )
     parts = call(
-        down_kernel,
+        functools.partial(down_kernel, 3),
         [shape(rows, width)] + [shape(rows, width, dtype=BF16)] * 7,
-        [x, gate, gate_other, up_b, up_other_b, units, w_down],
+        [x, gate, gate_other, *second, units, w_down, down0, down1, down2],
         experts * flops,
         experts * size,
-        5,
-    )
+        10,
+        [pltpu.VMEM((1, hidden, width), BF16), *sems(1)],
+        hbm=(6,),
+    )
+    far_sums = [xor_send(parts[4 ^ k], k) for k in (1, 2, 3)]
+    near_sums = [xor_send(parts[k], k) for k in (1, 2, 3)]
     add = lambda arrays: sum(a.astype(F32) for a in arrays)
-    far_sums = [xor_send(parts[4 ^ k], k) for k in (3, 2, 1)]
-    leaving, *kept = lax.optimization_barrier(
-        (add([parts[4], *far_sums]).astype(BF16), *parts[1:4])
-    )
-    near_sums = [xor_send(kept[k - 1], k) for k in (3, 2, 1)]
-    crossing = xor_send(leaving, 4)
-    return add([parts[0], crossing, *near_sums]).astype(BF16)
+    crossing = xor_send(add([parts[4], *far_sums]).astype(BF16), 4)
+    return add([parts[0], *near_sums, crossing]).astype(BF16)
 
 
 def general(tokens, expert_ids, router, w_gate, w_up, w_down):

time: 74.2 us -> 59.4 us (0.80)
  Pallas kernels: 37.5 us -> 24.7 us
  waiting for transfers between devices: 12 us -> 9.85 us
  starting transfers between devices: 21.1 us -> 22 us
    pallas_call x6 -> x7, Pallas kernels: 37.5 us -> 24.7 us  [call(): pl.pallas_call(kernel, out_shape=outs, in_specs=specs, out_specs=[VMEM_BL...]
    ppermute x2, waiting for transfers between devices: 1.35 us -> 0.01 us  [up_call(): return ((part, lax.ppermute(sent, 'mp', SWAP)), held)]
    ppermute x14, starting transfers between devices: 20.4 us -> 21.3 us  [xor_send(): return lax.ppermute(block, 'batch', [(i, i ^ mask) for i in range(8)])]
    ppermute x14, waiting for transfers between devices: 10.7 us -> 9.84 us  [xor_send(): return lax.ppermute(block, 'batch', [(i, i ^ mask) for i in range(8)])]
    unnamed x16 -> x18, local copies, waits for them, and re-layouts: 1.61 us -> 1.6 us
  transfers between devices with their start and end apart: 17 -> 17, of which waited for: 7 -> 6; matrix products, arithmetic and copies ran while one was open for 1% -> 0% of each run, Pallas kernels for 20% -> 23%
where the time goes in v4:
time: 59.4 us; the launch traced here: 59.2 us
  Pallas kernels  24.7 us (42%)
  starting transfers between devices  22 us (37%)
  waiting for transfers between devices  9.85 us (17%)
  local copies, waits for them, and re-layouts  1.67 us (3%)
  other arithmetic  0.76 us (1%)
    pallas_call x7, Pallas kernels, call(): pl.pallas_call(kernel, out_shape=outs, in_specs=specs, out_specs=[VMEM_BL...  24.7 us
    ppermute x14, starting transfers between devices, xor_send(): return lax.ppermute(block, 'batch', [(i, i ^ mask) for i in range(8)])  21.3 us
    ppermute x14, waiting for transfers between devices, xor_send(): return lax.ppermute(block, 'batch', [(i, i ^ mask) for i in range(8)])  9.84 us
    unnamed x18, local copies, waits for them, and re-layouts  1.6 us
  transfers between devices with their start and end apart: 17, of which 6 were waited for; matrix products, arithmetic and copies ran while one was open for 0% of the time, Pallas kernels for 23%

profile of v4, /device:TPU:0, one launch (start us, length us, event | category | flops | bytes accessed | tf_op | source)
XLA Modules:
  0.0 59.2 jit_solution(16637126142592484263)
XLA Ops:
  0.0 0.9 %copy-done = bf16[16,3072]{1,0:T(8,128)(2,1)S(1)} copy-done((bf16[16,3072]{1,0:T(8,128)(2,1)S(1)}, bf16[16,3072]{1,0:T(8,128)(2,1)}, u32[]{:S(2)}) %copy-start) | copy-done | bytes 98328
  0.9 0.7 %copy-done.1 = s32[16,2]{0,1:T(2,128)S(1)} copy-done((s32[16,2]{0,1:T(2,128)S(1)}, s32[16,2]{0,1:T(2,128)}, u32[]{:S(2)}) %copy-start.1) | copy-done | bytes 152
  1.6 0.0 slice-start.3
  1.6 0.0 slice-start.4
  1.6 0.1 shard_map.64.refs_0_
  1.7 4.0 %collective-permute-start.3 = (bf16[16,3200]{1,0:T(8,128)(2,1)S(1)}, bf16[16,3200]{1,0:T(8,128)(2,1)S(1)}, u32[]{:S(2)}, u32[]{:S(2)}) collective-permute-start(bf16[16,3200]{1,0:T(8,128)(2,1)S(1)} %shard_map.64.refs_0_), channel_id=1, source_target_pairs={{0,8},{2,10},{4,12},{6,14},{8,0},{10,2},{12,4},{14,6},{1,9},{3,11}... | collective-permute-start | bytes 307208 | tf_op jit(solution)/shard_map/ppermute | solution.py:17
  5.7 2.5 %collective-permute-start.2 = (bf16[16,3200]{1,0:T(8,128)(2,1)S(1)}, bf16[16,3200]{1,0:T(8,128)(2,1)S(1)}, u32[]{:S(2)}, u32[]{:S(2)}) collective-permute-start(bf16[16,3200]{1,0:T(8,128)(2,1)S(1)} %shard_map.64.refs_0_), channel_id=1, source_target_pairs={{0,6},{2,4},{4,2},{6,0},{8,14},{10,12},{12,10},{14,8},{1,7},{3,5},... | collective-permute-start | bytes 307208 | tf_op jit(solution)/shard_map/ppermute | solution.py:17
  8.3 0.4 collective-permute-start.1
  8.7 0.5 collective-permute-start
  9.2 0.1 pad.4.refs_8_
  9.3 1.5 %collective-permute-done.3.refs_4_ = bf16[16,3200]{1,0:T(8,128)(2,1)S(1)} collective-permute-done((bf16[16,3200]{1,0:T(8,128)(2,1)S(1)}, bf16[16,3200]{1,0:T(8,128)(2,1)S(1)}, u32[]{:S(2)}, u32[]{:S(2)}) %collective-permute-start.3) | collective-permute-done | bytes 102432 | tf_op jit(solution)/shard_map/ppermute | solution.py:17
  10.8 1.7 %collective-permute-start.6 = (bf16[16,3200]{1,0:T(8,128)(2,1)S(1)}, bf16[16,3200]{1,0:T(8,128)(2,1)S(1)}, u32[]{:S(2)}, u32[]{:S(2)}) collective-permute-start(bf16[16,3200]{1,0:T(8,128)(2,1)S(1)} %collective-permute-done.3.refs_4_), channel_id=1, source_target_pairs={{0,6},{2,4},{4,2},{6,0},{8,14},{10,12},{12,10},{14,8},{1,7},{3,5},... | collective-permute-start | bytes 307208 | tf_op jit(solution)/shard_map/ppermute | solution.py:17
  12.5 1.4 %collective-permute-start.5 = (bf16[16,3200]{1,0:T(8,128)(2,1)S(1)}, bf16[16,3200]{1,0:T(8,128)(2,1)S(1)}, u32[]{:S(2)}, u32[]{:S(2)}) collective-permute-start(bf16[16,3200]{1,0:T(8,128)(2,1)S(1)} %collective-permute-done.3.refs_4_), channel_id=1, source_target_pairs={{0,4},{2,6},{4,0},{6,2},{8,12},{10,14},{12,8},{14,10},{1,5},{3,7},... | collective-permute-start | bytes 307208 | tf_op jit(solution)/shard_map/ppermute | solution.py:17
  13.9 0.0 collective-permute-done.2.refs_3_
  13.9 0.4 collective-permute-start.4
  14.3 2.8 %shard_map.65.refs_11_.refs_0_ = bf16[1024,3072]{1,0:T(8,128)(2,1)S(1)} custom-call(bf16[16,128]{1,0:T(8,128)(2,1)S(1)} %slice.4._, bf16[4,1024,3072]{2,1,0:T(8,128)(2,1)} %up_ref.3), custom_call_target="tpu_custom_call" | custom-call | flops 14000000000 | tf_op jit(solution)/shard_map/pallas_call | solution.py:26
  17.1 0.0 collective-permute-done.1.refs_2_
  17.1 0.0 collective-permute-done.refs_1_
  17.1 0.4 collective-permute-done.6.refs_7_
  17.5 1.1 %collective-permute-done.5.refs_6_ = bf16[16,3200]{1,0:T(8,128)(2,1)S(1)} collective-permute-done((bf16[16,3200]{1,0:T(8,128)(2,1)S(1)}, bf16[16,3200]{1,0:T(8,128)(2,1)S(1)}, u32[]{:S(2)}, u32[]{:S(2)}) %collective-permute-start.5) | collective-permute-done | bytes 102432 | tf_op jit(solution)/shard_map/ppermute | solution.py:17
  18.6 0.0 collective-permute-done.4.refs_5_
  18.7 6.9 %shard_map.66 = (bf16[128,3200]{1,0:T(8,128)(2,1)S(1)}, f32[4224,128]{1,0:T(8,128)S(1)}, bf16[1024,3072]{1,0:T(8,128)(2,1)S(1)}, bf16[1024,3072]{1,0:T(8,128)(2,1)S(1)}) custom-call(bf16[16,3200]{1,0:T(8,128)(2,1)S(1)} %shard_map.64.refs_0_, bf16[16,3200]{1,0:T(8,128)(2,1)S(1)} %collective-permute-done.refs_1_, ...), custom_call_target="tpu_custom_call" | custom-call | flops 3221225472 | bytes 25165824 | tf_op jit(solution)/shard_map/pallas_call | solution.py:26
  25.6 0.1 collective-permute-start.7
  25.6 3.4 %shard_map.67 = (f32[2048,128]{1,0:T(8,128)S(1)}, bf16[2048,128]{1,0:T(8,128)(2,1)S(1)}, bf16[1024,3072]{1,0:T(8,128)(2,1)S(1)}) custom-call(bf16[128,3200]{1,0:T(8,128)(2,1)S(1)} %get-tuple-element.26.x_ref, bf16[4,1024,3072]{2,1,0:T(8,128)(2,1)} %up_ref.3, bf16[4,1024,3072]{2,1,0:T(8,128)(2,1)} %down_ref.7, ...), custom_call_target="tpu_custom_call" | custom-call | flops 1610612736 | bytes 12582912 | tf_op jit(solution)/shard_map/pallas_call | solution.py:26
  29.1 0.5 collective-permute-start.9
  29.6 4.6 %shard_map.68 = (f32[2048,128]{1,0:T(8,128)S(1)}, bf16[2048,128]{1,0:T(8,128)(2,1)S(1)}, bf16[1024,3072]{1,0:T(8,128)(2,1)S(1)}, bf16[1024,3072]{1,0:T(8,128)(2,1)S(1)}) custom-call(bf16[128,3200]{1,0:T(8,128)(2,1)S(1)} %get-tuple-element.26.x_ref, bf16[4,1024,3072]{2,1,0:T(8,128)(2,1)} %up_ref.3, bf16[4,1024,3072]{2,1,0:T(8,128)(2,1)} %down_ref.7, ...), custom_call_target="tpu_custom_call" | custom-call | flops 1610612736 | bytes 12582912 | tf_op jit(solution)/shard_map/pallas_call | solution.py:26
  34.3 0.1 collective-permute-start.8
  34.4 0.0 collective-permute-done.9.up_b
  34.4 0.0 collective-permute-done.7.gate_b
  34.4 2.8 %shard_map.69 = (bf16[2,128,1024]{2,1,0:T(8,128)(2,1)S(1)}, bf16[1024,3072]{1,0:T(8,128)(2,1)S(1)}) custom-call(f32[4224,128]{1,0:T(8,128)S(1)} %get-tuple-element.27.gate_a, f32[4224,128]{1,0:T(8,128)S(1)} %collective-permute-done.7.gate_b, f32[2048,128]{1,0:T(8,128)S(1)} %get-tuple-element.33.up_a, bf16[2048,128]{1,0:T(8,128)(2,1)S(1)} %collective-permute-done.9.up_b, ...), custom_call_target="tpu_custom_call" | custom-call | bytes 3145728 | tf_op jit(solution)/shard_map/pallas_call | solution.py:26
  37.2 0.0 collective-permute-done.8.up_b
  37.2 4.1 %shard_map.70 = (f32[16,3072]{1,0:T(8,128)S(1)}, bf16[16,3072]{1,0:T(8,128)(2,1)S(1)}, bf16[16,3072]{1,0:T(8,128)(2,1)S(1)}, bf16[16,3072]{1,0:T(8,128)(2,1)S(1)...) custom-call(bf16[128,3200]{1,0:T(8,128)(2,1)S(1)} %get-tuple-element, ...), custom_call_target="tpu_custom_call" | custom-call | flops 3221225472 | bytes 25165824 | tf_op jit(solution)/shard_map/pallas_call | solution.py:26
  41.3 1.1 %collective-permute-start.13 = (bf16[16,3072]{1,0:T(8,128)(2,1)S(1)}, bf16[16,3072]{1,0:T(8,128)(2,1)S(1)}, u32[]{:S(2)}, u32[]{:S(2)}) collective-permute-start(bf16[16,3072]{1,0:T(8,128)(2,1)S(1)} %get-tuple-element.44), channel_id=1, source_target_pairs={{0,2},{2,0},{4,6},{6,4},{8,10},{10,8},{12,14},{14,12},{1,3},{3,1},... | collective-permute-start | bytes 294920 | tf_op jit(solution)/shard_map/ppermute | solution.py:17
  42.4 1.3 %collective-permute-start.14 = (bf16[16,3072]{1,0:T(8,128)(2,1)S(1)}, bf16[16,3072]{1,0:T(8,128)(2,1)S(1)}, u32[]{:S(2)}, u32[]{:S(2)}) collective-permute-start(bf16[16,3072]{1,0:T(8,128)(2,1)S(1)} %get-tuple-element.45), channel_id=1, source_target_pairs={{0,4},{2,6},{4,0},{6,2},{8,12},{10,14},{12,8},{14,10},{1,5},{3,7},... | collective-permute-start | bytes 294920 | tf_op jit(solution)/shard_map/ppermute | solution.py:17
  43.7 1.1 %collective-permute-start.15 = (bf16[16,3072]{1,0:T(8,128)(2,1)S(1)}, bf16[16,3072]{1,0:T(8,128)(2,1)S(1)}, u32[]{:S(2)}, u32[]{:S(2)}) collective-permute-start(bf16[16,3072]{1,0:T(8,128)(2,1)S(1)} %get-tuple-element.46), channel_id=1, source_target_pairs={{0,6},{2,4},{4,2},{6,0},{8,14},{10,12},{12,10},{14,8},{1,7},{3,5},... | collective-permute-start | bytes 294920 | tf_op jit(solution)/shard_map/ppermute | solution.py:17
  44.8 1.0 %collective-permute-start.10 = (bf16[16,3072]{1,0:T(8,128)(2,1)S(1)}, bf16[16,3072]{1,0:T(8,128)(2,1)S(1)}, u32[]{:S(2)}, u32[]{:S(2)}) collective-permute-start(bf16[16,3072]{1,0:T(8,128)(2,1)S(1)} %get-tuple-element.40), channel_id=1, source_target_pairs={{0,2},{2,0},{4,6},{6,4},{8,10},{10,8},{12,14},{14,12},{1,3},{3,1},... | collective-permute-start | bytes 294920 | tf_op jit(solution)/shard_map/ppermute | solution.py:17
  45.9 1.3 %collective-permute-start.11 = (bf16[16,3072]{1,0:T(8,128)(2,1)S(1)}, bf16[16,3072]{1,0:T(8,128)(2,1)S(1)}, u32[]{:S(2)}, u32[]{:S(2)}) collective-permute-start(bf16[16,3072]{1,0:T(8,128)(2,1)S(1)} %get-tuple-element.41), channel_id=1, source_target_pairs={{0,4},{2,6},{4,0},{6,2},{8,12},{10,14},{12,8},{14,10},{1,5},{3,7},... | collective-permute-start | bytes 294920 | tf_op jit(solution)/shard_map/ppermute | solution.py:17
  47.2 0.0 collective-permute-done.13
  47.2 1.1 %collective-permute-start.12 = (bf16[16,3072]{1,0:T(8,128)(2,1)S(1)}, bf16[16,3072]{1,0:T(8,128)(2,1)S(1)}, u32[]{:S(2)}, u32[]{:S(2)}) collective-permute-start(bf16[16,3072]{1,0:T(8,128)(2,1)S(1)} %get-tuple-element.42), channel_id=1, source_target_pairs={{0,6},{2,4},{4,2},{6,0},{8,14},{10,12},{12,10},{14,8},{1,7},{3,5},... | collective-permute-start | bytes 294920 | tf_op jit(solution)/shard_map/ppermute | solution.py:17
  48.3 0.0 collective-permute-done.14
  48.3 2.1 %collective-permute-done.15 = bf16[16,3072]{1,0:T(8,128)(2,1)S(1)} collective-permute-done((bf16[16,3072]{1,0:T(8,128)(2,1)S(1)}, bf16[16,3072]{1,0:T(8,128)(2,1)S(1)}, u32[]{:S(2)}, u32[]{:S(2)}) %collective-permute-start.15) | collective-permute-done | bytes 98336 | tf_op jit(solution)/shard_map/ppermute | solution.py:17
  50.5 0.1 add_convert_fusion.1
  50.5 3.3 %collective-permute-start.16 = (bf16[16,3072]{1,0:T(8,128)(2,1)S(1)}, bf16[16,3072]{1,0:T(8,128)(2,1)S(1)}, u32[]{:S(2)}, u32[]{:S(2)}) collective-permute-start(bf16[16,3072]{1,0:T(8,128)(2,1)S(1)} %add_convert_fusion.1), channel_id=1, source_target_pairs={{0,8},{2,10},{4,12},{6,14},{8,0},{10,2},{12,4},{14,6},{1,9},{3,11}... | collective-permute-start | bytes 294920 | tf_op jit(solution)/shard_map/ppermute | solution.py:17
  53.8 0.0 collective-permute-done.10
  53.8 0.0 collective-permute-done.11
  53.8 1.3 %collective-permute-done.12 = bf16[16,3072]{1,0:T(8,128)(2,1)S(1)} collective-permute-done((bf16[16,3072]{1,0:T(8,128)(2,1)S(1)}, bf16[16,3072]{1,0:T(8,128)(2,1)S(1)}, u32[]{:S(2)}, u32[]{:S(2)}) %collective-permute-start.12) | collective-permute-done | bytes 98336 | tf_op jit(solution)/shard_map/ppermute | solution.py:17
  55.1 3.4 %collective-permute-done.16 = bf16[16,3072]{1,0:T(8,128)(2,1)S(1)} collective-permute-done((bf16[16,3072]{1,0:T(8,128)(2,1)S(1)}, bf16[16,3072]{1,0:T(8,128)(2,1)S(1)}, u32[]{:S(2)}, u32[]{:S(2)}) %collective-permute-start.16) | collective-permute-done | bytes 98336 | tf_op jit(solution)/shard_map/ppermute | solution.py:17
  58.5 0.7 %add_convert_fusion = bf16[16,3072]{1,0:T(8,128)(2,1)} fusion(bf16[16,3072]{1,0:T(8,128)(2,1)S(1)} %collective-permute-done.16, bf16[16,3072]{1,0:T(8,128)(2,1)S(1)} %collective-permute-done.12, bf16[16,3072]{1,0:T(8,128)(2,1)S(1)} %collective-permute-done.11, f32[16,3072]{1,0:T(8,128)S(1)} %get-tuple-element.39, bf16[16,3072]{1,0:T(8,128)(2,1)S(1)} %collective-permute-done.10), kind=kLoop, calls=%fused_computation | loop fusion | flops 442368 | bytes 688128 | tf_op jit(solution)/shard_map/convert_element_type | solution.py:266
  (16 shorter events, 0.0 us)
Async XLA Ops:
  0.0 0.9 %copy-start = (bf16[16,3072]{1,0:T(8,128)(2,1)S(1)}, bf16[16,3072]{1,0:T(8,128)(2,1)}, u32[]{:S(2)}) copy-start(bf16[16,3072]{1,0:T(8,128)(2,1)} %tokens_ref.1) | copy-start | bytes 294916
  0.9 0.7 %copy-start.1 = (s32[16,2]{0,1:T(2,128)S(1)}, s32[16,2]{0,1:T(2,128)}, u32[]{:S(2)}) copy-start(s32[16,2]{0,1:T(2,128)} %param.7) | copy-start | bytes 388
  1.6 7.6 %copy-start.2 = (bf16[3072,4]{0,1:T(4,128)(2,1)S(1)}, bf16[3072,4]{0,1:T(4,128)(2,1)}, u32[]{:S(2)}) copy-start(bf16[3072,4]{0,1:T(4,128)(2,1)} %param.8) | copy-start | bytes 73732
  1.6 17.0 %slice-start = ((s8[25165824]{0:T(1024)(128)(4,1)}), s8[4194304]{0:T(1024)(128)(4,1)S(1)}, s32[]{:S(2)}) async-start(s8[25165824]{0:T(1024)(128)(4,1)} %bitcast.2), calls=%async_computation | async-start | bytes 8388608
  1.6 17.0 %slice-start.1 = ((s8[25165824]{0:T(1024)(128)(4,1)}), s8[4194304]{0:T(1024)(128)(4,1)S(1)}, s32[]{:S(2)}) async-start(s8[25165824]{0:T(1024)(128)(4,1)} %bitcast.2), calls=%async_computation.1 | async-start | bytes 8388608
  1.6 17.0 %slice-start.2 = ((s8[25165824]{0:T(1024)(128)(4,1)}), s8[4194304]{0:T(1024)(128)(4,1)S(1)}, s32[]{:S(2)}) async-start(s8[25165824]{0:T(1024)(128)(4,1)} %bitcast.2), calls=%async_computation.2 | async-start | bytes 8388608
  1.6 17.0 %slice-start.3 = ((s8[25165824]{0:T(1024)(128)(4,1)}), s8[4194304]{0:T(1024)(128)(4,1)S(1)}, s32[]{:S(2)}) async-start(s8[25165824]{0:T(1024)(128)(4,1)} %bitcast.2), calls=%async_computation.3 | async-start | bytes 8388608
  1.6 17.0 %slice-start.4 = ((s8[25165824]{0:T(1024)(128)(4,1)}), s8[4194304]{0:T(1024)(128)(4,1)S(1)}, s32[]{:S(2)}) async-start(s8[25165824]{0:T(1024)(128)(4,1)} %bitcast.2), calls=%async_computation.4 | async-start | bytes 8388608
  1.7 9.1 %collective-permute-start.3 = (bf16[16,3200]{1,0:T(8,128)(2,1)S(1)}, bf16[16,3200]{1,0:T(8,128)(2,1)S(1)}, u32[]{:S(2)}, u32[]{:S(2)}) collective-permute-start(bf16[16,3200]{1,0:T(8,128)(2,1)S(1)} %shard_map.64.refs_0_), channel_id=1, source_target_pairs={{0,8},{2,10},{4,12},{6,14},{8,0},{10,2},{12,4},{14,6},{1,9},{3,11}... | collective-permute-start | bytes 307208 | tf_op jit(solution)/shard_map/ppermute | solution.py:17
  5.7 8.2 %collective-permute-start.2 = (bf16[16,3200]{1,0:T(8,128)(2,1)S(1)}, bf16[16,3200]{1,0:T(8,128)(2,1)S(1)}, u32[]{:S(2)}, u32[]{:S(2)}) collective-permute-start(bf16[16,3200]{1,0:T(8,128)(2,1)S(1)} %shard_map.64.refs_0_), channel_id=1, source_target_pairs={{0,6},{2,4},{4,2},{6,0},{8,14},{10,12},{12,10},{14,8},{1,7},{3,5},... | collective-permute-start | bytes 307208 | tf_op jit(solution)/shard_map/ppermute | solution.py:17
  8.3 8.8 %collective-permute-start.1 = (bf16[16,3200]{1,0:T(8,128)(2,1)S(1)}, bf16[16,3200]{1,0:T(8,128)(2,1)S(1)}, u32[]{:S(2)}, u32[]{:S(2)}) collective-permute-start(bf16[16,3200]{1,0:T(8,128)(2,1)S(1)} %shard_map.64.refs_0_), channel_id=1, source_target_pairs={{0,4},{2,6},{4,0},{6,2},{8,12},{10,14},{12,8},{14,10},{1,5},{3,7},... | collective-permute-start | bytes 307208 | tf_op jit(solution)/shard_map/ppermute | solution.py:17
  8.7 8.4 %collective-permute-start = (bf16[16,3200]{1,0:T(8,128)(2,1)S(1)}, bf16[16,3200]{1,0:T(8,128)(2,1)S(1)}, u32[]{:S(2)}, u32[]{:S(2)}) collective-permute-start(bf16[16,3200]{1,0:T(8,128)(2,1)S(1)} %shard_map.64.refs_0_), channel_id=1, source_target_pairs={{0,2},{2,0},{4,6},{6,4},{8,10},{10,8},{12,14},{14,12},{1,3},{3,1},... | collective-permute-start | bytes 307208 | tf_op jit(solution)/shard_map/ppermute | solution.py:17
  10.8 7.8 %slice-start.5 = ((s8[25165824]{0:T(1024)(128)(4,1)}), s8[4194304]{0:T(1024)(128)(4,1)S(1)}, s32[]{:S(2)}) async-start(s8[25165824]{0:T(1024)(128)(4,1)} %bitcast.2), calls=%async_computation.5 | async-start | bytes 8388608
  10.8 6.7 %collective-permute-start.6 = (bf16[16,3200]{1,0:T(8,128)(2,1)S(1)}, bf16[16,3200]{1,0:T(8,128)(2,1)S(1)}, u32[]{:S(2)}, u32[]{:S(2)}) collective-permute-start(bf16[16,3200]{1,0:T(8,128)(2,1)S(1)} %collective-permute-done.3.refs_4_), channel_id=1, source_target_pairs={{0,6},{2,4},{4,2},{6,0},{8,14},{10,12},{12,10},{14,8},{1,7},{3,5},... | collective-permute-start | bytes 307208 | tf_op jit(solution)/shard_map/ppermute | solution.py:17
  12.5 6.1 %collective-permute-start.5 = (bf16[16,3200]{1,0:T(8,128)(2,1)S(1)}, bf16[16,3200]{1,0:T(8,128)(2,1)S(1)}, u32[]{:S(2)}, u32[]{:S(2)}) collective-permute-start(bf16[16,3200]{1,0:T(8,128)(2,1)S(1)} %collective-permute-done.3.refs_4_), channel_id=1, source_target_pairs={{0,4},{2,6},{4,0},{6,2},{8,12},{10,14},{12,8},{14,10},{1,5},{3,7},... | collective-permute-start | bytes 307208 | tf_op jit(solution)/shard_map/ppermute | solution.py:17
  13.9 4.7 %collective-permute-start.4 = (bf16[16,3200]{1,0:T(8,128)(2,1)S(1)}, bf16[16,3200]{1,0:T(8,128)(2,1)S(1)}, u32[]{:S(2)}, u32[]{:S(2)}) collective-permute-start(bf16[16,3200]{1,0:T(8,128)(2,1)S(1)} %collective-permute-done.3.refs_4_), channel_id=1, source_target_pairs={{0,2},{2,0},{4,6},{6,4},{8,10},{10,8},{12,14},{14,12},{1,3},{3,1},... | collective-permute-start | bytes 307208 | tf_op jit(solution)/shard_map/ppermute | solution.py:17
  25.6 8.8 %collective-permute-start.7 = (f32[4224,128]{1,0:T(8,128)S(1)}, f32[4224,128]{1,0:T(8,128)S(1)}, u32[]{:S(2)}, u32[]{:S(2)}) collective-permute-start(f32[4224,128]{1,0:T(8,128)S(1)} %get-tuple-element.27.gate_a), channel_id=1, source_target_pairs={{0,1},{1,0},{2,3},{3,2},{4,5},{5,4},{6,7},{7,6},{8,9},{9,8},{10,11... | collective-permute-start | bytes 6488072 | tf_op jit(solution)/shard_map/ppermute | solution.py:220
  29.1 5.3 %collective-permute-start.9 = (bf16[2048,128]{1,0:T(8,128)(2,1)S(1)}, bf16[2048,128]{1,0:T(8,128)(2,1)S(1)}, u32[]{:S(2)}, u32[]{:S(2)}) collective-permute-start(bf16[2048,128]{1,0:T(8,128)(2,1)S(1)} %get-tuple-element.34), channel_id=1, source_target_pairs={{0,1},{1,0},{2,3},{3,2},{4,5},{5,4},{6,7},{7,6},{8,9},{9,8},{10,11... | collective-permute-start | bytes 1572872 | tf_op jit(solution)/shard_map/ppermute | solution.py:238
  34.3 2.9 %collective-permute-start.8 = (bf16[2048,128]{1,0:T(8,128)(2,1)S(1)}, bf16[2048,128]{1,0:T(8,128)(2,1)S(1)}, u32[]{:S(2)}, u32[]{:S(2)}) collective-permute-start(bf16[2048,128]{1,0:T(8,128)(2,1)S(1)} %get-tuple-element.32), channel_id=1, source_target_pairs={{0,1},{1,0},{2,3},{3,2},{4,5},{5,4},{6,7},{7,6},{8,9},{9,8},{10,11... | collective-permute-start | bytes 1572872 | tf_op jit(solution)/shard_map/ppermute | solution.py:238
  41.3 5.9 %collective-permute-start.13 = (bf16[16,3072]{1,0:T(8,128)(2,1)S(1)}, bf16[16,3072]{1,0:T(8,128)(2,1)S(1)}, u32[]{:S(2)}, u32[]{:S(2)}) collective-permute-start(bf16[16,3072]{1,0:T(8,128)(2,1)S(1)} %get-tuple-element.44), channel_id=1, source_target_pairs={{0,2},{2,0},{4,6},{6,4},{8,10},{10,8},{12,14},{14,12},{1,3},{3,1},... | collective-permute-start | bytes 294920 | tf_op jit(solution)/shard_map/ppermute | solution.py:17
  42.4 6.0 %collective-permute-start.14 = (bf16[16,3072]{1,0:T(8,128)(2,1)S(1)}, bf16[16,3072]{1,0:T(8,128)(2,1)S(1)}, u32[]{:S(2)}, u32[]{:S(2)}) collective-permute-start(bf16[16,3072]{1,0:T(8,128)(2,1)S(1)} %get-tuple-element.45), channel_id=1, source_target_pairs={{0,4},{2,6},{4,0},{6,2},{8,12},{10,14},{12,8},{14,10},{1,5},{3,7},... | collective-permute-start | bytes 294920 | tf_op jit(solution)/shard_map/ppermute | solution.py:17
  43.7 6.8 %collective-permute-start.15 = (bf16[16,3072]{1,0:T(8,128)(2,1)S(1)}, bf16[16,3072]{1,0:T(8,128)(2,1)S(1)}, u32[]{:S(2)}, u32[]{:S(2)}) collective-permute-start(bf16[16,3072]{1,0:T(8,128)(2,1)S(1)} %get-tuple-element.46), channel_id=1, source_target_pairs={{0,6},{2,4},{4,2},{6,0},{8,14},{10,12},{12,10},{14,8},{1,7},{3,5},... | collective-permute-start | bytes 294920 | tf_op jit(solution)/shard_map/ppermute | solution.py:17
  44.8 9.0 %collective-permute-start.10 = (bf16[16,3072]{1,0:T(8,128)(2,1)S(1)}, bf16[16,3072]{1,0:T(8,128)(2,1)S(1)}, u32[]{:S(2)}, u32[]{:S(2)}) collective-permute-start(bf16[16,3072]{1,0:T(8,128)(2,1)S(1)} %get-tuple-element.40), channel_id=1, source_target_pairs={{0,2},{2,0},{4,6},{6,4},{8,10},{10,8},{12,14},{14,12},{1,3},{3,1},... | collective-permute-start | bytes 294920 | tf_op jit(solution)/shard_map/ppermute | solution.py:17
  45.9 8.0 %collective-permute-start.11 = (bf16[16,3072]{1,0:T(8,128)(2,1)S(1)}, bf16[16,3072]{1,0:T(8,128)(2,1)S(1)}, u32[]{:S(2)}, u32[]{:S(2)}) collective-permute-start(bf16[16,3072]{1,0:T(8,128)(2,1)S(1)} %get-tuple-element.41), channel_id=1, source_target_pairs={{0,4},{2,6},{4,0},{6,2},{8,12},{10,14},{12,8},{14,10},{1,5},{3,7},... | collective-permute-start | bytes 294920 | tf_op jit(solution)/shard_map/ppermute | solution.py:17
  47.2 7.9 %collective-permute-start.12 = (bf16[16,3072]{1,0:T(8,128)(2,1)S(1)}, bf16[16,3072]{1,0:T(8,128)(2,1)S(1)}, u32[]{:S(2)}, u32[]{:S(2)}) collective-permute-start(bf16[16,3072]{1,0:T(8,128)(2,1)S(1)} %get-tuple-element.42), channel_id=1, source_target_pairs={{0,6},{2,4},{4,2},{6,0},{8,14},{10,12},{12,10},{14,8},{1,7},{3,5},... | collective-permute-start | bytes 294920 | tf_op jit(solution)/shard_map/ppermute | solution.py:17
  50.5 8.0 %collective-permute-start.16 = (bf16[16,3072]{1,0:T(8,128)(2,1)S(1)}, bf16[16,3072]{1,0:T(8,128)(2,1)S(1)}, u32[]{:S(2)}, u32[]{:S(2)}) collective-permute-start(bf16[16,3072]{1,0:T(8,128)(2,1)S(1)} %add_convert_fusion.1), channel_id=1, source_target_pairs={{0,8},{2,10},{4,12},{6,14},{8,0},{10,2},{12,4},{14,6},{1,9},{3,11}... | collective-permute-start | bytes 294920 | tf_op jit(solution)/shard_map/ppermute | solution.py:17

commit v5 on v4

--- a/solution.py
+++ b/solution.py
@@ -41,14 +41,21 @@
     return jnp.sum(jnp.where(diagonal, row, 0.0), axis=1, keepdims=True)
 
 
-def pack_kernel(tokens_ref, ids_ref, out_ref):
+def pack_kernel(tokens_ref, ids_ref, out_ref, held_ref, sems):
     rows, width = tokens_ref.shape
-    out_ref[:, :width] = tokens_ref[...]
-    ids = ids_ref[...].astype(F32)
+    copies = [
+        pltpu.make_async_copy(ids_ref, held_ref, sems.at[0]),
+        pltpu.make_async_copy(tokens_ref, out_ref.at[:, pl.ds(0, width)], sems.at[1]),
+    ]
+    for copy in copies:
+        copy.start()
+    copies[0].wait()
+    ids = held_ref[...].astype(F32)
     lane = lax.broadcasted_iota(jnp.int32, (rows, IDS), 1)
     out_ref[:, width:] = jnp.where(
         lane == 0, column(ids[0:1], rows), column(ids[1:2], rows)
     ).astype(BF16)
+    copies[1].wait()
 
 
 def over_width(a, b):
@@ -173,20 +180,22 @@
     experts, hidden, _ = w_gate.shape
     count, half = 8 * rows, experts // 2
     shape = lambda *s, dtype=F32: jax.ShapeDtypeStruct(s, dtype)
+    in_hbm = lambda array: pltpu.with_memory_space_constraint(array, pltpu.HBM)
     (own,) = call(
         pack_kernel,
         [shape(rows, width + IDS, dtype=BF16)],
-        [tokens, expert_ids.T],
+        [in_hbm(tokens), in_hbm(expert_ids.T)],
         30_000_000_000,
         4 * rows * width,
         1,
+        [pltpu.VMEM(expert_ids.shape[::-1], jnp.int32), pltpu.SemaphoreType.DMA((2,))],
+        hbm=(0, 1),
     )
     far = xor_send(own, 4)
     near = [xor_send(own, k) for k in (1, 2, 3)]
     forwarded = [xor_send(far, k) for k in (1, 2, 3)]
     blocks = [own, *near, far, *forwarded]
 
-    in_hbm = lambda array: pltpu.with_memory_space_constraint(array, pltpu.HBM)
     w_gate, w_up, w_down = in_vmem(w_gate), in_hbm(w_up), in_hbm(w_down)
     flops = 2 * count * hidden * width
     size = 2 * hidden * width
@@ -259,8 +268,8 @@
         [pltpu.VMEM((1, hidden, width), BF16), *sems(1)],
         hbm=(6,),
     )
-    far_sums = [xor_send(parts[4 ^ k], k) for k in (1, 2, 3)]
-    near_sums = [xor_send(parts[k], k) for k in (1, 2, 3)]
+    far_sums = [xor_send(parts[4 ^ k], k) for k in (3, 2, 1)]
+    near_sums = [xor_send(parts[k], k) for k in (3, 2, 1)]
     add = lambda arrays: sum(a.astype(F32) for a in arrays)
     crossing = xor_send(add([parts[4], *far_sums]).astype(BF16), 4)
     return add([parts[0], *near_sums, crossing]).astype(BF16)

time: 59.4 us -> 58.1 us (0.978)
  local copies, waits for them, and re-layouts: 1.67 us -> 0.1 us
  Pallas kernels: 24.7 us -> 25.7 us
    unnamed x18 -> x14, local copies, waits for them, and re-layouts: 1.6 us -> 0.03 us
    pallas_call x7, Pallas kernels: 24.7 us -> 25.7 us  [call(): pl.pallas_call(kernel, out_shape=outs, in_specs=specs, out_specs=[VMEM_BL...]
  transfers between devices with their start and end apart: 17 -> 17, of which waited for: 6 -> 9; matrix products, arithmetic and copies ran while one was open for 0% -> 0% of each run, Pallas kernels for 23% -> 24%
where the time goes in v5:
time: 58.1 us; the launch traced here: 57.9 us
  Pallas kernels  25.7 us (44%)
  starting transfers between devices  21.5 us (37%)
  waiting for transfers between devices  9.69 us (17%)
  other arithmetic  0.76 us (1%)
    pallas_call x7, Pallas kernels, call(): pl.pallas_call(kernel, out_shape=outs, in_specs=specs, out_specs=[VMEM_BL...  25.7 us
    ppermute x14, starting transfers between devices, xor_send(): return lax.ppermute(block, 'batch', [(i, i ^ mask) for i in range(8)])  20.8 us
    ppermute x14, waiting for transfers between devices, xor_send(): return lax.ppermute(block, 'batch', [(i, i ^ mask) for i in range(8)])  9.69 us
  transfers between devices with their start and end apart: 17, of which 9 were waited for; matrix products, arithmetic and copies ran while one was open for 0% of the time, Pallas kernels for 24%

profile of v5, /device:TPU:0, one launch (start us, length us, event | category | flops | bytes accessed | tf_op | source)
XLA Modules:
  0.0 57.9 jit_solution(18304411963669790899)
XLA Ops:
  0.0 0.0 slice-start.4
  0.0 1.1 %shard_map.64.refs_0_ = bf16[16,3200]{1,0:T(8,128)(2,1)S(1)} custom-call(bf16[16,3072]{1,0:T(8,128)(2,1)} %tokens_ref.1, s32[2,16]{1,0:T(2,128)} %bitcast.5), custom_call_target="tpu_custom_call" | custom-call | flops 30000001024 | bytes 196608 | tf_op jit(solution)/shard_map/pallas_call | solution.py:26
  1.1 4.1 %collective-permute-start.3 = (bf16[16,3200]{1,0:T(8,128)(2,1)S(1)}, bf16[16,3200]{1,0:T(8,128)(2,1)S(1)}, u32[]{:S(2)}, u32[]{:S(2)}) collective-permute-start(bf16[16,3200]{1,0:T(8,128)(2,1)S(1)} %shard_map.64.refs_0_), channel_id=1, source_target_pairs={{0,8},{2,10},{4,12},{6,14},{8,0},{10,2},{12,4},{14,6},{1,9},{3,11}... | collective-permute-start | bytes 307208 | tf_op jit(solution)/shard_map/ppermute | solution.py:17
  5.2 2.5 %collective-permute-start.2 = (bf16[16,3200]{1,0:T(8,128)(2,1)S(1)}, bf16[16,3200]{1,0:T(8,128)(2,1)S(1)}, u32[]{:S(2)}, u32[]{:S(2)}) collective-permute-start(bf16[16,3200]{1,0:T(8,128)(2,1)S(1)} %shard_map.64.refs_0_), channel_id=1, source_target_pairs={{0,6},{2,4},{4,2},{6,0},{8,14},{10,12},{12,10},{14,8},{1,7},{3,5},... | collective-permute-start | bytes 307208 | tf_op jit(solution)/shard_map/ppermute | solution.py:17
  7.8 0.4 collective-permute-start.1
  8.2 0.5 collective-permute-start
  8.7 0.0 copy-done
  8.7 0.1 pad.4.refs_8_
  8.8 1.5 %collective-permute-done.3.refs_4_ = bf16[16,3200]{1,0:T(8,128)(2,1)S(1)} collective-permute-done((bf16[16,3200]{1,0:T(8,128)(2,1)S(1)}, bf16[16,3200]{1,0:T(8,128)(2,1)S(1)}, u32[]{:S(2)}, u32[]{:S(2)}) %collective-permute-start.3) | collective-permute-done | bytes 102432 | tf_op jit(solution)/shard_map/ppermute | solution.py:17
  10.3 1.7 %collective-permute-start.6 = (bf16[16,3200]{1,0:T(8,128)(2,1)S(1)}, bf16[16,3200]{1,0:T(8,128)(2,1)S(1)}, u32[]{:S(2)}, u32[]{:S(2)}) collective-permute-start(bf16[16,3200]{1,0:T(8,128)(2,1)S(1)} %collective-permute-done.3.refs_4_), channel_id=1, source_target_pairs={{0,6},{2,4},{4,2},{6,0},{8,14},{10,12},{12,10},{14,8},{1,7},{3,5},... | collective-permute-start | bytes 307208 | tf_op jit(solution)/shard_map/ppermute | solution.py:17
  12.0 1.4 %collective-permute-start.5 = (bf16[16,3200]{1,0:T(8,128)(2,1)S(1)}, bf16[16,3200]{1,0:T(8,128)(2,1)S(1)}, u32[]{:S(2)}, u32[]{:S(2)}) collective-permute-start(bf16[16,3200]{1,0:T(8,128)(2,1)S(1)} %collective-permute-done.3.refs_4_), channel_id=1, source_target_pairs={{0,4},{2,6},{4,0},{6,2},{8,12},{10,14},{12,8},{14,10},{1,5},{3,7},... | collective-permute-start | bytes 307208 | tf_op jit(solution)/shard_map/ppermute | solution.py:17
  13.4 0.0 collective-permute-done.2.refs_3_
  13.4 0.4 collective-permute-start.4
  13.8 2.8 %shard_map.65.refs_11_.refs_0_ = bf16[1024,3072]{1,0:T(8,128)(2,1)S(1)} custom-call(bf16[16,128]{1,0:T(8,128)(2,1)S(1)} %slice.4._, bf16[4,1024,3072]{2,1,0:T(8,128)(2,1)} %up_ref.3), custom_call_target="tpu_custom_call" | custom-call | flops 14000000000 | tf_op jit(solution)/shard_map/pallas_call | solution.py:26
  16.6 0.0 collective-permute-done.1.refs_2_
  16.6 0.0 collective-permute-done.refs_1_
  16.6 0.4 collective-permute-done.6.refs_7_
  17.0 1.1 %collective-permute-done.5.refs_6_ = bf16[16,3200]{1,0:T(8,128)(2,1)S(1)} collective-permute-done((bf16[16,3200]{1,0:T(8,128)(2,1)S(1)}, bf16[16,3200]{1,0:T(8,128)(2,1)S(1)}, u32[]{:S(2)}, u32[]{:S(2)}) %collective-permute-start.5) | collective-permute-done | bytes 102432 | tf_op jit(solution)/shard_map/ppermute | solution.py:17
  18.1 0.0 collective-permute-done.4.refs_5_
  18.1 0.0 slice-done
  18.1 0.0 slice-done.1
  18.2 6.9 %shard_map.66 = (bf16[128,3200]{1,0:T(8,128)(2,1)S(1)}, f32[4224,128]{1,0:T(8,128)S(1)}, bf16[1024,3072]{1,0:T(8,128)(2,1)S(1)}, bf16[1024,3072]{1,0:T(8,128)(2,1)S(1)}) custom-call(bf16[16,3200]{1,0:T(8,128)(2,1)S(1)} %shard_map.64.refs_0_, bf16[16,3200]{1,0:T(8,128)(2,1)S(1)} %collective-permute-done.refs_1_, ...), custom_call_target="tpu_custom_call" | custom-call | flops 3221225472 | bytes 25165824 | tf_op jit(solution)/shard_map/pallas_call | solution.py:26
  25.1 0.1 collective-permute-start.7
  25.1 3.4 %shard_map.67 = (f32[2048,128]{1,0:T(8,128)S(1)}, bf16[2048,128]{1,0:T(8,128)(2,1)S(1)}, bf16[1024,3072]{1,0:T(8,128)(2,1)S(1)}) custom-call(bf16[128,3200]{1,0:T(8,128)(2,1)S(1)} %get-tuple-element.26.x_ref, bf16[4,1024,3072]{2,1,0:T(8,128)(2,1)} %up_ref.3, bf16[4,1024,3072]{2,1,0:T(8,128)(2,1)} %down_ref.7, ...), custom_call_target="tpu_custom_call" | custom-call | flops 1610612736 | bytes 12582912 | tf_op jit(solution)/shard_map/pallas_call | solution.py:26
  28.6 0.6 collective-permute-start.9
  29.1 4.6 %shard_map.68 = (f32[2048,128]{1,0:T(8,128)S(1)}, bf16[2048,128]{1,0:T(8,128)(2,1)S(1)}, bf16[1024,3072]{1,0:T(8,128)(2,1)S(1)}, bf16[1024,3072]{1,0:T(8,128)(2,1)S(1)}) custom-call(bf16[128,3200]{1,0:T(8,128)(2,1)S(1)} %get-tuple-element.26.x_ref, bf16[4,1024,3072]{2,1,0:T(8,128)(2,1)} %up_ref.3, bf16[4,1024,3072]{2,1,0:T(8,128)(2,1)} %down_ref.7, ...), custom_call_target="tpu_custom_call" | custom-call | flops 1610612736 | bytes 12582912 | tf_op jit(solution)/shard_map/pallas_call | solution.py:26
  33.7 0.1 collective-permute-start.8
  33.8 0.0 collective-permute-done.9.up_b
  33.8 0.0 collective-permute-done.7.gate_b
  33.8 2.8 %shard_map.69 = (bf16[2,128,1024]{2,1,0:T(8,128)(2,1)S(1)}, bf16[1024,3072]{1,0:T(8,128)(2,1)S(1)}) custom-call(f32[4224,128]{1,0:T(8,128)S(1)} %get-tuple-element.27.gate_a, f32[4224,128]{1,0:T(8,128)S(1)} %collective-permute-done.7.gate_b, f32[2048,128]{1,0:T(8,128)S(1)} %get-tuple-element.33.up_a, bf16[2048,128]{1,0:T(8,128)(2,1)S(1)} %collective-permute-done.9.up_b, ...), custom_call_target="tpu_custom_call" | custom-call | bytes 3145728 | tf_op jit(solution)/shard_map/pallas_call | solution.py:26
  36.7 0.0 collective-permute-done.8.up_b
  36.7 4.1 %shard_map.70 = (f32[16,3072]{1,0:T(8,128)S(1)}, bf16[16,3072]{1,0:T(8,128)(2,1)S(1)}, bf16[16,3072]{1,0:T(8,128)(2,1)S(1)}, bf16[16,3072]{1,0:T(8,128)(2,1)S(1)...) custom-call(bf16[128,3200]{1,0:T(8,128)(2,1)S(1)} %get-tuple-element, ...), custom_call_target="tpu_custom_call" | custom-call | flops 3221225472 | bytes 25165824 | tf_op jit(solution)/shard_map/pallas_call | solution.py:26
  40.8 1.8 %collective-permute-start.13 = (bf16[16,3072]{1,0:T(8,128)(2,1)S(1)}, bf16[16,3072]{1,0:T(8,128)(2,1)S(1)}, u32[]{:S(2)}, u32[]{:S(2)}) collective-permute-start(bf16[16,3072]{1,0:T(8,128)(2,1)S(1)} %get-tuple-element.44), channel_id=1, source_target_pairs={{0,6},{2,4},{4,2},{6,0},{8,14},{10,12},{12,10},{14,8},{1,7},{3,5},... | collective-permute-start | bytes 294920 | tf_op jit(solution)/shard_map/ppermute | solution.py:17
  42.6 0.7 %collective-permute-start.14 = (bf16[16,3072]{1,0:T(8,128)(2,1)S(1)}, bf16[16,3072]{1,0:T(8,128)(2,1)S(1)}, u32[]{:S(2)}, u32[]{:S(2)}) collective-permute-start(bf16[16,3072]{1,0:T(8,128)(2,1)S(1)} %get-tuple-element.45), channel_id=1, source_target_pairs={{0,4},{2,6},{4,0},{6,2},{8,12},{10,14},{12,8},{14,10},{1,5},{3,7},... | collective-permute-start | bytes 294920 | tf_op jit(solution)/shard_map/ppermute | solution.py:17
  43.3 1.0 %collective-permute-start.15 = (bf16[16,3072]{1,0:T(8,128)(2,1)S(1)}, bf16[16,3072]{1,0:T(8,128)(2,1)S(1)}, u32[]{:S(2)}, u32[]{:S(2)}) collective-permute-start(bf16[16,3072]{1,0:T(8,128)(2,1)S(1)} %get-tuple-element.46), channel_id=1, source_target_pairs={{0,2},{2,0},{4,6},{6,4},{8,10},{10,8},{12,14},{14,12},{1,3},{3,1},... | collective-permute-start | bytes 294920 | tf_op jit(solution)/shard_map/ppermute | solution.py:17
  44.3 1.8 %collective-permute-start.10 = (bf16[16,3072]{1,0:T(8,128)(2,1)S(1)}, bf16[16,3072]{1,0:T(8,128)(2,1)S(1)}, u32[]{:S(2)}, u32[]{:S(2)}) collective-permute-start(bf16[16,3072]{1,0:T(8,128)(2,1)S(1)} %get-tuple-element.40), channel_id=1, source_target_pairs={{0,6},{2,4},{4,2},{6,0},{8,14},{10,12},{12,10},{14,8},{1,7},{3,5},... | collective-permute-start | bytes 294920 | tf_op jit(solution)/shard_map/ppermute | solution.py:17
  46.1 0.7 %collective-permute-start.11 = (bf16[16,3072]{1,0:T(8,128)(2,1)S(1)}, bf16[16,3072]{1,0:T(8,128)(2,1)S(1)}, u32[]{:S(2)}, u32[]{:S(2)}) collective-permute-start(bf16[16,3072]{1,0:T(8,128)(2,1)S(1)} %get-tuple-element.41), channel_id=1, source_target_pairs={{0,4},{2,6},{4,0},{6,2},{8,12},{10,14},{12,8},{14,10},{1,5},{3,7},... | collective-permute-start | bytes 294920 | tf_op jit(solution)/shard_map/ppermute | solution.py:17
  46.8 0.5 collective-permute-done.13
  47.3 1.0 %collective-permute-start.12 = (bf16[16,3072]{1,0:T(8,128)(2,1)S(1)}, bf16[16,3072]{1,0:T(8,128)(2,1)S(1)}, u32[]{:S(2)}, u32[]{:S(2)}) collective-permute-start(bf16[16,3072]{1,0:T(8,128)(2,1)S(1)} %get-tuple-element.42), channel_id=1, source_target_pairs={{0,2},{2,0},{4,6},{6,4},{8,10},{10,8},{12,14},{14,12},{1,3},{3,1},... | collective-permute-start | bytes 294920 | tf_op jit(solution)/shard_map/ppermute | solution.py:17
  48.3 0.6 %collective-permute-done.14 = bf16[16,3072]{1,0:T(8,128)(2,1)S(1)} collective-permute-done((bf16[16,3072]{1,0:T(8,128)(2,1)S(1)}, bf16[16,3072]{1,0:T(8,128)(2,1)S(1)}, u32[]{:S(2)}, u32[]{:S(2)}) %collective-permute-start.14) | collective-permute-done | bytes 98336 | tf_op jit(solution)/shard_map/ppermute | solution.py:17
  49.0 0.5 collective-permute-done.15
  49.5 0.1 add_convert_fusion.1
  49.5 2.6 %collective-permute-start.16 = (bf16[16,3072]{1,0:T(8,128)(2,1)S(1)}, bf16[16,3072]{1,0:T(8,128)(2,1)S(1)}, u32[]{:S(2)}, u32[]{:S(2)}) collective-permute-start(bf16[16,3072]{1,0:T(8,128)(2,1)S(1)} %add_convert_fusion.1), channel_id=1, source_target_pairs={{0,8},{2,10},{4,12},{6,14},{8,0},{10,2},{12,4},{14,6},{1,9},{3,11}... | collective-permute-start | bytes 294920 | tf_op jit(solution)/shard_map/ppermute | solution.py:17
  52.2 0.0 collective-permute-done.10
  52.2 0.7 %collective-permute-done.11 = bf16[16,3072]{1,0:T(8,128)(2,1)S(1)} collective-permute-done((bf16[16,3072]{1,0:T(8,128)(2,1)S(1)}, bf16[16,3072]{1,0:T(8,128)(2,1)S(1)}, u32[]{:S(2)}, u32[]{:S(2)}) %collective-permute-start.11) | collective-permute-done | bytes 98336 | tf_op jit(solution)/shard_map/ppermute | solution.py:17
  52.8 0.4 collective-permute-done.12
  53.2 3.9 %collective-permute-done.16 = bf16[16,3072]{1,0:T(8,128)(2,1)S(1)} collective-permute-done((bf16[16,3072]{1,0:T(8,128)(2,1)S(1)}, bf16[16,3072]{1,0:T(8,128)(2,1)S(1)}, u32[]{:S(2)}, u32[]{:S(2)}) %collective-permute-start.16) | collective-permute-done | bytes 98336 | tf_op jit(solution)/shard_map/ppermute | solution.py:17
  57.2 0.7 %add_convert_fusion = bf16[16,3072]{1,0:T(8,128)(2,1)} fusion(bf16[16,3072]{1,0:T(8,128)(2,1)S(1)} %collective-permute-done.16, bf16[16,3072]{1,0:T(8,128)(2,1)S(1)} %collective-permute-done.12, bf16[16,3072]{1,0:T(8,128)(2,1)S(1)} %collective-permute-done.11, f32[16,3072]{1,0:T(8,128)S(1)} %get-tuple-element.39, bf16[16,3072]{1,0:T(8,128)(2,1)S(1)} %collective-permute-done.10), kind=kLoop, calls=%fused_computation | loop fusion | flops 442368 | bytes 688128 | tf_op jit(solution)/shard_map/convert_element_type | solution.py:275
  (12 shorter events, 0.0 us)
Async XLA Ops:
  0.0 8.7 %copy-start = (bf16[3072,4]{0,1:T(4,128)(2,1)S(1)}, bf16[3072,4]{0,1:T(4,128)(2,1)}, u32[]{:S(2)}) copy-start(bf16[3072,4]{0,1:T(4,128)(2,1)} %param.8) | copy-start | bytes 73732
  0.0 18.1 %slice-start = ((s8[25165824]{0:T(1024)(128)(4,1)}), s8[4194304]{0:T(1024)(128)(4,1)S(1)}, s32[]{:S(2)}) async-start(s8[25165824]{0:T(1024)(128)(4,1)} %bitcast.2), calls=%async_computation | async-start | bytes 8388608
  0.0 18.1 %slice-start.1 = ((s8[25165824]{0:T(1024)(128)(4,1)}), s8[4194304]{0:T(1024)(128)(4,1)S(1)}, s32[]{:S(2)}) async-start(s8[25165824]{0:T(1024)(128)(4,1)} %bitcast.2), calls=%async_computation.1 | async-start | bytes 8388608
  0.0 18.1 %slice-start.2 = ((s8[25165824]{0:T(1024)(128)(4,1)}), s8[4194304]{0:T(1024)(128)(4,1)S(1)}, s32[]{:S(2)}) async-start(s8[25165824]{0:T(1024)(128)(4,1)} %bitcast.2), calls=%async_computation.2 | async-start | bytes 8388608
  0.0 18.1 %slice-start.3 = ((s8[25165824]{0:T(1024)(128)(4,1)}), s8[4194304]{0:T(1024)(128)(4,1)S(1)}, s32[]{:S(2)}) async-start(s8[25165824]{0:T(1024)(128)(4,1)} %bitcast.2), calls=%async_computation.3 | async-start | bytes 8388608
  0.0 18.1 %slice-start.4 = ((s8[25165824]{0:T(1024)(128)(4,1)}), s8[4194304]{0:T(1024)(128)(4,1)S(1)}, s32[]{:S(2)}) async-start(s8[25165824]{0:T(1024)(128)(4,1)} %bitcast.2), calls=%async_computation.4 | async-start | bytes 8388608
  1.1 9.2 %collective-permute-start.3 = (bf16[16,3200]{1,0:T(8,128)(2,1)S(1)}, bf16[16,3200]{1,0:T(8,128)(2,1)S(1)}, u32[]{:S(2)}, u32[]{:S(2)}) collective-permute-start(bf16[16,3200]{1,0:T(8,128)(2,1)S(1)} %shard_map.64.refs_0_), channel_id=1, source_target_pairs={{0,8},{2,10},{4,12},{6,14},{8,0},{10,2},{12,4},{14,6},{1,9},{3,11}... | collective-permute-start | bytes 307208 | tf_op jit(solution)/shard_map/ppermute | solution.py:17
  5.2 8.2 %collective-permute-start.2 = (bf16[16,3200]{1,0:T(8,128)(2,1)S(1)}, bf16[16,3200]{1,0:T(8,128)(2,1)S(1)}, u32[]{:S(2)}, u32[]{:S(2)}) collective-permute-start(bf16[16,3200]{1,0:T(8,128)(2,1)S(1)} %shard_map.64.refs_0_), channel_id=1, source_target_pairs={{0,6},{2,4},{4,2},{6,0},{8,14},{10,12},{12,10},{14,8},{1,7},{3,5},... | collective-permute-start | bytes 307208 | tf_op jit(solution)/shard_map/ppermute | solution.py:17
  7.8 8.8 %collective-permute-start.1 = (bf16[16,3200]{1,0:T(8,128)(2,1)S(1)}, bf16[16,3200]{1,0:T(8,128)(2,1)S(1)}, u32[]{:S(2)}, u32[]{:S(2)}) collective-permute-start(bf16[16,3200]{1,0:T(8,128)(2,1)S(1)} %shard_map.64.refs_0_), channel_id=1, source_target_pairs={{0,4},{2,6},{4,0},{6,2},{8,12},{10,14},{12,8},{14,10},{1,5},{3,7},... | collective-permute-start | bytes 307208 | tf_op jit(solution)/shard_map/ppermute | solution.py:17
  8.2 8.4 %collective-permute-start = (bf16[16,3200]{1,0:T(8,128)(2,1)S(1)}, bf16[16,3200]{1,0:T(8,128)(2,1)S(1)}, u32[]{:S(2)}, u32[]{:S(2)}) collective-permute-start(bf16[16,3200]{1,0:T(8,128)(2,1)S(1)} %shard_map.64.refs_0_), channel_id=1, source_target_pairs={{0,2},{2,0},{4,6},{6,4},{8,10},{10,8},{12,14},{14,12},{1,3},{3,1},... | collective-permute-start | bytes 307208 | tf_op jit(solution)/shard_map/ppermute | solution.py:17
  10.3 7.8 %slice-start.5 = ((s8[25165824]{0:T(1024)(128)(4,1)}), s8[4194304]{0:T(1024)(128)(4,1)S(1)}, s32[]{:S(2)}) async-start(s8[25165824]{0:T(1024)(128)(4,1)} %bitcast.2), calls=%async_computation.5 | async-start | bytes 8388608
  10.3 6.7 %collective-permute-start.6 = (bf16[16,3200]{1,0:T(8,128)(2,1)S(1)}, bf16[16,3200]{1,0:T(8,128)(2,1)S(1)}, u32[]{:S(2)}, u32[]{:S(2)}) collective-permute-start(bf16[16,3200]{1,0:T(8,128)(2,1)S(1)} %collective-permute-done.3.refs_4_), channel_id=1, source_target_pairs={{0,6},{2,4},{4,2},{6,0},{8,14},{10,12},{12,10},{14,8},{1,7},{3,5},... | collective-permute-start | bytes 307208 | tf_op jit(solution)/shard_map/ppermute | solution.py:17
  12.0 6.1 %collective-permute-start.5 = (bf16[16,3200]{1,0:T(8,128)(2,1)S(1)}, bf16[16,3200]{1,0:T(8,128)(2,1)S(1)}, u32[]{:S(2)}, u32[]{:S(2)}) collective-permute-start(bf16[16,3200]{1,0:T(8,128)(2,1)S(1)} %collective-permute-done.3.refs_4_), channel_id=1, source_target_pairs={{0,4},{2,6},{4,0},{6,2},{8,12},{10,14},{12,8},{14,10},{1,5},{3,7},... | collective-permute-start | bytes 307208 | tf_op jit(solution)/shard_map/ppermute | solution.py:17
  13.4 4.7 %collective-permute-start.4 = (bf16[16,3200]{1,0:T(8,128)(2,1)S(1)}, bf16[16,3200]{1,0:T(8,128)(2,1)S(1)}, u32[]{:S(2)}, u32[]{:S(2)}) collective-permute-start(bf16[16,3200]{1,0:T(8,128)(2,1)S(1)} %collective-permute-done.3.refs_4_), channel_id=1, source_target_pairs={{0,2},{2,0},{4,6},{6,4},{8,10},{10,8},{12,14},{14,12},{1,3},{3,1},... | collective-permute-start | bytes 307208 | tf_op jit(solution)/shard_map/ppermute | solution.py:17
  25.1 8.8 %collective-permute-start.7 = (f32[4224,128]{1,0:T(8,128)S(1)}, f32[4224,128]{1,0:T(8,128)S(1)}, u32[]{:S(2)}, u32[]{:S(2)}) collective-permute-start(f32[4224,128]{1,0:T(8,128)S(1)} %get-tuple-element.27.gate_a), channel_id=1, source_target_pairs={{0,1},{1,0},{2,3},{3,2},{4,5},{5,4},{6,7},{7,6},{8,9},{9,8},{10,11... | collective-permute-start | bytes 6488072 | tf_op jit(solution)/shard_map/ppermute | solution.py:229
  28.6 5.3 %collective-permute-start.9 = (bf16[2048,128]{1,0:T(8,128)(2,1)S(1)}, bf16[2048,128]{1,0:T(8,128)(2,1)S(1)}, u32[]{:S(2)}, u32[]{:S(2)}) collective-permute-start(bf16[2048,128]{1,0:T(8,128)(2,1)S(1)} %get-tuple-element.34), channel_id=1, source_target_pairs={{0,1},{1,0},{2,3},{3,2},{4,5},{5,4},{6,7},{7,6},{8,9},{9,8},{10,11... | collective-permute-start | bytes 1572872 | tf_op jit(solution)/shard_map/ppermute | solution.py:247
  33.7 2.9 %collective-permute-start.8 = (bf16[2048,128]{1,0:T(8,128)(2,1)S(1)}, bf16[2048,128]{1,0:T(8,128)(2,1)S(1)}, u32[]{:S(2)}, u32[]{:S(2)}) collective-permute-start(bf16[2048,128]{1,0:T(8,128)(2,1)S(1)} %get-tuple-element.32), channel_id=1, source_target_pairs={{0,1},{1,0},{2,3},{3,2},{4,5},{5,4},{6,7},{7,6},{8,9},{9,8},{10,11... | collective-permute-start | bytes 1572872 | tf_op jit(solution)/shard_map/ppermute | solution.py:247
  40.8 6.6 %collective-permute-start.13 = (bf16[16,3072]{1,0:T(8,128)(2,1)S(1)}, bf16[16,3072]{1,0:T(8,128)(2,1)S(1)}, u32[]{:S(2)}, u32[]{:S(2)}) collective-permute-start(bf16[16,3072]{1,0:T(8,128)(2,1)S(1)} %get-tuple-element.44), channel_id=1, source_target_pairs={{0,6},{2,4},{4,2},{6,0},{8,14},{10,12},{12,10},{14,8},{1,7},{3,5},... | collective-permute-start | bytes 294920 | tf_op jit(solution)/shard_map/ppermute | solution.py:17
  42.6 6.4 %collective-permute-start.14 = (bf16[16,3072]{1,0:T(8,128)(2,1)S(1)}, bf16[16,3072]{1,0:T(8,128)(2,1)S(1)}, u32[]{:S(2)}, u32[]{:S(2)}) collective-permute-start(bf16[16,3072]{1,0:T(8,128)(2,1)S(1)} %get-tuple-element.45), channel_id=1, source_target_pairs={{0,4},{2,6},{4,0},{6,2},{8,12},{10,14},{12,8},{14,10},{1,5},{3,7},... | collective-permute-start | bytes 294920 | tf_op jit(solution)/shard_map/ppermute | solution.py:17
  43.3 6.2 %collective-permute-start.15 = (bf16[16,3072]{1,0:T(8,128)(2,1)S(1)}, bf16[16,3072]{1,0:T(8,128)(2,1)S(1)}, u32[]{:S(2)}, u32[]{:S(2)}) collective-permute-start(bf16[16,3072]{1,0:T(8,128)(2,1)S(1)} %get-tuple-element.46), channel_id=1, source_target_pairs={{0,2},{2,0},{4,6},{6,4},{8,10},{10,8},{12,14},{14,12},{1,3},{3,1},... | collective-permute-start | bytes 294920 | tf_op jit(solution)/shard_map/ppermute | solution.py:17
  44.3 7.8 %collective-permute-start.10 = (bf16[16,3072]{1,0:T(8,128)(2,1)S(1)}, bf16[16,3072]{1,0:T(8,128)(2,1)S(1)}, u32[]{:S(2)}, u32[]{:S(2)}) collective-permute-start(bf16[16,3072]{1,0:T(8,128)(2,1)S(1)} %get-tuple-element.40), channel_id=1, source_target_pairs={{0,6},{2,4},{4,2},{6,0},{8,14},{10,12},{12,10},{14,8},{1,7},{3,5},... | collective-permute-start | bytes 294920 | tf_op jit(solution)/shard_map/ppermute | solution.py:17
  46.1 6.7 %collective-permute-start.11 = (bf16[16,3072]{1,0:T(8,128)(2,1)S(1)}, bf16[16,3072]{1,0:T(8,128)(2,1)S(1)}, u32[]{:S(2)}, u32[]{:S(2)}) collective-permute-start(bf16[16,3072]{1,0:T(8,128)(2,1)S(1)} %get-tuple-element.41), channel_id=1, source_target_pairs={{0,4},{2,6},{4,0},{6,2},{8,12},{10,14},{12,8},{14,10},{1,5},{3,7},... | collective-permute-start | bytes 294920 | tf_op jit(solution)/shard_map/ppermute | solution.py:17
  47.3 5.9 %collective-permute-start.12 = (bf16[16,3072]{1,0:T(8,128)(2,1)S(1)}, bf16[16,3072]{1,0:T(8,128)(2,1)S(1)}, u32[]{:S(2)}, u32[]{:S(2)}) collective-permute-start(bf16[16,3072]{1,0:T(8,128)(2,1)S(1)} %get-tuple-element.42), channel_id=1, source_target_pairs={{0,2},{2,0},{4,6},{6,4},{8,10},{10,8},{12,14},{14,12},{1,3},{3,1},... | collective-permute-start | bytes 294920 | tf_op jit(solution)/shard_map/ppermute | solution.py:17
  49.5 7.6 %collective-permute-start.16 = (bf16[16,3072]{1,0:T(8,128)(2,1)S(1)}, bf16[16,3072]{1,0:T(8,128)(2,1)S(1)}, u32[]{:S(2)}, u32[]{:S(2)}) collective-permute-start(bf16[16,3072]{1,0:T(8,128)(2,1)S(1)} %add_convert_fusion.1), channel_id=1, source_target_pairs={{0,8},{2,10},{4,12},{6,14},{8,0},{10,2},{12,4},{14,6},{1,9},{3,11}... | collective-permute-start | bytes 294920 | tf_op jit(solution)/shard_map/ppermute | solution.py:17

commit v6 on v5

--- a/solution.py
+++ b/solution.py
@@ -62,11 +62,13 @@
     return lax.dot_general(a, b, (((1,), (1,)), ((), ())), preferred_element_type=F32)
 
 
-def fetches(source_ref, experts, targets, sems, at=0):
-    return [
-        pltpu.make_async_copy(source_ref.at[e], target, sems.at[at + i])
-        for i, (e, target) in enumerate(zip(experts, targets))
-    ]
+def fetches(source_ref, units, targets, sems, at=0):
+    rows, copies = targets[0].shape[0] if targets else 0, []
+    for i, (unit, target) in enumerate(zip(units, targets)):
+        per_expert = source_ref.shape[1] // rows
+        source = source_ref.at[unit // per_expert, pl.ds(unit % per_expert * rows, rows)]
+        copies.append(pltpu.make_async_copy(source, target, sems.at[at + i]))
+    return copies
 
 
 def fetch_kernel(fetched, _, source_ref, *refs):
@@ -78,8 +80,9 @@
         copy.wait()
 
 
-def gate_kernel(fetched, *refs):
-    blocks, (router_ref, w_ref, up_ref, _, x_ref, part_ref, *held, sems) = refs[:8], refs[8:]
+def gate_kernel(fetched, carried, *refs):
+    blocks, (router_ref, w_ref, up_ref), refs = refs[:8], refs[8:11], refs[11 + carried :]
+    x_ref, part_ref, *held, sems = refs
     experts, hidden, width = w_ref.shape
     copies = fetches(up_ref, fetched, held, sems)
     for copy in copies:
@@ -95,9 +98,9 @@
         copy.wait()
 
 
-def up_kernel(up_fetched, down_fetched, x_ref, up_ref, down_ref, *refs):
-    weights, (part_ref, sent_ref, *held, sems) = refs[:2], refs[2:]
-    hidden, width = weights[0].shape
+def up_kernel(ready, carried, up_fetched, down_fetched, x_ref, up_ref, down_ref, *refs):
+    weights, (part_ref, sent_ref, *held, sems) = refs[:ready], refs[ready + carried :]
+    rows, width = weights[0].shape
     n = len(up_fetched)
     copies = fetches(up_ref, up_fetched, held[:n], sems) + fetches(
         down_ref, down_fetched, held[n:], sems, n
@@ -106,7 +109,7 @@
         copy.start()
     x = x_ref[:, :width]
     for i, w_ref in enumerate(weights):
-        own = slice(i * hidden, (i + 1) * hidden)
+        own = slice(i * rows, (i + 1) * rows)
         part = over_width(w_ref[...], x)
         part_ref[own] = part
         sent_ref[own] = part.astype(BF16)
@@ -136,8 +139,8 @@
     return (gate / (1.0 + jnp.exp(-gate)) * up).T.astype(BF16)
 
 
-def hidden_kernel(experts, fetched, gate_a, gate_b, up_a, up_b, down_ref, out_ref, *refs):
-    *held, sems = refs
+def hidden_kernel(experts, fetched, carried, gate_a, gate_b, up_a, up_b, down_ref, *refs):
+    out_ref, *held, sems = refs[carried:]
     copies = fetches(down_ref, fetched, held, sems)
     for copy in copies:
         copy.start()
@@ -151,11 +154,12 @@
 def down_kernel(ready, x_ref, gate_a, gate_b, up_a, up_b, h_ref, down_ref, *refs):
     weights, outs, (held_ref, sems) = refs[:ready], refs[ready : ready + 8], refs[ready + 8 :]
     experts, hidden, width = down_ref.shape
-    late = [held_ref.at[i] for i in range(experts - ready)]
-    copies = fetches(down_ref, range(ready, experts), late, sems)
-    for copy in copies:
-        copy.start()
-    half = h_ref.shape[0]
+    late, tile = held_ref.shape[:2]
+    weights = list(weights) + [held_ref.at[i] for i in range(late)]
+    copies = fetches(down_ref, range(ready, ready + late), weights[ready:], sems)
+    for copy in copies:
+        copy.start()
+    half, per_expert = h_ref.shape[0], hidden // tile
     factor = factors(x_ref, gate_a, gate_b, width, experts * hidden)
     total = None
     for e in range(experts):
@@ -163,12 +167,16 @@
             h = h_ref[e]
         else:
             h = hidden_units(e, e - half, hidden, gate_a, gate_b, up_a, up_b)
-        if e < ready:
-            w = weights[e][...]
-        else:
-            copies[e - ready].wait()
-            w = late[e - ready][...]
-        term = factor[:, e : e + 1] * jnp.dot(h, w, preferred_element_type=F32)
+        term = None
+        for i in range(per_expert):
+            unit = e * per_expert + i
+            if unit >= ready:
+                copies[unit - ready].wait()
+            dot = jnp.dot(
+                h[:, i * tile : (i + 1) * tile], weights[unit][...], preferred_element_type=F32
+            )
+            term = dot if term is None else term + dot
+        term = factor[:, e : e + 1] * term
         total = term if total is None else total + term
     rows = outs[0].shape[0]
     for j, out in enumerate(outs):
@@ -200,44 +208,47 @@
     flops = 2 * count * hidden * width
     size = 2 * hidden * width
     lines = jnp.pad(router.T, ((0, 128 - experts), (0, 0)))
-    one = pltpu.VMEM((hidden, width), BF16)
+    tile = hidden // 2
+    one = pltpu.VMEM((tile, width), BF16)
     sems = lambda n: [pltpu.SemaphoreType.DMA((n,))]
-    (up0,) = call(
-        functools.partial(fetch_kernel, (0,)),
-        [one],
+    up_early, up_next, up_last = (0, 1, 2), (3, 4, 5, 6), (7,)
+    down_first, down_second, down_third, late = (0, 1), (2, 3, 4), (5,), 2
+    early = call(
+        functools.partial(fetch_kernel, up_early),
+        [one] * len(up_early),
         [far[:, :128], w_up],
-        14_000_000_000,
+        8_000_000_000,
         0,
         1,
-        sems(1),
+        sems(len(up_early)),
         hbm=(1,),
     )
-    x, gate, up1, up2 = call(
-        functools.partial(gate_kernel, (1, 2)),
+    x, gate, *following = call(
+        functools.partial(gate_kernel, up_next, len(up_early)),
         [
             shape(count, width + IDS, dtype=BF16),
             shape(experts * hidden + count, count),
-            *[one] * 2,
+            *[one] * len(up_next),
         ],
-        [*blocks, lines, w_gate, w_up, up0],
+        [*blocks, lines, w_gate, w_up, *early],
         experts * flops,
         experts * size,
         3,
-        sems(2),
+        sems(len(up_next)),
         hbm=(10,),
     )
     gate_other = lax.ppermute(gate, "mp", SWAP)
 
-    def up_call(up_fetched, down_fetched, weights):
+    def up_call(up_fetched, down_fetched, weights, carried):
         n = len(up_fetched) + len(down_fetched)
         part, sent, *held = call(
-            functools.partial(up_kernel, up_fetched, down_fetched),
+            functools.partial(up_kernel, len(weights), len(carried), up_fetched, down_fetched),
             [
                 shape(half * hidden, count),
                 shape(half * hidden, count, dtype=BF16),
                 *[one] * n,
             ],
-            [x, w_up, w_down, *weights],
+            [x, w_up, w_down, *weights, *carried],
             half * flops,
             half * size,
             3,
@@ -246,26 +257,31 @@
         )
         return (part, lax.ppermute(sent, "mp", SWAP)), held
 
-    first, (up3,) = up_call((3,), (), (up0, up1))
-    second, (down0, down1) = up_call((), (0, 1), (up2, up3))
-    units, down2 = call(
-        functools.partial(hidden_kernel, range(half), (2,)),
-        [shape(half, count, hidden, dtype=BF16), one],
-        [gate, gate_other, *first, w_down],
+    units = [*early, *following]
+    first, held = up_call(up_last, down_first, units[:experts], units[experts:])
+    units += held[: len(up_last)]
+    downs = held[len(up_last) :]
+    second, held = up_call((), down_second, units[experts:], downs)
+    downs += held
+    h, *held = call(
+        functools.partial(hidden_kernel, range(half), down_third, len(downs)),
+        [shape(half, count, hidden, dtype=BF16)] + [one] * len(down_third),
+        [gate, gate_other, *first, w_down, *downs],
         0,
         12 * half * hidden * count,
         4,
-        sems(1),
+        sems(len(down_third)),
         hbm=(4,),
     )
+    downs += held
     parts = call(
-        functools.partial(down_kernel, 3),
+        functools.partial(down_kernel, len(downs)),
         [shape(rows, width)] + [shape(rows, width, dtype=BF16)] * 7,
-        [x, gate, gate_other, *second, units, w_down, down0, down1, down2],
+        [x, gate, gate_other, *second, h, w_down, *downs],
         experts * flops,
         experts * size,
-        10,
-        [pltpu.VMEM((1, hidden, width), BF16), *sems(1)],
+        16,
+        [pltpu.VMEM((late, tile, width), BF16), *sems(late)],
         hbm=(6,),
     )
     far_sums = [xor_send(parts[4 ^ k], k) for k in (3, 2, 1)]

time: 58.1 us -> 60.3 us (1.038)
  Pallas kernels: 25.7 us -> 29.6 us
  waiting for transfers between devices: 9.69 us -> 7.63 us
    pallas_call x7, Pallas kernels: 25.7 us -> 29.6 us  [call(): pl.pallas_call(kernel, out_shape=outs, in_specs=specs, out_specs=[VMEM_BL...]
    ppermute x14, waiting for transfers between devices: 9.69 us -> 7.62 us  [xor_send(): return lax.ppermute(block, 'batch', [(i, i ^ mask) for i in range(8)])]
  transfers between devices with their start and end apart: 17 -> 17, of which waited for: 9 -> 7; matrix products, arithmetic and copies ran while one was open for 0% -> 0% of each run, Pallas kernels for 24% -> 26%
where the time goes in v6:
time: 60.3 us; the launch traced here: 60.2 us
  Pallas kernels  29.6 us (49%)
  starting transfers between devices  21.9 us (36%)
  waiting for transfers between devices  7.63 us (13%)
  other arithmetic  0.76 us (1%)
    pallas_call x7, Pallas kernels, call(): pl.pallas_call(kernel, out_shape=outs, in_specs=specs, out_specs=[VMEM_BL...  29.6 us
    ppermute x14, starting transfers between devices, xor_send(): return lax.ppermute(block, 'batch', [(i, i ^ mask) for i in range(8)])  21.1 us
    ppermute x14, waiting for transfers between devices, xor_send(): return lax.ppermute(block, 'batch', [(i, i ^ mask) for i in range(8)])  7.62 us
  transfers between devices with their start and end apart: 17, of which 7 were waited for; matrix products, arithmetic and copies ran while one was open for 0% of the time, Pallas kernels for 26%

profile of v6, /device:TPU:0, one launch (start us, length us, event | category | flops | bytes accessed | tf_op | source)
XLA Modules:
  0.0 60.2 jit_solution(14542874166219907621)
XLA Ops:
  0.0 0.0 slice-start.4
  0.0 1.1 %shard_map.64.refs_0_ = bf16[16,3200]{1,0:T(8,128)(2,1)S(1)} custom-call(bf16[16,3072]{1,0:T(8,128)(2,1)} %tokens_ref.1, s32[2,16]{1,0:T(2,128)} %bitcast.5), custom_call_target="tpu_custom_call" | custom-call | flops 30000001024 | bytes 196608 | tf_op jit(solution)/shard_map/pallas_call | solution.py:26
  1.1 4.1 %collective-permute-start.3 = (bf16[16,3200]{1,0:T(8,128)(2,1)S(1)}, bf16[16,3200]{1,0:T(8,128)(2,1)S(1)}, u32[]{:S(2)}, u32[]{:S(2)}) collective-permute-start(bf16[16,3200]{1,0:T(8,128)(2,1)S(1)} %shard_map.64.refs_0_), channel_id=1, source_target_pairs={{0,8},{2,10},{4,12},{6,14},{8,0},{10,2},{12,4},{14,6},{1,9},{3,11}... | collective-permute-start | bytes 307208 | tf_op jit(solution)/shard_map/ppermute | solution.py:17
  5.2 2.5 %collective-permute-start.2 = (bf16[16,3200]{1,0:T(8,128)(2,1)S(1)}, bf16[16,3200]{1,0:T(8,128)(2,1)S(1)}, u32[]{:S(2)}, u32[]{:S(2)}) collective-permute-start(bf16[16,3200]{1,0:T(8,128)(2,1)S(1)} %shard_map.64.refs_0_), channel_id=1, source_target_pairs={{0,6},{2,4},{4,2},{6,0},{8,14},{10,12},{12,10},{14,8},{1,7},{3,5},... | collective-permute-start | bytes 307208 | tf_op jit(solution)/shard_map/ppermute | solution.py:17
  7.8 0.4 collective-permute-start.1
  8.2 0.5 collective-permute-start
  8.7 0.1 pad.4.refs_8_
  8.8 1.5 %collective-permute-done.3.refs_4_ = bf16[16,3200]{1,0:T(8,128)(2,1)S(1)} collective-permute-done((bf16[16,3200]{1,0:T(8,128)(2,1)S(1)}, bf16[16,3200]{1,0:T(8,128)(2,1)S(1)}, u32[]{:S(2)}, u32[]{:S(2)}) %collective-permute-start.3) | collective-permute-done | bytes 102432 | tf_op jit(solution)/shard_map/ppermute | solution.py:17
  10.3 1.7 %collective-permute-start.6 = (bf16[16,3200]{1,0:T(8,128)(2,1)S(1)}, bf16[16,3200]{1,0:T(8,128)(2,1)S(1)}, u32[]{:S(2)}, u32[]{:S(2)}) collective-permute-start(bf16[16,3200]{1,0:T(8,128)(2,1)S(1)} %collective-permute-done.3.refs_4_), channel_id=1, source_target_pairs={{0,6},{2,4},{4,2},{6,0},{8,14},{10,12},{12,10},{14,8},{1,7},{3,5},... | collective-permute-start | bytes 307208 | tf_op jit(solution)/shard_map/ppermute | solution.py:17
  12.0 1.4 %collective-permute-start.5 = (bf16[16,3200]{1,0:T(8,128)(2,1)S(1)}, bf16[16,3200]{1,0:T(8,128)(2,1)S(1)}, u32[]{:S(2)}, u32[]{:S(2)}) collective-permute-start(bf16[16,3200]{1,0:T(8,128)(2,1)S(1)} %collective-permute-done.3.refs_4_), channel_id=1, source_target_pairs={{0,4},{2,6},{4,0},{6,2},{8,12},{10,14},{12,8},{14,10},{1,5},{3,7},... | collective-permute-start | bytes 307208 | tf_op jit(solution)/shard_map/ppermute | solution.py:17
  13.4 0.0 collective-permute-done.2.refs_3_
  13.4 0.4 collective-permute-start.4
  13.8 3.8 %shard_map.65 = (bf16[512,3072]{1,0:T(8,128)(2,1)S(1)}, bf16[512,3072]{1,0:T(8,128)(2,1)S(1)}, bf16[512,3072]{1,0:T(8,128)(2,1)S(1)}) custom-call(bf16[16,128]{1,0:T(8,128)(2,1)S(1)} %slice.4._, bf16[4,1024,3072]{2,1,0:T(8,128)(2,1)} %up_ref.3), custom_call_target="tpu_custom_call" | custom-call | flops 8000000000 | tf_op jit(solution)/shard_map/pallas_call | solution.py:26
  17.6 0.0 collective-permute-done.1.refs_2_
  17.6 0.0 collective-permute-done.refs_1_
  17.6 0.0 collective-permute-done.6.refs_7_
  17.6 0.5 collective-permute-done.5.refs_6_
  18.1 0.0 collective-permute-done.4.refs_5_
  18.1 0.0 slice-done
  18.1 0.0 slice-done.2
  18.2 6.9 %shard_map.66 = (bf16[128,3200]{1,0:T(8,128)(2,1)S(1)}, f32[4224,128]{1,0:T(8,128)S(1)}, bf16[512,3072]{1,0:T(8,128)(2,1)S(1)}, bf16[512,3072]{1,0:T(8,128)(2,1)...) custom-call(bf16[16,3200]{1,0:T(8,128)(2,1)S(1)} %shard_map.64.refs_0_, ...), custom_call_target="tpu_custom_call" | custom-call | flops 3221225472 | bytes 25165824 | tf_op jit(solution)/shard_map/pallas_call | solution.py:26
  25.1 0.1 collective-permute-start.7
  25.2 4.2 %shard_map.67 = (f32[2048,128]{1,0:T(8,128)S(1)}, bf16[2048,128]{1,0:T(8,128)(2,1)S(1)}, bf16[512,3072]{1,0:T(8,128)(2,1)S(1)}, bf16[512,3072]{1,0:T(8,128)(2,1)S(1)}, bf16[512,3072]{1,0:T(8,128)(2,1)S(1)}) custom-call(bf16[128,3200]{1,0:T(8,128)(2,1)S(1)} %get-tuple-element.37.x_ref, bf16[4,1024,3072]{2,1,0:T(8,128)(2,1)} %up_ref.3, ...), custom_call_target="tpu_custom_call" | custom-call | flops 1610612736 | bytes 12582912 | tf_op jit(solution)/shard_map/pallas_call | solution.py:26
  29.4 0.3 collective-permute-start.9
  29.8 5.6 %shard_map.68 = (f32[2048,128]{1,0:T(8,128)S(1)}, bf16[2048,128]{1,0:T(8,128)(2,1)S(1)}, bf16[512,3072]{1,0:T(8,128)(2,1)S(1)}, bf16[512,3072]{1,0:T(8,128)(2,1)S(1)}, bf16[512,3072]{1,0:T(8,128)(2,1)S(1)}) custom-call(bf16[128,3200]{1,0:T(8,128)(2,1)S(1)} %get-tuple-element.37.x_ref, bf16[4,1024,3072]{2,1,0:T(8,128)(2,1)} %up_ref.3, ...), custom_call_target="tpu_custom_call" | custom-call | flops 1610612736 | bytes 12582912 | tf_op jit(solution)/shard_map/pallas_call | solution.py:26
  35.4 0.3 collective-permute-start.8
  35.7 0.0 collective-permute-done.9.up_b
  35.7 0.0 collective-permute-done.7.gate_b
  35.7 2.0 %shard_map.69 = (bf16[2,128,1024]{2,1,0:T(8,128)(2,1)S(1)}, bf16[512,3072]{1,0:T(8,128)(2,1)S(1)}) custom-call(f32[4224,128]{1,0:T(8,128)S(1)} %get-tuple-element.38.gate_a, f32[4224,128]{1,0:T(8,128)S(1)} %collective-permute-done.7.gate_b, f32[2048,128]{1,0:T(8,128)S(1)} %get-tuple-element.48.up_a, bf16[2048,128]{1,0:T(8,128)(2,1)S(1)} %collective-permute-done.9.up_b, ...), custom_call_target="tpu_custom_call" | custom-call | bytes 3145728 | tf_op jit(solution)/shard_map/pallas_call | solution.py:26
  37.7 0.0 collective-permute-done.8.up_b
  37.7 0.1 copy-done.1
  37.8 5.9 %shard_map.70 = (f32[16,3072]{1,0:T(8,128)S(1)}, bf16[16,3072]{1,0:T(8,128)(2,1)S(1)}, bf16[16,3072]{1,0:T(8,128)(2,1)S(1)}, bf16[16,3072]{1,0:T(8,128)(2,1)S(1)...) custom-call(bf16[128,3200]{1,0:T(8,128)(2,1)S(1)} %copy-done.1, ...), custom_call_target="tpu_custom_call" | custom-call | flops 3221225472 | bytes 25165824 | tf_op jit(solution)/shard_map/pallas_call | solution.py:26
  43.8 1.8 %collective-permute-start.13 = (bf16[16,3072]{1,0:T(8,128)(2,1)S(1)}, bf16[16,3072]{1,0:T(8,128)(2,1)S(1)}, u32[]{:S(2)}, u32[]{:S(2)}) collective-permute-start(bf16[16,3072]{1,0:T(8,128)(2,1)S(1)} %get-tuple-element.60), channel_id=1, source_target_pairs={{0,6},{2,4},{4,2},{6,0},{8,14},{10,12},{12,10},{14,8},{1,7},{3,5},... | collective-permute-start | bytes 294920 | tf_op jit(solution)/shard_map/ppermute | solution.py:17
  45.6 0.9 %collective-permute-start.14 = (bf16[16,3072]{1,0:T(8,128)(2,1)S(1)}, bf16[16,3072]{1,0:T(8,128)(2,1)S(1)}, u32[]{:S(2)}, u32[]{:S(2)}) collective-permute-start(bf16[16,3072]{1,0:T(8,128)(2,1)S(1)} %get-tuple-element.61), channel_id=1, source_target_pairs={{0,4},{2,6},{4,0},{6,2},{8,12},{10,14},{12,8},{14,10},{1,5},{3,7},... | collective-permute-start | bytes 294920 | tf_op jit(solution)/shard_map/ppermute | solution.py:17
  46.5 0.8 %collective-permute-start.15 = (bf16[16,3072]{1,0:T(8,128)(2,1)S(1)}, bf16[16,3072]{1,0:T(8,128)(2,1)S(1)}, u32[]{:S(2)}, u32[]{:S(2)}) collective-permute-start(bf16[16,3072]{1,0:T(8,128)(2,1)S(1)} %get-tuple-element.62), channel_id=1, source_target_pairs={{0,2},{2,0},{4,6},{6,4},{8,10},{10,8},{12,14},{14,12},{1,3},{3,1},... | collective-permute-start | bytes 294920 | tf_op jit(solution)/shard_map/ppermute | solution.py:17
  47.3 1.8 %collective-permute-start.10 = (bf16[16,3072]{1,0:T(8,128)(2,1)S(1)}, bf16[16,3072]{1,0:T(8,128)(2,1)S(1)}, u32[]{:S(2)}, u32[]{:S(2)}) collective-permute-start(bf16[16,3072]{1,0:T(8,128)(2,1)S(1)} %get-tuple-element.56), channel_id=1, source_target_pairs={{0,6},{2,4},{4,2},{6,0},{8,14},{10,12},{12,10},{14,8},{1,7},{3,5},... | collective-permute-start | bytes 294920 | tf_op jit(solution)/shard_map/ppermute | solution.py:17
  49.1 0.9 %collective-permute-start.11 = (bf16[16,3072]{1,0:T(8,128)(2,1)S(1)}, bf16[16,3072]{1,0:T(8,128)(2,1)S(1)}, u32[]{:S(2)}, u32[]{:S(2)}) collective-permute-start(bf16[16,3072]{1,0:T(8,128)(2,1)S(1)} %get-tuple-element.57), channel_id=1, source_target_pairs={{0,4},{2,6},{4,0},{6,2},{8,12},{10,14},{12,8},{14,10},{1,5},{3,7},... | collective-permute-start | bytes 294920 | tf_op jit(solution)/shard_map/ppermute | solution.py:17
  50.0 0.3 collective-permute-done.13
  50.3 1.2 %collective-permute-start.12 = (bf16[16,3072]{1,0:T(8,128)(2,1)S(1)}, bf16[16,3072]{1,0:T(8,128)(2,1)S(1)}, u32[]{:S(2)}, u32[]{:S(2)}) collective-permute-start(bf16[16,3072]{1,0:T(8,128)(2,1)S(1)} %get-tuple-element.58), channel_id=1, source_target_pairs={{0,2},{2,0},{4,6},{6,4},{8,10},{10,8},{12,14},{14,12},{1,3},{3,1},... | collective-permute-start | bytes 294920 | tf_op jit(solution)/shard_map/ppermute | solution.py:17
  51.6 0.6 %collective-permute-done.14 = bf16[16,3072]{1,0:T(8,128)(2,1)S(1)} collective-permute-done((bf16[16,3072]{1,0:T(8,128)(2,1)S(1)}, bf16[16,3072]{1,0:T(8,128)(2,1)S(1)}, u32[]{:S(2)}, u32[]{:S(2)}) %collective-permute-start.14) | collective-permute-done | bytes 98336 | tf_op jit(solution)/shard_map/ppermute | solution.py:17
  52.2 1.6 %collective-permute-done.15 = bf16[16,3072]{1,0:T(8,128)(2,1)S(1)} collective-permute-done((bf16[16,3072]{1,0:T(8,128)(2,1)S(1)}, bf16[16,3072]{1,0:T(8,128)(2,1)S(1)}, u32[]{:S(2)}, u32[]{:S(2)}) %collective-permute-start.15) | collective-permute-done | bytes 98336 | tf_op jit(solution)/shard_map/ppermute | solution.py:17
  53.8 0.1 add_convert_fusion.1
  53.9 2.6 %collective-permute-start.16 = (bf16[16,3072]{1,0:T(8,128)(2,1)S(1)}, bf16[16,3072]{1,0:T(8,128)(2,1)S(1)}, u32[]{:S(2)}, u32[]{:S(2)}) collective-permute-start(bf16[16,3072]{1,0:T(8,128)(2,1)S(1)} %add_convert_fusion.1), channel_id=1, source_target_pairs={{0,8},{2,10},{4,12},{6,14},{8,0},{10,2},{12,4},{14,6},{1,9},{3,11}... | collective-permute-start | bytes 294920 | tf_op jit(solution)/shard_map/ppermute | solution.py:17
  56.5 0.0 collective-permute-done.10
  56.5 0.3 collective-permute-done.11
  56.8 0.0 collective-permute-done.12
  56.8 2.7 %collective-permute-done.16 = bf16[16,3072]{1,0:T(8,128)(2,1)S(1)} collective-permute-done((bf16[16,3072]{1,0:T(8,128)(2,1)S(1)}, bf16[16,3072]{1,0:T(8,128)(2,1)S(1)}, u32[]{:S(2)}, u32[]{:S(2)}) %collective-permute-start.16) | collective-permute-done | bytes 98336 | tf_op jit(solution)/shard_map/ppermute | solution.py:17
  59.5 0.7 %add_convert_fusion = bf16[16,3072]{1,0:T(8,128)(2,1)} fusion(bf16[16,3072]{1,0:T(8,128)(2,1)S(1)} %collective-permute-done.16, bf16[16,3072]{1,0:T(8,128)(2,1)S(1)} %collective-permute-done.12, bf16[16,3072]{1,0:T(8,128)(2,1)S(1)} %collective-permute-done.11, f32[16,3072]{1,0:T(8,128)S(1)} %get-tuple-element.55, bf16[16,3072]{1,0:T(8,128)(2,1)S(1)} %collective-permute-done.10), kind=kLoop, calls=%fused_computation | loop fusion | flops 442368 | bytes 688128 | tf_op jit(solution)/shard_map/convert_element_type | solution.py:291
  (16 shorter events, 0.0 us)
Async XLA Ops:
  0.0 8.7 %copy-start.2 = (bf16[3072,4]{0,1:T(4,128)(2,1)S(1)}, bf16[3072,4]{0,1:T(4,128)(2,1)}, u32[]{:S(2)}) copy-start(bf16[3072,4]{0,1:T(4,128)(2,1)} %param.8) | copy-start | bytes 73732
  0.0 18.1 %slice-start = ((s8[25165824]{0:T(1024)(128)(4,1)}), s8[4194304]{0:T(1024)(128)(4,1)S(1)}, s32[]{:S(2)}) async-start(s8[25165824]{0:T(1024)(128)(4,1)} %bitcast.2), calls=%async_computation | async-start | bytes 8388608
  0.0 18.1 %slice-start.1 = ((s8[25165824]{0:T(1024)(128)(4,1)}), s8[4194304]{0:T(1024)(128)(4,1)S(1)}, s32[]{:S(2)}) async-start(s8[25165824]{0:T(1024)(128)(4,1)} %bitcast.2), calls=%async_computation.1 | async-start | bytes 8388608
  0.0 18.1 %slice-start.2 = ((s8[25165824]{0:T(1024)(128)(4,1)}), s8[4194304]{0:T(1024)(128)(4,1)S(1)}, s32[]{:S(2)}) async-start(s8[25165824]{0:T(1024)(128)(4,1)} %bitcast.2), calls=%async_computation.2 | async-start | bytes 8388608
  0.0 18.1 %slice-start.3 = ((s8[25165824]{0:T(1024)(128)(4,1)}), s8[4194304]{0:T(1024)(128)(4,1)S(1)}, s32[]{:S(2)}) async-start(s8[25165824]{0:T(1024)(128)(4,1)} %bitcast.2), calls=%async_computation.3 | async-start | bytes 8388608
  0.0 18.1 %slice-start.4 = ((s8[25165824]{0:T(1024)(128)(4,1)}), s8[4194304]{0:T(1024)(128)(4,1)S(1)}, s32[]{:S(2)}) async-start(s8[25165824]{0:T(1024)(128)(4,1)} %bitcast.2), calls=%async_computation.4 | async-start | bytes 8388608
  1.1 9.2 %collective-permute-start.3 = (bf16[16,3200]{1,0:T(8,128)(2,1)S(1)}, bf16[16,3200]{1,0:T(8,128)(2,1)S(1)}, u32[]{:S(2)}, u32[]{:S(2)}) collective-permute-start(bf16[16,3200]{1,0:T(8,128)(2,1)S(1)} %shard_map.64.refs_0_), channel_id=1, source_target_pairs={{0,8},{2,10},{4,12},{6,14},{8,0},{10,2},{12,4},{14,6},{1,9},{3,11}... | collective-permute-start | bytes 307208 | tf_op jit(solution)/shard_map/ppermute | solution.py:17
  5.2 8.2 %collective-permute-start.2 = (bf16[16,3200]{1,0:T(8,128)(2,1)S(1)}, bf16[16,3200]{1,0:T(8,128)(2,1)S(1)}, u32[]{:S(2)}, u32[]{:S(2)}) collective-permute-start(bf16[16,3200]{1,0:T(8,128)(2,1)S(1)} %shard_map.64.refs_0_), channel_id=1, source_target_pairs={{0,6},{2,4},{4,2},{6,0},{8,14},{10,12},{12,10},{14,8},{1,7},{3,5},... | collective-permute-start | bytes 307208 | tf_op jit(solution)/shard_map/ppermute | solution.py:17
  7.8 9.8 %collective-permute-start.1 = (bf16[16,3200]{1,0:T(8,128)(2,1)S(1)}, bf16[16,3200]{1,0:T(8,128)(2,1)S(1)}, u32[]{:S(2)}, u32[]{:S(2)}) collective-permute-start(bf16[16,3200]{1,0:T(8,128)(2,1)S(1)} %shard_map.64.refs_0_), channel_id=1, source_target_pairs={{0,4},{2,6},{4,0},{6,2},{8,12},{10,14},{12,8},{14,10},{1,5},{3,7},... | collective-permute-start | bytes 307208 | tf_op jit(solution)/shard_map/ppermute | solution.py:17
  8.2 9.4 %collective-permute-start = (bf16[16,3200]{1,0:T(8,128)(2,1)S(1)}, bf16[16,3200]{1,0:T(8,128)(2,1)S(1)}, u32[]{:S(2)}, u32[]{:S(2)}) collective-permute-start(bf16[16,3200]{1,0:T(8,128)(2,1)S(1)} %shard_map.64.refs_0_), channel_id=1, source_target_pairs={{0,2},{2,0},{4,6},{6,4},{8,10},{10,8},{12,14},{14,12},{1,3},{3,1},... | collective-permute-start | bytes 307208 | tf_op jit(solution)/shard_map/ppermute | solution.py:17
  10.3 7.8 %slice-start.5 = ((s8[25165824]{0:T(1024)(128)(4,1)}), s8[4194304]{0:T(1024)(128)(4,1)S(1)}, s32[]{:S(2)}) async-start(s8[25165824]{0:T(1024)(128)(4,1)} %bitcast.2), calls=%async_computation.5 | async-start | bytes 8388608
  10.3 7.3 %collective-permute-start.6 = (bf16[16,3200]{1,0:T(8,128)(2,1)S(1)}, bf16[16,3200]{1,0:T(8,128)(2,1)S(1)}, u32[]{:S(2)}, u32[]{:S(2)}) collective-permute-start(bf16[16,3200]{1,0:T(8,128)(2,1)S(1)} %collective-permute-done.3.refs_4_), channel_id=1, source_target_pairs={{0,6},{2,4},{4,2},{6,0},{8,14},{10,12},{12,10},{14,8},{1,7},{3,5},... | collective-permute-start | bytes 307208 | tf_op jit(solution)/shard_map/ppermute | solution.py:17
  12.0 6.1 %collective-permute-start.5 = (bf16[16,3200]{1,0:T(8,128)(2,1)S(1)}, bf16[16,3200]{1,0:T(8,128)(2,1)S(1)}, u32[]{:S(2)}, u32[]{:S(2)}) collective-permute-start(bf16[16,3200]{1,0:T(8,128)(2,1)S(1)} %collective-permute-done.3.refs_4_), channel_id=1, source_target_pairs={{0,4},{2,6},{4,0},{6,2},{8,12},{10,14},{12,8},{14,10},{1,5},{3,7},... | collective-permute-start | bytes 307208 | tf_op jit(solution)/shard_map/ppermute | solution.py:17
  13.4 4.7 %collective-permute-start.4 = (bf16[16,3200]{1,0:T(8,128)(2,1)S(1)}, bf16[16,3200]{1,0:T(8,128)(2,1)S(1)}, u32[]{:S(2)}, u32[]{:S(2)}) collective-permute-start(bf16[16,3200]{1,0:T(8,128)(2,1)S(1)} %collective-permute-done.3.refs_4_), channel_id=1, source_target_pairs={{0,2},{2,0},{4,6},{6,4},{8,10},{10,8},{12,14},{14,12},{1,3},{3,1},... | collective-permute-start | bytes 307208 | tf_op jit(solution)/shard_map/ppermute | solution.py:17
  25.1 4.7 %copy-start = (bf16[128,3200]{1,0:T(8,128)(2,1)}, bf16[128,3200]{1,0:T(8,128)(2,1)S(1)}, u32[]{:S(2)}) copy-start(bf16[128,3200]{1,0:T(8,128)(2,1)S(1)} %get-tuple-element.37.x_ref) | copy-start | bytes 2457604
  25.1 10.6 %collective-permute-start.7 = (f32[4224,128]{1,0:T(8,128)S(1)}, f32[4224,128]{1,0:T(8,128)S(1)}, u32[]{:S(2)}, u32[]{:S(2)}) collective-permute-start(f32[4224,128]{1,0:T(8,128)S(1)} %get-tuple-element.38.gate_a), channel_id=1, source_target_pairs={{0,1},{1,0},{2,3},{3,2},{4,5},{5,4},{6,7},{7,6},{8,9},{9,8},{10,11... | collective-permute-start | bytes 6488072 | tf_op jit(solution)/shard_map/ppermute | solution.py:240
  29.4 6.3 %collective-permute-start.9 = (bf16[2048,128]{1,0:T(8,128)(2,1)S(1)}, bf16[2048,128]{1,0:T(8,128)(2,1)S(1)}, u32[]{:S(2)}, u32[]{:S(2)}) collective-permute-start(bf16[2048,128]{1,0:T(8,128)(2,1)S(1)} %get-tuple-element.49), channel_id=1, source_target_pairs={{0,1},{1,0},{2,3},{3,2},{4,5},{5,4},{6,7},{7,6},{8,9},{9,8},{10,11... | collective-permute-start | bytes 1572872 | tf_op jit(solution)/shard_map/ppermute | solution.py:258
  35.4 2.3 %collective-permute-start.8 = (bf16[2048,128]{1,0:T(8,128)(2,1)S(1)}, bf16[2048,128]{1,0:T(8,128)(2,1)S(1)}, u32[]{:S(2)}, u32[]{:S(2)}) collective-permute-start(bf16[2048,128]{1,0:T(8,128)(2,1)S(1)} %get-tuple-element.47), channel_id=1, source_target_pairs={{0,1},{1,0},{2,3},{3,2},{4,5},{5,4},{6,7},{7,6},{8,9},{9,8},{10,11... | collective-permute-start | bytes 1572872 | tf_op jit(solution)/shard_map/ppermute | solution.py:258
  35.7 2.1 %copy-start.1 = (bf16[128,3200]{1,0:T(8,128)(2,1)S(1)}, bf16[128,3200]{1,0:T(8,128)(2,1)}, u32[]{:S(2)}) copy-start(bf16[128,3200]{1,0:T(8,128)(2,1)} %copy-done) | copy-start | bytes 2457604
  43.8 6.6 %collective-permute-start.13 = (bf16[16,3072]{1,0:T(8,128)(2,1)S(1)}, bf16[16,3072]{1,0:T(8,128)(2,1)S(1)}, u32[]{:S(2)}, u32[]{:S(2)}) collective-permute-start(bf16[16,3072]{1,0:T(8,128)(2,1)S(1)} %get-tuple-element.60), channel_id=1, source_target_pairs={{0,6},{2,4},{4,2},{6,0},{8,14},{10,12},{12,10},{14,8},{1,7},{3,5},... | collective-permute-start | bytes 294920 | tf_op jit(solution)/shard_map/ppermute | solution.py:17
  45.6 6.6 %collective-permute-start.14 = (bf16[16,3072]{1,0:T(8,128)(2,1)S(1)}, bf16[16,3072]{1,0:T(8,128)(2,1)S(1)}, u32[]{:S(2)}, u32[]{:S(2)}) collective-permute-start(bf16[16,3072]{1,0:T(8,128)(2,1)S(1)} %get-tuple-element.61), channel_id=1, source_target_pairs={{0,4},{2,6},{4,0},{6,2},{8,12},{10,14},{12,8},{14,10},{1,5},{3,7},... | collective-permute-start | bytes 294920 | tf_op jit(solution)/shard_map/ppermute | solution.py:17
  46.5 7.3 %collective-permute-start.15 = (bf16[16,3072]{1,0:T(8,128)(2,1)S(1)}, bf16[16,3072]{1,0:T(8,128)(2,1)S(1)}, u32[]{:S(2)}, u32[]{:S(2)}) collective-permute-start(bf16[16,3072]{1,0:T(8,128)(2,1)S(1)} %get-tuple-element.62), channel_id=1, source_target_pairs={{0,2},{2,0},{4,6},{6,4},{8,10},{10,8},{12,14},{14,12},{1,3},{3,1},... | collective-permute-start | bytes 294920 | tf_op jit(solution)/shard_map/ppermute | solution.py:17
  47.3 9.2 %collective-permute-start.10 = (bf16[16,3072]{1,0:T(8,128)(2,1)S(1)}, bf16[16,3072]{1,0:T(8,128)(2,1)S(1)}, u32[]{:S(2)}, u32[]{:S(2)}) collective-permute-start(bf16[16,3072]{1,0:T(8,128)(2,1)S(1)} %get-tuple-element.56), channel_id=1, source_target_pairs={{0,6},{2,4},{4,2},{6,0},{8,14},{10,12},{12,10},{14,8},{1,7},{3,5},... | collective-permute-start | bytes 294920 | tf_op jit(solution)/shard_map/ppermute | solution.py:17
  49.1 7.7 %collective-permute-start.11 = (bf16[16,3072]{1,0:T(8,128)(2,1)S(1)}, bf16[16,3072]{1,0:T(8,128)(2,1)S(1)}, u32[]{:S(2)}, u32[]{:S(2)}) collective-permute-start(bf16[16,3072]{1,0:T(8,128)(2,1)S(1)} %get-tuple-element.57), channel_id=1, source_target_pairs={{0,4},{2,6},{4,0},{6,2},{8,12},{10,14},{12,8},{14,10},{1,5},{3,7},... | collective-permute-start | bytes 294920 | tf_op jit(solution)/shard_map/ppermute | solution.py:17
  50.3 6.5 %collective-permute-start.12 = (bf16[16,3072]{1,0:T(8,128)(2,1)S(1)}, bf16[16,3072]{1,0:T(8,128)(2,1)S(1)}, u32[]{:S(2)}, u32[]{:S(2)}) collective-permute-start(bf16[16,3072]{1,0:T(8,128)(2,1)S(1)} %get-tuple-element.58), channel_id=1, source_target_pairs={{0,2},{2,0},{4,6},{6,4},{8,10},{10,8},{12,14},{14,12},{1,3},{3,1},... | collective-permute-start | bytes 294920 | tf_op jit(solution)/shard_map/ppermute | solution.py:17
  53.9 5.6 %collective-permute-start.16 = (bf16[16,3072]{1,0:T(8,128)(2,1)S(1)}, bf16[16,3072]{1,0:T(8,128)(2,1)S(1)}, u32[]{:S(2)}, u32[]{:S(2)}) collective-permute-start(bf16[16,3072]{1,0:T(8,128)(2,1)S(1)} %add_convert_fusion.1), channel_id=1, source_target_pairs={{0,8},{2,10},{4,12},{6,14},{8,0},{10,2},{12,4},{14,6},{1,9},{3,11}... | collective-permute-start | bytes 294920 | tf_op jit(solution)/shard_map/ppermute | solution.py:17

commit v7 on v5

--- a/solution.py
+++ b/solution.py
@@ -62,11 +62,17 @@
     return lax.dot_general(a, b, (((1,), (1,)), ((), ())), preferred_element_type=F32)
 
 
-def fetches(source_ref, experts, targets, sems, at=0):
-    return [
-        pltpu.make_async_copy(source_ref.at[e], target, sems.at[at + i])
-        for i, (e, target) in enumerate(zip(experts, targets))
-    ]
+def fetches(source_ref, wanted, targets, sems, at=0):
+    copies = []
+    for i, (place, target) in enumerate(zip(wanted, targets)):
+        rows = target.shape[0]
+        e, first = place if isinstance(place, tuple) else (place, 0)
+        copies.append(
+            pltpu.make_async_copy(
+                source_ref.at[e, pl.ds(first, rows)], target, sems.at[at + i]
+            )
+        )
+    return copies
 
 
 def fetch_kernel(fetched, _, source_ref, *refs):
@@ -78,8 +84,9 @@
         copy.wait()
 
 
-def gate_kernel(fetched, *refs):
-    blocks, (router_ref, w_ref, up_ref, _, x_ref, part_ref, *held, sems) = refs[:8], refs[8:]
+def gate_kernel(fetched, carried, *refs):
+    blocks, (router_ref, w_ref, up_ref), refs = refs[:8], refs[8:11], refs[11 + carried :]
+    x_ref, part_ref, *held, sems = refs
     experts, hidden, width = w_ref.shape
     copies = fetches(up_ref, fetched, held, sems)
     for copy in copies:
@@ -95,21 +102,22 @@
         copy.wait()
 
 
-def up_kernel(up_fetched, down_fetched, x_ref, up_ref, down_ref, *refs):
-    weights, (part_ref, sent_ref, *held, sems) = refs[:2], refs[2:]
-    hidden, width = weights[0].shape
+def up_kernel(ready, carried, up_fetched, down_fetched, x_ref, up_ref, down_ref, *refs):
+    weights, (part_ref, sent_ref, *held, sems) = refs[:ready], refs[ready + carried :]
+    width = weights[0].shape[1]
     n = len(up_fetched)
     copies = fetches(up_ref, up_fetched, held[:n], sems) + fetches(
         down_ref, down_fetched, held[n:], sems, n
     )
     for copy in copies:
         copy.start()
-    x = x_ref[:, :width]
-    for i, w_ref in enumerate(weights):
-        own = slice(i * hidden, (i + 1) * hidden)
+    x, at = x_ref[:, :width], 0
+    for w_ref in weights:
+        own = slice(at, at + w_ref.shape[0])
         part = over_width(w_ref[...], x)
         part_ref[own] = part
         sent_ref[own] = part.astype(BF16)
+        at += w_ref.shape[0]
     for copy in copies:
         copy.wait()
 
@@ -136,8 +144,8 @@
     return (gate / (1.0 + jnp.exp(-gate)) * up).T.astype(BF16)
 
 
-def hidden_kernel(experts, fetched, gate_a, gate_b, up_a, up_b, down_ref, out_ref, *refs):
-    *held, sems = refs
+def hidden_kernel(experts, fetched, gate_a, gate_b, up_a, up_b, down_ref, *refs):
+    out_ref, *held, sems = refs[2:]
     copies = fetches(down_ref, fetched, held, sems)
     for copy in copies:
         copy.start()
@@ -192,19 +200,20 @@
         hbm=(0, 1),
     )
     far = xor_send(own, 4)
-    near = [xor_send(own, k) for k in (1, 2, 3)]
-    forwarded = [xor_send(far, k) for k in (1, 2, 3)]
-    blocks = [own, *near, far, *forwarded]
+    near = [xor_send(own, k) for k in (3, 2, 1)]
+    forwarded = [xor_send(far, k) for k in (3, 2, 1)]
+    blocks = [own, *near[::-1], far, *forwarded[::-1]]
 
     w_gate, w_up, w_down = in_vmem(w_gate), in_hbm(w_up), in_hbm(w_down)
     flops = 2 * count * hidden * width
     size = 2 * hidden * width
     lines = jnp.pad(router.T, ((0, 128 - experts), (0, 0)))
     one = pltpu.VMEM((hidden, width), BF16)
+    part_of_one = pltpu.VMEM((hidden // 2, width), BF16)
     sems = lambda n: [pltpu.SemaphoreType.DMA((n,))]
     (up0,) = call(
         functools.partial(fetch_kernel, (0,)),
-        [one],
+        [one] * 1,
         [far[:, :128], w_up],
         14_000_000_000,
         0,
@@ -212,46 +221,49 @@
         sems(1),
         hbm=(1,),
     )
-    x, gate, up1, up2 = call(
-        functools.partial(gate_kernel, (1, 2)),
+    x, gate, up1, up2, up3a = call(
+        functools.partial(gate_kernel, (1, 2, (3, 0)), 1),
         [
             shape(count, width + IDS, dtype=BF16),
             shape(experts * hidden + count, count),
             *[one] * 2,
+            part_of_one,
         ],
         [*blocks, lines, w_gate, w_up, up0],
         experts * flops,
         experts * size,
         3,
-        sems(2),
+        sems(3),
         hbm=(10,),
     )
     gate_other = lax.ppermute(gate, "mp", SWAP)
 
-    def up_call(up_fetched, down_fetched, weights):
-        n = len(up_fetched) + len(down_fetched)
+    def up_call(up_fetched, down_fetched, weights, held, carried):
+        n = len(held)
         part, sent, *held = call(
-            functools.partial(up_kernel, up_fetched, down_fetched),
+            functools.partial(up_kernel, len(weights), len(carried), up_fetched, down_fetched),
             [
                 shape(half * hidden, count),
                 shape(half * hidden, count, dtype=BF16),
-                *[one] * n,
+                *held,
             ],
-            [x, w_up, w_down, *weights],
+            [x, w_up, w_down, *weights, *carried],
             half * flops,
             half * size,
             3,
-            sems(n),
+            sems(max(n, 1)),
             hbm=(1, 2),
         )
         return (part, lax.ppermute(sent, "mp", SWAP)), held
 
-    first, (up3,) = up_call((3,), (), (up0, up1))
-    second, (down0, down1) = up_call((), (0, 1), (up2, up3))
+    first, (up3b, down0) = up_call(
+        ((3, hidden // 2),), (0,), (up0, up1), (part_of_one, one), (up3a,)
+    )
+    second, (down1,) = up_call((), (1,), (up2, up3a, up3b), (one,), ())
     units, down2 = call(
         functools.partial(hidden_kernel, range(half), (2,)),
-        [shape(half, count, hidden, dtype=BF16), one],
-        [gate, gate_other, *first, w_down],
+        [shape(half, count, hidden, dtype=BF16)] + [one] * 1,
+        [gate, gate_other, *first, w_down, down0, down1],
         0,
         12 * half * hidden * count,
         4,

time: 58.1 us -> 61.5 us (1.059)
  Pallas kernels: 25.7 us -> 28.4 us
    pallas_call x7, Pallas kernels: 25.7 us -> 28.4 us  [call(): pl.pallas_call(kernel, out_shape=outs, in_specs=specs, out_specs=[VMEM_BL...]
  transfers between devices with their start and end apart: 17 -> 17, of which waited for: 9 -> 9; matrix products, arithmetic and copies ran while one was open for 0% -> 0% of each run, Pallas kernels for 24% -> 21%
where the time goes in v7:
time: 61.5 us; the launch traced here: 61.3 us
  Pallas kernels  28.4 us (46%)
  starting transfers between devices  21.9 us (36%)
  waiting for transfers between devices  9.99 us (16%)
  other arithmetic  0.76 us (1%)
    pallas_call x7, Pallas kernels, call(): pl.pallas_call(kernel, out_shape=outs, in_specs=specs, out_specs=[VMEM_BL...  28.4 us
    ppermute x14, starting transfers between devices, xor_send(): return lax.ppermute(block, 'batch', [(i, i ^ mask) for i in range(8)])  21.2 us
    ppermute x14, waiting for transfers between devices, xor_send(): return lax.ppermute(block, 'batch', [(i, i ^ mask) for i in range(8)])  9.99 us
  transfers between devices with their start and end apart: 17, of which 9 were waited for; matrix products, arithmetic and copies ran while one was open for 0% of the time, Pallas kernels for 21%

profile of v7, /device:TPU:0, one launch (start us, length us, event | category | flops | bytes accessed | tf_op | source)
XLA Modules:
  0.0 61.3 jit_solution(18380520755030924291)
XLA Ops:
  0.0 0.0 slice-start.4
  0.0 1.1 %shard_map.64.refs_0_ = bf16[16,3200]{1,0:T(8,128)(2,1)S(1)} custom-call(bf16[16,3072]{1,0:T(8,128)(2,1)} %tokens_ref.1, s32[2,16]{1,0:T(2,128)} %bitcast.5), custom_call_target="tpu_custom_call" | custom-call | flops 30000001024 | bytes 196608 | tf_op jit(solution)/shard_map/pallas_call | solution.py:26
  1.1 4.1 %collective-permute-start.3 = (bf16[16,3200]{1,0:T(8,128)(2,1)S(1)}, bf16[16,3200]{1,0:T(8,128)(2,1)S(1)}, u32[]{:S(2)}, u32[]{:S(2)}) collective-permute-start(bf16[16,3200]{1,0:T(8,128)(2,1)S(1)} %shard_map.64.refs_0_), channel_id=1, source_target_pairs={{0,8},{2,10},{4,12},{6,14},{8,0},{10,2},{12,4},{14,6},{1,9},{3,11}... | collective-permute-start | bytes 307208 | tf_op jit(solution)/shard_map/ppermute | solution.py:17
  5.2 1.5 %collective-permute-start = (bf16[16,3200]{1,0:T(8,128)(2,1)S(1)}, bf16[16,3200]{1,0:T(8,128)(2,1)S(1)}, u32[]{:S(2)}, u32[]{:S(2)}) collective-permute-start(bf16[16,3200]{1,0:T(8,128)(2,1)S(1)} %shard_map.64.refs_0_), channel_id=1, source_target_pairs={{0,2},{2,0},{4,6},{6,4},{8,10},{10,8},{12,14},{14,12},{1,3},{3,1},... | collective-permute-start | bytes 307208 | tf_op jit(solution)/shard_map/ppermute | solution.py:17
  6.7 1.6 %collective-permute-start.1 = (bf16[16,3200]{1,0:T(8,128)(2,1)S(1)}, bf16[16,3200]{1,0:T(8,128)(2,1)S(1)}, u32[]{:S(2)}, u32[]{:S(2)}) collective-permute-start(bf16[16,3200]{1,0:T(8,128)(2,1)S(1)} %shard_map.64.refs_0_), channel_id=1, source_target_pairs={{0,4},{2,6},{4,0},{6,2},{8,12},{10,14},{12,8},{14,10},{1,5},{3,7},... | collective-permute-start | bytes 307208 | tf_op jit(solution)/shard_map/ppermute | solution.py:17
  8.3 0.4 collective-permute-start.2
  8.7 0.0 copy-done
  8.7 0.1 pad.4.refs_8_
  8.8 1.6 %collective-permute-done.3.refs_4_ = bf16[16,3200]{1,0:T(8,128)(2,1)S(1)} collective-permute-done((bf16[16,3200]{1,0:T(8,128)(2,1)S(1)}, bf16[16,3200]{1,0:T(8,128)(2,1)S(1)}, u32[]{:S(2)}, u32[]{:S(2)}) %collective-permute-start.3) | collective-permute-done | bytes 102432 | tf_op jit(solution)/shard_map/ppermute | solution.py:17
  10.4 1.6 %collective-permute-start.4 = (bf16[16,3200]{1,0:T(8,128)(2,1)S(1)}, bf16[16,3200]{1,0:T(8,128)(2,1)S(1)}, u32[]{:S(2)}, u32[]{:S(2)}) collective-permute-start(bf16[16,3200]{1,0:T(8,128)(2,1)S(1)} %collective-permute-done.3.refs_4_), channel_id=1, source_target_pairs={{0,2},{2,0},{4,6},{6,4},{8,10},{10,8},{12,14},{14,12},{1,3},{3,1},... | collective-permute-start | bytes 307208 | tf_op jit(solution)/shard_map/ppermute | solution.py:17
  12.0 0.6 collective-permute-start.5
  12.6 0.0 collective-permute-done.refs_1_
  12.6 1.4 %collective-permute-start.6 = (bf16[16,3200]{1,0:T(8,128)(2,1)S(1)}, bf16[16,3200]{1,0:T(8,128)(2,1)S(1)}, u32[]{:S(2)}, u32[]{:S(2)}) collective-permute-start(bf16[16,3200]{1,0:T(8,128)(2,1)S(1)} %collective-permute-done.3.refs_4_), channel_id=1, source_target_pairs={{0,6},{2,4},{4,2},{6,0},{8,14},{10,12},{12,10},{14,8},{1,7},{3,5},... | collective-permute-start | bytes 307208 | tf_op jit(solution)/shard_map/ppermute | solution.py:17
  13.9 2.8 %shard_map.65.refs_11_.refs_0_ = bf16[1024,3072]{1,0:T(8,128)(2,1)S(1)} custom-call(bf16[16,128]{1,0:T(8,128)(2,1)S(1)} %slice.4._, bf16[4,1024,3072]{2,1,0:T(8,128)(2,1)} %up_ref.3), custom_call_target="tpu_custom_call" | custom-call | flops 14000000000 | tf_op jit(solution)/shard_map/pallas_call | solution.py:26
  16.7 0.0 collective-permute-done.1.refs_2_
  16.7 0.0 collective-permute-done.2.refs_3_
  16.7 0.0 collective-permute-done.4.refs_5_
  16.7 0.5 collective-permute-done.5.refs_6_
  17.3 1.5 %collective-permute-done.6.refs_7_ = bf16[16,3200]{1,0:T(8,128)(2,1)S(1)} collective-permute-done((bf16[16,3200]{1,0:T(8,128)(2,1)S(1)}, bf16[16,3200]{1,0:T(8,128)(2,1)S(1)}, u32[]{:S(2)}, u32[]{:S(2)}) %collective-permute-start.6) | collective-permute-done | bytes 102432 | tf_op jit(solution)/shard_map/ppermute | solution.py:17
  18.7 0.0 slice-done
  18.7 0.0 slice-done.1
  18.8 10.4 %shard_map.66 = (bf16[128,3200]{1,0:T(8,128)(2,1)S(1)}, f32[4224,128]{1,0:T(8,128)S(1)}, bf16[1024,3072]{1,0:T(8,128)(2,1)S(1)}, bf16[1024,3072]{1,0:T(8,128)(2,1)S(1)}, bf16[512,3072]{1,0:T(8,128)(2,1)S(1)}) custom-call(bf16[16,3200]{1,0:T(8,128)(2,1)S(1)} %shard_map.64.refs_0_, bf16[16,3200]{1,0:T(8,128)(2,1)S(1)} %collective-permute-done.refs_1_, ...), custom_call_target="tpu_custom_call" | custom-call | flops 3221225472 | bytes 25165824 | tf_op jit(solution)/shard_map/pallas_call | solution.py:26
  29.2 0.1 collective-permute-start.7
  29.3 3.8 %shard_map.67 = (f32[2048,128]{1,0:T(8,128)S(1)}, bf16[2048,128]{1,0:T(8,128)(2,1)S(1)}, bf16[512,3072]{1,0:T(8,128)(2,1)S(1)}, bf16[1024,3072]{1,0:T(8,128)(2,1)S(1)}) custom-call(bf16[128,3200]{1,0:T(8,128)(2,1)S(1)} %get-tuple-element.27.x_ref, bf16[4,1024,3072]{2,1,0:T(8,128)(2,1)} %up_ref.3, bf16[4,1024,3072]{2,1,0:T(8,128)(2,1)} %down_ref.7, ...), custom_call_target="tpu_custom_call" | custom-call | flops 1610612736 | bytes 12582912 | tf_op jit(solution)/shard_map/pallas_call | solution.py:26
  33.1 0.6 collective-permute-start.9
  33.7 3.4 %shard_map.68 = (f32[2048,128]{1,0:T(8,128)S(1)}, bf16[2048,128]{1,0:T(8,128)(2,1)S(1)}, bf16[1024,3072]{1,0:T(8,128)(2,1)S(1)}) custom-call(bf16[128,3200]{1,0:T(8,128)(2,1)S(1)} %get-tuple-element.27.x_ref, bf16[4,1024,3072]{2,1,0:T(8,128)(2,1)} %up_ref.3, bf16[4,1024,3072]{2,1,0:T(8,128)(2,1)} %down_ref.7, ...), custom_call_target="tpu_custom_call" | custom-call | flops 1610612736 | bytes 12582912 | tf_op jit(solution)/shard_map/pallas_call | solution.py:26
  37.1 0.1 collective-permute-start.8
  37.2 0.0 collective-permute-done.9.up_b
  37.2 0.0 collective-permute-done.7.gate_b
  37.2 2.8 %shard_map.69 = (bf16[2,128,1024]{2,1,0:T(8,128)(2,1)S(1)}, bf16[1024,3072]{1,0:T(8,128)(2,1)S(1)}) custom-call(f32[4224,128]{1,0:T(8,128)S(1)} %get-tuple-element.28.gate_a, f32[4224,128]{1,0:T(8,128)S(1)} %collective-permute-done.7.gate_b, f32[2048,128]{1,0:T(8,128)S(1)} %get-tuple-element.35.up_a, bf16[2048,128]{1,0:T(8,128)(2,1)S(1)} %collective-permute-done.9.up_b, ...), custom_call_target="tpu_custom_call" | custom-call | bytes 3145728 | tf_op jit(solution)/shard_map/pallas_call | solution.py:26
  40.0 0.0 collective-permute-done.8.up_b
  40.0 4.1 %shard_map.70 = (f32[16,3072]{1,0:T(8,128)S(1)}, bf16[16,3072]{1,0:T(8,128)(2,1)S(1)}, bf16[16,3072]{1,0:T(8,128)(2,1)S(1)}, bf16[16,3072]{1,0:T(8,128)(2,1)S(1)...) custom-call(bf16[128,3200]{1,0:T(8,128)(2,1)S(1)} %get-tuple-element, ...), custom_call_target="tpu_custom_call" | custom-call | flops 3221225472 | bytes 25165824 | tf_op jit(solution)/shard_map/pallas_call | solution.py:26
  44.1 1.5 %collective-permute-start.13 = (bf16[16,3072]{1,0:T(8,128)(2,1)S(1)}, bf16[16,3072]{1,0:T(8,128)(2,1)S(1)}, u32[]{:S(2)}, u32[]{:S(2)}) collective-permute-start(bf16[16,3072]{1,0:T(8,128)(2,1)S(1)} %get-tuple-element.46), channel_id=1, source_target_pairs={{0,6},{2,4},{4,2},{6,0},{8,14},{10,12},{12,10},{14,8},{1,7},{3,5},... | collective-permute-start | bytes 294920 | tf_op jit(solution)/shard_map/ppermute | solution.py:17
  45.6 1.1 %collective-permute-start.14 = (bf16[16,3072]{1,0:T(8,128)(2,1)S(1)}, bf16[16,3072]{1,0:T(8,128)(2,1)S(1)}, u32[]{:S(2)}, u32[]{:S(2)}) collective-permute-start(bf16[16,3072]{1,0:T(8,128)(2,1)S(1)} %get-tuple-element.47), channel_id=1, source_target_pairs={{0,4},{2,6},{4,0},{6,2},{8,12},{10,14},{12,8},{14,10},{1,5},{3,7},... | collective-permute-start | bytes 294920 | tf_op jit(solution)/shard_map/ppermute | solution.py:17
  46.7 0.9 %collective-permute-start.15 = (bf16[16,3072]{1,0:T(8,128)(2,1)S(1)}, bf16[16,3072]{1,0:T(8,128)(2,1)S(1)}, u32[]{:S(2)}, u32[]{:S(2)}) collective-permute-start(bf16[16,3072]{1,0:T(8,128)(2,1)S(1)} %get-tuple-element.48), channel_id=1, source_target_pairs={{0,2},{2,0},{4,6},{6,4},{8,10},{10,8},{12,14},{14,12},{1,3},{3,1},... | collective-permute-start | bytes 294920 | tf_op jit(solution)/shard_map/ppermute | solution.py:17
  47.7 1.4 %collective-permute-start.10 = (bf16[16,3072]{1,0:T(8,128)(2,1)S(1)}, bf16[16,3072]{1,0:T(8,128)(2,1)S(1)}, u32[]{:S(2)}, u32[]{:S(2)}) collective-permute-start(bf16[16,3072]{1,0:T(8,128)(2,1)S(1)} %get-tuple-element.42), channel_id=1, source_target_pairs={{0,6},{2,4},{4,2},{6,0},{8,14},{10,12},{12,10},{14,8},{1,7},{3,5},... | collective-permute-start | bytes 294920 | tf_op jit(solution)/shard_map/ppermute | solution.py:17
  49.1 1.1 %collective-permute-start.11 = (bf16[16,3072]{1,0:T(8,128)(2,1)S(1)}, bf16[16,3072]{1,0:T(8,128)(2,1)S(1)}, u32[]{:S(2)}, u32[]{:S(2)}) collective-permute-start(bf16[16,3072]{1,0:T(8,128)(2,1)S(1)} %get-tuple-element.43), channel_id=1, source_target_pairs={{0,4},{2,6},{4,0},{6,2},{8,12},{10,14},{12,8},{14,10},{1,5},{3,7},... | collective-permute-start | bytes 294920 | tf_op jit(solution)/shard_map/ppermute | solution.py:17
  50.2 0.4 collective-permute-done.13
  50.7 1.1 %collective-permute-start.12 = (bf16[16,3072]{1,0:T(8,128)(2,1)S(1)}, bf16[16,3072]{1,0:T(8,128)(2,1)S(1)}, u32[]{:S(2)}, u32[]{:S(2)}) collective-permute-start(bf16[16,3072]{1,0:T(8,128)(2,1)S(1)} %get-tuple-element.44), channel_id=1, source_target_pairs={{0,2},{2,0},{4,6},{6,4},{8,10},{10,8},{12,14},{14,12},{1,3},{3,1},... | collective-permute-start | bytes 294920 | tf_op jit(solution)/shard_map/ppermute | solution.py:17
  51.8 0.6 %collective-permute-done.14 = bf16[16,3072]{1,0:T(8,128)(2,1)S(1)} collective-permute-done((bf16[16,3072]{1,0:T(8,128)(2,1)S(1)}, bf16[16,3072]{1,0:T(8,128)(2,1)S(1)}, u32[]{:S(2)}, u32[]{:S(2)}) %collective-permute-start.14) | collective-permute-done | bytes 98336 | tf_op jit(solution)/shard_map/ppermute | solution.py:17
  52.4 0.4 collective-permute-done.15
  52.8 0.1 add_convert_fusion.1
  52.9 2.8 %collective-permute-start.16 = (bf16[16,3072]{1,0:T(8,128)(2,1)S(1)}, bf16[16,3072]{1,0:T(8,128)(2,1)S(1)}, u32[]{:S(2)}, u32[]{:S(2)}) collective-permute-start(bf16[16,3072]{1,0:T(8,128)(2,1)S(1)} %add_convert_fusion.1), channel_id=1, source_target_pairs={{0,8},{2,10},{4,12},{6,14},{8,0},{10,2},{12,4},{14,6},{1,9},{3,11}... | collective-permute-start | bytes 294920 | tf_op jit(solution)/shard_map/ppermute | solution.py:17
  55.7 0.0 collective-permute-done.10
  55.7 0.5 collective-permute-done.11
  56.3 0.3 collective-permute-done.12
  56.6 4.0 %collective-permute-done.16 = bf16[16,3072]{1,0:T(8,128)(2,1)S(1)} collective-permute-done((bf16[16,3072]{1,0:T(8,128)(2,1)S(1)}, bf16[16,3072]{1,0:T(8,128)(2,1)S(1)}, u32[]{:S(2)}, u32[]{:S(2)}) %collective-permute-start.16) | collective-permute-done | bytes 98336 | tf_op jit(solution)/shard_map/ppermute | solution.py:17
  60.6 0.7 %add_convert_fusion = bf16[16,3072]{1,0:T(8,128)(2,1)} fusion(bf16[16,3072]{1,0:T(8,128)(2,1)S(1)} %collective-permute-done.16, bf16[16,3072]{1,0:T(8,128)(2,1)S(1)} %collective-permute-done.12, bf16[16,3072]{1,0:T(8,128)(2,1)S(1)} %collective-permute-done.11, f32[16,3072]{1,0:T(8,128)S(1)} %get-tuple-element.41, bf16[16,3072]{1,0:T(8,128)(2,1)S(1)} %collective-permute-done.10), kind=kLoop, calls=%fused_computation | loop fusion | flops 442368 | bytes 688128 | tf_op jit(solution)/shard_map/convert_element_type | solution.py:287
  (12 shorter events, 0.0 us)
Async XLA Ops:
  0.0 8.7 %copy-start = (bf16[3072,4]{0,1:T(4,128)(2,1)S(1)}, bf16[3072,4]{0,1:T(4,128)(2,1)}, u32[]{:S(2)}) copy-start(bf16[3072,4]{0,1:T(4,128)(2,1)} %param.8) | copy-start | bytes 73732
  0.0 18.7 %slice-start = ((s8[25165824]{0:T(1024)(128)(4,1)}), s8[4194304]{0:T(1024)(128)(4,1)S(1)}, s32[]{:S(2)}) async-start(s8[25165824]{0:T(1024)(128)(4,1)} %bitcast.2), calls=%async_computation | async-start | bytes 8388608
  0.0 18.7 %slice-start.1 = ((s8[25165824]{0:T(1024)(128)(4,1)}), s8[4194304]{0:T(1024)(128)(4,1)S(1)}, s32[]{:S(2)}) async-start(s8[25165824]{0:T(1024)(128)(4,1)} %bitcast.2), calls=%async_computation.1 | async-start | bytes 8388608
  0.0 18.7 %slice-start.2 = ((s8[25165824]{0:T(1024)(128)(4,1)}), s8[4194304]{0:T(1024)(128)(4,1)S(1)}, s32[]{:S(2)}) async-start(s8[25165824]{0:T(1024)(128)(4,1)} %bitcast.2), calls=%async_computation.2 | async-start | bytes 8388608
  0.0 18.7 %slice-start.3 = ((s8[25165824]{0:T(1024)(128)(4,1)}), s8[4194304]{0:T(1024)(128)(4,1)S(1)}, s32[]{:S(2)}) async-start(s8[25165824]{0:T(1024)(128)(4,1)} %bitcast.2), calls=%async_computation.3 | async-start | bytes 8388608
  0.0 18.7 %slice-start.4 = ((s8[25165824]{0:T(1024)(128)(4,1)}), s8[4194304]{0:T(1024)(128)(4,1)S(1)}, s32[]{:S(2)}) async-start(s8[25165824]{0:T(1024)(128)(4,1)} %bitcast.2), calls=%async_computation.4 | async-start | bytes 8388608
  1.1 9.3 %collective-permute-start.3 = (bf16[16,3200]{1,0:T(8,128)(2,1)S(1)}, bf16[16,3200]{1,0:T(8,128)(2,1)S(1)}, u32[]{:S(2)}, u32[]{:S(2)}) collective-permute-start(bf16[16,3200]{1,0:T(8,128)(2,1)S(1)} %shard_map.64.refs_0_), channel_id=1, source_target_pairs={{0,8},{2,10},{4,12},{6,14},{8,0},{10,2},{12,4},{14,6},{1,9},{3,11}... | collective-permute-start | bytes 307208 | tf_op jit(solution)/shard_map/ppermute | solution.py:17
  5.2 7.3 %collective-permute-start = (bf16[16,3200]{1,0:T(8,128)(2,1)S(1)}, bf16[16,3200]{1,0:T(8,128)(2,1)S(1)}, u32[]{:S(2)}, u32[]{:S(2)}) collective-permute-start(bf16[16,3200]{1,0:T(8,128)(2,1)S(1)} %shard_map.64.refs_0_), channel_id=1, source_target_pairs={{0,2},{2,0},{4,6},{6,4},{8,10},{10,8},{12,14},{14,12},{1,3},{3,1},... | collective-permute-start | bytes 307208 | tf_op jit(solution)/shard_map/ppermute | solution.py:17
  6.7 10.0 %collective-permute-start.1 = (bf16[16,3200]{1,0:T(8,128)(2,1)S(1)}, bf16[16,3200]{1,0:T(8,128)(2,1)S(1)}, u32[]{:S(2)}, u32[]{:S(2)}) collective-permute-start(bf16[16,3200]{1,0:T(8,128)(2,1)S(1)} %shard_map.64.refs_0_), channel_id=1, source_target_pairs={{0,4},{2,6},{4,0},{6,2},{8,12},{10,14},{12,8},{14,10},{1,5},{3,7},... | collective-permute-start | bytes 307208 | tf_op jit(solution)/shard_map/ppermute | solution.py:17
  8.3 8.4 %collective-permute-start.2 = (bf16[16,3200]{1,0:T(8,128)(2,1)S(1)}, bf16[16,3200]{1,0:T(8,128)(2,1)S(1)}, u32[]{:S(2)}, u32[]{:S(2)}) collective-permute-start(bf16[16,3200]{1,0:T(8,128)(2,1)S(1)} %shard_map.64.refs_0_), channel_id=1, source_target_pairs={{0,6},{2,4},{4,2},{6,0},{8,14},{10,12},{12,10},{14,8},{1,7},{3,5},... | collective-permute-start | bytes 307208 | tf_op jit(solution)/shard_map/ppermute | solution.py:17
  10.4 8.4 %slice-start.5 = ((s8[25165824]{0:T(1024)(128)(4,1)}), s8[4194304]{0:T(1024)(128)(4,1)S(1)}, s32[]{:S(2)}) async-start(s8[25165824]{0:T(1024)(128)(4,1)} %bitcast.2), calls=%async_computation.5 | async-start | bytes 8388608
  10.4 6.3 %collective-permute-start.4 = (bf16[16,3200]{1,0:T(8,128)(2,1)S(1)}, bf16[16,3200]{1,0:T(8,128)(2,1)S(1)}, u32[]{:S(2)}, u32[]{:S(2)}) collective-permute-start(bf16[16,3200]{1,0:T(8,128)(2,1)S(1)} %collective-permute-done.3.refs_4_), channel_id=1, source_target_pairs={{0,2},{2,0},{4,6},{6,4},{8,10},{10,8},{12,14},{14,12},{1,3},{3,1},... | collective-permute-start | bytes 307208 | tf_op jit(solution)/shard_map/ppermute | solution.py:17
  12.0 5.3 %collective-permute-start.5 = (bf16[16,3200]{1,0:T(8,128)(2,1)S(1)}, bf16[16,3200]{1,0:T(8,128)(2,1)S(1)}, u32[]{:S(2)}, u32[]{:S(2)}) collective-permute-start(bf16[16,3200]{1,0:T(8,128)(2,1)S(1)} %collective-permute-done.3.refs_4_), channel_id=1, source_target_pairs={{0,4},{2,6},{4,0},{6,2},{8,12},{10,14},{12,8},{14,10},{1,5},{3,7},... | collective-permute-start | bytes 307208 | tf_op jit(solution)/shard_map/ppermute | solution.py:17
  12.6 6.2 %collective-permute-start.6 = (bf16[16,3200]{1,0:T(8,128)(2,1)S(1)}, bf16[16,3200]{1,0:T(8,128)(2,1)S(1)}, u32[]{:S(2)}, u32[]{:S(2)}) collective-permute-start(bf16[16,3200]{1,0:T(8,128)(2,1)S(1)} %collective-permute-done.3.refs_4_), channel_id=1, source_target_pairs={{0,6},{2,4},{4,2},{6,0},{8,14},{10,12},{12,10},{14,8},{1,7},{3,5},... | collective-permute-start | bytes 307208 | tf_op jit(solution)/shard_map/ppermute | solution.py:17
  29.2 7.9 %collective-permute-start.7 = (f32[4224,128]{1,0:T(8,128)S(1)}, f32[4224,128]{1,0:T(8,128)S(1)}, u32[]{:S(2)}, u32[]{:S(2)}) collective-permute-start(f32[4224,128]{1,0:T(8,128)S(1)} %get-tuple-element.28.gate_a), channel_id=1, source_target_pairs={{0,1},{1,0},{2,3},{3,2},{4,5},{5,4},{6,7},{7,6},{8,9},{9,8},{10,11... | collective-permute-start | bytes 6488072 | tf_op jit(solution)/shard_map/ppermute | solution.py:239
  33.1 4.1 %collective-permute-start.9 = (bf16[2048,128]{1,0:T(8,128)(2,1)S(1)}, bf16[2048,128]{1,0:T(8,128)(2,1)S(1)}, u32[]{:S(2)}, u32[]{:S(2)}) collective-permute-start(bf16[2048,128]{1,0:T(8,128)(2,1)S(1)} %get-tuple-element.36), channel_id=1, source_target_pairs={{0,1},{1,0},{2,3},{3,2},{4,5},{5,4},{6,7},{7,6},{8,9},{9,8},{10,11... | collective-permute-start | bytes 1572872 | tf_op jit(solution)/shard_map/ppermute | solution.py:257
  37.1 2.9 %collective-permute-start.8 = (bf16[2048,128]{1,0:T(8,128)(2,1)S(1)}, bf16[2048,128]{1,0:T(8,128)(2,1)S(1)}, u32[]{:S(2)}, u32[]{:S(2)}) collective-permute-start(bf16[2048,128]{1,0:T(8,128)(2,1)S(1)} %get-tuple-element.34), channel_id=1, source_target_pairs={{0,1},{1,0},{2,3},{3,2},{4,5},{5,4},{6,7},{7,6},{8,9},{9,8},{10,11... | collective-permute-start | bytes 1572872 | tf_op jit(solution)/shard_map/ppermute | solution.py:257
  44.1 6.6 %collective-permute-start.13 = (bf16[16,3072]{1,0:T(8,128)(2,1)S(1)}, bf16[16,3072]{1,0:T(8,128)(2,1)S(1)}, u32[]{:S(2)}, u32[]{:S(2)}) collective-permute-start(bf16[16,3072]{1,0:T(8,128)(2,1)S(1)} %get-tuple-element.46), channel_id=1, source_target_pairs={{0,6},{2,4},{4,2},{6,0},{8,14},{10,12},{12,10},{14,8},{1,7},{3,5},... | collective-permute-start | bytes 294920 | tf_op jit(solution)/shard_map/ppermute | solution.py:17
  45.6 6.8 %collective-permute-start.14 = (bf16[16,3072]{1,0:T(8,128)(2,1)S(1)}, bf16[16,3072]{1,0:T(8,128)(2,1)S(1)}, u32[]{:S(2)}, u32[]{:S(2)}) collective-permute-start(bf16[16,3072]{1,0:T(8,128)(2,1)S(1)} %get-tuple-element.47), channel_id=1, source_target_pairs={{0,4},{2,6},{4,0},{6,2},{8,12},{10,14},{12,8},{14,10},{1,5},{3,7},... | collective-permute-start | bytes 294920 | tf_op jit(solution)/shard_map/ppermute | solution.py:17
  46.7 6.1 %collective-permute-start.15 = (bf16[16,3072]{1,0:T(8,128)(2,1)S(1)}, bf16[16,3072]{1,0:T(8,128)(2,1)S(1)}, u32[]{:S(2)}, u32[]{:S(2)}) collective-permute-start(bf16[16,3072]{1,0:T(8,128)(2,1)S(1)} %get-tuple-element.48), channel_id=1, source_target_pairs={{0,2},{2,0},{4,6},{6,4},{8,10},{10,8},{12,14},{14,12},{1,3},{3,1},... | collective-permute-start | bytes 294920 | tf_op jit(solution)/shard_map/ppermute | solution.py:17
  47.7 8.1 %collective-permute-start.10 = (bf16[16,3072]{1,0:T(8,128)(2,1)S(1)}, bf16[16,3072]{1,0:T(8,128)(2,1)S(1)}, u32[]{:S(2)}, u32[]{:S(2)}) collective-permute-start(bf16[16,3072]{1,0:T(8,128)(2,1)S(1)} %get-tuple-element.42), channel_id=1, source_target_pairs={{0,6},{2,4},{4,2},{6,0},{8,14},{10,12},{12,10},{14,8},{1,7},{3,5},... | collective-permute-start | bytes 294920 | tf_op jit(solution)/shard_map/ppermute | solution.py:17
  49.1 7.2 %collective-permute-start.11 = (bf16[16,3072]{1,0:T(8,128)(2,1)S(1)}, bf16[16,3072]{1,0:T(8,128)(2,1)S(1)}, u32[]{:S(2)}, u32[]{:S(2)}) collective-permute-start(bf16[16,3072]{1,0:T(8,128)(2,1)S(1)} %get-tuple-element.43), channel_id=1, source_target_pairs={{0,4},{2,6},{4,0},{6,2},{8,12},{10,14},{12,8},{14,10},{1,5},{3,7},... | collective-permute-start | bytes 294920 | tf_op jit(solution)/shard_map/ppermute | solution.py:17
  50.7 5.9 %collective-permute-start.12 = (bf16[16,3072]{1,0:T(8,128)(2,1)S(1)}, bf16[16,3072]{1,0:T(8,128)(2,1)S(1)}, u32[]{:S(2)}, u32[]{:S(2)}) collective-permute-start(bf16[16,3072]{1,0:T(8,128)(2,1)S(1)} %get-tuple-element.44), channel_id=1, source_target_pairs={{0,2},{2,0},{4,6},{6,4},{8,10},{10,8},{12,14},{14,12},{1,3},{3,1},... | collective-permute-start | bytes 294920 | tf_op jit(solution)/shard_map/ppermute | solution.py:17
  52.9 7.7 %collective-permute-start.16 = (bf16[16,3072]{1,0:T(8,128)(2,1)S(1)}, bf16[16,3072]{1,0:T(8,128)(2,1)S(1)}, u32[]{:S(2)}, u32[]{:S(2)}) collective-permute-start(bf16[16,3072]{1,0:T(8,128)(2,1)S(1)} %add_convert_fusion.1), channel_id=1, source_target_pairs={{0,8},{2,10},{4,12},{6,14},{8,0},{10,2},{12,4},{14,6},{1,9},{3,11}... | collective-permute-start | bytes 294920 | tf_op jit(solution)/shard_map/ppermute | solution.py:17

commit v8 on v7

--- a/solution.py
+++ b/solution.py
@@ -145,7 +145,7 @@
 
 
 def hidden_kernel(experts, fetched, gate_a, gate_b, up_a, up_b, down_ref, *refs):
-    out_ref, *held, sems = refs[2:]
+    out_ref, *held, sems = refs
     copies = fetches(down_ref, fetched, held, sems)
     for copy in copies:
         copy.start()
@@ -200,9 +200,9 @@
         hbm=(0, 1),
     )
     far = xor_send(own, 4)
-    near = [xor_send(own, k) for k in (3, 2, 1)]
-    forwarded = [xor_send(far, k) for k in (3, 2, 1)]
-    blocks = [own, *near[::-1], far, *forwarded[::-1]]
+    near = [xor_send(own, k) for k in (1, 2, 3)]
+    forwarded = [xor_send(far, k) for k in (1, 2, 3)]
+    blocks = [own, *near, far, *forwarded]
 
     w_gate, w_up, w_down = in_vmem(w_gate), in_hbm(w_up), in_hbm(w_down)
     flops = 2 * count * hidden * width
@@ -211,25 +211,26 @@
     one = pltpu.VMEM((hidden, width), BF16)
     part_of_one = pltpu.VMEM((hidden // 2, width), BF16)
     sems = lambda n: [pltpu.SemaphoreType.DMA((n,))]
-    (up0,) = call(
-        functools.partial(fetch_kernel, (0,)),
-        [one] * 1,
+    up0, up1a = call(
+        functools.partial(fetch_kernel, (0, (1, 0))),
+        [one, part_of_one],
         [far[:, :128], w_up],
-        14_000_000_000,
+        8_000_000_000,
         0,
         1,
-        sems(1),
+        sems(2),
         hbm=(1,),
     )
-    x, gate, up1, up2, up3a = call(
-        functools.partial(gate_kernel, (1, 2, (3, 0)), 1),
+    x, gate, up1b, up2, up3a = call(
+        functools.partial(gate_kernel, ((1, hidden // 2), 2, (3, 0)), 2),
         [
             shape(count, width + IDS, dtype=BF16),
             shape(experts * hidden + count, count),
-            *[one] * 2,
+            part_of_one,
+            one,
             part_of_one,
         ],
-        [*blocks, lines, w_gate, w_up, up0],
+        [*blocks, lines, w_gate, w_up, up0, up1a],
         experts * flops,
         experts * size,
         3,
@@ -257,13 +258,13 @@
         return (part, lax.ppermute(sent, "mp", SWAP)), held
 
     first, (up3b, down0) = up_call(
-        ((3, hidden // 2),), (0,), (up0, up1), (part_of_one, one), (up3a,)
+        ((3, hidden // 2),), (0,), (up0, up1a, up1b), (part_of_one, one), (up3a,)
     )
     second, (down1,) = up_call((), (1,), (up2, up3a, up3b), (one,), ())
     units, down2 = call(
         functools.partial(hidden_kernel, range(half), (2,)),
         [shape(half, count, hidden, dtype=BF16)] + [one] * 1,
-        [gate, gate_other, *first, w_down, down0, down1],
+        [gate, gate_other, *first, w_down],
         0,
         12 * half * hidden * count,
         4,

time: 61.5 us -> 60.6 us (0.985)
  waiting for transfers between devices: 9.99 us -> 8.5 us
  Pallas kernels: 28.4 us -> 29.2 us
    ppermute x14, waiting for transfers between devices: 9.99 us -> 8.49 us  [xor_send(): return lax.ppermute(block, 'batch', [(i, i ^ mask) for i in range(8)])]
    pallas_call x7, Pallas kernels: 28.4 us -> 29.2 us  [call(): pl.pallas_call(kernel, out_shape=outs, in_specs=specs, out_specs=[VMEM_BL...]
  transfers between devices with their start and end apart: 17 -> 17, of which waited for: 9 -> 7; matrix products, arithmetic and copies ran while one was open for 0% -> 0% of each run, Pallas kernels for 21% -> 23%
where the time goes in v8:
time: 60.6 us; the launch traced here: 60.5 us
  Pallas kernels  29.2 us (48%)
  starting transfers between devices  21.7 us (36%)
  waiting for transfers between devices  8.5 us (14%)
  other arithmetic  0.76 us (1%)
    pallas_call x7, Pallas kernels, call(): pl.pallas_call(kernel, out_shape=outs, in_specs=specs, out_specs=[VMEM_BL...  29.2 us
    ppermute x14, starting transfers between devices, xor_send(): return lax.ppermute(block, 'batch', [(i, i ^ mask) for i in range(8)])  21 us
    ppermute x14, waiting for transfers between devices, xor_send(): return lax.ppermute(block, 'batch', [(i, i ^ mask) for i in range(8)])  8.49 us
  transfers between devices with their start and end apart: 17, of which 7 were waited for; matrix products, arithmetic and copies ran while one was open for 0% of the time, Pallas kernels for 23%

profile of v8, /device:TPU:0, one launch (start us, length us, event | category | flops | bytes accessed | tf_op | source)
XLA Modules:
  0.0 60.5 jit_solution(4508338180180094569)
XLA Ops:
  0.0 0.0 slice-start.4
  0.0 1.1 %shard_map.64.refs_0_ = bf16[16,3200]{1,0:T(8,128)(2,1)S(1)} custom-call(bf16[16,3072]{1,0:T(8,128)(2,1)} %tokens_ref.1, s32[2,16]{1,0:T(2,128)} %bitcast.5), custom_call_target="tpu_custom_call" | custom-call | flops 30000001024 | bytes 196608 | tf_op jit(solution)/shard_map/pallas_call | solution.py:26
  1.1 4.1 %collective-permute-start.3 = (bf16[16,3200]{1,0:T(8,128)(2,1)S(1)}, bf16[16,3200]{1,0:T(8,128)(2,1)S(1)}, u32[]{:S(2)}, u32[]{:S(2)}) collective-permute-start(bf16[16,3200]{1,0:T(8,128)(2,1)S(1)} %shard_map.64.refs_0_), channel_id=1, source_target_pairs={{0,8},{2,10},{4,12},{6,14},{8,0},{10,2},{12,4},{14,6},{1,9},{3,11}... | collective-permute-start | bytes 307208 | tf_op jit(solution)/shard_map/ppermute | solution.py:17
  5.2 2.5 %collective-permute-start.2 = (bf16[16,3200]{1,0:T(8,128)(2,1)S(1)}, bf16[16,3200]{1,0:T(8,128)(2,1)S(1)}, u32[]{:S(2)}, u32[]{:S(2)}) collective-permute-start(bf16[16,3200]{1,0:T(8,128)(2,1)S(1)} %shard_map.64.refs_0_), channel_id=1, source_target_pairs={{0,6},{2,4},{4,2},{6,0},{8,14},{10,12},{12,10},{14,8},{1,7},{3,5},... | collective-permute-start | bytes 307208 | tf_op jit(solution)/shard_map/ppermute | solution.py:17
  7.8 0.4 collective-permute-start.1
  8.2 0.5 collective-permute-start
  8.7 0.0 copy-done
  8.7 0.1 pad.4.refs_8_
  8.8 1.5 %collective-permute-done.3.refs_4_ = bf16[16,3200]{1,0:T(8,128)(2,1)S(1)} collective-permute-done((bf16[16,3200]{1,0:T(8,128)(2,1)S(1)}, bf16[16,3200]{1,0:T(8,128)(2,1)S(1)}, u32[]{:S(2)}, u32[]{:S(2)}) %collective-permute-start.3) | collective-permute-done | bytes 102432 | tf_op jit(solution)/shard_map/ppermute | solution.py:17
  10.3 1.7 %collective-permute-start.6 = (bf16[16,3200]{1,0:T(8,128)(2,1)S(1)}, bf16[16,3200]{1,0:T(8,128)(2,1)S(1)}, u32[]{:S(2)}, u32[]{:S(2)}) collective-permute-start(bf16[16,3200]{1,0:T(8,128)(2,1)S(1)} %collective-permute-done.3.refs_4_), channel_id=1, source_target_pairs={{0,6},{2,4},{4,2},{6,0},{8,14},{10,12},{12,10},{14,8},{1,7},{3,5},... | collective-permute-start | bytes 307208 | tf_op jit(solution)/shard_map/ppermute | solution.py:17
  12.0 1.4 %collective-permute-start.5 = (bf16[16,3200]{1,0:T(8,128)(2,1)S(1)}, bf16[16,3200]{1,0:T(8,128)(2,1)S(1)}, u32[]{:S(2)}, u32[]{:S(2)}) collective-permute-start(bf16[16,3200]{1,0:T(8,128)(2,1)S(1)} %collective-permute-done.3.refs_4_), channel_id=1, source_target_pairs={{0,4},{2,6},{4,0},{6,2},{8,12},{10,14},{12,8},{14,10},{1,5},{3,7},... | collective-permute-start | bytes 307208 | tf_op jit(solution)/shard_map/ppermute | solution.py:17
  13.4 0.0 collective-permute-done.2.refs_3_
  13.4 0.4 collective-permute-start.4
  13.8 3.7 %shard_map.65 = (bf16[1024,3072]{1,0:T(8,128)(2,1)S(1)}, bf16[512,3072]{1,0:T(8,128)(2,1)S(1)}) custom-call(bf16[16,128]{1,0:T(8,128)(2,1)S(1)} %slice.4._, bf16[4,1024,3072]{2,1,0:T(8,128)(2,1)} %up_ref.3), custom_call_target="tpu_custom_call" | custom-call | flops 8000000000 | tf_op jit(solution)/shard_map/pallas_call | solution.py:26
  17.5 0.0 collective-permute-done.1.refs_2_
  17.5 0.0 collective-permute-done.refs_1_
  17.6 0.0 collective-permute-done.6.refs_7_
  17.6 0.5 collective-permute-done.5.refs_6_
  18.1 0.0 collective-permute-done.4.refs_5_
  18.1 0.0 slice-done
  18.1 0.0 slice-done.1
  18.2 10.5 %shard_map.66 = (bf16[128,3200]{1,0:T(8,128)(2,1)S(1)}, f32[4224,128]{1,0:T(8,128)S(1)}, bf16[512,3072]{1,0:T(8,128)(2,1)S(1)}, bf16[1024,3072]{1,0:T(8,128)(2,1)S(1)}, bf16[512,3072]{1,0:T(8,128)(2,1)S(1)}) custom-call(bf16[16,3200]{1,0:T(8,128)(2,1)S(1)} %shard_map.64.refs_0_, bf16[16,3200]{1,0:T(8,128)(2,1)S(1)} %collective-permute-done.refs_1_, ...), custom_call_target="tpu_custom_call" | custom-call | flops 3221225472 | bytes 25165824 | tf_op jit(solution)/shard_map/pallas_call | solution.py:26
  28.6 0.1 collective-permute-start.7
  28.7 3.8 %shard_map.67 = (f32[2048,128]{1,0:T(8,128)S(1)}, bf16[2048,128]{1,0:T(8,128)(2,1)S(1)}, bf16[512,3072]{1,0:T(8,128)(2,1)S(1)}, bf16[1024,3072]{1,0:T(8,128)(2,1)S(1)}) custom-call(bf16[128,3200]{1,0:T(8,128)(2,1)S(1)} %get-tuple-element.31.x_ref, bf16[4,1024,3072]{2,1,0:T(8,128)(2,1)} %up_ref.3, bf16[4,1024,3072]{2,1,0:T(8,128)(2,1)} %down_ref.7, ...), custom_call_target="tpu_custom_call" | custom-call | flops 1610612736 | bytes 12582912 | tf_op jit(solution)/shard_map/pallas_call | solution.py:26
  32.5 0.6 collective-permute-start.9
  33.1 3.4 %shard_map.68 = (f32[2048,128]{1,0:T(8,128)S(1)}, bf16[2048,128]{1,0:T(8,128)(2,1)S(1)}, bf16[1024,3072]{1,0:T(8,128)(2,1)S(1)}) custom-call(bf16[128,3200]{1,0:T(8,128)(2,1)S(1)} %get-tuple-element.31.x_ref, bf16[4,1024,3072]{2,1,0:T(8,128)(2,1)} %up_ref.3, bf16[4,1024,3072]{2,1,0:T(8,128)(2,1)} %down_ref.7, ...), custom_call_target="tpu_custom_call" | custom-call | flops 1610612736 | bytes 12582912 | tf_op jit(solution)/shard_map/pallas_call | solution.py:26
  36.5 0.1 collective-permute-start.8
  36.6 0.0 collective-permute-done.9.up_b
  36.6 0.0 collective-permute-done.7.gate_b
  36.6 2.8 %shard_map.69 = (bf16[2,128,1024]{2,1,0:T(8,128)(2,1)S(1)}, bf16[1024,3072]{1,0:T(8,128)(2,1)S(1)}) custom-call(f32[4224,128]{1,0:T(8,128)S(1)} %get-tuple-element.32.gate_a, f32[4224,128]{1,0:T(8,128)S(1)} %collective-permute-done.7.gate_b, f32[2048,128]{1,0:T(8,128)S(1)} %get-tuple-element.39.up_a, bf16[2048,128]{1,0:T(8,128)(2,1)S(1)} %collective-permute-done.9.up_b, ...), custom_call_target="tpu_custom_call" | custom-call | bytes 3145728 | tf_op jit(solution)/shard_map/pallas_call | solution.py:26
  39.4 0.0 collective-permute-done.8.up_b
  39.4 3.9 %shard_map.70 = (f32[16,3072]{1,0:T(8,128)S(1)}, bf16[16,3072]{1,0:T(8,128)(2,1)S(1)}, bf16[16,3072]{1,0:T(8,128)(2,1)S(1)}, bf16[16,3072]{1,0:T(8,128)(2,1)S(1)...) custom-call(bf16[128,3200]{1,0:T(8,128)(2,1)S(1)} %get-tuple-element, ...), custom_call_target="tpu_custom_call" | custom-call | flops 3221225472 | bytes 25165824 | tf_op jit(solution)/shard_map/pallas_call | solution.py:26
  43.4 1.8 %collective-permute-start.13 = (bf16[16,3072]{1,0:T(8,128)(2,1)S(1)}, bf16[16,3072]{1,0:T(8,128)(2,1)S(1)}, u32[]{:S(2)}, u32[]{:S(2)}) collective-permute-start(bf16[16,3072]{1,0:T(8,128)(2,1)S(1)} %get-tuple-element.50), channel_id=1, source_target_pairs={{0,6},{2,4},{4,2},{6,0},{8,14},{10,12},{12,10},{14,8},{1,7},{3,5},... | collective-permute-start | bytes 294920 | tf_op jit(solution)/shard_map/ppermute | solution.py:17
  45.2 0.9 %collective-permute-start.14 = (bf16[16,3072]{1,0:T(8,128)(2,1)S(1)}, bf16[16,3072]{1,0:T(8,128)(2,1)S(1)}, u32[]{:S(2)}, u32[]{:S(2)}) collective-permute-start(bf16[16,3072]{1,0:T(8,128)(2,1)S(1)} %get-tuple-element.51), channel_id=1, source_target_pairs={{0,4},{2,6},{4,0},{6,2},{8,12},{10,14},{12,8},{14,10},{1,5},{3,7},... | collective-permute-start | bytes 294920 | tf_op jit(solution)/shard_map/ppermute | solution.py:17
  46.0 0.9 %collective-permute-start.15 = (bf16[16,3072]{1,0:T(8,128)(2,1)S(1)}, bf16[16,3072]{1,0:T(8,128)(2,1)S(1)}, u32[]{:S(2)}, u32[]{:S(2)}) collective-permute-start(bf16[16,3072]{1,0:T(8,128)(2,1)S(1)} %get-tuple-element.52), channel_id=1, source_target_pairs={{0,2},{2,0},{4,6},{6,4},{8,10},{10,8},{12,14},{14,12},{1,3},{3,1},... | collective-permute-start | bytes 294920 | tf_op jit(solution)/shard_map/ppermute | solution.py:17
  46.9 1.8 %collective-permute-start.10 = (bf16[16,3072]{1,0:T(8,128)(2,1)S(1)}, bf16[16,3072]{1,0:T(8,128)(2,1)S(1)}, u32[]{:S(2)}, u32[]{:S(2)}) collective-permute-start(bf16[16,3072]{1,0:T(8,128)(2,1)S(1)} %get-tuple-element.46), channel_id=1, source_target_pairs={{0,6},{2,4},{4,2},{6,0},{8,14},{10,12},{12,10},{14,8},{1,7},{3,5},... | collective-permute-start | bytes 294920 | tf_op jit(solution)/shard_map/ppermute | solution.py:17
  48.7 0.9 %collective-permute-start.11 = (bf16[16,3072]{1,0:T(8,128)(2,1)S(1)}, bf16[16,3072]{1,0:T(8,128)(2,1)S(1)}, u32[]{:S(2)}, u32[]{:S(2)}) collective-permute-start(bf16[16,3072]{1,0:T(8,128)(2,1)S(1)} %get-tuple-element.47), channel_id=1, source_target_pairs={{0,4},{2,6},{4,0},{6,2},{8,12},{10,14},{12,8},{14,10},{1,5},{3,7},... | collective-permute-start | bytes 294920 | tf_op jit(solution)/shard_map/ppermute | solution.py:17
  49.5 0.4 collective-permute-done.13
  49.9 1.2 %collective-permute-start.12 = (bf16[16,3072]{1,0:T(8,128)(2,1)S(1)}, bf16[16,3072]{1,0:T(8,128)(2,1)S(1)}, u32[]{:S(2)}, u32[]{:S(2)}) collective-permute-start(bf16[16,3072]{1,0:T(8,128)(2,1)S(1)} %get-tuple-element.48), channel_id=1, source_target_pairs={{0,2},{2,0},{4,6},{6,4},{8,10},{10,8},{12,14},{14,12},{1,3},{3,1},... | collective-permute-start | bytes 294920 | tf_op jit(solution)/shard_map/ppermute | solution.py:17
  51.1 0.6 %collective-permute-done.14 = bf16[16,3072]{1,0:T(8,128)(2,1)S(1)} collective-permute-done((bf16[16,3072]{1,0:T(8,128)(2,1)S(1)}, bf16[16,3072]{1,0:T(8,128)(2,1)S(1)}, u32[]{:S(2)}, u32[]{:S(2)}) %collective-permute-start.14) | collective-permute-done | bytes 98336 | tf_op jit(solution)/shard_map/ppermute | solution.py:17
  51.7 0.4 collective-permute-done.15
  52.1 0.1 add_convert_fusion.1
  52.1 2.6 %collective-permute-start.16 = (bf16[16,3072]{1,0:T(8,128)(2,1)S(1)}, bf16[16,3072]{1,0:T(8,128)(2,1)S(1)}, u32[]{:S(2)}, u32[]{:S(2)}) collective-permute-start(bf16[16,3072]{1,0:T(8,128)(2,1)S(1)} %add_convert_fusion.1), channel_id=1, source_target_pairs={{0,8},{2,10},{4,12},{6,14},{8,0},{10,2},{12,4},{14,6},{1,9},{3,11}... | collective-permute-start | bytes 294920 | tf_op jit(solution)/shard_map/ppermute | solution.py:17
  54.7 0.0 collective-permute-done.10
  54.7 1.9 %collective-permute-done.11 = bf16[16,3072]{1,0:T(8,128)(2,1)S(1)} collective-permute-done((bf16[16,3072]{1,0:T(8,128)(2,1)S(1)}, bf16[16,3072]{1,0:T(8,128)(2,1)S(1)}, u32[]{:S(2)}, u32[]{:S(2)}) %collective-permute-start.11) | collective-permute-done | bytes 98336 | tf_op jit(solution)/shard_map/ppermute | solution.py:17
  56.6 0.0 collective-permute-done.12
  56.6 3.2 %collective-permute-done.16 = bf16[16,3072]{1,0:T(8,128)(2,1)S(1)} collective-permute-done((bf16[16,3072]{1,0:T(8,128)(2,1)S(1)}, bf16[16,3072]{1,0:T(8,128)(2,1)S(1)}, u32[]{:S(2)}, u32[]{:S(2)}) %collective-permute-start.16) | collective-permute-done | bytes 98336 | tf_op jit(solution)/shard_map/ppermute | solution.py:17
  59.8 0.7 %add_convert_fusion = bf16[16,3072]{1,0:T(8,128)(2,1)} fusion(bf16[16,3072]{1,0:T(8,128)(2,1)S(1)} %collective-permute-done.16, bf16[16,3072]{1,0:T(8,128)(2,1)S(1)} %collective-permute-done.12, bf16[16,3072]{1,0:T(8,128)(2,1)S(1)} %collective-permute-done.11, f32[16,3072]{1,0:T(8,128)S(1)} %get-tuple-element.45, bf16[16,3072]{1,0:T(8,128)(2,1)S(1)} %collective-permute-done.10), kind=kLoop, calls=%fused_computation | loop fusion | flops 442368 | bytes 688128 | tf_op jit(solution)/shard_map/convert_element_type | solution.py:288
  (12 shorter events, 0.0 us)
Async XLA Ops:
  0.0 8.7 %copy-start = (bf16[3072,4]{0,1:T(4,128)(2,1)S(1)}, bf16[3072,4]{0,1:T(4,128)(2,1)}, u32[]{:S(2)}) copy-start(bf16[3072,4]{0,1:T(4,128)(2,1)} %param.8) | copy-start | bytes 73732
  0.0 18.1 %slice-start = ((s8[25165824]{0:T(1024)(128)(4,1)}), s8[4194304]{0:T(1024)(128)(4,1)S(1)}, s32[]{:S(2)}) async-start(s8[25165824]{0:T(1024)(128)(4,1)} %bitcast.2), calls=%async_computation | async-start | bytes 8388608
  0.0 18.1 %slice-start.1 = ((s8[25165824]{0:T(1024)(128)(4,1)}), s8[4194304]{0:T(1024)(128)(4,1)S(1)}, s32[]{:S(2)}) async-start(s8[25165824]{0:T(1024)(128)(4,1)} %bitcast.2), calls=%async_computation.1 | async-start | bytes 8388608
  0.0 18.1 %slice-start.2 = ((s8[25165824]{0:T(1024)(128)(4,1)}), s8[4194304]{0:T(1024)(128)(4,1)S(1)}, s32[]{:S(2)}) async-start(s8[25165824]{0:T(1024)(128)(4,1)} %bitcast.2), calls=%async_computation.2 | async-start | bytes 8388608
  0.0 18.1 %slice-start.3 = ((s8[25165824]{0:T(1024)(128)(4,1)}), s8[4194304]{0:T(1024)(128)(4,1)S(1)}, s32[]{:S(2)}) async-start(s8[25165824]{0:T(1024)(128)(4,1)} %bitcast.2), calls=%async_computation.3 | async-start | bytes 8388608
  0.0 18.1 %slice-start.4 = ((s8[25165824]{0:T(1024)(128)(4,1)}), s8[4194304]{0:T(1024)(128)(4,1)S(1)}, s32[]{:S(2)}) async-start(s8[25165824]{0:T(1024)(128)(4,1)} %bitcast.2), calls=%async_computation.4 | async-start | bytes 8388608
  1.1 9.2 %collective-permute-start.3 = (bf16[16,3200]{1,0:T(8,128)(2,1)S(1)}, bf16[16,3200]{1,0:T(8,128)(2,1)S(1)}, u32[]{:S(2)}, u32[]{:S(2)}) collective-permute-start(bf16[16,3200]{1,0:T(8,128)(2,1)S(1)} %shard_map.64.refs_0_), channel_id=1, source_target_pairs={{0,8},{2,10},{4,12},{6,14},{8,0},{10,2},{12,4},{14,6},{1,9},{3,11}... | collective-permute-start | bytes 307208 | tf_op jit(solution)/shard_map/ppermute | solution.py:17
  5.2 8.2 %collective-permute-start.2 = (bf16[16,3200]{1,0:T(8,128)(2,1)S(1)}, bf16[16,3200]{1,0:T(8,128)(2,1)S(1)}, u32[]{:S(2)}, u32[]{:S(2)}) collective-permute-start(bf16[16,3200]{1,0:T(8,128)(2,1)S(1)} %shard_map.64.refs_0_), channel_id=1, source_target_pairs={{0,6},{2,4},{4,2},{6,0},{8,14},{10,12},{12,10},{14,8},{1,7},{3,5},... | collective-permute-start | bytes 307208 | tf_op jit(solution)/shard_map/ppermute | solution.py:17
  7.8 9.8 %collective-permute-start.1 = (bf16[16,3200]{1,0:T(8,128)(2,1)S(1)}, bf16[16,3200]{1,0:T(8,128)(2,1)S(1)}, u32[]{:S(2)}, u32[]{:S(2)}) collective-permute-start(bf16[16,3200]{1,0:T(8,128)(2,1)S(1)} %shard_map.64.refs_0_), channel_id=1, source_target_pairs={{0,4},{2,6},{4,0},{6,2},{8,12},{10,14},{12,8},{14,10},{1,5},{3,7},... | collective-permute-start | bytes 307208 | tf_op jit(solution)/shard_map/ppermute | solution.py:17
  8.2 9.3 %collective-permute-start = (bf16[16,3200]{1,0:T(8,128)(2,1)S(1)}, bf16[16,3200]{1,0:T(8,128)(2,1)S(1)}, u32[]{:S(2)}, u32[]{:S(2)}) collective-permute-start(bf16[16,3200]{1,0:T(8,128)(2,1)S(1)} %shard_map.64.refs_0_), channel_id=1, source_target_pairs={{0,2},{2,0},{4,6},{6,4},{8,10},{10,8},{12,14},{14,12},{1,3},{3,1},... | collective-permute-start | bytes 307208 | tf_op jit(solution)/shard_map/ppermute | solution.py:17
  10.3 7.8 %slice-start.5 = ((s8[25165824]{0:T(1024)(128)(4,1)}), s8[4194304]{0:T(1024)(128)(4,1)S(1)}, s32[]{:S(2)}) async-start(s8[25165824]{0:T(1024)(128)(4,1)} %bitcast.2), calls=%async_computation.5 | async-start | bytes 8388608
  10.3 7.3 %collective-permute-start.6 = (bf16[16,3200]{1,0:T(8,128)(2,1)S(1)}, bf16[16,3200]{1,0:T(8,128)(2,1)S(1)}, u32[]{:S(2)}, u32[]{:S(2)}) collective-permute-start(bf16[16,3200]{1,0:T(8,128)(2,1)S(1)} %collective-permute-done.3.refs_4_), channel_id=1, source_target_pairs={{0,6},{2,4},{4,2},{6,0},{8,14},{10,12},{12,10},{14,8},{1,7},{3,5},... | collective-permute-start | bytes 307208 | tf_op jit(solution)/shard_map/ppermute | solution.py:17
  12.0 6.1 %collective-permute-start.5 = (bf16[16,3200]{1,0:T(8,128)(2,1)S(1)}, bf16[16,3200]{1,0:T(8,128)(2,1)S(1)}, u32[]{:S(2)}, u32[]{:S(2)}) collective-permute-start(bf16[16,3200]{1,0:T(8,128)(2,1)S(1)} %collective-permute-done.3.refs_4_), channel_id=1, source_target_pairs={{0,4},{2,6},{4,0},{6,2},{8,12},{10,14},{12,8},{14,10},{1,5},{3,7},... | collective-permute-start | bytes 307208 | tf_op jit(solution)/shard_map/ppermute | solution.py:17
  13.4 4.7 %collective-permute-start.4 = (bf16[16,3200]{1,0:T(8,128)(2,1)S(1)}, bf16[16,3200]{1,0:T(8,128)(2,1)S(1)}, u32[]{:S(2)}, u32[]{:S(2)}) collective-permute-start(bf16[16,3200]{1,0:T(8,128)(2,1)S(1)} %collective-permute-done.3.refs_4_), channel_id=1, source_target_pairs={{0,2},{2,0},{4,6},{6,4},{8,10},{10,8},{12,14},{14,12},{1,3},{3,1},... | collective-permute-start | bytes 307208 | tf_op jit(solution)/shard_map/ppermute | solution.py:17
  28.6 7.9 %collective-permute-start.7 = (f32[4224,128]{1,0:T(8,128)S(1)}, f32[4224,128]{1,0:T(8,128)S(1)}, u32[]{:S(2)}, u32[]{:S(2)}) collective-permute-start(f32[4224,128]{1,0:T(8,128)S(1)} %get-tuple-element.32.gate_a), channel_id=1, source_target_pairs={{0,1},{1,0},{2,3},{3,2},{4,5},{5,4},{6,7},{7,6},{8,9},{9,8},{10,11... | collective-permute-start | bytes 6488072 | tf_op jit(solution)/shard_map/ppermute | solution.py:240
  32.5 4.1 %collective-permute-start.9 = (bf16[2048,128]{1,0:T(8,128)(2,1)S(1)}, bf16[2048,128]{1,0:T(8,128)(2,1)S(1)}, u32[]{:S(2)}, u32[]{:S(2)}) collective-permute-start(bf16[2048,128]{1,0:T(8,128)(2,1)S(1)} %get-tuple-element.40), channel_id=1, source_target_pairs={{0,1},{1,0},{2,3},{3,2},{4,5},{5,4},{6,7},{7,6},{8,9},{9,8},{10,11... | collective-permute-start | bytes 1572872 | tf_op jit(solution)/shard_map/ppermute | solution.py:258
  36.5 2.9 %collective-permute-start.8 = (bf16[2048,128]{1,0:T(8,128)(2,1)S(1)}, bf16[2048,128]{1,0:T(8,128)(2,1)S(1)}, u32[]{:S(2)}, u32[]{:S(2)}) collective-permute-start(bf16[2048,128]{1,0:T(8,128)(2,1)S(1)} %get-tuple-element.38), channel_id=1, source_target_pairs={{0,1},{1,0},{2,3},{3,2},{4,5},{5,4},{6,7},{7,6},{8,9},{9,8},{10,11... | collective-permute-start | bytes 1572872 | tf_op jit(solution)/shard_map/ppermute | solution.py:258
  43.4 6.6 %collective-permute-start.13 = (bf16[16,3072]{1,0:T(8,128)(2,1)S(1)}, bf16[16,3072]{1,0:T(8,128)(2,1)S(1)}, u32[]{:S(2)}, u32[]{:S(2)}) collective-permute-start(bf16[16,3072]{1,0:T(8,128)(2,1)S(1)} %get-tuple-element.50), channel_id=1, source_target_pairs={{0,6},{2,4},{4,2},{6,0},{8,14},{10,12},{12,10},{14,8},{1,7},{3,5},... | collective-permute-start | bytes 294920 | tf_op jit(solution)/shard_map/ppermute | solution.py:17
  45.2 6.5 %collective-permute-start.14 = (bf16[16,3072]{1,0:T(8,128)(2,1)S(1)}, bf16[16,3072]{1,0:T(8,128)(2,1)S(1)}, u32[]{:S(2)}, u32[]{:S(2)}) collective-permute-start(bf16[16,3072]{1,0:T(8,128)(2,1)S(1)} %get-tuple-element.51), channel_id=1, source_target_pairs={{0,4},{2,6},{4,0},{6,2},{8,12},{10,14},{12,8},{14,10},{1,5},{3,7},... | collective-permute-start | bytes 294920 | tf_op jit(solution)/shard_map/ppermute | solution.py:17
  46.0 6.1 %collective-permute-start.15 = (bf16[16,3072]{1,0:T(8,128)(2,1)S(1)}, bf16[16,3072]{1,0:T(8,128)(2,1)S(1)}, u32[]{:S(2)}, u32[]{:S(2)}) collective-permute-start(bf16[16,3072]{1,0:T(8,128)(2,1)S(1)} %get-tuple-element.52), channel_id=1, source_target_pairs={{0,2},{2,0},{4,6},{6,4},{8,10},{10,8},{12,14},{14,12},{1,3},{3,1},... | collective-permute-start | bytes 294920 | tf_op jit(solution)/shard_map/ppermute | solution.py:17
  46.9 7.8 %collective-permute-start.10 = (bf16[16,3072]{1,0:T(8,128)(2,1)S(1)}, bf16[16,3072]{1,0:T(8,128)(2,1)S(1)}, u32[]{:S(2)}, u32[]{:S(2)}) collective-permute-start(bf16[16,3072]{1,0:T(8,128)(2,1)S(1)} %get-tuple-element.46), channel_id=1, source_target_pairs={{0,6},{2,4},{4,2},{6,0},{8,14},{10,12},{12,10},{14,8},{1,7},{3,5},... | collective-permute-start | bytes 294920 | tf_op jit(solution)/shard_map/ppermute | solution.py:17
  48.7 7.9 %collective-permute-start.11 = (bf16[16,3072]{1,0:T(8,128)(2,1)S(1)}, bf16[16,3072]{1,0:T(8,128)(2,1)S(1)}, u32[]{:S(2)}, u32[]{:S(2)}) collective-permute-start(bf16[16,3072]{1,0:T(8,128)(2,1)S(1)} %get-tuple-element.47), channel_id=1, source_target_pairs={{0,4},{2,6},{4,0},{6,2},{8,12},{10,14},{12,8},{14,10},{1,5},{3,7},... | collective-permute-start | bytes 294920 | tf_op jit(solution)/shard_map/ppermute | solution.py:17
  49.9 6.7 %collective-permute-start.12 = (bf16[16,3072]{1,0:T(8,128)(2,1)S(1)}, bf16[16,3072]{1,0:T(8,128)(2,1)S(1)}, u32[]{:S(2)}, u32[]{:S(2)}) collective-permute-start(bf16[16,3072]{1,0:T(8,128)(2,1)S(1)} %get-tuple-element.48), channel_id=1, source_target_pairs={{0,2},{2,0},{4,6},{6,4},{8,10},{10,8},{12,14},{14,12},{1,3},{3,1},... | collective-permute-start | bytes 294920 | tf_op jit(solution)/shard_map/ppermute | solution.py:17
  52.1 7.6 %collective-permute-start.16 = (bf16[16,3072]{1,0:T(8,128)(2,1)S(1)}, bf16[16,3072]{1,0:T(8,128)(2,1)S(1)}, u32[]{:S(2)}, u32[]{:S(2)}) collective-permute-start(bf16[16,3072]{1,0:T(8,128)(2,1)S(1)} %add_convert_fusion.1), channel_id=1, source_target_pairs={{0,8},{2,10},{4,12},{6,14},{8,0},{10,2},{12,4},{14,6},{1,9},{3,11}... | collective-permute-start | bytes 294920 | tf_op jit(solution)/shard_map/ppermute | solution.py:17

commit v9 on v8

--- a/solution.py
+++ b/solution.py
@@ -211,30 +211,29 @@
     one = pltpu.VMEM((hidden, width), BF16)
     part_of_one = pltpu.VMEM((hidden // 2, width), BF16)
     sems = lambda n: [pltpu.SemaphoreType.DMA((n,))]
-    up0, up1a = call(
-        functools.partial(fetch_kernel, (0, (1, 0))),
-        [one, part_of_one],
+    tile = hidden // 2
+    early = call(
+        functools.partial(fetch_kernel, ((0, 0), (0, tile), (1, 0))),
+        [part_of_one] * 3,
         [far[:, :128], w_up],
         8_000_000_000,
         0,
         1,
-        sems(2),
+        sems(3),
         hbm=(1,),
     )
-    x, gate, up1b, up2, up3a = call(
-        functools.partial(gate_kernel, ((1, hidden // 2), 2, (3, 0)), 2),
+    x, gate, *following = call(
+        functools.partial(gate_kernel, ((1, tile), (2, 0), (2, tile), (3, 0)), 3),
         [
             shape(count, width + IDS, dtype=BF16),
             shape(experts * hidden + count, count),
-            part_of_one,
-            one,
-            part_of_one,
+            *[part_of_one] * 4,
         ],
-        [*blocks, lines, w_gate, w_up, up0, up1a],
+        [*blocks, lines, w_gate, w_up, *early],
         experts * flops,
         experts * size,
         3,
-        sems(3),
+        sems(4),
         hbm=(10,),
     )
     gate_other = lax.ppermute(gate, "mp", SWAP)
@@ -258,9 +257,9 @@
         return (part, lax.ppermute(sent, "mp", SWAP)), held
 
     first, (up3b, down0) = up_call(
-        ((3, hidden // 2),), (0,), (up0, up1a, up1b), (part_of_one, one), (up3a,)
-    )
-    second, (down1,) = up_call((), (1,), (up2, up3a, up3b), (one,), ())
+        ((3, tile),), (0,), (*early, following[0]), (part_of_one, one), ()
+    )
+    second, (down1,) = up_call((), (1,), (*following[1:], up3b), (one,), ())
     units, down2 = call(
         functools.partial(hidden_kernel, range(half), (2,)),
         [shape(half, count, hidden, dtype=BF16)] + [one] * 1,

time: 60.6 us -> 57.2 us (0.944)
  Pallas kernels: 29.2 us -> 25.9 us
    pallas_call x7, Pallas kernels: 29.2 us -> 25.9 us  [call(): pl.pallas_call(kernel, out_shape=outs, in_specs=specs, out_specs=[VMEM_BL...]
  transfers between devices with their start and end apart: 17 -> 17, of which waited for: 7 -> 7; matrix products, arithmetic and copies ran while one was open for 0% -> 0% of each run, Pallas kernels for 23% -> 24%
where the time goes in v9:
time: 57.2 us; the launch traced here: 57.1 us
  Pallas kernels  25.9 us (45%)
  starting transfers between devices  21.9 us (38%)
  waiting for transfers between devices  8.28 us (14%)
  other arithmetic  0.76 us (1%)
    pallas_call x7, Pallas kernels, call(): pl.pallas_call(kernel, out_shape=outs, in_specs=specs, out_specs=[VMEM_BL...  25.9 us
    ppermute x14, starting transfers between devices, xor_send(): return lax.ppermute(block, 'batch', [(i, i ^ mask) for i in range(8)])  21.2 us
    ppermute x14, waiting for transfers between devices, xor_send(): return lax.ppermute(block, 'batch', [(i, i ^ mask) for i in range(8)])  8.27 us
  transfers between devices with their start and end apart: 17, of which 7 were waited for; matrix products, arithmetic and copies ran while one was open for 0% of the time, Pallas kernels for 24%

profile of v9, /device:TPU:0, one launch (start us, length us, event | category | flops | bytes accessed | tf_op | source)
XLA Modules:
  0.0 57.1 jit_solution(8657491088127123948)
XLA Ops:
  0.0 0.0 slice-start.4
  0.0 1.1 %shard_map.64.refs_0_ = bf16[16,3200]{1,0:T(8,128)(2,1)S(1)} custom-call(bf16[16,3072]{1,0:T(8,128)(2,1)} %tokens_ref.1, s32[2,16]{1,0:T(2,128)} %bitcast.5), custom_call_target="tpu_custom_call" | custom-call | flops 30000001024 | bytes 196608 | tf_op jit(solution)/shard_map/pallas_call | solution.py:26
  1.1 4.1 %collective-permute-start.3 = (bf16[16,3200]{1,0:T(8,128)(2,1)S(1)}, bf16[16,3200]{1,0:T(8,128)(2,1)S(1)}, u32[]{:S(2)}, u32[]{:S(2)}) collective-permute-start(bf16[16,3200]{1,0:T(8,128)(2,1)S(1)} %shard_map.64.refs_0_), channel_id=1, source_target_pairs={{0,8},{2,10},{4,12},{6,14},{8,0},{10,2},{12,4},{14,6},{1,9},{3,11}... | collective-permute-start | bytes 307208 | tf_op jit(solution)/shard_map/ppermute | solution.py:17
  5.2 2.5 %collective-permute-start.2 = (bf16[16,3200]{1,0:T(8,128)(2,1)S(1)}, bf16[16,3200]{1,0:T(8,128)(2,1)S(1)}, u32[]{:S(2)}, u32[]{:S(2)}) collective-permute-start(bf16[16,3200]{1,0:T(8,128)(2,1)S(1)} %shard_map.64.refs_0_), channel_id=1, source_target_pairs={{0,6},{2,4},{4,2},{6,0},{8,14},{10,12},{12,10},{14,8},{1,7},{3,5},... | collective-permute-start | bytes 307208 | tf_op jit(solution)/shard_map/ppermute | solution.py:17
  7.8 0.4 collective-permute-start.1
  8.2 0.5 collective-permute-start
  8.7 0.0 copy-done
  8.7 0.1 pad.4.refs_8_
  8.8 1.5 %collective-permute-done.3.refs_4_ = bf16[16,3200]{1,0:T(8,128)(2,1)S(1)} collective-permute-done((bf16[16,3200]{1,0:T(8,128)(2,1)S(1)}, bf16[16,3200]{1,0:T(8,128)(2,1)S(1)}, u32[]{:S(2)}, u32[]{:S(2)}) %collective-permute-start.3) | collective-permute-done | bytes 102432 | tf_op jit(solution)/shard_map/ppermute | solution.py:17
  10.3 1.7 %collective-permute-start.6 = (bf16[16,3200]{1,0:T(8,128)(2,1)S(1)}, bf16[16,3200]{1,0:T(8,128)(2,1)S(1)}, u32[]{:S(2)}, u32[]{:S(2)}) collective-permute-start(bf16[16,3200]{1,0:T(8,128)(2,1)S(1)} %collective-permute-done.3.refs_4_), channel_id=1, source_target_pairs={{0,6},{2,4},{4,2},{6,0},{8,14},{10,12},{12,10},{14,8},{1,7},{3,5},... | collective-permute-start | bytes 307208 | tf_op jit(solution)/shard_map/ppermute | solution.py:17
  12.0 1.4 %collective-permute-start.5 = (bf16[16,3200]{1,0:T(8,128)(2,1)S(1)}, bf16[16,3200]{1,0:T(8,128)(2,1)S(1)}, u32[]{:S(2)}, u32[]{:S(2)}) collective-permute-start(bf16[16,3200]{1,0:T(8,128)(2,1)S(1)} %collective-permute-done.3.refs_4_), channel_id=1, source_target_pairs={{0,4},{2,6},{4,0},{6,2},{8,12},{10,14},{12,8},{14,10},{1,5},{3,7},... | collective-permute-start | bytes 307208 | tf_op jit(solution)/shard_map/ppermute | solution.py:17
  13.4 0.0 collective-permute-done.2.refs_3_
  13.4 0.4 collective-permute-start.4
  13.8 3.8 %shard_map.65 = (bf16[512,3072]{1,0:T(8,128)(2,1)S(1)}, bf16[512,3072]{1,0:T(8,128)(2,1)S(1)}, bf16[512,3072]{1,0:T(8,128)(2,1)S(1)}) custom-call(bf16[16,128]{1,0:T(8,128)(2,1)S(1)} %slice.4._, bf16[4,1024,3072]{2,1,0:T(8,128)(2,1)} %up_ref.3), custom_call_target="tpu_custom_call" | custom-call | flops 8000000000 | tf_op jit(solution)/shard_map/pallas_call | solution.py:26
  17.6 0.0 collective-permute-done.1.refs_2_
  17.6 0.0 collective-permute-done.refs_1_
  17.6 0.0 collective-permute-done.6.refs_7_
  17.6 0.5 collective-permute-done.5.refs_6_
  18.1 0.0 collective-permute-done.4.refs_5_
  18.1 0.0 slice-done
  18.1 0.0 slice-done.1
  18.2 6.9 %shard_map.66 = (bf16[128,3200]{1,0:T(8,128)(2,1)S(1)}, f32[4224,128]{1,0:T(8,128)S(1)}, bf16[512,3072]{1,0:T(8,128)(2,1)S(1)}, bf16[512,3072]{1,0:T(8,128)(2,1)...) custom-call(bf16[16,3200]{1,0:T(8,128)(2,1)S(1)} %shard_map.64.refs_0_, ...), custom_call_target="tpu_custom_call" | custom-call | flops 3221225472 | bytes 25165824 | tf_op jit(solution)/shard_map/pallas_call | solution.py:26
  25.1 0.1 collective-permute-start.7
  25.2 3.8 %shard_map.67 = (f32[2048,128]{1,0:T(8,128)S(1)}, bf16[2048,128]{1,0:T(8,128)(2,1)S(1)}, bf16[512,3072]{1,0:T(8,128)(2,1)S(1)}, bf16[1024,3072]{1,0:T(8,128)(2,1)S(1)}) custom-call(bf16[128,3200]{1,0:T(8,128)(2,1)S(1)} %get-tuple-element.34.x_ref, bf16[4,1024,3072]{2,1,0:T(8,128)(2,1)} %up_ref.3, bf16[4,1024,3072]{2,1,0:T(8,128)(2,1)} %down_ref.7, ...), custom_call_target="tpu_custom_call" | custom-call | flops 1610612736 | bytes 12582912 | tf_op jit(solution)/shard_map/pallas_call | solution.py:26
  28.9 0.6 collective-permute-start.9
  29.5 3.4 %shard_map.68 = (f32[2048,128]{1,0:T(8,128)S(1)}, bf16[2048,128]{1,0:T(8,128)(2,1)S(1)}, bf16[1024,3072]{1,0:T(8,128)(2,1)S(1)}) custom-call(bf16[128,3200]{1,0:T(8,128)(2,1)S(1)} %get-tuple-element.34.x_ref, bf16[4,1024,3072]{2,1,0:T(8,128)(2,1)} %up_ref.3, bf16[4,1024,3072]{2,1,0:T(8,128)(2,1)} %down_ref.7, ...), custom_call_target="tpu_custom_call" | custom-call | flops 1610612736 | bytes 12582912 | tf_op jit(solution)/shard_map/pallas_call | solution.py:26
  32.9 0.1 collective-permute-start.8
  33.0 0.0 collective-permute-done.9.up_b
  33.0 0.0 collective-permute-done.7.gate_b
  33.0 2.8 %shard_map.69 = (bf16[2,128,1024]{2,1,0:T(8,128)(2,1)S(1)}, bf16[1024,3072]{1,0:T(8,128)(2,1)S(1)}) custom-call(f32[4224,128]{1,0:T(8,128)S(1)} %get-tuple-element.35.gate_a, f32[4224,128]{1,0:T(8,128)S(1)} %collective-permute-done.7.gate_b, f32[2048,128]{1,0:T(8,128)S(1)} %get-tuple-element.43.up_a, bf16[2048,128]{1,0:T(8,128)(2,1)S(1)} %collective-permute-done.9.up_b, ...), custom_call_target="tpu_custom_call" | custom-call | bytes 3145728 | tf_op jit(solution)/shard_map/pallas_call | solution.py:26
  35.8 0.0 collective-permute-done.8.up_b
  35.8 4.1 %shard_map.70 = (f32[16,3072]{1,0:T(8,128)S(1)}, bf16[16,3072]{1,0:T(8,128)(2,1)S(1)}, bf16[16,3072]{1,0:T(8,128)(2,1)S(1)}, bf16[16,3072]{1,0:T(8,128)(2,1)S(1)...) custom-call(bf16[128,3200]{1,0:T(8,128)(2,1)S(1)} %get-tuple-element, ...), custom_call_target="tpu_custom_call" | custom-call | flops 3221225472 | bytes 25165824 | tf_op jit(solution)/shard_map/pallas_call | solution.py:26
  39.9 1.8 %collective-permute-start.13 = (bf16[16,3072]{1,0:T(8,128)(2,1)S(1)}, bf16[16,3072]{1,0:T(8,128)(2,1)S(1)}, u32[]{:S(2)}, u32[]{:S(2)}) collective-permute-start(bf16[16,3072]{1,0:T(8,128)(2,1)S(1)} %get-tuple-element.54), channel_id=1, source_target_pairs={{0,6},{2,4},{4,2},{6,0},{8,14},{10,12},{12,10},{14,8},{1,7},{3,5},... | collective-permute-start | bytes 294920 | tf_op jit(solution)/shard_map/ppermute | solution.py:17
  41.8 0.9 %collective-permute-start.14 = (bf16[16,3072]{1,0:T(8,128)(2,1)S(1)}, bf16[16,3072]{1,0:T(8,128)(2,1)S(1)}, u32[]{:S(2)}, u32[]{:S(2)}) collective-permute-start(bf16[16,3072]{1,0:T(8,128)(2,1)S(1)} %get-tuple-element.55), channel_id=1, source_target_pairs={{0,4},{2,6},{4,0},{6,2},{8,12},{10,14},{12,8},{14,10},{1,5},{3,7},... | collective-permute-start | bytes 294920 | tf_op jit(solution)/shard_map/ppermute | solution.py:17
  42.7 0.8 %collective-permute-start.15 = (bf16[16,3072]{1,0:T(8,128)(2,1)S(1)}, bf16[16,3072]{1,0:T(8,128)(2,1)S(1)}, u32[]{:S(2)}, u32[]{:S(2)}) collective-permute-start(bf16[16,3072]{1,0:T(8,128)(2,1)S(1)} %get-tuple-element.56), channel_id=1, source_target_pairs={{0,2},{2,0},{4,6},{6,4},{8,10},{10,8},{12,14},{14,12},{1,3},{3,1},... | collective-permute-start | bytes 294920 | tf_op jit(solution)/shard_map/ppermute | solution.py:17
  43.5 1.8 %collective-permute-start.10 = (bf16[16,3072]{1,0:T(8,128)(2,1)S(1)}, bf16[16,3072]{1,0:T(8,128)(2,1)S(1)}, u32[]{:S(2)}, u32[]{:S(2)}) collective-permute-start(bf16[16,3072]{1,0:T(8,128)(2,1)S(1)} %get-tuple-element.50), channel_id=1, source_target_pairs={{0,6},{2,4},{4,2},{6,0},{8,14},{10,12},{12,10},{14,8},{1,7},{3,5},... | collective-permute-start | bytes 294920 | tf_op jit(solution)/shard_map/ppermute | solution.py:17
  45.3 0.9 %collective-permute-start.11 = (bf16[16,3072]{1,0:T(8,128)(2,1)S(1)}, bf16[16,3072]{1,0:T(8,128)(2,1)S(1)}, u32[]{:S(2)}, u32[]{:S(2)}) collective-permute-start(bf16[16,3072]{1,0:T(8,128)(2,1)S(1)} %get-tuple-element.51), channel_id=1, source_target_pairs={{0,4},{2,6},{4,0},{6,2},{8,12},{10,14},{12,8},{14,10},{1,5},{3,7},... | collective-permute-start | bytes 294920 | tf_op jit(solution)/shard_map/ppermute | solution.py:17
  46.2 0.3 collective-permute-done.13
  46.5 1.2 %collective-permute-start.12 = (bf16[16,3072]{1,0:T(8,128)(2,1)S(1)}, bf16[16,3072]{1,0:T(8,128)(2,1)S(1)}, u32[]{:S(2)}, u32[]{:S(2)}) collective-permute-start(bf16[16,3072]{1,0:T(8,128)(2,1)S(1)} %get-tuple-element.52), channel_id=1, source_target_pairs={{0,2},{2,0},{4,6},{6,4},{8,10},{10,8},{12,14},{14,12},{1,3},{3,1},... | collective-permute-start | bytes 294920 | tf_op jit(solution)/shard_map/ppermute | solution.py:17
  47.7 0.6 %collective-permute-done.14 = bf16[16,3072]{1,0:T(8,128)(2,1)S(1)} collective-permute-done((bf16[16,3072]{1,0:T(8,128)(2,1)S(1)}, bf16[16,3072]{1,0:T(8,128)(2,1)S(1)}, u32[]{:S(2)}, u32[]{:S(2)}) %collective-permute-start.14) | collective-permute-done | bytes 98336 | tf_op jit(solution)/shard_map/ppermute | solution.py:17
  48.4 0.3 collective-permute-done.15
  48.7 0.1 add_convert_fusion.1
  48.7 2.6 %collective-permute-start.16 = (bf16[16,3072]{1,0:T(8,128)(2,1)S(1)}, bf16[16,3072]{1,0:T(8,128)(2,1)S(1)}, u32[]{:S(2)}, u32[]{:S(2)}) collective-permute-start(bf16[16,3072]{1,0:T(8,128)(2,1)S(1)} %add_convert_fusion.1), channel_id=1, source_target_pairs={{0,8},{2,10},{4,12},{6,14},{8,0},{10,2},{12,4},{14,6},{1,9},{3,11}... | collective-permute-start | bytes 294920 | tf_op jit(solution)/shard_map/ppermute | solution.py:17
  51.4 0.0 collective-permute-done.10
  51.4 1.9 %collective-permute-done.11 = bf16[16,3072]{1,0:T(8,128)(2,1)S(1)} collective-permute-done((bf16[16,3072]{1,0:T(8,128)(2,1)S(1)}, bf16[16,3072]{1,0:T(8,128)(2,1)S(1)}, u32[]{:S(2)}, u32[]{:S(2)}) %collective-permute-start.11) | collective-permute-done | bytes 98336 | tf_op jit(solution)/shard_map/ppermute | solution.py:17
  53.3 0.0 collective-permute-done.12
  53.3 3.1 %collective-permute-done.16 = bf16[16,3072]{1,0:T(8,128)(2,1)S(1)} collective-permute-done((bf16[16,3072]{1,0:T(8,128)(2,1)S(1)}, bf16[16,3072]{1,0:T(8,128)(2,1)S(1)}, u32[]{:S(2)}, u32[]{:S(2)}) %collective-permute-start.16) | collective-permute-done | bytes 98336 | tf_op jit(solution)/shard_map/ppermute | solution.py:17
  56.4 0.7 %add_convert_fusion = bf16[16,3072]{1,0:T(8,128)(2,1)} fusion(bf16[16,3072]{1,0:T(8,128)(2,1)S(1)} %collective-permute-done.16, bf16[16,3072]{1,0:T(8,128)(2,1)S(1)} %collective-permute-done.12, bf16[16,3072]{1,0:T(8,128)(2,1)S(1)} %collective-permute-done.11, f32[16,3072]{1,0:T(8,128)S(1)} %get-tuple-element.49, bf16[16,3072]{1,0:T(8,128)(2,1)S(1)} %collective-permute-done.10), kind=kLoop, calls=%fused_computation | loop fusion | flops 442368 | bytes 688128 | tf_op jit(solution)/shard_map/convert_element_type | solution.py:287
  (12 shorter events, 0.0 us)
Async XLA Ops:
  0.0 8.7 %copy-start = (bf16[3072,4]{0,1:T(4,128)(2,1)S(1)}, bf16[3072,4]{0,1:T(4,128)(2,1)}, u32[]{:S(2)}) copy-start(bf16[3072,4]{0,1:T(4,128)(2,1)} %param.8) | copy-start | bytes 73732
  0.0 18.1 %slice-start = ((s8[25165824]{0:T(1024)(128)(4,1)}), s8[4194304]{0:T(1024)(128)(4,1)S(1)}, s32[]{:S(2)}) async-start(s8[25165824]{0:T(1024)(128)(4,1)} %bitcast.2), calls=%async_computation | async-start | bytes 8388608
  0.0 18.1 %slice-start.1 = ((s8[25165824]{0:T(1024)(128)(4,1)}), s8[4194304]{0:T(1024)(128)(4,1)S(1)}, s32[]{:S(2)}) async-start(s8[25165824]{0:T(1024)(128)(4,1)} %bitcast.2), calls=%async_computation.1 | async-start | bytes 8388608
  0.0 18.1 %slice-start.2 = ((s8[25165824]{0:T(1024)(128)(4,1)}), s8[4194304]{0:T(1024)(128)(4,1)S(1)}, s32[]{:S(2)}) async-start(s8[25165824]{0:T(1024)(128)(4,1)} %bitcast.2), calls=%async_computation.2 | async-start | bytes 8388608
  0.0 18.1 %slice-start.3 = ((s8[25165824]{0:T(1024)(128)(4,1)}), s8[4194304]{0:T(1024)(128)(4,1)S(1)}, s32[]{:S(2)}) async-start(s8[25165824]{0:T(1024)(128)(4,1)} %bitcast.2), calls=%async_computation.3 | async-start | bytes 8388608
  0.0 18.1 %slice-start.4 = ((s8[25165824]{0:T(1024)(128)(4,1)}), s8[4194304]{0:T(1024)(128)(4,1)S(1)}, s32[]{:S(2)}) async-start(s8[25165824]{0:T(1024)(128)(4,1)} %bitcast.2), calls=%async_computation.4 | async-start | bytes 8388608
  1.1 9.2 %collective-permute-start.3 = (bf16[16,3200]{1,0:T(8,128)(2,1)S(1)}, bf16[16,3200]{1,0:T(8,128)(2,1)S(1)}, u32[]{:S(2)}, u32[]{:S(2)}) collective-permute-start(bf16[16,3200]{1,0:T(8,128)(2,1)S(1)} %shard_map.64.refs_0_), channel_id=1, source_target_pairs={{0,8},{2,10},{4,12},{6,14},{8,0},{10,2},{12,4},{14,6},{1,9},{3,11}... | collective-permute-start | bytes 307208 | tf_op jit(solution)/shard_map/ppermute | solution.py:17
  5.2 8.2 %collective-permute-start.2 = (bf16[16,3200]{1,0:T(8,128)(2,1)S(1)}, bf16[16,3200]{1,0:T(8,128)(2,1)S(1)}, u32[]{:S(2)}, u32[]{:S(2)}) collective-permute-start(bf16[16,3200]{1,0:T(8,128)(2,1)S(1)} %shard_map.64.refs_0_), channel_id=1, source_target_pairs={{0,6},{2,4},{4,2},{6,0},{8,14},{10,12},{12,10},{14,8},{1,7},{3,5},... | collective-permute-start | bytes 307208 | tf_op jit(solution)/shard_map/ppermute | solution.py:17
  7.8 9.8 %collective-permute-start.1 = (bf16[16,3200]{1,0:T(8,128)(2,1)S(1)}, bf16[16,3200]{1,0:T(8,128)(2,1)S(1)}, u32[]{:S(2)}, u32[]{:S(2)}) collective-permute-start(bf16[16,3200]{1,0:T(8,128)(2,1)S(1)} %shard_map.64.refs_0_), channel_id=1, source_target_pairs={{0,4},{2,6},{4,0},{6,2},{8,12},{10,14},{12,8},{14,10},{1,5},{3,7},... | collective-permute-start | bytes 307208 | tf_op jit(solution)/shard_map/ppermute | solution.py:17
  8.2 9.4 %collective-permute-start = (bf16[16,3200]{1,0:T(8,128)(2,1)S(1)}, bf16[16,3200]{1,0:T(8,128)(2,1)S(1)}, u32[]{:S(2)}, u32[]{:S(2)}) collective-permute-start(bf16[16,3200]{1,0:T(8,128)(2,1)S(1)} %shard_map.64.refs_0_), channel_id=1, source_target_pairs={{0,2},{2,0},{4,6},{6,4},{8,10},{10,8},{12,14},{14,12},{1,3},{3,1},... | collective-permute-start | bytes 307208 | tf_op jit(solution)/shard_map/ppermute | solution.py:17
  10.3 7.8 %slice-start.5 = ((s8[25165824]{0:T(1024)(128)(4,1)}), s8[4194304]{0:T(1024)(128)(4,1)S(1)}, s32[]{:S(2)}) async-start(s8[25165824]{0:T(1024)(128)(4,1)} %bitcast.2), calls=%async_computation.5 | async-start | bytes 8388608
  10.3 7.3 %collective-permute-start.6 = (bf16[16,3200]{1,0:T(8,128)(2,1)S(1)}, bf16[16,3200]{1,0:T(8,128)(2,1)S(1)}, u32[]{:S(2)}, u32[]{:S(2)}) collective-permute-start(bf16[16,3200]{1,0:T(8,128)(2,1)S(1)} %collective-permute-done.3.refs_4_), channel_id=1, source_target_pairs={{0,6},{2,4},{4,2},{6,0},{8,14},{10,12},{12,10},{14,8},{1,7},{3,5},... | collective-permute-start | bytes 307208 | tf_op jit(solution)/shard_map/ppermute | solution.py:17
  12.0 6.1 %collective-permute-start.5 = (bf16[16,3200]{1,0:T(8,128)(2,1)S(1)}, bf16[16,3200]{1,0:T(8,128)(2,1)S(1)}, u32[]{:S(2)}, u32[]{:S(2)}) collective-permute-start(bf16[16,3200]{1,0:T(8,128)(2,1)S(1)} %collective-permute-done.3.refs_4_), channel_id=1, source_target_pairs={{0,4},{2,6},{4,0},{6,2},{8,12},{10,14},{12,8},{14,10},{1,5},{3,7},... | collective-permute-start | bytes 307208 | tf_op jit(solution)/shard_map/ppermute | solution.py:17
  13.4 4.7 %collective-permute-start.4 = (bf16[16,3200]{1,0:T(8,128)(2,1)S(1)}, bf16[16,3200]{1,0:T(8,128)(2,1)S(1)}, u32[]{:S(2)}, u32[]{:S(2)}) collective-permute-start(bf16[16,3200]{1,0:T(8,128)(2,1)S(1)} %collective-permute-done.3.refs_4_), channel_id=1, source_target_pairs={{0,2},{2,0},{4,6},{6,4},{8,10},{10,8},{12,14},{14,12},{1,3},{3,1},... | collective-permute-start | bytes 307208 | tf_op jit(solution)/shard_map/ppermute | solution.py:17
  25.1 7.9 %collective-permute-start.7 = (f32[4224,128]{1,0:T(8,128)S(1)}, f32[4224,128]{1,0:T(8,128)S(1)}, u32[]{:S(2)}, u32[]{:S(2)}) collective-permute-start(f32[4224,128]{1,0:T(8,128)S(1)} %get-tuple-element.35.gate_a), channel_id=1, source_target_pairs={{0,1},{1,0},{2,3},{3,2},{4,5},{5,4},{6,7},{7,6},{8,9},{9,8},{10,11... | collective-permute-start | bytes 6488072 | tf_op jit(solution)/shard_map/ppermute | solution.py:239
  28.9 4.1 %collective-permute-start.9 = (bf16[2048,128]{1,0:T(8,128)(2,1)S(1)}, bf16[2048,128]{1,0:T(8,128)(2,1)S(1)}, u32[]{:S(2)}, u32[]{:S(2)}) collective-permute-start(bf16[2048,128]{1,0:T(8,128)(2,1)S(1)} %get-tuple-element.44), channel_id=1, source_target_pairs={{0,1},{1,0},{2,3},{3,2},{4,5},{5,4},{6,7},{7,6},{8,9},{9,8},{10,11... | collective-permute-start | bytes 1572872 | tf_op jit(solution)/shard_map/ppermute | solution.py:257
  32.9 2.9 %collective-permute-start.8 = (bf16[2048,128]{1,0:T(8,128)(2,1)S(1)}, bf16[2048,128]{1,0:T(8,128)(2,1)S(1)}, u32[]{:S(2)}, u32[]{:S(2)}) collective-permute-start(bf16[2048,128]{1,0:T(8,128)(2,1)S(1)} %get-tuple-element.42), channel_id=1, source_target_pairs={{0,1},{1,0},{2,3},{3,2},{4,5},{5,4},{6,7},{7,6},{8,9},{9,8},{10,11... | collective-permute-start | bytes 1572872 | tf_op jit(solution)/shard_map/ppermute | solution.py:257
  39.9 6.6 %collective-permute-start.13 = (bf16[16,3072]{1,0:T(8,128)(2,1)S(1)}, bf16[16,3072]{1,0:T(8,128)(2,1)S(1)}, u32[]{:S(2)}, u32[]{:S(2)}) collective-permute-start(bf16[16,3072]{1,0:T(8,128)(2,1)S(1)} %get-tuple-element.54), channel_id=1, source_target_pairs={{0,6},{2,4},{4,2},{6,0},{8,14},{10,12},{12,10},{14,8},{1,7},{3,5},... | collective-permute-start | bytes 294920 | tf_op jit(solution)/shard_map/ppermute | solution.py:17
  41.8 6.6 %collective-permute-start.14 = (bf16[16,3072]{1,0:T(8,128)(2,1)S(1)}, bf16[16,3072]{1,0:T(8,128)(2,1)S(1)}, u32[]{:S(2)}, u32[]{:S(2)}) collective-permute-start(bf16[16,3072]{1,0:T(8,128)(2,1)S(1)} %get-tuple-element.55), channel_id=1, source_target_pairs={{0,4},{2,6},{4,0},{6,2},{8,12},{10,14},{12,8},{14,10},{1,5},{3,7},... | collective-permute-start | bytes 294920 | tf_op jit(solution)/shard_map/ppermute | solution.py:17
  42.7 6.0 %collective-permute-start.15 = (bf16[16,3072]{1,0:T(8,128)(2,1)S(1)}, bf16[16,3072]{1,0:T(8,128)(2,1)S(1)}, u32[]{:S(2)}, u32[]{:S(2)}) collective-permute-start(bf16[16,3072]{1,0:T(8,128)(2,1)S(1)} %get-tuple-element.56), channel_id=1, source_target_pairs={{0,2},{2,0},{4,6},{6,4},{8,10},{10,8},{12,14},{14,12},{1,3},{3,1},... | collective-permute-start | bytes 294920 | tf_op jit(solution)/shard_map/ppermute | solution.py:17
  43.5 7.9 %collective-permute-start.10 = (bf16[16,3072]{1,0:T(8,128)(2,1)S(1)}, bf16[16,3072]{1,0:T(8,128)(2,1)S(1)}, u32[]{:S(2)}, u32[]{:S(2)}) collective-permute-start(bf16[16,3072]{1,0:T(8,128)(2,1)S(1)} %get-tuple-element.50), channel_id=1, source_target_pairs={{0,6},{2,4},{4,2},{6,0},{8,14},{10,12},{12,10},{14,8},{1,7},{3,5},... | collective-permute-start | bytes 294920 | tf_op jit(solution)/shard_map/ppermute | solution.py:17
  45.3 8.0 %collective-permute-start.11 = (bf16[16,3072]{1,0:T(8,128)(2,1)S(1)}, bf16[16,3072]{1,0:T(8,128)(2,1)S(1)}, u32[]{:S(2)}, u32[]{:S(2)}) collective-permute-start(bf16[16,3072]{1,0:T(8,128)(2,1)S(1)} %get-tuple-element.51), channel_id=1, source_target_pairs={{0,4},{2,6},{4,0},{6,2},{8,12},{10,14},{12,8},{14,10},{1,5},{3,7},... | collective-permute-start | bytes 294920 | tf_op jit(solution)/shard_map/ppermute | solution.py:17
  46.5 6.8 %collective-permute-start.12 = (bf16[16,3072]{1,0:T(8,128)(2,1)S(1)}, bf16[16,3072]{1,0:T(8,128)(2,1)S(1)}, u32[]{:S(2)}, u32[]{:S(2)}) collective-permute-start(bf16[16,3072]{1,0:T(8,128)(2,1)S(1)} %get-tuple-element.52), channel_id=1, source_target_pairs={{0,2},{2,0},{4,6},{6,4},{8,10},{10,8},{12,14},{14,12},{1,3},{3,1},... | collective-permute-start | bytes 294920 | tf_op jit(solution)/shard_map/ppermute | solution.py:17
  48.7 7.6 %collective-permute-start.16 = (bf16[16,3072]{1,0:T(8,128)(2,1)S(1)}, bf16[16,3072]{1,0:T(8,128)(2,1)S(1)}, u32[]{:S(2)}, u32[]{:S(2)}) collective-permute-start(bf16[16,3072]{1,0:T(8,128)(2,1)S(1)} %add_convert_fusion.1), channel_id=1, source_target_pairs={{0,8},{2,10},{4,12},{6,14},{8,0},{10,2},{12,4},{14,6},{1,9},{3,11}... | collective-permute-start | bytes 294920 | tf_op jit(solution)/shard_map/ppermute | solution.py:17

commit v10 on v9

--- a/solution.py
+++ b/solution.py
@@ -281,7 +281,7 @@
         hbm=(6,),
     )
     far_sums = [xor_send(parts[4 ^ k], k) for k in (3, 2, 1)]
-    near_sums = [xor_send(parts[k], k) for k in (3, 2, 1)]
+    near_sums = [xor_send(parts[k], k) for k in (2, 1, 3)]
     add = lambda arrays: sum(a.astype(F32) for a in arrays)
     crossing = xor_send(add([parts[4], *far_sums]).astype(BF16), 4)
     return add([parts[0], *near_sums, crossing]).astype(BF16)

time: 57.2 us -> 57.2 us (level)
  waiting for transfers between devices: 8.28 us -> 7.36 us
  starting transfers between devices: 21.9 us -> 22.8 us
    ppermute x14, waiting for transfers between devices: 8.27 us -> 7.36 us  [xor_send(): return lax.ppermute(block, 'batch', [(i, i ^ mask) for i in range(8)])]
    ppermute x14, starting transfers between devices: 21.2 us -> 22.1 us  [xor_send(): return lax.ppermute(block, 'batch', [(i, i ^ mask) for i in range(8)])]
where the time goes in v10:
time: 57.2 us; the launch traced here: 57 us
  Pallas kernels  25.9 us (45%)
  starting transfers between devices  22.8 us (40%)
  waiting for transfers between devices  7.36 us (13%)
  other arithmetic  0.76 us (1%)
    pallas_call x7, Pallas kernels, call(): pl.pallas_call(kernel, out_shape=outs, in_specs=specs, out_specs=[VMEM_BL...  25.9 us
    ppermute x14, starting transfers between devices, xor_send(): return lax.ppermute(block, 'batch', [(i, i ^ mask) for i in range(8)])  22.1 us
    ppermute x14, waiting for transfers between devices, xor_send(): return lax.ppermute(block, 'batch', [(i, i ^ mask) for i in range(8)])  7.36 us
  transfers between devices with their start and end apart: 17, of which 7 were waited for; matrix products, arithmetic and copies ran while one was open for 0% of the time, Pallas kernels for 24%

profile of v10, /device:TPU:0, one launch (start us, length us, event | category | flops | bytes accessed | tf_op | source)
XLA Modules:
  0.0 57.0 jit_solution(12736143516145561091)
XLA Ops:
  0.0 0.0 slice-start.4
  0.0 1.1 %shard_map.64.refs_0_ = bf16[16,3200]{1,0:T(8,128)(2,1)S(1)} custom-call(bf16[16,3072]{1,0:T(8,128)(2,1)} %tokens_ref.1, s32[2,16]{1,0:T(2,128)} %bitcast.5), custom_call_target="tpu_custom_call" | custom-call | flops 30000001024 | bytes 196608 | tf_op jit(solution)/shard_map/pallas_call | solution.py:26
  1.1 4.1 %collective-permute-start.3 = (bf16[16,3200]{1,0:T(8,128)(2,1)S(1)}, bf16[16,3200]{1,0:T(8,128)(2,1)S(1)}, u32[]{:S(2)}, u32[]{:S(2)}) collective-permute-start(bf16[16,3200]{1,0:T(8,128)(2,1)S(1)} %shard_map.64.refs_0_), channel_id=1, source_target_pairs={{0,8},{2,10},{4,12},{6,14},{8,0},{10,2},{12,4},{14,6},{1,9},{3,11}... | collective-permute-start | bytes 307208 | tf_op jit(solution)/shard_map/ppermute | solution.py:17
  5.2 2.5 %collective-permute-start.2 = (bf16[16,3200]{1,0:T(8,128)(2,1)S(1)}, bf16[16,3200]{1,0:T(8,128)(2,1)S(1)}, u32[]{:S(2)}, u32[]{:S(2)}) collective-permute-start(bf16[16,3200]{1,0:T(8,128)(2,1)S(1)} %shard_map.64.refs_0_), channel_id=1, source_target_pairs={{0,6},{2,4},{4,2},{6,0},{8,14},{10,12},{12,10},{14,8},{1,7},{3,5},... | collective-permute-start | bytes 307208 | tf_op jit(solution)/shard_map/ppermute | solution.py:17
  7.8 0.4 collective-permute-start.1
  8.2 0.5 collective-permute-start
  8.7 0.0 copy-done
  8.7 0.1 pad.4.refs_8_
  8.8 1.5 %collective-permute-done.3.refs_4_ = bf16[16,3200]{1,0:T(8,128)(2,1)S(1)} collective-permute-done((bf16[16,3200]{1,0:T(8,128)(2,1)S(1)}, bf16[16,3200]{1,0:T(8,128)(2,1)S(1)}, u32[]{:S(2)}, u32[]{:S(2)}) %collective-permute-start.3) | collective-permute-done | bytes 102432 | tf_op jit(solution)/shard_map/ppermute | solution.py:17
  10.3 1.7 %collective-permute-start.6 = (bf16[16,3200]{1,0:T(8,128)(2,1)S(1)}, bf16[16,3200]{1,0:T(8,128)(2,1)S(1)}, u32[]{:S(2)}, u32[]{:S(2)}) collective-permute-start(bf16[16,3200]{1,0:T(8,128)(2,1)S(1)} %collective-permute-done.3.refs_4_), channel_id=1, source_target_pairs={{0,6},{2,4},{4,2},{6,0},{8,14},{10,12},{12,10},{14,8},{1,7},{3,5},... | collective-permute-start | bytes 307208 | tf_op jit(solution)/shard_map/ppermute | solution.py:17
  12.0 1.4 %collective-permute-start.5 = (bf16[16,3200]{1,0:T(8,128)(2,1)S(1)}, bf16[16,3200]{1,0:T(8,128)(2,1)S(1)}, u32[]{:S(2)}, u32[]{:S(2)}) collective-permute-start(bf16[16,3200]{1,0:T(8,128)(2,1)S(1)} %collective-permute-done.3.refs_4_), channel_id=1, source_target_pairs={{0,4},{2,6},{4,0},{6,2},{8,12},{10,14},{12,8},{14,10},{1,5},{3,7},... | collective-permute-start | bytes 307208 | tf_op jit(solution)/shard_map/ppermute | solution.py:17
  13.4 0.0 collective-permute-done.2.refs_3_
  13.4 0.4 collective-permute-start.4
  13.8 3.8 %shard_map.65 = (bf16[512,3072]{1,0:T(8,128)(2,1)S(1)}, bf16[512,3072]{1,0:T(8,128)(2,1)S(1)}, bf16[512,3072]{1,0:T(8,128)(2,1)S(1)}) custom-call(bf16[16,128]{1,0:T(8,128)(2,1)S(1)} %slice.4._, bf16[4,1024,3072]{2,1,0:T(8,128)(2,1)} %up_ref.3), custom_call_target="tpu_custom_call" | custom-call | flops 8000000000 | tf_op jit(solution)/shard_map/pallas_call | solution.py:26
  17.6 0.0 collective-permute-done.1.refs_2_
  17.6 0.0 collective-permute-done.refs_1_
  17.6 0.0 collective-permute-done.6.refs_7_
  17.6 0.5 collective-permute-done.5.refs_6_
  18.1 0.0 collective-permute-done.4.refs_5_
  18.1 0.0 slice-done
  18.1 0.0 slice-done.1
  18.2 6.9 %shard_map.66 = (bf16[128,3200]{1,0:T(8,128)(2,1)S(1)}, f32[4224,128]{1,0:T(8,128)S(1)}, bf16[512,3072]{1,0:T(8,128)(2,1)S(1)}, bf16[512,3072]{1,0:T(8,128)(2,1)...) custom-call(bf16[16,3200]{1,0:T(8,128)(2,1)S(1)} %shard_map.64.refs_0_, ...), custom_call_target="tpu_custom_call" | custom-call | flops 3221225472 | bytes 25165824 | tf_op jit(solution)/shard_map/pallas_call | solution.py:26
  25.1 0.1 collective-permute-start.7
  25.2 3.8 %shard_map.67 = (f32[2048,128]{1,0:T(8,128)S(1)}, bf16[2048,128]{1,0:T(8,128)(2,1)S(1)}, bf16[512,3072]{1,0:T(8,128)(2,1)S(1)}, bf16[1024,3072]{1,0:T(8,128)(2,1)S(1)}) custom-call(bf16[128,3200]{1,0:T(8,128)(2,1)S(1)} %get-tuple-element.34.x_ref, bf16[4,1024,3072]{2,1,0:T(8,128)(2,1)} %up_ref.3, bf16[4,1024,3072]{2,1,0:T(8,128)(2,1)} %down_ref.7, ...), custom_call_target="tpu_custom_call" | custom-call | flops 1610612736 | bytes 12582912 | tf_op jit(solution)/shard_map/pallas_call | solution.py:26
  28.9 0.6 collective-permute-start.9
  29.5 3.4 %shard_map.68 = (f32[2048,128]{1,0:T(8,128)S(1)}, bf16[2048,128]{1,0:T(8,128)(2,1)S(1)}, bf16[1024,3072]{1,0:T(8,128)(2,1)S(1)}) custom-call(bf16[128,3200]{1,0:T(8,128)(2,1)S(1)} %get-tuple-element.34.x_ref, bf16[4,1024,3072]{2,1,0:T(8,128)(2,1)} %up_ref.3, bf16[4,1024,3072]{2,1,0:T(8,128)(2,1)} %down_ref.7, ...), custom_call_target="tpu_custom_call" | custom-call | flops 1610612736 | bytes 12582912 | tf_op jit(solution)/shard_map/pallas_call | solution.py:26
  32.9 0.1 collective-permute-start.8
  33.0 0.0 collective-permute-done.9.up_b
  33.0 0.0 collective-permute-done.7.gate_b
  33.0 2.8 %shard_map.69 = (bf16[2,128,1024]{2,1,0:T(8,128)(2,1)S(1)}, bf16[1024,3072]{1,0:T(8,128)(2,1)S(1)}) custom-call(f32[4224,128]{1,0:T(8,128)S(1)} %get-tuple-element.35.gate_a, f32[4224,128]{1,0:T(8,128)S(1)} %collective-permute-done.7.gate_b, f32[2048,128]{1,0:T(8,128)S(1)} %get-tuple-element.43.up_a, bf16[2048,128]{1,0:T(8,128)(2,1)S(1)} %collective-permute-done.9.up_b, ...), custom_call_target="tpu_custom_call" | custom-call | bytes 3145728 | tf_op jit(solution)/shard_map/pallas_call | solution.py:26
  35.8 0.0 collective-permute-done.8.up_b
  35.8 4.1 %shard_map.70 = (f32[16,3072]{1,0:T(8,128)S(1)}, bf16[16,3072]{1,0:T(8,128)(2,1)S(1)}, bf16[16,3072]{1,0:T(8,128)(2,1)S(1)}, bf16[16,3072]{1,0:T(8,128)(2,1)S(1)...) custom-call(bf16[128,3200]{1,0:T(8,128)(2,1)S(1)} %get-tuple-element, ...), custom_call_target="tpu_custom_call" | custom-call | flops 3221225472 | bytes 25165824 | tf_op jit(solution)/shard_map/pallas_call | solution.py:26
  39.9 1.8 %collective-permute-start.13 = (bf16[16,3072]{1,0:T(8,128)(2,1)S(1)}, bf16[16,3072]{1,0:T(8,128)(2,1)S(1)}, u32[]{:S(2)}, u32[]{:S(2)}) collective-permute-start(bf16[16,3072]{1,0:T(8,128)(2,1)S(1)} %get-tuple-element.54), channel_id=1, source_target_pairs={{0,6},{2,4},{4,2},{6,0},{8,14},{10,12},{12,10},{14,8},{1,7},{3,5},... | collective-permute-start | bytes 294920 | tf_op jit(solution)/shard_map/ppermute | solution.py:17
  41.8 0.9 %collective-permute-start.14 = (bf16[16,3072]{1,0:T(8,128)(2,1)S(1)}, bf16[16,3072]{1,0:T(8,128)(2,1)S(1)}, u32[]{:S(2)}, u32[]{:S(2)}) collective-permute-start(bf16[16,3072]{1,0:T(8,128)(2,1)S(1)} %get-tuple-element.55), channel_id=1, source_target_pairs={{0,4},{2,6},{4,0},{6,2},{8,12},{10,14},{12,8},{14,10},{1,5},{3,7},... | collective-permute-start | bytes 294920 | tf_op jit(solution)/shard_map/ppermute | solution.py:17
  42.7 0.8 %collective-permute-start.15 = (bf16[16,3072]{1,0:T(8,128)(2,1)S(1)}, bf16[16,3072]{1,0:T(8,128)(2,1)S(1)}, u32[]{:S(2)}, u32[]{:S(2)}) collective-permute-start(bf16[16,3072]{1,0:T(8,128)(2,1)S(1)} %get-tuple-element.56), channel_id=1, source_target_pairs={{0,2},{2,0},{4,6},{6,4},{8,10},{10,8},{12,14},{14,12},{1,3},{3,1},... | collective-permute-start | bytes 294920 | tf_op jit(solution)/shard_map/ppermute | solution.py:17
  43.5 1.5 %collective-permute-start.10 = (bf16[16,3072]{1,0:T(8,128)(2,1)S(1)}, bf16[16,3072]{1,0:T(8,128)(2,1)S(1)}, u32[]{:S(2)}, u32[]{:S(2)}) collective-permute-start(bf16[16,3072]{1,0:T(8,128)(2,1)S(1)} %get-tuple-element.50), channel_id=1, source_target_pairs={{0,4},{2,6},{4,0},{6,2},{8,12},{10,14},{12,8},{14,10},{1,5},{3,7},... | collective-permute-start | bytes 294920 | tf_op jit(solution)/shard_map/ppermute | solution.py:17
  45.0 0.8 %collective-permute-start.11 = (bf16[16,3072]{1,0:T(8,128)(2,1)S(1)}, bf16[16,3072]{1,0:T(8,128)(2,1)S(1)}, u32[]{:S(2)}, u32[]{:S(2)}) collective-permute-start(bf16[16,3072]{1,0:T(8,128)(2,1)S(1)} %get-tuple-element.51), channel_id=1, source_target_pairs={{0,2},{2,0},{4,6},{6,4},{8,10},{10,8},{12,14},{14,12},{1,3},{3,1},... | collective-permute-start | bytes 294920 | tf_op jit(solution)/shard_map/ppermute | solution.py:17
  45.8 0.7 %collective-permute-done.13 = bf16[16,3072]{1,0:T(8,128)(2,1)S(1)} collective-permute-done((bf16[16,3072]{1,0:T(8,128)(2,1)S(1)}, bf16[16,3072]{1,0:T(8,128)(2,1)S(1)}, u32[]{:S(2)}, u32[]{:S(2)}) %collective-permute-start.13) | collective-permute-done | bytes 98336 | tf_op jit(solution)/shard_map/ppermute | solution.py:17
  46.5 1.8 %collective-permute-start.12 = (bf16[16,3072]{1,0:T(8,128)(2,1)S(1)}, bf16[16,3072]{1,0:T(8,128)(2,1)S(1)}, u32[]{:S(2)}, u32[]{:S(2)}) collective-permute-start(bf16[16,3072]{1,0:T(8,128)(2,1)S(1)} %get-tuple-element.52), channel_id=1, source_target_pairs={{0,6},{2,4},{4,2},{6,0},{8,14},{10,12},{12,10},{14,8},{1,7},{3,5},... | collective-permute-start | bytes 294920 | tf_op jit(solution)/shard_map/ppermute | solution.py:17
  48.3 0.1 collective-permute-done.14
  48.4 0.1 collective-permute-done.15
  48.5 0.1 add_convert_fusion.1
  48.5 3.3 %collective-permute-start.16 = (bf16[16,3072]{1,0:T(8,128)(2,1)S(1)}, bf16[16,3072]{1,0:T(8,128)(2,1)S(1)}, u32[]{:S(2)}, u32[]{:S(2)}) collective-permute-start(bf16[16,3072]{1,0:T(8,128)(2,1)S(1)} %add_convert_fusion.1), channel_id=1, source_target_pairs={{0,8},{2,10},{4,12},{6,14},{8,0},{10,2},{12,4},{14,6},{1,9},{3,11}... | collective-permute-start | bytes 294920 | tf_op jit(solution)/shard_map/ppermute | solution.py:17
  51.8 0.0 collective-permute-done.10
  51.8 0.0 collective-permute-done.11
  51.8 0.6 %collective-permute-done.12 = bf16[16,3072]{1,0:T(8,128)(2,1)S(1)} collective-permute-done((bf16[16,3072]{1,0:T(8,128)(2,1)S(1)}, bf16[16,3072]{1,0:T(8,128)(2,1)S(1)}, u32[]{:S(2)}, u32[]{:S(2)}) %collective-permute-start.12) | collective-permute-done | bytes 98336 | tf_op jit(solution)/shard_map/ppermute | solution.py:17
  52.4 3.9 %collective-permute-done.16 = bf16[16,3072]{1,0:T(8,128)(2,1)S(1)} collective-permute-done((bf16[16,3072]{1,0:T(8,128)(2,1)S(1)}, bf16[16,3072]{1,0:T(8,128)(2,1)S(1)}, u32[]{:S(2)}, u32[]{:S(2)}) %collective-permute-start.16) | collective-permute-done | bytes 98336 | tf_op jit(solution)/shard_map/ppermute | solution.py:17
  56.3 0.7 %add_convert_fusion = bf16[16,3072]{1,0:T(8,128)(2,1)} fusion(bf16[16,3072]{1,0:T(8,128)(2,1)S(1)} %collective-permute-done.16, bf16[16,3072]{1,0:T(8,128)(2,1)S(1)} %collective-permute-done.12, bf16[16,3072]{1,0:T(8,128)(2,1)S(1)} %collective-permute-done.11, f32[16,3072]{1,0:T(8,128)S(1)} %get-tuple-element.49, bf16[16,3072]{1,0:T(8,128)(2,1)S(1)} %collective-permute-done.10), kind=kLoop, calls=%fused_computation | loop fusion | flops 442368 | bytes 688128 | tf_op jit(solution)/shard_map/convert_element_type | solution.py:287
  (12 shorter events, 0.0 us)
Async XLA Ops:
  0.0 8.7 %copy-start = (bf16[3072,4]{0,1:T(4,128)(2,1)S(1)}, bf16[3072,4]{0,1:T(4,128)(2,1)}, u32[]{:S(2)}) copy-start(bf16[3072,4]{0,1:T(4,128)(2,1)} %param.8) | copy-start | bytes 73732
  0.0 18.1 %slice-start = ((s8[25165824]{0:T(1024)(128)(4,1)}), s8[4194304]{0:T(1024)(128)(4,1)S(1)}, s32[]{:S(2)}) async-start(s8[25165824]{0:T(1024)(128)(4,1)} %bitcast.2), calls=%async_computation | async-start | bytes 8388608
  0.0 18.1 %slice-start.1 = ((s8[25165824]{0:T(1024)(128)(4,1)}), s8[4194304]{0:T(1024)(128)(4,1)S(1)}, s32[]{:S(2)}) async-start(s8[25165824]{0:T(1024)(128)(4,1)} %bitcast.2), calls=%async_computation.1 | async-start | bytes 8388608
  0.0 18.1 %slice-start.2 = ((s8[25165824]{0:T(1024)(128)(4,1)}), s8[4194304]{0:T(1024)(128)(4,1)S(1)}, s32[]{:S(2)}) async-start(s8[25165824]{0:T(1024)(128)(4,1)} %bitcast.2), calls=%async_computation.2 | async-start | bytes 8388608
  0.0 18.1 %slice-start.3 = ((s8[25165824]{0:T(1024)(128)(4,1)}), s8[4194304]{0:T(1024)(128)(4,1)S(1)}, s32[]{:S(2)}) async-start(s8[25165824]{0:T(1024)(128)(4,1)} %bitcast.2), calls=%async_computation.3 | async-start | bytes 8388608
  0.0 18.1 %slice-start.4 = ((s8[25165824]{0:T(1024)(128)(4,1)}), s8[4194304]{0:T(1024)(128)(4,1)S(1)}, s32[]{:S(2)}) async-start(s8[25165824]{0:T(1024)(128)(4,1)} %bitcast.2), calls=%async_computation.4 | async-start | bytes 8388608
  1.1 9.2 %collective-permute-start.3 = (bf16[16,3200]{1,0:T(8,128)(2,1)S(1)}, bf16[16,3200]{1,0:T(8,128)(2,1)S(1)}, u32[]{:S(2)}, u32[]{:S(2)}) collective-permute-start(bf16[16,3200]{1,0:T(8,128)(2,1)S(1)} %shard_map.64.refs_0_), channel_id=1, source_target_pairs={{0,8},{2,10},{4,12},{6,14},{8,0},{10,2},{12,4},{14,6},{1,9},{3,11}... | collective-permute-start | bytes 307208 | tf_op jit(solution)/shard_map/ppermute | solution.py:17
  5.2 8.2 %collective-permute-start.2 = (bf16[16,3200]{1,0:T(8,128)(2,1)S(1)}, bf16[16,3200]{1,0:T(8,128)(2,1)S(1)}, u32[]{:S(2)}, u32[]{:S(2)}) collective-permute-start(bf16[16,3200]{1,0:T(8,128)(2,1)S(1)} %shard_map.64.refs_0_), channel_id=1, source_target_pairs={{0,6},{2,4},{4,2},{6,0},{8,14},{10,12},{12,10},{14,8},{1,7},{3,5},... | collective-permute-start | bytes 307208 | tf_op jit(solution)/shard_map/ppermute | solution.py:17
  7.8 9.8 %collective-permute-start.1 = (bf16[16,3200]{1,0:T(8,128)(2,1)S(1)}, bf16[16,3200]{1,0:T(8,128)(2,1)S(1)}, u32[]{:S(2)}, u32[]{:S(2)}) collective-permute-start(bf16[16,3200]{1,0:T(8,128)(2,1)S(1)} %shard_map.64.refs_0_), channel_id=1, source_target_pairs={{0,4},{2,6},{4,0},{6,2},{8,12},{10,14},{12,8},{14,10},{1,5},{3,7},... | collective-permute-start | bytes 307208 | tf_op jit(solution)/shard_map/ppermute | solution.py:17
  8.2 9.4 %collective-permute-start = (bf16[16,3200]{1,0:T(8,128)(2,1)S(1)}, bf16[16,3200]{1,0:T(8,128)(2,1)S(1)}, u32[]{:S(2)}, u32[]{:S(2)}) collective-permute-start(bf16[16,3200]{1,0:T(8,128)(2,1)S(1)} %shard_map.64.refs_0_), channel_id=1, source_target_pairs={{0,2},{2,0},{4,6},{6,4},{8,10},{10,8},{12,14},{14,12},{1,3},{3,1},... | collective-permute-start | bytes 307208 | tf_op jit(solution)/shard_map/ppermute | solution.py:17
  10.3 7.8 %slice-start.5 = ((s8[25165824]{0:T(1024)(128)(4,1)}), s8[4194304]{0:T(1024)(128)(4,1)S(1)}, s32[]{:S(2)}) async-start(s8[25165824]{0:T(1024)(128)(4,1)} %bitcast.2), calls=%async_computation.5 | async-start | bytes 8388608
  10.3 7.3 %collective-permute-start.6 = (bf16[16,3200]{1,0:T(8,128)(2,1)S(1)}, bf16[16,3200]{1,0:T(8,128)(2,1)S(1)}, u32[]{:S(2)}, u32[]{:S(2)}) collective-permute-start(bf16[16,3200]{1,0:T(8,128)(2,1)S(1)} %collective-permute-done.3.refs_4_), channel_id=1, source_target_pairs={{0,6},{2,4},{4,2},{6,0},{8,14},{10,12},{12,10},{14,8},{1,7},{3,5},... | collective-permute-start | bytes 307208 | tf_op jit(solution)/shard_map/ppermute | solution.py:17
  12.0 6.1 %collective-permute-start.5 = (bf16[16,3200]{1,0:T(8,128)(2,1)S(1)}, bf16[16,3200]{1,0:T(8,128)(2,1)S(1)}, u32[]{:S(2)}, u32[]{:S(2)}) collective-permute-start(bf16[16,3200]{1,0:T(8,128)(2,1)S(1)} %collective-permute-done.3.refs_4_), channel_id=1, source_target_pairs={{0,4},{2,6},{4,0},{6,2},{8,12},{10,14},{12,8},{14,10},{1,5},{3,7},... | collective-permute-start | bytes 307208 | tf_op jit(solution)/shard_map/ppermute | solution.py:17
  13.4 4.7 %collective-permute-start.4 = (bf16[16,3200]{1,0:T(8,128)(2,1)S(1)}, bf16[16,3200]{1,0:T(8,128)(2,1)S(1)}, u32[]{:S(2)}, u32[]{:S(2)}) collective-permute-start(bf16[16,3200]{1,0:T(8,128)(2,1)S(1)} %collective-permute-done.3.refs_4_), channel_id=1, source_target_pairs={{0,2},{2,0},{4,6},{6,4},{8,10},{10,8},{12,14},{14,12},{1,3},{3,1},... | collective-permute-start | bytes 307208 | tf_op jit(solution)/shard_map/ppermute | solution.py:17
  25.1 7.9 %collective-permute-start.7 = (f32[4224,128]{1,0:T(8,128)S(1)}, f32[4224,128]{1,0:T(8,128)S(1)}, u32[]{:S(2)}, u32[]{:S(2)}) collective-permute-start(f32[4224,128]{1,0:T(8,128)S(1)} %get-tuple-element.35.gate_a), channel_id=1, source_target_pairs={{0,1},{1,0},{2,3},{3,2},{4,5},{5,4},{6,7},{7,6},{8,9},{9,8},{10,11... | collective-permute-start | bytes 6488072 | tf_op jit(solution)/shard_map/ppermute | solution.py:239
  28.9 4.1 %collective-permute-start.9 = (bf16[2048,128]{1,0:T(8,128)(2,1)S(1)}, bf16[2048,128]{1,0:T(8,128)(2,1)S(1)}, u32[]{:S(2)}, u32[]{:S(2)}) collective-permute-start(bf16[2048,128]{1,0:T(8,128)(2,1)S(1)} %get-tuple-element.44), channel_id=1, source_target_pairs={{0,1},{1,0},{2,3},{3,2},{4,5},{5,4},{6,7},{7,6},{8,9},{9,8},{10,11... | collective-permute-start | bytes 1572872 | tf_op jit(solution)/shard_map/ppermute | solution.py:257
  32.9 2.9 %collective-permute-start.8 = (bf16[2048,128]{1,0:T(8,128)(2,1)S(1)}, bf16[2048,128]{1,0:T(8,128)(2,1)S(1)}, u32[]{:S(2)}, u32[]{:S(2)}) collective-permute-start(bf16[2048,128]{1,0:T(8,128)(2,1)S(1)} %get-tuple-element.42), channel_id=1, source_target_pairs={{0,1},{1,0},{2,3},{3,2},{4,5},{5,4},{6,7},{7,6},{8,9},{9,8},{10,11... | collective-permute-start | bytes 1572872 | tf_op jit(solution)/shard_map/ppermute | solution.py:257
  39.9 6.6 %collective-permute-start.13 = (bf16[16,3072]{1,0:T(8,128)(2,1)S(1)}, bf16[16,3072]{1,0:T(8,128)(2,1)S(1)}, u32[]{:S(2)}, u32[]{:S(2)}) collective-permute-start(bf16[16,3072]{1,0:T(8,128)(2,1)S(1)} %get-tuple-element.54), channel_id=1, source_target_pairs={{0,6},{2,4},{4,2},{6,0},{8,14},{10,12},{12,10},{14,8},{1,7},{3,5},... | collective-permute-start | bytes 294920 | tf_op jit(solution)/shard_map/ppermute | solution.py:17
  41.8 6.6 %collective-permute-start.14 = (bf16[16,3072]{1,0:T(8,128)(2,1)S(1)}, bf16[16,3072]{1,0:T(8,128)(2,1)S(1)}, u32[]{:S(2)}, u32[]{:S(2)}) collective-permute-start(bf16[16,3072]{1,0:T(8,128)(2,1)S(1)} %get-tuple-element.55), channel_id=1, source_target_pairs={{0,4},{2,6},{4,0},{6,2},{8,12},{10,14},{12,8},{14,10},{1,5},{3,7},... | collective-permute-start | bytes 294920 | tf_op jit(solution)/shard_map/ppermute | solution.py:17
  42.7 5.8 %collective-permute-start.15 = (bf16[16,3072]{1,0:T(8,128)(2,1)S(1)}, bf16[16,3072]{1,0:T(8,128)(2,1)S(1)}, u32[]{:S(2)}, u32[]{:S(2)}) collective-permute-start(bf16[16,3072]{1,0:T(8,128)(2,1)S(1)} %get-tuple-element.56), channel_id=1, source_target_pairs={{0,2},{2,0},{4,6},{6,4},{8,10},{10,8},{12,14},{14,12},{1,3},{3,1},... | collective-permute-start | bytes 294920 | tf_op jit(solution)/shard_map/ppermute | solution.py:17
  43.5 8.3 %collective-permute-start.10 = (bf16[16,3072]{1,0:T(8,128)(2,1)S(1)}, bf16[16,3072]{1,0:T(8,128)(2,1)S(1)}, u32[]{:S(2)}, u32[]{:S(2)}) collective-permute-start(bf16[16,3072]{1,0:T(8,128)(2,1)S(1)} %get-tuple-element.50), channel_id=1, source_target_pairs={{0,4},{2,6},{4,0},{6,2},{8,12},{10,14},{12,8},{14,10},{1,5},{3,7},... | collective-permute-start | bytes 294920 | tf_op jit(solution)/shard_map/ppermute | solution.py:17
  45.0 6.8 %collective-permute-start.11 = (bf16[16,3072]{1,0:T(8,128)(2,1)S(1)}, bf16[16,3072]{1,0:T(8,128)(2,1)S(1)}, u32[]{:S(2)}, u32[]{:S(2)}) collective-permute-start(bf16[16,3072]{1,0:T(8,128)(2,1)S(1)} %get-tuple-element.51), channel_id=1, source_target_pairs={{0,2},{2,0},{4,6},{6,4},{8,10},{10,8},{12,14},{14,12},{1,3},{3,1},... | collective-permute-start | bytes 294920 | tf_op jit(solution)/shard_map/ppermute | solution.py:17
  46.5 5.9 %collective-permute-start.12 = (bf16[16,3072]{1,0:T(8,128)(2,1)S(1)}, bf16[16,3072]{1,0:T(8,128)(2,1)S(1)}, u32[]{:S(2)}, u32[]{:S(2)}) collective-permute-start(bf16[16,3072]{1,0:T(8,128)(2,1)S(1)} %get-tuple-element.52), channel_id=1, source_target_pairs={{0,6},{2,4},{4,2},{6,0},{8,14},{10,12},{12,10},{14,8},{1,7},{3,5},... | collective-permute-start | bytes 294920 | tf_op jit(solution)/shard_map/ppermute | solution.py:17
  48.5 7.8 %collective-permute-start.16 = (bf16[16,3072]{1,0:T(8,128)(2,1)S(1)}, bf16[16,3072]{1,0:T(8,128)(2,1)S(1)}, u32[]{:S(2)}, u32[]{:S(2)}) collective-permute-start(bf16[16,3072]{1,0:T(8,128)(2,1)S(1)} %add_convert_fusion.1), channel_id=1, source_target_pairs={{0,8},{2,10},{4,12},{6,14},{8,0},{10,2},{12,4},{14,6},{1,9},{3,11}... | collective-permute-start | bytes 294920 | tf_op jit(solution)/shard_map/ppermute | solution.py:17

commit v11 on v10

--- a/solution.py
+++ b/solution.py
@@ -280,8 +280,8 @@
         [pltpu.VMEM((1, hidden, width), BF16), *sems(1)],
         hbm=(6,),
     )
-    far_sums = [xor_send(parts[4 ^ k], k) for k in (3, 2, 1)]
-    near_sums = [xor_send(parts[k], k) for k in (2, 1, 3)]
+    far_sums = [xor_send(parts[4 ^ k], k) for k in (3, 1, 2)]
+    near_sums = [xor_send(parts[k], k) for k in (1, 2, 3)]
     add = lambda arrays: sum(a.astype(F32) for a in arrays)
     crossing = xor_send(add([parts[4], *far_sums]).astype(BF16), 4)
     return add([parts[0], *near_sums, crossing]).astype(BF16)

time: 57.2 us -> 57.3 us (level)
  transfers between devices with their start and end apart: 17 -> 17, of which waited for: 7 -> 6; matrix products, arithmetic and copies ran while one was open for 0% -> 0% of each run, Pallas kernels for 24% -> 24%
where the time goes in v11:
time: 57.3 us; the launch traced here: 57.1 us
  Pallas kernels  25.9 us (45%)
  starting transfers between devices  22.8 us (40%)
  waiting for transfers between devices  7.46 us (13%)
  other arithmetic  0.76 us (1%)
    pallas_call x7, Pallas kernels, call(): pl.pallas_call(kernel, out_shape=outs, in_specs=specs, out_specs=[VMEM_BL...  25.9 us
    ppermute x14, starting transfers between devices, xor_send(): return lax.ppermute(block, 'batch', [(i, i ^ mask) for i in range(8)])  22.1 us
    ppermute x14, waiting for transfers between devices, xor_send(): return lax.ppermute(block, 'batch', [(i, i ^ mask) for i in range(8)])  7.45 us
  transfers between devices with their start and end apart: 17, of which 6 were waited for; matrix products, arithmetic and copies ran while one was open for 0% of the time, Pallas kernels for 24%

profile of v11, /device:TPU:0, one launch (start us, length us, event | category | flops | bytes accessed | tf_op | source)
XLA Modules:
  0.0 57.1 jit_solution(2020273057232440489)
XLA Ops:
  0.0 0.0 slice-start.4
  0.0 1.1 %shard_map.64.refs_0_ = bf16[16,3200]{1,0:T(8,128)(2,1)S(1)} custom-call(bf16[16,3072]{1,0:T(8,128)(2,1)} %tokens_ref.1, s32[2,16]{1,0:T(2,128)} %bitcast.5), custom_call_target="tpu_custom_call" | custom-call | flops 30000001024 | bytes 196608 | tf_op jit(solution)/shard_map/pallas_call | solution.py:26
  1.1 4.1 %collective-permute-start.3 = (bf16[16,3200]{1,0:T(8,128)(2,1)S(1)}, bf16[16,3200]{1,0:T(8,128)(2,1)S(1)}, u32[]{:S(2)}, u32[]{:S(2)}) collective-permute-start(bf16[16,3200]{1,0:T(8,128)(2,1)S(1)} %shard_map.64.refs_0_), channel_id=1, source_target_pairs={{0,8},{2,10},{4,12},{6,14},{8,0},{10,2},{12,4},{14,6},{1,9},{3,11}... | collective-permute-start | bytes 307208 | tf_op jit(solution)/shard_map/ppermute | solution.py:17
  5.2 2.5 %collective-permute-start.2 = (bf16[16,3200]{1,0:T(8,128)(2,1)S(1)}, bf16[16,3200]{1,0:T(8,128)(2,1)S(1)}, u32[]{:S(2)}, u32[]{:S(2)}) collective-permute-start(bf16[16,3200]{1,0:T(8,128)(2,1)S(1)} %shard_map.64.refs_0_), channel_id=1, source_target_pairs={{0,6},{2,4},{4,2},{6,0},{8,14},{10,12},{12,10},{14,8},{1,7},{3,5},... | collective-permute-start | bytes 307208 | tf_op jit(solution)/shard_map/ppermute | solution.py:17
  7.8 0.4 collective-permute-start.1
  8.2 0.5 collective-permute-start
  8.7 0.0 copy-done
  8.7 0.1 pad.4.refs_8_
  8.8 1.5 %collective-permute-done.3.refs_4_ = bf16[16,3200]{1,0:T(8,128)(2,1)S(1)} collective-permute-done((bf16[16,3200]{1,0:T(8,128)(2,1)S(1)}, bf16[16,3200]{1,0:T(8,128)(2,1)S(1)}, u32[]{:S(2)}, u32[]{:S(2)}) %collective-permute-start.3) | collective-permute-done | bytes 102432 | tf_op jit(solution)/shard_map/ppermute | solution.py:17
  10.3 1.7 %collective-permute-start.6 = (bf16[16,3200]{1,0:T(8,128)(2,1)S(1)}, bf16[16,3200]{1,0:T(8,128)(2,1)S(1)}, u32[]{:S(2)}, u32[]{:S(2)}) collective-permute-start(bf16[16,3200]{1,0:T(8,128)(2,1)S(1)} %collective-permute-done.3.refs_4_), channel_id=1, source_target_pairs={{0,6},{2,4},{4,2},{6,0},{8,14},{10,12},{12,10},{14,8},{1,7},{3,5},... | collective-permute-start | bytes 307208 | tf_op jit(solution)/shard_map/ppermute | solution.py:17
  12.0 1.4 %collective-permute-start.5 = (bf16[16,3200]{1,0:T(8,128)(2,1)S(1)}, bf16[16,3200]{1,0:T(8,128)(2,1)S(1)}, u32[]{:S(2)}, u32[]{:S(2)}) collective-permute-start(bf16[16,3200]{1,0:T(8,128)(2,1)S(1)} %collective-permute-done.3.refs_4_), channel_id=1, source_target_pairs={{0,4},{2,6},{4,0},{6,2},{8,12},{10,14},{12,8},{14,10},{1,5},{3,7},... | collective-permute-start | bytes 307208 | tf_op jit(solution)/shard_map/ppermute | solution.py:17
  13.4 0.0 collective-permute-done.2.refs_3_
  13.4 0.4 collective-permute-start.4
  13.8 3.8 %shard_map.65 = (bf16[512,3072]{1,0:T(8,128)(2,1)S(1)}, bf16[512,3072]{1,0:T(8,128)(2,1)S(1)}, bf16[512,3072]{1,0:T(8,128)(2,1)S(1)}) custom-call(bf16[16,128]{1,0:T(8,128)(2,1)S(1)} %slice.4._, bf16[4,1024,3072]{2,1,0:T(8,128)(2,1)} %up_ref.3), custom_call_target="tpu_custom_call" | custom-call | flops 8000000000 | tf_op jit(solution)/shard_map/pallas_call | solution.py:26
  17.6 0.0 collective-permute-done.1.refs_2_
  17.6 0.0 collective-permute-done.refs_1_
  17.6 0.0 collective-permute-done.6.refs_7_
  17.6 0.5 collective-permute-done.5.refs_6_
  18.1 0.0 collective-permute-done.4.refs_5_
  18.1 0.0 slice-done
  18.1 0.0 slice-done.1
  18.2 6.9 %shard_map.66 = (bf16[128,3200]{1,0:T(8,128)(2,1)S(1)}, f32[4224,128]{1,0:T(8,128)S(1)}, bf16[512,3072]{1,0:T(8,128)(2,1)S(1)}, bf16[512,3072]{1,0:T(8,128)(2,1)...) custom-call(bf16[16,3200]{1,0:T(8,128)(2,1)S(1)} %shard_map.64.refs_0_, ...), custom_call_target="tpu_custom_call" | custom-call | flops 3221225472 | bytes 25165824 | tf_op jit(solution)/shard_map/pallas_call | solution.py:26
  25.1 0.1 collective-permute-start.7
  25.2 3.8 %shard_map.67 = (f32[2048,128]{1,0:T(8,128)S(1)}, bf16[2048,128]{1,0:T(8,128)(2,1)S(1)}, bf16[512,3072]{1,0:T(8,128)(2,1)S(1)}, bf16[1024,3072]{1,0:T(8,128)(2,1)S(1)}) custom-call(bf16[128,3200]{1,0:T(8,128)(2,1)S(1)} %get-tuple-element.34.x_ref, bf16[4,1024,3072]{2,1,0:T(8,128)(2,1)} %up_ref.3, bf16[4,1024,3072]{2,1,0:T(8,128)(2,1)} %down_ref.7, ...), custom_call_target="tpu_custom_call" | custom-call | flops 1610612736 | bytes 12582912 | tf_op jit(solution)/shard_map/pallas_call | solution.py:26
  28.9 0.6 collective-permute-start.9
  29.5 3.4 %shard_map.68 = (f32[2048,128]{1,0:T(8,128)S(1)}, bf16[2048,128]{1,0:T(8,128)(2,1)S(1)}, bf16[1024,3072]{1,0:T(8,128)(2,1)S(1)}) custom-call(bf16[128,3200]{1,0:T(8,128)(2,1)S(1)} %get-tuple-element.34.x_ref, bf16[4,1024,3072]{2,1,0:T(8,128)(2,1)} %up_ref.3, bf16[4,1024,3072]{2,1,0:T(8,128)(2,1)} %down_ref.7, ...), custom_call_target="tpu_custom_call" | custom-call | flops 1610612736 | bytes 12582912 | tf_op jit(solution)/shard_map/pallas_call | solution.py:26
  32.9 0.1 collective-permute-start.8
  33.0 0.0 collective-permute-done.9.up_b
  33.0 0.0 collective-permute-done.7.gate_b
  33.0 2.8 %shard_map.69 = (bf16[2,128,1024]{2,1,0:T(8,128)(2,1)S(1)}, bf16[1024,3072]{1,0:T(8,128)(2,1)S(1)}) custom-call(f32[4224,128]{1,0:T(8,128)S(1)} %get-tuple-element.35.gate_a, f32[4224,128]{1,0:T(8,128)S(1)} %collective-permute-done.7.gate_b, f32[2048,128]{1,0:T(8,128)S(1)} %get-tuple-element.43.up_a, bf16[2048,128]{1,0:T(8,128)(2,1)S(1)} %collective-permute-done.9.up_b, ...), custom_call_target="tpu_custom_call" | custom-call | bytes 3145728 | tf_op jit(solution)/shard_map/pallas_call | solution.py:26
  35.8 0.0 collective-permute-done.8.up_b
  35.8 4.1 %shard_map.70 = (f32[16,3072]{1,0:T(8,128)S(1)}, bf16[16,3072]{1,0:T(8,128)(2,1)S(1)}, bf16[16,3072]{1,0:T(8,128)(2,1)S(1)}, bf16[16,3072]{1,0:T(8,128)(2,1)S(1)...) custom-call(bf16[128,3200]{1,0:T(8,128)(2,1)S(1)} %get-tuple-element, ...), custom_call_target="tpu_custom_call" | custom-call | flops 3221225472 | bytes 25165824 | tf_op jit(solution)/shard_map/pallas_call | solution.py:26
  39.9 1.8 %collective-permute-start.13 = (bf16[16,3072]{1,0:T(8,128)(2,1)S(1)}, bf16[16,3072]{1,0:T(8,128)(2,1)S(1)}, u32[]{:S(2)}, u32[]{:S(2)}) collective-permute-start(bf16[16,3072]{1,0:T(8,128)(2,1)S(1)} %get-tuple-element.54), channel_id=1, source_target_pairs={{0,6},{2,4},{4,2},{6,0},{8,14},{10,12},{12,10},{14,8},{1,7},{3,5},... | collective-permute-start | bytes 294920 | tf_op jit(solution)/shard_map/ppermute | solution.py:17
  41.8 1.2 %collective-permute-start.14 = (bf16[16,3072]{1,0:T(8,128)(2,1)S(1)}, bf16[16,3072]{1,0:T(8,128)(2,1)S(1)}, u32[]{:S(2)}, u32[]{:S(2)}) collective-permute-start(bf16[16,3072]{1,0:T(8,128)(2,1)S(1)} %get-tuple-element.55), channel_id=1, source_target_pairs={{0,2},{2,0},{4,6},{6,4},{8,10},{10,8},{12,14},{14,12},{1,3},{3,1},... | collective-permute-start | bytes 294920 | tf_op jit(solution)/shard_map/ppermute | solution.py:17
  43.0 0.5 collective-permute-start.15
  43.5 1.2 %collective-permute-start.10 = (bf16[16,3072]{1,0:T(8,128)(2,1)S(1)}, bf16[16,3072]{1,0:T(8,128)(2,1)S(1)}, u32[]{:S(2)}, u32[]{:S(2)}) collective-permute-start(bf16[16,3072]{1,0:T(8,128)(2,1)S(1)} %get-tuple-element.50), channel_id=1, source_target_pairs={{0,2},{2,0},{4,6},{6,4},{8,10},{10,8},{12,14},{14,12},{1,3},{3,1},... | collective-permute-start | bytes 294920 | tf_op jit(solution)/shard_map/ppermute | solution.py:17
  44.7 1.1 %collective-permute-start.11 = (bf16[16,3072]{1,0:T(8,128)(2,1)S(1)}, bf16[16,3072]{1,0:T(8,128)(2,1)S(1)}, u32[]{:S(2)}, u32[]{:S(2)}) collective-permute-start(bf16[16,3072]{1,0:T(8,128)(2,1)S(1)} %get-tuple-element.51), channel_id=1, source_target_pairs={{0,4},{2,6},{4,0},{6,2},{8,12},{10,14},{12,8},{14,10},{1,5},{3,7},... | collective-permute-start | bytes 294920 | tf_op jit(solution)/shard_map/ppermute | solution.py:17
  45.8 0.6 collective-permute-done.13
  46.4 1.9 %collective-permute-start.12 = (bf16[16,3072]{1,0:T(8,128)(2,1)S(1)}, bf16[16,3072]{1,0:T(8,128)(2,1)S(1)}, u32[]{:S(2)}, u32[]{:S(2)}) collective-permute-start(bf16[16,3072]{1,0:T(8,128)(2,1)S(1)} %get-tuple-element.52), channel_id=1, source_target_pairs={{0,6},{2,4},{4,2},{6,0},{8,14},{10,12},{12,10},{14,8},{1,7},{3,5},... | collective-permute-start | bytes 294920 | tf_op jit(solution)/shard_map/ppermute | solution.py:17
  48.3 0.0 collective-permute-done.14
  48.3 0.3 collective-permute-done.15
  48.7 0.1 add_convert_fusion.1
  48.7 3.2 %collective-permute-start.16 = (bf16[16,3072]{1,0:T(8,128)(2,1)S(1)}, bf16[16,3072]{1,0:T(8,128)(2,1)S(1)}, u32[]{:S(2)}, u32[]{:S(2)}) collective-permute-start(bf16[16,3072]{1,0:T(8,128)(2,1)S(1)} %add_convert_fusion.1), channel_id=1, source_target_pairs={{0,8},{2,10},{4,12},{6,14},{8,0},{10,2},{12,4},{14,6},{1,9},{3,11}... | collective-permute-start | bytes 294920 | tf_op jit(solution)/shard_map/ppermute | solution.py:17
  51.9 0.0 collective-permute-done.10
  51.9 0.0 collective-permute-done.11
  51.9 0.5 collective-permute-done.12
  52.4 4.0 %collective-permute-done.16 = bf16[16,3072]{1,0:T(8,128)(2,1)S(1)} collective-permute-done((bf16[16,3072]{1,0:T(8,128)(2,1)S(1)}, bf16[16,3072]{1,0:T(8,128)(2,1)S(1)}, u32[]{:S(2)}, u32[]{:S(2)}) %collective-permute-start.16) | collective-permute-done | bytes 98336 | tf_op jit(solution)/shard_map/ppermute | solution.py:17
  56.4 0.7 %add_convert_fusion = bf16[16,3072]{1,0:T(8,128)(2,1)} fusion(bf16[16,3072]{1,0:T(8,128)(2,1)S(1)} %collective-permute-done.16, bf16[16,3072]{1,0:T(8,128)(2,1)S(1)} %collective-permute-done.12, bf16[16,3072]{1,0:T(8,128)(2,1)S(1)} %collective-permute-done.11, f32[16,3072]{1,0:T(8,128)S(1)} %get-tuple-element.49, bf16[16,3072]{1,0:T(8,128)(2,1)S(1)} %collective-permute-done.10), kind=kLoop, calls=%fused_computation | loop fusion | flops 442368 | bytes 688128 | tf_op jit(solution)/shard_map/convert_element_type | solution.py:287
  (12 shorter events, 0.0 us)
Async XLA Ops:
  0.0 8.7 %copy-start = (bf16[3072,4]{0,1:T(4,128)(2,1)S(1)}, bf16[3072,4]{0,1:T(4,128)(2,1)}, u32[]{:S(2)}) copy-start(bf16[3072,4]{0,1:T(4,128)(2,1)} %param.8) | copy-start | bytes 73732
  0.0 18.1 %slice-start = ((s8[25165824]{0:T(1024)(128)(4,1)}), s8[4194304]{0:T(1024)(128)(4,1)S(1)}, s32[]{:S(2)}) async-start(s8[25165824]{0:T(1024)(128)(4,1)} %bitcast.2), calls=%async_computation | async-start | bytes 8388608
  0.0 18.1 %slice-start.1 = ((s8[25165824]{0:T(1024)(128)(4,1)}), s8[4194304]{0:T(1024)(128)(4,1)S(1)}, s32[]{:S(2)}) async-start(s8[25165824]{0:T(1024)(128)(4,1)} %bitcast.2), calls=%async_computation.1 | async-start | bytes 8388608
  0.0 18.1 %slice-start.2 = ((s8[25165824]{0:T(1024)(128)(4,1)}), s8[4194304]{0:T(1024)(128)(4,1)S(1)}, s32[]{:S(2)}) async-start(s8[25165824]{0:T(1024)(128)(4,1)} %bitcast.2), calls=%async_computation.2 | async-start | bytes 8388608
  0.0 18.1 %slice-start.3 = ((s8[25165824]{0:T(1024)(128)(4,1)}), s8[4194304]{0:T(1024)(128)(4,1)S(1)}, s32[]{:S(2)}) async-start(s8[25165824]{0:T(1024)(128)(4,1)} %bitcast.2), calls=%async_computation.3 | async-start | bytes 8388608
  0.0 18.1 %slice-start.4 = ((s8[25165824]{0:T(1024)(128)(4,1)}), s8[4194304]{0:T(1024)(128)(4,1)S(1)}, s32[]{:S(2)}) async-start(s8[25165824]{0:T(1024)(128)(4,1)} %bitcast.2), calls=%async_computation.4 | async-start | bytes 8388608
  1.1 9.2 %collective-permute-start.3 = (bf16[16,3200]{1,0:T(8,128)(2,1)S(1)}, bf16[16,3200]{1,0:T(8,128)(2,1)S(1)}, u32[]{:S(2)}, u32[]{:S(2)}) collective-permute-start(bf16[16,3200]{1,0:T(8,128)(2,1)S(1)} %shard_map.64.refs_0_), channel_id=1, source_target_pairs={{0,8},{2,10},{4,12},{6,14},{8,0},{10,2},{12,4},{14,6},{1,9},{3,11}... | collective-permute-start | bytes 307208 | tf_op jit(solution)/shard_map/ppermute | solution.py:17
  5.2 8.2 %collective-permute-start.2 = (bf16[16,3200]{1,0:T(8,128)(2,1)S(1)}, bf16[16,3200]{1,0:T(8,128)(2,1)S(1)}, u32[]{:S(2)}, u32[]{:S(2)}) collective-permute-start(bf16[16,3200]{1,0:T(8,128)(2,1)S(1)} %shard_map.64.refs_0_), channel_id=1, source_target_pairs={{0,6},{2,4},{4,2},{6,0},{8,14},{10,12},{12,10},{14,8},{1,7},{3,5},... | collective-permute-start | bytes 307208 | tf_op jit(solution)/shard_map/ppermute | solution.py:17
  7.8 9.8 %collective-permute-start.1 = (bf16[16,3200]{1,0:T(8,128)(2,1)S(1)}, bf16[16,3200]{1,0:T(8,128)(2,1)S(1)}, u32[]{:S(2)}, u32[]{:S(2)}) collective-permute-start(bf16[16,3200]{1,0:T(8,128)(2,1)S(1)} %shard_map.64.refs_0_), channel_id=1, source_target_pairs={{0,4},{2,6},{4,0},{6,2},{8,12},{10,14},{12,8},{14,10},{1,5},{3,7},... | collective-permute-start | bytes 307208 | tf_op jit(solution)/shard_map/ppermute | solution.py:17
  8.2 9.4 %collective-permute-start = (bf16[16,3200]{1,0:T(8,128)(2,1)S(1)}, bf16[16,3200]{1,0:T(8,128)(2,1)S(1)}, u32[]{:S(2)}, u32[]{:S(2)}) collective-permute-start(bf16[16,3200]{1,0:T(8,128)(2,1)S(1)} %shard_map.64.refs_0_), channel_id=1, source_target_pairs={{0,2},{2,0},{4,6},{6,4},{8,10},{10,8},{12,14},{14,12},{1,3},{3,1},... | collective-permute-start | bytes 307208 | tf_op jit(solution)/shard_map/ppermute | solution.py:17
  10.3 7.8 %slice-start.5 = ((s8[25165824]{0:T(1024)(128)(4,1)}), s8[4194304]{0:T(1024)(128)(4,1)S(1)}, s32[]{:S(2)}) async-start(s8[25165824]{0:T(1024)(128)(4,1)} %bitcast.2), calls=%async_computation.5 | async-start | bytes 8388608
  10.3 7.3 %collective-permute-start.6 = (bf16[16,3200]{1,0:T(8,128)(2,1)S(1)}, bf16[16,3200]{1,0:T(8,128)(2,1)S(1)}, u32[]{:S(2)}, u32[]{:S(2)}) collective-permute-start(bf16[16,3200]{1,0:T(8,128)(2,1)S(1)} %collective-permute-done.3.refs_4_), channel_id=1, source_target_pairs={{0,6},{2,4},{4,2},{6,0},{8,14},{10,12},{12,10},{14,8},{1,7},{3,5},... | collective-permute-start | bytes 307208 | tf_op jit(solution)/shard_map/ppermute | solution.py:17
  12.0 6.1 %collective-permute-start.5 = (bf16[16,3200]{1,0:T(8,128)(2,1)S(1)}, bf16[16,3200]{1,0:T(8,128)(2,1)S(1)}, u32[]{:S(2)}, u32[]{:S(2)}) collective-permute-start(bf16[16,3200]{1,0:T(8,128)(2,1)S(1)} %collective-permute-done.3.refs_4_), channel_id=1, source_target_pairs={{0,4},{2,6},{4,0},{6,2},{8,12},{10,14},{12,8},{14,10},{1,5},{3,7},... | collective-permute-start | bytes 307208 | tf_op jit(solution)/shard_map/ppermute | solution.py:17
  13.4 4.7 %collective-permute-start.4 = (bf16[16,3200]{1,0:T(8,128)(2,1)S(1)}, bf16[16,3200]{1,0:T(8,128)(2,1)S(1)}, u32[]{:S(2)}, u32[]{:S(2)}) collective-permute-start(bf16[16,3200]{1,0:T(8,128)(2,1)S(1)} %collective-permute-done.3.refs_4_), channel_id=1, source_target_pairs={{0,2},{2,0},{4,6},{6,4},{8,10},{10,8},{12,14},{14,12},{1,3},{3,1},... | collective-permute-start | bytes 307208 | tf_op jit(solution)/shard_map/ppermute | solution.py:17
  25.1 7.9 %collective-permute-start.7 = (f32[4224,128]{1,0:T(8,128)S(1)}, f32[4224,128]{1,0:T(8,128)S(1)}, u32[]{:S(2)}, u32[]{:S(2)}) collective-permute-start(f32[4224,128]{1,0:T(8,128)S(1)} %get-tuple-element.35.gate_a), channel_id=1, source_target_pairs={{0,1},{1,0},{2,3},{3,2},{4,5},{5,4},{6,7},{7,6},{8,9},{9,8},{10,11... | collective-permute-start | bytes 6488072 | tf_op jit(solution)/shard_map/ppermute | solution.py:239
  28.9 4.1 %collective-permute-start.9 = (bf16[2048,128]{1,0:T(8,128)(2,1)S(1)}, bf16[2048,128]{1,0:T(8,128)(2,1)S(1)}, u32[]{:S(2)}, u32[]{:S(2)}) collective-permute-start(bf16[2048,128]{1,0:T(8,128)(2,1)S(1)} %get-tuple-element.44), channel_id=1, source_target_pairs={{0,1},{1,0},{2,3},{3,2},{4,5},{5,4},{6,7},{7,6},{8,9},{9,8},{10,11... | collective-permute-start | bytes 1572872 | tf_op jit(solution)/shard_map/ppermute | solution.py:257
  32.9 2.9 %collective-permute-start.8 = (bf16[2048,128]{1,0:T(8,128)(2,1)S(1)}, bf16[2048,128]{1,0:T(8,128)(2,1)S(1)}, u32[]{:S(2)}, u32[]{:S(2)}) collective-permute-start(bf16[2048,128]{1,0:T(8,128)(2,1)S(1)} %get-tuple-element.42), channel_id=1, source_target_pairs={{0,1},{1,0},{2,3},{3,2},{4,5},{5,4},{6,7},{7,6},{8,9},{9,8},{10,11... | collective-permute-start | bytes 1572872 | tf_op jit(solution)/shard_map/ppermute | solution.py:257
  39.9 6.4 %collective-permute-start.13 = (bf16[16,3072]{1,0:T(8,128)(2,1)S(1)}, bf16[16,3072]{1,0:T(8,128)(2,1)S(1)}, u32[]{:S(2)}, u32[]{:S(2)}) collective-permute-start(bf16[16,3072]{1,0:T(8,128)(2,1)S(1)} %get-tuple-element.54), channel_id=1, source_target_pairs={{0,6},{2,4},{4,2},{6,0},{8,14},{10,12},{12,10},{14,8},{1,7},{3,5},... | collective-permute-start | bytes 294920 | tf_op jit(solution)/shard_map/ppermute | solution.py:17
  41.8 6.5 %collective-permute-start.14 = (bf16[16,3072]{1,0:T(8,128)(2,1)S(1)}, bf16[16,3072]{1,0:T(8,128)(2,1)S(1)}, u32[]{:S(2)}, u32[]{:S(2)}) collective-permute-start(bf16[16,3072]{1,0:T(8,128)(2,1)S(1)} %get-tuple-element.55), channel_id=1, source_target_pairs={{0,2},{2,0},{4,6},{6,4},{8,10},{10,8},{12,14},{14,12},{1,3},{3,1},... | collective-permute-start | bytes 294920 | tf_op jit(solution)/shard_map/ppermute | solution.py:17
  43.0 5.7 %collective-permute-start.15 = (bf16[16,3072]{1,0:T(8,128)(2,1)S(1)}, bf16[16,3072]{1,0:T(8,128)(2,1)S(1)}, u32[]{:S(2)}, u32[]{:S(2)}) collective-permute-start(bf16[16,3072]{1,0:T(8,128)(2,1)S(1)} %get-tuple-element.56), channel_id=1, source_target_pairs={{0,4},{2,6},{4,0},{6,2},{8,12},{10,14},{12,8},{14,10},{1,5},{3,7},... | collective-permute-start | bytes 294920 | tf_op jit(solution)/shard_map/ppermute | solution.py:17
  43.5 8.4 %collective-permute-start.10 = (bf16[16,3072]{1,0:T(8,128)(2,1)S(1)}, bf16[16,3072]{1,0:T(8,128)(2,1)S(1)}, u32[]{:S(2)}, u32[]{:S(2)}) collective-permute-start(bf16[16,3072]{1,0:T(8,128)(2,1)S(1)} %get-tuple-element.50), channel_id=1, source_target_pairs={{0,2},{2,0},{4,6},{6,4},{8,10},{10,8},{12,14},{14,12},{1,3},{3,1},... | collective-permute-start | bytes 294920 | tf_op jit(solution)/shard_map/ppermute | solution.py:17
  44.7 7.2 %collective-permute-start.11 = (bf16[16,3072]{1,0:T(8,128)(2,1)S(1)}, bf16[16,3072]{1,0:T(8,128)(2,1)S(1)}, u32[]{:S(2)}, u32[]{:S(2)}) collective-permute-start(bf16[16,3072]{1,0:T(8,128)(2,1)S(1)} %get-tuple-element.51), channel_id=1, source_target_pairs={{0,4},{2,6},{4,0},{6,2},{8,12},{10,14},{12,8},{14,10},{1,5},{3,7},... | collective-permute-start | bytes 294920 | tf_op jit(solution)/shard_map/ppermute | solution.py:17
  46.4 6.0 %collective-permute-start.12 = (bf16[16,3072]{1,0:T(8,128)(2,1)S(1)}, bf16[16,3072]{1,0:T(8,128)(2,1)S(1)}, u32[]{:S(2)}, u32[]{:S(2)}) collective-permute-start(bf16[16,3072]{1,0:T(8,128)(2,1)S(1)} %get-tuple-element.52), channel_id=1, source_target_pairs={{0,6},{2,4},{4,2},{6,0},{8,14},{10,12},{12,10},{14,8},{1,7},{3,5},... | collective-permute-start | bytes 294920 | tf_op jit(solution)/shard_map/ppermute | solution.py:17
  48.7 7.7 %collective-permute-start.16 = (bf16[16,3072]{1,0:T(8,128)(2,1)S(1)}, bf16[16,3072]{1,0:T(8,128)(2,1)S(1)}, u32[]{:S(2)}, u32[]{:S(2)}) collective-permute-start(bf16[16,3072]{1,0:T(8,128)(2,1)S(1)} %add_convert_fusion.1), channel_id=1, source_target_pairs={{0,8},{2,10},{4,12},{6,14},{8,0},{10,2},{12,4},{14,6},{1,9},{3,11}... | collective-permute-start | bytes 294920 | tf_op jit(solution)/shard_map/ppermute | solution.py:17
